TPU v7x, 32 devices: a whole 2x2x4 slice. The times are simulated.
32 devices in a mesh: lat: 8 (over z, y), fld: 4 (over x, core).
Axes of the slice: x: 2, y: 2, z: 4, core: 2. Of those that a mesh axis runs over, the one named last changes fastest.
Arguments:
- grid: bfloat16 [20, 8, 2, 5248], P('fld', 'lat'), may hold values from -6 to 6
- row_lengths: int32 [8], replicated, may hold values from 20 to 5136, as said below
- band_map: int32 [8], replicated, may hold values from 0 to 7, each once
- fold_map: int32 [32, 40], replicated, may hold values from 0 to 1279, as said below
- legendre: float32 [640, 1281, 8], P(('lat', 'fld')), may hold values from -1.5 to 1.5
- to_modes: float32 [20, 20], replicated, may hold values from -1.25 to 1.25
- back_modes: float32 [20, 20], replicated, may hold values from -1.25 to 1.25
- mode_rates: float32 [20], replicated, may hold values from 0.1 to 30
Outputs:
- spectral: float32 [20, 2, 640, 1281], P(None, None, ('lat', 'fld'))
- grid_out: bfloat16 [20, 8, 2, 5248], P('fld', 'lat')
Inputs may be any that keep to these rules, and one draw needn't show every extreme that they name: `row_lengths`: entry j is 20 + 4 i for an octahedral row index i with j * S <= i < (j + 1) * S, S = 160; entry 0 is 20 and the last entry is 5136; every entry is a multiple of 4. `fold_map`: every wavenumber 0 to 1279 stands exactly once; in every row, entries 2 s and 2 s + 1 are m and 1279 - m with m < 640. Row d lists the wavenumbers of the device with joined index d of lat+fld (lat index times the size of fld plus fld index). `band_map`: A permutation.
All inputs are finite; a program needn't handle non-finite values.
Results may differ from a plain program's by a relative error of at most 0.006.
Values sent between devices are 32-bit elements; how exact they have to be, the bound alone decides.
No kernel may reach another device: no remote copies, remote signals or barrier semaphores. Data moves between devices by JAX's collectives and lax.ppermute only.
A program may use at most 128 MiB of HBM per device.

v0:
```python
import math

import jax
import jax.numpy as jnp
from jax import lax
from jax.sharding import PartitionSpec as P

HIGH = lax.Precision.HIGHEST
TWO_PI = 2.0 * math.pi


def row_tables(length, quarter_pad, cut_off):
    quarter = length // 4
    top = jnp.minimum(cut_off, (length - 1) // 2)
    across = jnp.arange(quarter_pad, dtype=jnp.int32)[:, None]
    wave = jnp.arange(cut_off + 1, dtype=jnp.int32)[None, :]
    keep = (across < quarter) & (wave <= top)
    inner = (across * wave % quarter).astype(jnp.float32) * (TWO_PI / quarter.astype(jnp.float32))
    cos_table = jnp.where(keep, jnp.cos(inner), 0.0).astype(jnp.bfloat16)
    sin_table = jnp.where(keep, jnp.sin(inner), 0.0).astype(jnp.bfloat16)
    phase = jnp.arange(4, dtype=jnp.int32)[:, None]
    twist = (phase * wave % length).astype(jnp.float32) * (TWO_PI / length.astype(jnp.float32))
    weight = jnp.where(wave == 0, 1.0, 2.0) * (wave <= top).astype(jnp.float32)
    scale = 1.0 / jnp.sqrt(length.astype(jnp.float32))
    return (cos_table, sin_table, jnp.cos(twist), jnp.sin(twist), weight, scale)


def forward_row(values, length, cut_off):
    quarter_pad = values.shape[1] // 4
    cos_table, sin_table, cos_twist, sin_twist, weight, scale = row_tables(
        length, quarter_pad, cut_off
    )
    phases = jnp.stack([values[:, phase::4] for phase in range(4)], axis=0)
    real_part = jnp.einsum("bfa,am->bfm", phases, cos_table, preferred_element_type=jnp.float32)
    imag_part = -jnp.einsum("bfa,am->bfm", phases, sin_table, preferred_element_type=jnp.float32)
    cos_b = cos_twist[:, None, :]
    sin_b = sin_twist[:, None, :]
    four_re = scale * jnp.sum(cos_b * real_part + sin_b * imag_part, axis=0)
    four_im = scale * jnp.sum(cos_b * imag_part - sin_b * real_part, axis=0)
    return jnp.stack([four_re, four_im], axis=1)


def inverse_row(four, length, quarter_pad, cut_off):
    cos_table, sin_table, cos_twist, sin_twist, weight, scale = row_tables(
        length, quarter_pad, cut_off
    )
    fields = four.shape[0]
    cos_b = cos_twist[:, None, :]
    sin_b = sin_twist[:, None, :]
    four_re = (four[:, 0] * weight)[None]
    four_im = (four[:, 1] * weight)[None]
    twisted_re = (cos_b * four_re - sin_b * four_im).astype(jnp.bfloat16)
    twisted_im = (sin_b * four_re + cos_b * four_im).astype(jnp.bfloat16)
    total = jnp.einsum("bfm,am->bfa", twisted_re, cos_table, preferred_element_type=jnp.float32)
    total = total - jnp.einsum(
        "bfm,am->bfa", twisted_im, sin_table, preferred_element_type=jnp.float32
    )
    scaled = (scale * total).astype(jnp.bfloat16)
    return jnp.transpose(scaled, (1, 2, 0)).reshape(fields, quarter_pad * 4)


def pair_layout(first, cut_off):
    place = jnp.arange(cut_off + 2, dtype=jnp.int32)[None, :]
    start = first[:, None]
    second = cut_off - start
    partner = place > second
    degree = jnp.where(partner, place - 1, start + place)
    wave = jnp.where(partner, second, start)
    odd = (degree + wave) % 2 == 1
    return (partner, odd, degree)


def direct_legendre(sym, asym, table, partner, odd):
    nlat, fields, two, slots = sym.shape
    pairs = slots // 2
    both = jnp.stack([sym, asym], axis=1).reshape(nlat, 2, fields, 2, pairs, 2)
    stacked = jnp.transpose(both, (4, 0, 5, 1, 2, 3)).reshape(pairs, nlat, 8 * fields)
    raw = jnp.einsum("pqj,pjx->pqx", table, stacked, precision=HIGH)
    raw = raw.reshape(pairs, table.shape[1], 2, 2, fields, 2)
    pick = jnp.where(partner[:, :, None, None, None], raw[:, :, 1], raw[:, :, 0])
    pick = jnp.where(odd[:, :, None, None], pick[:, :, 1], pick[:, :, 0])
    return jnp.transpose(pick, (2, 3, 0, 1))


def inverse_legendre(spectral, table, partner, odd):
    fields = spectral.shape[0]
    pairs, places, nlat = table.shape
    coef = jnp.transpose(spectral, (2, 3, 0, 1))
    parts = []
    for chosen in (jnp.logical_not(partner), partner):
        for parity in (jnp.logical_not(odd), odd):
            parts.append(jnp.where((chosen & parity)[:, :, None, None], coef, 0.0))
    spread = jnp.stack(parts, axis=2).reshape(pairs, places, 8 * fields)
    sums = jnp.einsum("pqj,pqx->pjx", table, spread, precision=HIGH).reshape(
        pairs, nlat, 2, 2, fields, 2
    )
    north = sums[:, :, :, 0] + sums[:, :, :, 1]
    south = sums[:, :, :, 0] - sums[:, :, :, 1]
    north = jnp.transpose(north, (1, 3, 4, 0, 2)).reshape(nlat, fields, 2, 2 * pairs)
    south = jnp.transpose(south, (1, 3, 4, 0, 2)).reshape(nlat, fields, 2, 2 * pairs)
    return (north, south)


def implicit_solve(raw, degree, cut_off, to_modes, back_modes, mode_rates):
    modes = jnp.einsum("kf,fcpq->kcpq", to_modes, raw, precision=HIGH)
    tau = (degree * (degree + 1)).astype(jnp.float32) / float(cut_off * (cut_off + 1))
    damped = modes / (1.0 + tau[None, None] * mode_rates[:, None, None, None])
    return jnp.einsum("gk,kcpq->gcpq", back_modes, damped, precision=HIGH)


def per_device(grid, row_lengths, band_map, fold_map, legendre, to_modes, back_modes, mode_rates):
    fields, single, rows, width = grid.shape
    lat_dev = rows // 2
    quarter_pad = width // 4
    pairs, places, nlat = legendre.shape
    cut_off = places - 2
    lat_count = lax.axis_size("lat")
    fld_count = lax.axis_size("fld")
    per_owner = fold_map.shape[1]
    everyone = fields * fld_count
    band = band_map[lax.axis_index("lat")]
    mine = band * lat_dev + jnp.arange(rows, dtype=jnp.int32) % lat_dev
    lengths = row_lengths[mine]
    values = jnp.transpose(grid[:, 0], (1, 0, 2))
    four = lax.map(lambda item: forward_row(item[0], item[1], cut_off), (values, lengths))
    order = fold_map.reshape(-1)
    sending = jnp.take(four, order, axis=3)
    sending = sending.reshape(rows, fields, 2, lat_count, fld_count, per_owner)
    arrived = lax.all_to_all(
        lax.all_to_all(sending, "lat", split_axis=3, concat_axis=0, tiled=True),
        "fld",
        split_axis=4,
        concat_axis=1,
        tiled=True,
    )
    arrived = arrived.reshape(lat_count, rows, everyone, 2, per_owner)
    band_ids = jnp.arange(lat_count, dtype=jnp.int32)
    holder = jnp.sum(
        jnp.where(band_map[:, None] == band_ids[None, :], band_ids[:, None], 0), axis=0
    )
    by_band = jnp.take(arrived, holder, axis=0)
    north = by_band[:, :lat_dev].reshape(nlat, everyone, 2, per_owner)
    south = by_band[:, lat_dev:].reshape(nlat, everyone, 2, per_owner)
    owner = lax.axis_index(("lat", "fld"))
    first = lax.dynamic_index_in_dim(fold_map, owner, 0, keepdims=False)[0::2]
    partner, odd, degree = pair_layout(first, cut_off)
    raw = direct_legendre(north + south, north - south, legendre, partner, odd)
    spectral = implicit_solve(raw, degree, cut_off, to_modes, back_modes, mode_rates)
    north_back, south_back = inverse_legendre(spectral, legendre, partner, odd)
    rows_back = jnp.concatenate(
        [
            north_back.reshape(lat_count, lat_dev, everyone, 2, per_owner),
            south_back.reshape(lat_count, lat_dev, everyone, 2, per_owner),
        ],
        axis=1,
    )
    rows_back = jnp.take(rows_back, band_map, axis=0)
    leaving = rows_back.reshape(lat_count, rows, fld_count, fields, 2, 1, 1, per_owner)
    returned = lax.all_to_all(
        lax.all_to_all(leaving, "lat", split_axis=0, concat_axis=5, tiled=True),
        "fld",
        split_axis=2,
        concat_axis=6,
        tiled=True,
    )
    returned = returned.reshape(rows, fields, 2, lat_count * fld_count * per_owner)
    back_four = jnp.zeros((rows, fields, 2, cut_off + 1), jnp.float32).at[..., order].set(returned)
    outgoing = lax.map(
        lambda item: inverse_row(item[0], item[1], quarter_pad, cut_off), (back_four, lengths)
    )
    grid_out = jnp.transpose(outgoing, (1, 0, 2))[:, None]
    return (spectral, grid_out)


def solution(mesh):
    placed = (
        P("fld", "lat", None, None),
        P(),
        P(),
        P(),
        P(("lat", "fld"), None, None),
        P(),
        P(),
        P(),
    )
    return jax.shard_map(
        per_device,
        mesh=mesh,
        in_specs=placed,
        out_specs=(P(None, None, ("lat", "fld"), None), P("fld", "lat", None, None)),
        check_vma=False,
    )
```

profile of v0, /device:TPU:0, one launch (start us, length us, event | category | flops | bytes accessed | tf_op | source)
XLA Modules:
  0.0 1153.0 jit_solution(2621772154810145874)
XLA Ops:
  6.2 403.3 %while.26 = (s32[]{:T(128)}, f32[2,5,2,1280]{3,2,1,0:T(2,128)S(1)}, s32[2]{0:T(128)S(1)}, bf16[2,5,5248]{2,1,0:T(8,128)(2,1)S(1)}, s32[]{:T(128)}, /*index=5*/f3...) while((s32[]{:T(128)}, f32[2,5,2,1280]{3,2,1,0:T(2,128)S(1)}, ...), condition=%wide.region_3.4_spmd, body=%wide.region_0.3_spmd.sunk | while | flops 178466624 | bytes 968382 | solution.py:125
  12.8 95.9 %fusion.139 = f32[4,5,1280]{2,1,0:T(8,128)S(1)} fusion(f32[]{:T(128)S(6)} %div.104, s32[]{:T(128)S(6)} %select_n.527, pred[]{:T(512)S(6)} %lt.288, pred[1280]{0:T(1024)(128)(4,1)S(1)} %iota_compare_fusion.11, pred[1312]{0:T(1024)(128)(4,1)S(1)} %iota_compare_fusion.12, bf16[1,5,1312]{2,1,0:T(8,128)(2,1)S(1)} %bitcast.247, ...), kind=kOutput, calls=%fused_computation.19.clone.1 | convolution fusion | flops 89084800 | bytes 157481 | tf_op jit(solution)/shard_map/while/body/eval_jaxpr/bfa,am->bfm/dot_general | solution.py:34
  111.3 96.2 %add_reduce_fusion.2 = (f32[5,1280]{1,0:T(8,128)S(1)}, f32[5,1280]{1,0:T(8,128)S(1)}) fusion(f32[4,5,1280]{2,1,0:T(8,128)S(1)} %fusion.139, f32[4,1280]{1,0:T(4,128)S(1)} %get-tuple-element.297, f32[4,1280]{1,0:T(4,128)S(1)} %get-tuple-element.298, f32[]{:T(128)S(6)} %div.104, s32[]{:T(128)S(6)} %select_n.527, pred[]{:T(512)S(6)} %lt.288, ...), kind=kOutput, calls=%fused_computation.27.clone.1 | convolution fusion | flops 89302400 | bytes 249641 | tf_op jit(solution)/shard_map/while/body/eval_jaxpr/bfa,am->bfm/dot_general | solution.py:35
  214.3 95.9 %fusion.139 = f32[4,5,1280]{2,1,0:T(8,128)S(1)} fusion(f32[]{:T(128)S(6)} %div.104, s32[]{:T(128)S(6)} %select_n.527, pred[]{:T(512)S(6)} %lt.288, pred[1280]{0:T(1024)(128)(4,1)S(1)} %iota_compare_fusion.11, pred[1312]{0:T(1024)(128)(4,1)S(1)} %iota_compare_fusion.12, bf16[1,5,1312]{2,1,0:T(8,128)(2,1)S(1)} %bitcast.247, ...), kind=kOutput, calls=%fused_computation.19.clone.1 | convolution fusion | flops 89084800 | bytes 157481 | tf_op jit(solution)/shard_map/while/body/eval_jaxpr/bfa,am->bfm/dot_general | solution.py:34
  312.8 96.2 %add_reduce_fusion.2 = (f32[5,1280]{1,0:T(8,128)S(1)}, f32[5,1280]{1,0:T(8,128)S(1)}) fusion(f32[4,5,1280]{2,1,0:T(8,128)S(1)} %fusion.139, f32[4,1280]{1,0:T(4,128)S(1)} %get-tuple-element.297, f32[4,1280]{1,0:T(4,128)S(1)} %get-tuple-element.298, f32[]{:T(128)S(6)} %div.104, s32[]{:T(128)S(6)} %select_n.527, pred[]{:T(512)S(6)} %lt.288, ...), kind=kOutput, calls=%fused_computation.27.clone.1 | convolution fusion | flops 89302400 | bytes 249641 | tf_op jit(solution)/shard_map/while/body/eval_jaxpr/bfa,am->bfm/dot_general | solution.py:35
  413.2 5.8 gather_fusion.1
  419.0 3.1 copy.99
  423.6 7.3 all-to-all-start
  441.2 3.3 all-to-all-start.1
  444.6 4.3 all-to-all-done.1
  453.0 16.9 %convolution_bitcast_fusion = f32[20,1281,160]{1,2,0:T(8,128)} fusion(f32[20,8,160]{2,1,0:T(8,128)S(1)} %copy.105, f32[20,1281,8]{1,2,0:T(8,128)S(1)} %copy-done), kind=kOutput, calls=%fused_computation.111 | convolution fusion | flops 393523200 | bytes 17319040 | tf_op jit(solution)/shard_map/pqj,pjx->pqx/dot_general | solution.py:78
  469.9 21.2 %reshape.726 = f32[20,1281,2,2,20,2]{1,5,4,3,2,0:T(2,128)} reshape(f32[20,1281,160]{1,2,0:T(8,128)} %convolution_bitcast_fusion) | data formatting | bytes 32793600 | tf_op jit(solution)/shard_map/reshape | solution.py:79
  491.1 16.6 %fusion.112 = (f32[20,1281,1,2,20,2]{1,5,4,3,2,0:T(2,128)}, f32[20,1281,1,2,20,2]{1,5,4,3,2,0:T(2,128)}) fusion(f32[20,1281,2,2,20,2]{1,5,4,3,2,0:T(2,128)} %reshape.726), kind=kLoop, calls=%fused_computation.175 | loop fusion | bytes 32793600 | tf_op jit(solution)/shard_map/slice | solution.py:80
  507.7 11.8 %fusion.92 = f32[20,1281,2,20,2]{1,3,0,4,2:T(8,128)} fusion(f32[20,1281,1,2,20,2]{1,5,4,3,2,0:T(2,128)} %get-tuple-element.228, f32[20,1281,1,2,20,2]{1,5,4,3,2,0:T(2,128)} %get-tuple-element.227, pred[20,1281]{1,0:T(8,128)(4,1)S(1)} %get-tuple-element.242), kind=kLoop, calls=%fused_computation.113 | loop fusion | flops 2049600 | bytes 24620820 | tf_op jit(solution)/shard_map/jit(_where)/select_n | solution.py:80
  519.5 8.4 fusion.95
  527.9 5.3 fusion.97
  533.2 3.9 select_bitcast_fusion.3
  537.2 9.6 pad_maximum_fusion.3
  546.9 26.2 %copy.108 = f32[20,1281,4,20,2]{1,4,3,2,0:T(2,128)} copy(f32[20,1281,4,20,2]{1,3,0,4,2:T(8,128)} %pad_maximum_fusion.3) | data formatting | bytes 32793600 | tf_op jit(solution)/shard_map/stack | solution.py:93
  573.1 22.2 %reshape.727 = f32[20,1281,160]{1,2,0:T(8,128)} reshape(f32[20,1281,4,20,2]{1,4,3,2,0:T(2,128)} %copy.108) | data formatting | bytes 32793600 | tf_op jit(solution)/shard_map/reshape | solution.py:93
  595.3 18.7 %convolution_bitcast_fusion.1 = f32[20,8,160]{2,1,0:T(8,128)S(1)} fusion(f32[20,1281,160]{1,2,0:T(8,128)} %reshape.727, f32[20,1281,8]{1,2,0:T(8,128)S(1)} %copy-done), kind=kOutput, calls=%fused_computation.129 | convolution fusion | flops 393523200 | bytes 17319040 | tf_op jit(solution)/shard_map/pqj,pqx->pjx/dot_general | solution.py:94
  619.2 10.2 all_to_all.66
  631.9 3.8 all-to-all-start.3
  635.7 8.1 copy.121
  649.1 90.9 %scatter_fusion = f32[2,5,2,1280]{1,2,3,0:T(2,128)S(1)} fusion(f32[2,5,2,1280]{1,2,3,0:T(2,128)S(1)} %broadcast.902, s32[1280]{0:T(1024)S(1)} %fusion.111, f32[1280,2,5,2]{2,3,1,0:T(2,128)} %copy.118), kind=kCustom, calls=%fused_computation.4 | custom fusion | bytes 312320 | tf_op jit(solution)/shard_map/scatter | solution.py:167
  742.0 408.9 %while.27 = (s32[]{:T(128)}, bf16[2,5,5248]{2,1,0:T(8,128)(2,1)}, s32[2]{0:T(128)S(1)}, f32[2,5,2,1280]{3,1,2,0:T(8,128)}, s32[]{:T(128)}, /*index=5*/f32[]{:T(1...) while((s32[]{:T(128)}, bf16[2,5,5248]{2,1,0:T(8,128)(2,1)}, s32[2]{0:T(128)S(1)}, ...), condition=%wide.region_7.9_spmd, body=%wide.region_6.8_spmd.sunk | while | flops 178367424 | bytes 2133494 | solution.py:168
  749.7 95.5 %fusion.148 = f32[4,5,1312]{2,1,0:T(8,128)S(1)} fusion(f32[]{:T(128)S(6)} %div.112, s32[]{:T(128)S(6)} %select_n.537, pred[]{:T(512)S(6)} %lt.295, pred[1280]{0:T(1024)(128)(4,1)S(1)} %iota_compare_fusion.13, pred[1312]{0:T(1024)(128)(4,1)S(1)} %iota_compare_fusion.14, bf16[4,5,1280]{2,1,0:T(8,128)(2,1)S(1)} %subtract_convert_fusion.7), kind=kOutput, calls=%fused_computation.66.clone.3 | convolution fusion | flops 89006080 | bytes 158761 | tf_op jit(solution)/shard_map/while/body/eval_jaxpr/bfm,am->bfa/dot_general | solution.py:54
  845.3 95.9 %fusion.149 = bf16[5,1312,4]{1,0,2:T(8,128)(2,1)S(1)} fusion(f32[4,5,1312]{2,1,0:T(8,128)S(1)} %fusion.148, f32[]{:T(128)S(6)} %div.112, s32[]{:T(128)S(6)} %select_n.537, pred[]{:T(512)S(6)} %lt.295, pred[1280]{0:T(1024)(128)(4,1)S(1)} %iota_compare_fusion.13, pred[1312]{0:T(1024)(128)(4,1)S(1)} %iota_compare_fusion.14, f32[]{:T(128)S(6)} %sqrt.9, ...), kind=kOutput, calls=%fused_computation.75.clone.3 | convolution fusion | flops 89084800 | bytes 211245 | tf_op jit(solution)/shard_map/while/body/eval_jaxpr/bfm,am->bfa/dot_general | solution.py:55
  942.6 3.3 broadcast_in_dim.268
  954.1 95.5 %fusion.148 = f32[4,5,1312]{2,1,0:T(8,128)S(1)} fusion(f32[]{:T(128)S(6)} %div.112, s32[]{:T(128)S(6)} %select_n.537, pred[]{:T(512)S(6)} %lt.295, pred[1280]{0:T(1024)(128)(4,1)S(1)} %iota_compare_fusion.13, pred[1312]{0:T(1024)(128)(4,1)S(1)} %iota_compare_fusion.14, bf16[4,5,1280]{2,1,0:T(8,128)(2,1)S(1)} %subtract_convert_fusion.7), kind=kOutput, calls=%fused_computation.66.clone.3 | convolution fusion | flops 89006080 | bytes 158761 | tf_op jit(solution)/shard_map/while/body/eval_jaxpr/bfm,am->bfa/dot_general | solution.py:54
  1049.7 95.9 %fusion.149 = bf16[5,1312,4]{1,0,2:T(8,128)(2,1)S(1)} fusion(f32[4,5,1312]{2,1,0:T(8,128)S(1)} %fusion.148, f32[]{:T(128)S(6)} %div.112, s32[]{:T(128)S(6)} %select_n.537, pred[]{:T(512)S(6)} %lt.295, pred[1280]{0:T(1024)(128)(4,1)S(1)} %iota_compare_fusion.13, pred[1312]{0:T(1024)(128)(4,1)S(1)} %iota_compare_fusion.14, f32[]{:T(128)S(6)} %sqrt.9, ...), kind=kOutput, calls=%fused_computation.75.clone.3 | convolution fusion | flops 89084800 | bytes 211245 | tf_op jit(solution)/shard_map/while/body/eval_jaxpr/bfm,am->bfa/dot_general | solution.py:55
  1146.9 3.3 broadcast_in_dim.268
  (149 shorter events, 55.9 us)
Async XLA Ops:
  0.6 452.3 %copy-start = (f32[20,1281,8]{1,2,0:T(8,128)S(1)}, f32[20,1281,8]{1,2,0:T(8,128)}, u32[]{:S(2)}) copy-start(f32[20,1281,8]{1,2,0:T(8,128)} %param.18) | copy-start | bytes 2459524
  6.2 406.9 %copy-start.6 = (s32[32,40]{1,0:T(8,128)S(1)}, s32[32,40]{1,0:T(8,128)}, u32[]{:S(2)}) copy-start(s32[32,40]{1,0:T(8,128)} %param.17) | copy-start | bytes 15364
  409.5 0.6 copy-start.5
  410.2 0.5 copy-start.8
  419.0 16.2 %copy-start.11 = (s32[8]{0:T(128)S(1)}, s32[8]{0:T(128)}, u32[]{:S(2)}) copy-start(s32[8]{0:T(128)} %param.16) | copy-start | bytes 100
  423.6 14.4 %all-to-all-start = ((f32[8,1,3200]{2,1,0:T(1,128)}), f32[8,1,3200]{2,1,0:T(1,128)S(1)}, u32[]{:S(2)}, u32[]{:S(2)}) async-start(f32[8,1,3200]{2,1,0:T(1,128)} %reshape.784), calls=%async_computation | async-start | bytes 204800 | tf_op jit(solution)/shard_map/all_to_all | solution.py:130
  441.2 7.6 all-to-all-start.1
  507.7 11.8 %copy-start.7 = (f32[20,20]{1,0:T(8,128)S(1)}, f32[20,20]{1,0:T(8,128)}, u32[]{:S(2)}) copy-start(f32[20,20]{1,0:T(8,128)} %param.19) | copy-start | bytes 4804
  519.5 8.5 copy-start.2
  519.5 8.5 copy-start.10
  533.2 4.0 copy-start.1
  631.9 11.9 %all-to-all-start.3 = ((f32[4,1,6400]{2,1,0:T(1,128)}), f32[4,1,6400]{2,1,0:T(1,128)S(1)}, u32[]{:S(2)}, u32[]{:S(2)}) async-start(f32[4,1,6400]{2,1,0:T(1,128)} %reshape.790), calls=%async_computation.3 | async-start | bytes 204800 | tf_op jit(solution)/shard_map/all_to_all | solution.py:159
  643.9 98.2 %copy-start.9 = (s32[2]{0:T(128)S(1)}, s32[2]{0:T(128)}, u32[]{:S(2)}) copy-start(s32[2]{0:T(128)} %copy-done.8) | copy-start | bytes 28
  845.3 100.6 %copy-start.3 = (bf16[2,5,5248]{2,1,0:T(8,128)(2,1)S(1)}, bf16[2,5,5248]{2,1,0:T(8,128)(2,1)}, u32[]{:S(2)}) copy-start(bf16[2,5,5248]{2,1,0:T(8,128)(2,1)} %get-tuple-element.354) | copy-start | bytes 314884 | tf_op jit(solution)/shard_map/while
  945.9 0.7 copy-start.4
  1049.7 100.6 %copy-start.3 = (bf16[2,5,5248]{2,1,0:T(8,128)(2,1)S(1)}, bf16[2,5,5248]{2,1,0:T(8,128)(2,1)}, u32[]{:S(2)}) copy-start(bf16[2,5,5248]{2,1,0:T(8,128)(2,1)} %get-tuple-element.354) | copy-start | bytes 314884 | tf_op jit(solution)/shard_map/while
  1150.3 0.7 copy-start.4
where the time goes:
time: 1180 us; the launch traced here: 1150 us
  matrix products  816 us (69%)
  local copies, waits for them, and re-layouts  240 us (20%)
  other arithmetic  39 us (3%)
  loops' own time  22.3 us (2%)
  starting transfers between devices  14.4 us (1%)
    dot_general x2, matrix products, forward_row(): jnp.einsum('bfa,am->bfm', phases, sin_table, preferred_element_type=jnp.f...  192 us
    dot_general x2, matrix products, forward_row(): jnp.einsum('bfa,am->bfm', phases, cos_table, preferred_element_type=jnp.f...  192 us
    dot_general x2, matrix products, inverse_row(): jnp.einsum('bfm,am->bfa', twisted_im, sin_table, preferred_element_type=j...  192 us
    dot_general x2, matrix products, inverse_row(): jnp.einsum('bfm,am->bfa', twisted_re, cos_table, preferred_element_type=j...  191 us
    scatter x1, local copies, waits for them, and re-layouts, per_device(): jnp.zeros((rows, fields, 2, cut_off + 1), jnp.float32).at[..., order]  90.9 us
    another operation x1, local copies, waits for them, and re-layouts, inverse_legendre(): spread = jnp.stack(parts, axis=2).reshape(pairs, places, 8 * fields)  26.2 us
  transfers between devices with their start and end apart: 3, of which 2 were waited for; matrix products, arithmetic and copies ran while one was open for 1% of the time, Pallas kernels for 0%

commit v1 on v0

v1 whole, which is shorter than its diff:
```python
import functools
import math

import jax
import jax.numpy as jnp
from jax import lax
from jax.experimental import pallas as pl
from jax.experimental.pallas import tpu as pltpu
from jax.sharding import PartitionSpec as P

LANES = 128
KPAD = 24
FPAD = 64
F32 = jnp.float32
BF16 = jnp.bfloat16
NT_DIMS = (((1,), (1,)), ((), ()))
SIN_POLY = (
    6.283185302447051,
    -41.34170038368319,
    81.60513023312113,
    -76.70299324464969,
    42.02573766814694,
    -14.899106966102595,
    3.237062655726421,
)
COS_POLY = (
    0.9999999889083757,
    -19.739204448887243,
    64.93911476570418,
    -85.45008785413638,
    60.167188450194914,
    -25.9658703083255,
    6.526145851512229,
)


def dot(a, b):
    return jnp.dot(a, b, preferred_element_type=F32)


def dot_nt(a, b):
    return lax.dot_general(a, b, NT_DIMS, preferred_element_type=F32)


def split(x):
    high = x.astype(BF16)
    return high, (x - high.astype(F32)).astype(BF16)


def horner(coefs, z):
    total = coefs[-1] * z + coefs[-2]
    for coef in coefs[-3::-1]:
        total = total * z + coef
    return total


def turn(steps, period, inverse):
    rest = steps - period * jnp.floor(steps * inverse + 0.5)
    part = rest * inverse
    z = part * part
    return horner(COS_POLY, z), part * horner(SIN_POLY, z)


def lane_iota(shape):
    return lax.broadcasted_iota(jnp.int32, shape, len(shape) - 1)


def row_iota(shape):
    return lax.broadcasted_iota(jnp.int32, shape, len(shape) - 2)


def spread_matrix():
    shape = (4 * LANES, LANES)
    picks = []
    for phase in range(4):
        picks.append(jnp.where(row_iota(shape) == 4 * lane_iota(shape) + phase, 1.0, 0.0))
    return jnp.concatenate(picks, axis=1).astype(BF16)


def forward_kernel(
    cut_off, groups, len_ref, band_ref, fold_ref, grid_ref,
    msg_ref, cos_ref, sin_ref, k1_ref, k2_ref, fold_s, mb, cb, sb, xs, xq, ys,
):
    fields, _, rows, width = grid_ref.shape
    owners, per_owner = fold_ref.shape
    slots, across = cos_ref.shape
    chunks = across // LANES
    padded = groups * 8
    unit = rows * fields * 2
    length = len_ref[band_ref[lax.axis_index("lat")]]
    top = jnp.minimum(cut_off, (length - 1) // 2)

    fold_s[...] = jnp.full(fold_s.shape, -1.0, F32)
    fold_s[0:owners, 0:per_owner] = fold_ref[...].astype(F32)
    waves = jnp.transpose(fold_s[...])[0:padded]
    small = waves.shape
    period = jnp.full(small, length // 4, jnp.int32).astype(F32)
    step_c, step_s = turn(waves * float(LANES), period, 1.0 / period)
    for owner in range(owners):
        put = pl.ds(owner * padded, padded)
        wide = (padded, LANES)
        mb[put, :] = jnp.broadcast_to(waves[:, owner:owner + 1], wide)
        cb[put, :] = jnp.broadcast_to(step_c[:, owner:owner + 1], wide)
        sb[put, :] = jnp.broadcast_to(step_s[:, owner:owner + 1], wide)

    xs[...] = jnp.zeros(xs.shape, F32)
    inside = lane_iota((rows, width)) < length
    for field in range(fields):
        points = grid_ref[field, 0].astype(F32)
        xs[rows * field:rows * (field + 1), 0:width] = jnp.where(inside, points, 0.0)
    stacked = jnp.concatenate(
        [xs[:, 4 * LANES * c:4 * LANES * (c + 1)] for c in range(chunks)], axis=0
    ).astype(BF16)
    phases = dot(stacked, spread_matrix()).astype(BF16)
    for c in range(chunks):
        for phase in range(4):
            piece = phases[16 * c:16 * (c + 1), LANES * phase:LANES * (phase + 1)]
            for half in (0, 64):
                xq[half + 16 * phase:half + 16 * (phase + 1), LANES * c:LANES * (c + 1)] = piece

    block = 32
    shape = (block, LANES)
    lane = lane_iota(shape)
    lane_f = lane.astype(F32)
    phase_f = ((lane % 64) // 16).astype(F32)
    quarter_v = jnp.full(shape, length // 4, jnp.int32).astype(F32)
    quarter_i = 1.0 / quarter_v
    length_v = jnp.full(shape, length, jnp.int32).astype(F32)
    length_i = 1.0 / length_v
    top_v = jnp.full(shape, top, jnp.int32).astype(F32)

    def table_block(i, carry):
        at = pl.ds(pl.multiple_of(i * block, block), block)
        wave = mb[at, :]
        c1 = cb[at, :]
        s1 = sb[at, :]
        c_old, s_old = turn(wave * lane_f, quarter_v, quarter_i)
        c_now = c_old * c1 - s_old * s1
        s_now = s_old * c1 + c_old * s1
        twice = c1 + c1
        cos_ref[at, 0:LANES] = c_old.astype(BF16)
        sin_ref[at, 0:LANES] = s_old.astype(BF16)
        for c in range(1, chunks):
            cos_ref[at, LANES * c:LANES * (c + 1)] = c_now.astype(BF16)
            sin_ref[at, LANES * c:LANES * (c + 1)] = s_now.astype(BF16)
            c_old, c_now = c_now, twice * c_now - c_old
            s_old, s_now = s_now, twice * s_now - s_old
        co, si = turn(wave * phase_f, length_v, length_i)
        weight = jnp.where(wave == 0.0, 1.0, 2.0)
        weight = jnp.where((wave >= 0.0) & (wave <= top_v), weight, 0.0)
        upper = lane >= 64
        k1_ref[at, :] = jnp.where(upper, -si, co) * weight
        k2_ref[at, :] = jnp.where(upper, co, si) * weight
        return carry

    lax.fori_loop(0, slots // block, table_block, 0)

    big = 256
    values = xq[...]

    def dot_block(i, carry):
        at = pl.ds(pl.multiple_of(i * big, big), big)
        both = jnp.concatenate([cos_ref[at, :], sin_ref[at, :]], axis=0)
        inner = dot_nt(both, values)
        fix = jnp.where(mb[at, :] == 0.0, 1.0, 0.5)
        ys[at, :] = (inner[0:big] * k1_ref[at, :] - inner[big:2 * big] * k2_ref[at, :]) * fix
        return carry

    lax.fori_loop(0, slots // big, dot_block, 0)

    turned = ys[...].reshape(owners, groups, 8, LANES)
    shape = (LANES, LANES)
    source = row_iota(shape)
    target = lane_iota(shape)
    vec = source % 16
    base = (vec % rows) * (fields * 2) + (vec // rows) * 2 + source // 64
    total = jnp.zeros((owners * 8, LANES), F32)
    for t in range(groups):
        place = jnp.where((vec < rows * fields) & (target == base + unit * t), 1.0, 0.0).astype(BF16)
        high, low = split(turned[:, t].reshape(owners * 8, LANES))
        total = total + dot(
            jnp.concatenate([high, low], axis=1), jnp.concatenate([place, place], axis=0)
        )
    scale = 1.0 / jnp.sqrt(jnp.full((owners * 8, LANES), length, jnp.int32).astype(F32))
    msg_ref[...] = (total * scale).reshape(owners, 8, LANES)


def inverse_kernel(
    groups, len_ref, band_ref, msg_ref, cos_ref, sin_ref, k1_ref, k2_ref, grid_ref, zs, os,
):
    fields, _, rows, width = grid_ref.shape
    owners = msg_ref.shape[0]
    slots, across = cos_ref.shape
    chunks = across // LANES
    unit = rows * fields * 2
    length = len_ref[band_ref[lax.axis_index("lat")]]
    high, low = split(msg_ref[...].reshape(owners * 8, LANES))
    pieces = jnp.concatenate([high, low], axis=1)
    shape = (LANES, 2 * LANES)
    source = row_iota(shape)
    target = lane_iota(shape)
    vec = target % 16
    upper = (target % LANES) >= 64
    imag = target >= LANES
    base = (vec % rows) * (fields * 2) + (vec // rows) * 2 + jnp.where(imag, 1, 0)
    sign = jnp.where(upper != imag, -1.0, 1.0)
    factor_a = k1_ref[...].reshape(owners, groups, 8, LANES)
    factor_b = k2_ref[...].reshape(owners, groups, 8, LANES)
    for t in range(groups):
        place = jnp.where((vec < rows * fields) & (source == base + unit * t), sign, 0.0).astype(BF16)
        both = dot(pieces, jnp.concatenate([place, place], axis=0))
        z = (
            both[:, 0:LANES] * factor_a[:, t].reshape(owners * 8, LANES)
            + both[:, LANES:] * factor_b[:, t].reshape(owners * 8, LANES)
        )
        zs[:, t] = z.reshape(owners, 8, LANES)
    turned = jnp.transpose(zs[...].reshape(slots, LANES)).astype(BF16)
    real = turned[0:64]
    imag_part = turned[64:128]
    scale = 1.0 / jnp.sqrt(jnp.full((64, 2 * LANES), length, jnp.int32).astype(F32))
    for start in range(0, across, 2 * LANES):
        size = min(2 * LANES, across - start)
        total = dot(real, cos_ref[:, start:start + size]) - dot(imag_part, sin_ref[:, start:start + size])
        out = total * scale[:, 0:size]
        for phase in range(4):
            for sub in range(size // LANES):
                c = start // LANES + sub
                os[16 * c:16 * (c + 1), LANES * phase:LANES * (phase + 1)] = out[
                    16 * phase:16 * (phase + 1), LANES * sub:LANES * (sub + 1)
                ].astype(BF16)
    merged = dot_nt(os[...], spread_matrix())
    for c in range(chunks):
        begin = 4 * LANES * c
        size = min(4 * LANES, width - begin)
        if size <= 0:
            continue
        inside = begin + lane_iota((16, size)) < length
        piece = jnp.where(inside, merged[16 * c:16 * (c + 1), 0:size], 0.0)
        for field in range(fields):
            grid_ref[field, 0, :, begin:begin + size] = piece[
                rows * field:rows * (field + 1)
            ].astype(BF16)


def spectral_kernel(
    cut_off, pairs, fields, rows, band_ref, fold_ref, rates_ref, msg_ref, leg_ref, tm_ref, bm_ref,
    spec_ref, out_ref, vs, fq, bk, pad_s, eh, sq, cs,
):
    everyone = tm_ref.shape[0]
    quad, lats, places = leg_ref.shape
    holders = band_ref.shape[0]
    groups_f = everyone // fields
    groups = fq.shape[0] // (4 * KPAD)
    wf = fields * 2
    unit = rows * wf
    span = eh.shape[1]
    step = pl.program_id(0)
    owner = lax.axis_index("lat") * groups_f + lax.axis_index("fld")
    eight = 8 * lats

    @pl.when(step == 0)
    def _():
        for holder in range(holders):
            lat = band_ref[holder]
            for g in range(groups_f):
                vs[pl.ds(pl.multiple_of((g * lats + lat) * 8, 8), 8), :] = msg_ref[holder * groups_f + g]
        tall = []
        for i8 in range(8):
            tall.append(
                jnp.concatenate(
                    [vs[pl.ds(g * lats * 8 + i8, lats, stride=8), :] for g in range(groups_f)], axis=1
                )
            )
        v_high, v_low = split(jnp.concatenate(tall, axis=0))
        pad_s[...] = jnp.zeros(pad_s.shape, F32)
        pad_s[0:everyone, 0:everyone] = tm_ref[...]
        m_high, m_low = split(pad_s[...])
        shape = (LANES, LANES)
        level = (lane_iota(shape) % wf) // 2
        wide_h, wide_l = [], []
        for g in range(groups_f):
            pick = jnp.where(row_iota(shape) == fields * g + level, 1.0, 0.0).astype(BF16)
            wide_h.append(dot(m_high, pick))
            wide_l.append(dot(m_low, pick))
        wide_h = jnp.concatenate(wide_h, axis=1)
        wide_l = jnp.concatenate(wide_l, axis=1)
        lane = lane_iota(wide_h.shape) % LANES
        total_h, total_l = [], []
        for t in range(groups):
            for r in range(rows):
                for c in range(2):
                    keep = (lane // wf == t * rows + r) & (lane % 2 == c)
                    total_h.append(jnp.where(keep, wide_h, 0.0))
                    total_l.append(jnp.where(keep, wide_l, 0.0))
        mix_h = jnp.concatenate(total_h, axis=0).astype(BF16)
        mix_l = jnp.concatenate(total_l, axis=0).astype(BF16)
        fq[...] = dot_nt(mix_h, v_high) + dot_nt(mix_l, v_high) + dot_nt(mix_h, v_low)

        pad_s[...] = jnp.zeros(pad_s.shape, F32)
        pad_s[0:everyone, 0:everyone] = bm_ref[...]
        b_high, b_low = split(pad_s[...])
        shape = (FPAD, KPAD)
        expand = jnp.where(row_iota(shape) // 2 == lane_iota(shape), 1.0, 0.0).astype(BF16)
        shape = (LANES, 8 * KPAD)
        repeat = jnp.where(row_iota(shape) == lane_iota(shape) % KPAD, 1.0, 0.0).astype(BF16)
        shape = (FPAD, 8 * KPAD)
        same = row_iota(shape) % 2 == (lane_iota(shape) // KPAD) % 2
        pair_of = lane_iota(shape) // (2 * KPAD)
        for part, piece in enumerate((b_high, b_low)):
            full = dot(dot(expand, piece).astype(BF16), repeat)
            for pp in range(4):
                bk[(4 * part + pp) * FPAD:(4 * part + pp + 1) * FPAD, :] = jnp.where(
                    same & (pair_of == pp), full, 0.0
                ).astype(BF16)

    whole = places // LANES * LANES
    waves, seconds, lasts = [], [], []
    for pp in range(4):
        pair = 4 * step + pp
        there = pair < pairs
        wave = fold_ref[owner, 2 * jnp.minimum(pair, pairs - 1)]
        waves.append(wave)
        seconds.append(jnp.where(there, cut_off - wave, -1))
        lasts.append(jnp.where(there, places - 1, -1))
    shape = (lats, span)
    place = lane_iota(shape)
    for pp in range(4):
        leg = jnp.concatenate(
            [
                leg_ref[pp, :, 0:whole],
                jnp.broadcast_to(leg_ref[pp, :, whole:places], (lats, span - whole)),
            ],
            axis=1,
        )
        first = place <= seconds[pp]
        second = (place > seconds[pp]) & (place <= lasts[pp])
        odd = ((place + jnp.where(first, 0, waves[pp])) & 1) == 1
        signed = jnp.where(odd, -leg, leg)
        for r, rowset in enumerate((leg, signed)):
            start = r * eight + 2 * pp * lats
            eh[start:start + 2 * lats, :] = jnp.concatenate(
                [jnp.where(first, rowset, 0.0), jnp.where(second, rowset, 0.0)], axis=0
            ).astype(BF16)

    mixed = fq[pl.ds(pl.multiple_of(step * 4 * KPAD, 8), 4 * KPAD), :]
    mixed = jnp.concatenate([mixed[0:2 * KPAD], mixed[2 * KPAD:4 * KPAD]], axis=1)
    slot_pair = (lane_iota(mixed.shape) % eight) // (2 * lats)
    left = jnp.concatenate([jnp.where(slot_pair == pp, mixed, 0.0) for pp in range(4)], axis=0)
    left_h, left_l = split(left)
    left = jnp.concatenate([left_h, left_l], axis=0)
    tall_rows = 8 * KPAD

    rate_shape = (KPAD, 2 * LANES)
    rate_row = row_iota(rate_shape)
    rate = jnp.zeros(rate_shape, F32)
    for k in range(everyone):
        rate = jnp.where(rate_row == k, rates_ref[k], rate)

    for start in range(0, span, 2 * LANES):
        size = min(2 * LANES, span - start)
        modes = dot(left, eh[:, start:start + size])
        modes = modes[0:tall_rows] + modes[tall_rows:]
        place = start + lane_iota((1, size))
        damped = []
        for pp in range(4):
            degree = jnp.where(place > seconds[pp], place - 1, place + waves[pp])
            tau = (degree * (degree + 1)).astype(F32) * (1.0 / float(cut_off * (cut_off + 1)))
            factor = 1.0 / (1.0 + tau * rate[:, 0:size])
            at = 2 * pp * KPAD
            damped.append(modes[at:at + KPAD] * factor)
            damped.append(modes[at + KPAD:at + 2 * KPAD] * factor)
        damped = jnp.concatenate(damped, axis=0).astype(BF16)
        spec = dot(bk[...], damped)
        spec = spec[0:4 * FPAD] + spec[4 * FPAD:]
        sq[:, start:start + size] = spec.astype(BF16)
        kept = min(size, places - start)
        for pp in range(4):
            for f in range(everyone):
                at = pp * FPAD + 2 * f
                spec_ref[f, pp, :, start:start + kept] = spec[at:at + 2, 0:kept]

    sums = dot_nt(eh[...], sq[...])
    for r in range(rows):
        for i8 in range(8):
            at = (r * 8 + i8) * lats
            pp = i8 // 2
            tile = sums[at:at + lats, LANES * (pp // 2):LANES * (pp // 2 + 1)]
            if pp % 2:
                tile = pltpu.roll(tile, 64, 1)
            cs[pl.ds(pl.multiple_of(step * 2 * eight + at, 8), lats), :] = tile

    @pl.when(step == groups - 1)
    def _():
        lane = lane_iota((8, LANES))
        for holder in range(holders):
            lat = band_ref[holder]
            tiles = [jnp.zeros((8, LANES), F32) for _ in range(groups_f)]
            for t in range(groups):
                for r in range(rows):
                    put = unit * t + wf * r
                    piece = cs[pl.ds((t * rows + r) * eight + lat, 8, stride=lats), :]
                    keep = (lane >= put) & (lane < put + wf)
                    for g in range(groups_f):
                        moved = pltpu.roll(piece, (put - wf * g) % LANES, 1)
                        tiles[g] = jnp.where(keep, moved, tiles[g])
            for g in range(groups_f):
                out_ref[holder * groups_f + g] = tiles[g]


def per_device(grid, row_lengths, band_map, fold_map, legendre, to_modes, back_modes, mode_rates):
    fields, single, rows, width = grid.shape
    pairs, places, lats = legendre.shape
    cut_off = places - 2
    everyone = to_modes.shape[0]
    owners, per_owner = fold_map.shape
    groups = -(-per_owner // 8)
    slots = owners * groups * 8
    chunks = -(-(width // 4) // LANES)
    across = chunks * LANES
    span = -(-places // LANES) * LANES
    smem = pl.BlockSpec(memory_space=pltpu.SMEM)
    vmem = pl.BlockSpec(memory_space=pltpu.VMEM)
    room = pltpu.CompilerParams(vmem_limit_bytes=48 * 1024 * 1024)
    message = jax.ShapeDtypeStruct((owners, 8, LANES), F32)

    sending, cos_table, sin_table, first_factor, second_factor = pl.pallas_call(
        functools.partial(forward_kernel, cut_off, groups),
        out_shape=(
            message,
            jax.ShapeDtypeStruct((slots, across), BF16),
            jax.ShapeDtypeStruct((slots, across), BF16),
            jax.ShapeDtypeStruct((slots, LANES), F32),
            jax.ShapeDtypeStruct((slots, LANES), F32),
        ),
        in_specs=[smem, smem, vmem, vmem],
        out_specs=(vmem,) * 5,
        scratch_shapes=[
            pltpu.VMEM((LANES, LANES), F32),
            pltpu.VMEM((slots, LANES), F32),
            pltpu.VMEM((slots, LANES), F32),
            pltpu.VMEM((slots, LANES), F32),
            pltpu.VMEM((16, 4 * across), F32),
            pltpu.VMEM((LANES, across), BF16),
            pltpu.VMEM((slots, LANES), F32),
        ],
        compiler_params=room,
        name="forward_rows",
    )(row_lengths, band_map, fold_map, grid)

    arrived = lax.all_to_all(sending, ("lat", "fld"), split_axis=0, concat_axis=0, tiled=True)

    spectral, leaving = pl.pallas_call(
        functools.partial(spectral_kernel, cut_off, pairs, fields, rows),
        grid=(groups,),
        out_shape=(jax.ShapeDtypeStruct((everyone, pairs, 2, places), F32), message),
        in_specs=[
            smem,
            smem,
            smem,
            pl.BlockSpec((owners, 8, LANES), lambda t: (0, 0, 0)),
            pl.BlockSpec((4, lats, places), lambda t: (t, 0, 0)),
            pl.BlockSpec((everyone, everyone), lambda t: (0, 0)),
            pl.BlockSpec((everyone, everyone), lambda t: (0, 0)),
        ],
        out_specs=(
            pl.BlockSpec((everyone, 4, 2, places), lambda t: (0, t, 0, 0)),
            pl.BlockSpec((owners, 8, LANES), lambda t: (0, 0, 0)),
        ),
        scratch_shapes=[
            pltpu.VMEM((owners * 8, LANES), F32),
            pltpu.VMEM((groups * 4 * KPAD, 8 * lats), F32),
            pltpu.VMEM((8 * FPAD, 8 * KPAD), BF16),
            pltpu.VMEM((KPAD, LANES), F32),
            pltpu.VMEM((16 * lats, span), BF16),
            pltpu.VMEM((4 * FPAD, span), BF16),
            pltpu.VMEM((groups * 16 * lats, LANES), F32),
        ],
        compiler_params=pltpu.CompilerParams(
            dimension_semantics=("arbitrary",), vmem_limit_bytes=48 * 1024 * 1024
        ),
        name="spectral_solve",
    )(band_map, fold_map, mode_rates, arrived, jnp.transpose(legendre, (0, 2, 1)), to_modes, back_modes)

    returned = lax.all_to_all(leaving, ("lat", "fld"), split_axis=0, concat_axis=0, tiled=True)

    grid_out = pl.pallas_call(
        functools.partial(inverse_kernel, groups),
        out_shape=jax.ShapeDtypeStruct(grid.shape, BF16),
        in_specs=[smem, smem, vmem, vmem, vmem, vmem, vmem],
        out_specs=vmem,
        scratch_shapes=[
            pltpu.VMEM((owners, groups, 8, LANES), F32),
            pltpu.VMEM((16 * chunks, 4 * LANES), BF16),
        ],
        compiler_params=room,
        name="inverse_rows",
    )(row_lengths, band_map, returned, cos_table, sin_table, first_factor, second_factor)
    return (jnp.transpose(spectral, (0, 2, 1, 3)), grid_out)


def solution(mesh):
    placed = (
        P("fld", "lat", None, None),
        P(),
        P(),
        P(),
        P(("lat", "fld"), None, None),
        P(),
        P(),
        P(),
    )
    return jax.shard_map(
        per_device,
        mesh=mesh,
        in_specs=placed,
        out_specs=(P(None, None, ("lat", "fld"), None), P("fld", "lat", None, None)),
        check_vma=False,
    )
```

time: 1180 us -> 60.7 us (0.05); the launches traced: 1150 us -> 60.2 us
  matrix products: 816 us -> 0 us
  local copies, waits for them, and re-layouts: 240 us -> 8.84 us
  other arithmetic: 39 us -> 0 us
  Pallas kernels: 0 us -> 25.4 us
  loops' own time: 22.3 us -> 0 us
  blocking collectives: 10.2 us -> 25.3 us
  starting transfers between devices: 14.4 us -> 0 us
    dot_general x12 -> x0, matrix products: 816 us -> none  [the longest x2 192 us: forward_row(): jnp.einsum('bfa,am->bfm', phases, sin_table, preferred_element_type=jnp.f...]
    scatter x1 -> x0, local copies, waits for them, and re-layouts: 90.9 us -> none  [per_device(): jnp.zeros((rows, fields, 2, cut_off + 1), jnp.float32).at[..., order]]
    reshape x6 -> x0, local copies, waits for them, and re-layouts: 46.9 us -> none  [the longest x1 22.2 us: inverse_legendre(): spread = jnp.stack(parts, axis=2).reshape(pairs, places, 8 * fields)]
    another operation x4 -> x0, local copies, waits for them, and re-layouts: 27.3 us -> none  [the longest x1 26.2 us: inverse_legendre(): spread = jnp.stack(parts, axis=2).reshape(pairs, places, 8 * fields)]
    pallas_call x0 -> x3, Pallas kernels: none -> 25.4 us  [the longest x1 12.3 us: per_device(): pl.pallas_call(functools.partial(spectral_kernel, cut_off, pairs, fields,...]
    another operation x2 -> x0, loops' own time: 22.3 us -> none  [the longest x1 11.3 us: per_device(): lax.map(lambda item: forward_row(item[0], item[1], cut_off), (values, len...]
    slice x10 -> x0, local copies, waits for them, and re-layouts: 21.9 us -> none  [the longest x1 16.6 us: direct_legendre(): raw[:, :, 1]]
    all_to_all x1 -> x2, blocking collectives: 10.2 us -> 25.3 us  [the longest x1 15.3 us: per_device(): lax.all_to_all(sending, ('lat', 'fld'), split_axis=0, concat_axis=0, tile...]
  transfers between devices with their start and end apart: 3 -> 0, of which waited for: 2 -> 0; matrix products, arithmetic and copies ran while one was open for 1% -> 0% of each run, Pallas kernels for 0% -> 0%
where the time goes in v1:
time: 60.7 us; the launch traced here: 60.2 us
  Pallas kernels  25.4 us (42%)
  blocking collectives  25.3 us (42%)
  local copies, waits for them, and re-layouts  8.84 us (15%)
  between operations  0.65 us (1%)
    all_to_all x1, blocking collectives, per_device(): lax.all_to_all(sending, ('lat', 'fld'), split_axis=0, concat_axis=0, tile...  15.3 us
    pallas_call x1, Pallas kernels, per_device(): pl.pallas_call(functools.partial(spectral_kernel, cut_off, pairs, fields,...  12.3 us
    all_to_all x1, blocking collectives, per_device(): lax.all_to_all(leaving, ('lat', 'fld'), split_axis=0, concat_axis=0, tile...  9.99 us
    unnamed x24, local copies, waits for them, and re-layouts  8.84 us
    pallas_call x1, Pallas kernels, per_device(): pl.pallas_call(functools.partial(forward_kernel, cut_off, groups), out_sh...  8.78 us
    pallas_call x1, Pallas kernels, per_device(): pl.pallas_call(functools.partial(inverse_kernel, groups), out_shape=jax.S...  4.31 us

profile of v1, /device:TPU:0, one launch (start us, length us, event | category | flops | bytes accessed | tf_op | source)
XLA Modules:
  0.0 60.2 jit_solution(14099335834449214345)
XLA Ops:
  0.6 0.0 copy-start.1
  0.6 0.9 %copy-done.1 = bf16[5,1,2,5248]{3,2,1,0:T(2,128)(2,1)S(1)} copy-done((bf16[5,1,2,5248]{3,2,1,0:T(2,128)(2,1)S(1)}, bf16[5,1,2,5248]{3,2,1,0:T(2,128)(2,1)}, u32[]{:S(2)}) %copy-start.1) | copy-done | bytes 104984
  1.5 0.0 copy-start.2
  1.5 0.7 %copy-done.2 = s32[32,40]{1,0:T(8,128)S(1)} copy-done((s32[32,40]{1,0:T(8,128)S(1)}, s32[32,40]{1,0:T(8,128)}, u32[]{:S(2)}) %copy-start.2) | copy-done | bytes 5144
  2.2 0.0 copy-start.6
  2.2 0.7 %copy-done.6 = s32[8]{0:T(128)S(1)} copy-done((s32[8]{0:T(128)S(1)}, s32[8]{0:T(128)}, u32[]{:S(2)}) %copy-start.6) | copy-done | bytes 56
  2.9 0.0 copy-start.9
  2.9 0.7 %copy-done.9 = s32[8]{0:T(128)S(1)} copy-done((s32[8]{0:T(128)S(1)}, s32[8]{0:T(128)}, u32[]{:S(2)}) %copy-start.9) | copy-done | bytes 56
  3.6 8.8 %forward_rows.1 = (f32[32,8,128]{2,1,0:T(8,128)S(1)}, bf16[1280,1408]{1,0:T(8,128)(2,1)S(1)}, bf16[1280,1408]{1,0:T(8,128)(2,1)}, f32[1280,128]{1,0:T(8,128)S(1)}, f32[1280,128]{1,0:T(8,128)S(1)}) custom-call(s32[8]{0:T(128)S(1)} %copy-done.9, s32[8]{0:T(128)S(1)} %copy-done.6, s32[32,40]{1,0:T(8,128)S(1)} %copy-done.2, bf16[5,1,2,5248]{3,2,1,0:T(2,128)(2,1)S(1)} %copy-done.1), custom_call_target="tpu_custom_call" | custom-call | tf_op jit(solution)/shard_map/forward_rows/pallas_call | solution.py:426
  12.3 15.3 %all_to_all.10.msg_ref = f32[32,8,128]{2,1,0:T(8,128)S(1)} all-to-all(f32[32,8,128]{2,1,0:T(8,128)S(1)} %get-tuple-element.9), channel_id=1, replica_groups=mesh['lat'=8,'fld'=4] {'lat','fld'}, dimensions={0} | all-to-all | bytes 262144 | tf_op jit(solution)/shard_map/all_to_all | solution.py:450
  27.7 0.0 copy-start
  27.7 1.2 %copy-done = f32[20,1281,8]{1,2,0:T(8,128)S(1)} copy-done((f32[20,1281,8]{1,2,0:T(8,128)S(1)}, f32[20,1281,8]{1,2,0:T(8,128)}, u32[]{:S(2)}) %copy-start) | copy-done | bytes 819864
  28.8 0.0 copy-start.3
  28.8 0.7 %copy-done.3 = s32[32,40]{1,0:T(8,128)S(1)} copy-done((s32[32,40]{1,0:T(8,128)S(1)}, s32[32,40]{1,0:T(8,128)}, u32[]{:S(2)}) %copy-start.3) | copy-done | bytes 5144
  29.5 0.0 copy-start.4
  29.5 0.7 %copy-done.4 = f32[20,20]{1,0:T(8,128)S(1)} copy-done((f32[20,20]{1,0:T(8,128)S(1)}, f32[20,20]{1,0:T(8,128)}, u32[]{:S(2)}) %copy-start.4) | copy-done | bytes 1624
  30.3 0.0 copy-start.5
  30.3 0.7 %copy-done.5 = f32[20,20]{1,0:T(8,128)S(1)} copy-done((f32[20,20]{1,0:T(8,128)S(1)}, f32[20,20]{1,0:T(8,128)}, u32[]{:S(2)}) %copy-start.5) | copy-done | bytes 1624
  31.0 0.0 copy-start.7
  31.0 0.7 %copy-done.7 = s32[8]{0:T(128)S(1)} copy-done((s32[8]{0:T(128)S(1)}, s32[8]{0:T(128)}, u32[]{:S(2)}) %copy-start.7) | copy-done | bytes 56
  31.6 0.0 copy-start.11
  31.6 0.7 %copy-done.11 = f32[20]{0:T(128)S(1)} copy-done((f32[20]{0:T(128)S(1)}, f32[20]{0:T(128)}, u32[]{:S(2)}) %copy-start.11) | copy-done | bytes 104
  32.3 12.3 %spectral_solve.1 = (f32[20,20,2,1281]{3,2,1,0:T(2,128)}, f32[32,8,128]{2,1,0:T(8,128)S(1)}) custom-call(s32[8]{0:T(128)S(1)} %copy-done.7, s32[32,40]{1,0:T(8,128)S(1)} %copy-done.3, f32[20]{0:T(128)S(1)} %copy-done.11, f32[32,8,128]{2,1,0:T(8,128)S(1)} %all_to_all.10.msg_ref, f32[20,8,1281]{2,1,0:T(8,128)S(1)} %bitcast.2, f32[20,20]{1,0:T(8,128)S(1)} %copy-done.4, ...), custom_call_target="tpu_custom_call" | custom-call | tf_op jit(solution)/shard_map/spectral_solve/pallas_call | solution.py:452
  44.5 10.0 %all_to_all.11.msg_ref = f32[32,8,128]{2,1,0:T(8,128)S(1)} all-to-all(f32[32,8,128]{2,1,0:T(8,128)S(1)} %get-tuple-element.11), channel_id=1, replica_groups=mesh['lat'=8,'fld'=4] {'lat','fld'}, dimensions={0} | all-to-all | bytes 262144 | tf_op jit(solution)/shard_map/all_to_all | solution.py:484
  54.5 0.0 copy-start.8
  54.5 0.7 %copy-done.8 = s32[8]{0:T(128)S(1)} copy-done((s32[8]{0:T(128)S(1)}, s32[8]{0:T(128)}, u32[]{:S(2)}) %copy-start.8) | copy-done | bytes 56
  55.2 0.0 copy-start.10
  55.2 0.7 %copy-done.10 = s32[8]{0:T(128)S(1)} copy-done((s32[8]{0:T(128)S(1)}, s32[8]{0:T(128)}, u32[]{:S(2)}) %copy-start.10) | copy-done | bytes 56
  55.9 4.3 %inverse_rows.1 = bf16[5,1,2,5248]{3,2,1,0:T(2,128)(2,1)} custom-call(s32[8]{0:T(128)S(1)} %copy-done.10, s32[8]{0:T(128)S(1)} %copy-done.8, f32[32,8,128]{2,1,0:T(8,128)S(1)} %all_to_all.11.msg_ref, bf16[1280,1408]{1,0:T(8,128)(2,1)S(1)} %get-tuple-element.12.cos_ref, bf16[1280,1408]{1,0:T(8,128)(2,1)} %get-tuple-element.13.sin_ref, ...), custom_call_target="tpu_custom_call" | custom-call | tf_op jit(solution)/shard_map/inverse_rows/pallas_call | solution.py:486
Async XLA Ops:
  0.6 0.9 %copy-start.1 = (bf16[5,1,2,5248]{3,2,1,0:T(2,128)(2,1)S(1)}, bf16[5,1,2,5248]{3,2,1,0:T(2,128)(2,1)}, u32[]{:S(2)}) copy-start(bf16[5,1,2,5248]{3,2,1,0:T(2,128)(2,1)} %grid_ref.1) | copy-start | bytes 314884
  1.5 0.7 %copy-start.2 = (s32[32,40]{1,0:T(8,128)S(1)}, s32[32,40]{1,0:T(8,128)}, u32[]{:S(2)}) copy-start(s32[32,40]{1,0:T(8,128)} %fold_ref.3) | copy-start | bytes 15364
  2.2 0.7 %copy-start.6 = (s32[8]{0:T(128)S(1)}, s32[8]{0:T(128)}, u32[]{:S(2)}) copy-start(s32[8]{0:T(128)} %band_ref.5) | copy-start | bytes 100
  2.9 0.7 %copy-start.9 = (s32[8]{0:T(128)S(1)}, s32[8]{0:T(128)}, u32[]{:S(2)}) copy-start(s32[8]{0:T(128)} %len_ref.3) | copy-start | bytes 100
  27.7 1.2 %copy-start = (f32[20,1281,8]{1,2,0:T(8,128)S(1)}, f32[20,1281,8]{1,2,0:T(8,128)}, u32[]{:S(2)}) copy-start(f32[20,1281,8]{1,2,0:T(8,128)} %param.12) | copy-start | bytes 2459524
  28.8 0.7 %copy-start.3 = (s32[32,40]{1,0:T(8,128)S(1)}, s32[32,40]{1,0:T(8,128)}, u32[]{:S(2)}) copy-start(s32[32,40]{1,0:T(8,128)} %fold_ref.3) | copy-start | bytes 15364
  29.5 0.7 %copy-start.4 = (f32[20,20]{1,0:T(8,128)S(1)}, f32[20,20]{1,0:T(8,128)}, u32[]{:S(2)}) copy-start(f32[20,20]{1,0:T(8,128)} %tm_ref.1) | copy-start | bytes 4804
  30.3 0.7 %copy-start.5 = (f32[20,20]{1,0:T(8,128)S(1)}, f32[20,20]{1,0:T(8,128)}, u32[]{:S(2)}) copy-start(f32[20,20]{1,0:T(8,128)} %bm_ref.1) | copy-start | bytes 4804
  31.0 0.7 %copy-start.7 = (s32[8]{0:T(128)S(1)}, s32[8]{0:T(128)}, u32[]{:S(2)}) copy-start(s32[8]{0:T(128)} %band_ref.5) | copy-start | bytes 100
  31.6 0.7 %copy-start.11 = (f32[20]{0:T(128)S(1)}, f32[20]{0:T(128)}, u32[]{:S(2)}) copy-start(f32[20]{0:T(128)} %rates_ref.1) | copy-start | bytes 244
  54.5 0.7 %copy-start.8 = (s32[8]{0:T(128)S(1)}, s32[8]{0:T(128)}, u32[]{:S(2)}) copy-start(s32[8]{0:T(128)} %band_ref.5) | copy-start | bytes 100
  55.2 0.7 %copy-start.10 = (s32[8]{0:T(128)S(1)}, s32[8]{0:T(128)}, u32[]{:S(2)}) copy-start(s32[8]{0:T(128)} %len_ref.3) | copy-start | bytes 100

commit v2 on v1

--- a/solution.py
+++ b/solution.py
@@ -11,6 +11,7 @@
 LANES = 128
 KPAD = 24
 FPAD = 64
+ROOM = 24 * 1024 * 1024
 F32 = jnp.float32
 BF16 = jnp.bfloat16
 NT_DIMS = (((1,), (1,)), ((), ()))
@@ -61,6 +62,17 @@
     return horner(COS_POLY, z), part * horner(SIN_POLY, z)
 
 
+def fetch_all(sources, targets, sems):
+    copies = [
+        pltpu.make_async_copy(source, target, sems.at[i])
+        for i, (source, target) in enumerate(zip(sources, targets))
+    ]
+    for copy in copies:
+        copy.start()
+    for copy in copies:
+        copy.wait()
+
+
 def lane_iota(shape):
     return lax.broadcasted_iota(jnp.int32, shape, len(shape) - 1)
 
@@ -78,9 +90,13 @@
 
 
 def forward_kernel(
-    cut_off, groups, len_ref, band_ref, fold_ref, grid_ref,
-    msg_ref, cos_ref, sin_ref, k1_ref, k2_ref, fold_s, mb, cb, sb, xs, xq, ys,
+    cut_off, groups, len_hbm, band_hbm, fold_hbm, grid_hbm,
+    msg_ref, cos_ref, sin_ref, k1_ref, k2_ref,
+    len_ref, band_ref, fold_ref, grid_ref, sems, fold_s, mb, cb, sb, xs, xq, ys,
 ):
+    fetch_all(
+        (len_hbm, band_hbm, fold_hbm, grid_hbm), (len_ref, band_ref, fold_ref, grid_ref), sems
+    )
     fields, _, rows, width = grid_ref.shape
     owners, per_owner = fold_ref.shape
     slots, across = cos_ref.shape
@@ -186,8 +202,10 @@
 
 
 def inverse_kernel(
-    groups, len_ref, band_ref, msg_ref, cos_ref, sin_ref, k1_ref, k2_ref, grid_ref, zs, os,
+    groups, len_hbm, band_hbm, msg_ref, cos_ref, sin_ref, k1_ref, k2_ref, grid_ref,
+    len_ref, band_ref, sems, zs, os,
 ):
+    fetch_all((len_hbm, band_hbm), (len_ref, band_ref), sems)
     fields, _, rows, width = grid_ref.shape
     owners = msg_ref.shape[0]
     slots, across = cos_ref.shape
@@ -242,169 +260,202 @@
             ].astype(BF16)
 
 
-def spectral_kernel(
-    cut_off, pairs, fields, rows, band_ref, fold_ref, rates_ref, msg_ref, leg_ref, tm_ref, bm_ref,
-    spec_ref, out_ref, vs, fq, bk, pad_s, eh, sq, cs,
+def prepare_kernel(
+    cut_off, pairs, fields, rows, fold_hbm, rates_hbm, leg_hbm, tm_hbm, bm_hbm,
+    eh_ref, factor_ref, mix_ref, back_ref,
+    fold_ref, rates_ref, leg_ref, tm_ref, bm_ref, sems, pad_s,
 ):
+    fetch_all(
+        (fold_hbm, rates_hbm, leg_hbm, tm_hbm, bm_hbm),
+        (fold_ref, rates_ref, leg_ref, tm_ref, bm_ref),
+        sems,
+    )
     everyone = tm_ref.shape[0]
-    quad, lats, places = leg_ref.shape
+    _, lats, places = leg_ref.shape
+    groups_f = everyone // fields
+    wf = fields * 2
+    span = eh_ref.shape[1]
+    eight = 8 * lats
+    groups = eh_ref.shape[0] // (2 * eight)
+    owner = lax.axis_index("lat") * groups_f + lax.axis_index("fld")
+
+    pad_s[...] = jnp.zeros(pad_s.shape, F32)
+    pad_s[0:everyone, 0:everyone] = tm_ref[...]
+    m_high, m_low = split(pad_s[...])
+    shape = (LANES, LANES)
+    level = (lane_iota(shape) % wf) // 2
+    wide = []
+    for piece in (m_high, m_low):
+        parts = []
+        for g in range(groups_f):
+            pick = jnp.where(row_iota(shape) == fields * g + level, 1.0, 0.0).astype(BF16)
+            parts.append(dot(piece, pick))
+        wide.append(jnp.concatenate(parts, axis=1))
+    lane = lane_iota(wide[0].shape) % LANES
+    for part, piece in enumerate(wide):
+        for t in range(groups):
+            total = []
+            for r in range(rows):
+                for c in range(2):
+                    keep = (lane // wf == t * rows + r) & (lane % 2 == c)
+                    total.append(jnp.where(keep, piece, 0.0))
+            at = (part * groups + t) * 4 * KPAD
+            mix_ref[at:at + 4 * KPAD, :] = jnp.concatenate(total, axis=0).astype(BF16)
+
+    pad_s[...] = jnp.zeros(pad_s.shape, F32)
+    pad_s[0:everyone, 0:everyone] = bm_ref[...]
+    shape = (FPAD, KPAD)
+    expand = jnp.where(row_iota(shape) // 2 == lane_iota(shape), 1.0, 0.0).astype(BF16)
+    shape = (LANES, 8 * KPAD)
+    repeat = jnp.where(row_iota(shape) == lane_iota(shape) % KPAD, 1.0, 0.0).astype(BF16)
+    shape = (FPAD, 8 * KPAD)
+    same = row_iota(shape) % 2 == (lane_iota(shape) // KPAD) % 2
+    for part, piece in enumerate(split(pad_s[...])):
+        full = dot(dot(expand, piece).astype(BF16), repeat)
+        back_ref[part * FPAD:(part + 1) * FPAD, :] = jnp.where(same, full, 0.0).astype(BF16)
+
+    rate_row = row_iota((KPAD, LANES))
+    rate = jnp.zeros((KPAD, LANES), F32)
+    for k in range(everyone):
+        rate = jnp.where(rate_row == k, rates_ref[k], rate)
+    rate = jnp.concatenate([rate] * (span // LANES), axis=1)
+
+    whole = places // LANES * LANES
+    shape = (lats, span)
+    place = lane_iota(shape)
+
+    def pair_block(pair, carry):
+        there = pair < pairs
+        index = jnp.minimum(pair, pairs - 1)
+        wave = fold_ref[owner, 2 * index]
+        limit = jnp.where(there, cut_off - wave, -1)
+        last = jnp.where(there, places - 1, -1)
+        leg = jnp.concatenate(
+            [
+                leg_ref[index, :, 0:whole],
+                jnp.broadcast_to(leg_ref[index, :, whole:places], (lats, span - whole)),
+            ],
+            axis=1,
+        )
+        first = place <= limit
+        second = (place > limit) & (place <= last)
+        odd = ((place + jnp.where(first, 0, wave)) & 1) == 1
+        signed = jnp.where(odd, -leg, leg)
+        base = (pair // 4) * 2 * eight + (pair % 4) * 2 * lats
+        for r, rowset in enumerate((leg, signed)):
+            eh_ref[pl.ds(pl.multiple_of(base + r * eight, 16), 2 * lats), :] = jnp.concatenate(
+                [jnp.where(first, rowset, 0.0), jnp.where(second, rowset, 0.0)], axis=0
+            ).astype(BF16)
+        row = lane_iota((1, span))
+        degree = jnp.where(row > limit, row - 1, row + wave)
+        tau = (degree * (degree + 1)).astype(F32) * (1.0 / float(cut_off * (cut_off + 1)))
+        factor_ref[pl.ds(pl.multiple_of(pair * KPAD, 8), KPAD), :] = 1.0 / (1.0 + tau * rate)
+        return carry
+
+    lax.fori_loop(0, 4 * groups, pair_block, 0)
+
+
+def solve_kernel(
+    fields, rows, band_hbm, msg_ref, eh_ref, factor_ref, mix_ref, back_ref,
+    damped_ref, out_ref,
+    band_ref, sems, vs, fq, sums, cs,
+):
+    fetch_all((band_hbm,), (band_ref,), sems)
     holders = band_ref.shape[0]
-    groups_f = everyone // fields
+    groups_f = msg_ref.shape[0] // holders
+    lats = holders
     groups = fq.shape[0] // (4 * KPAD)
     wf = fields * 2
     unit = rows * wf
-    span = eh.shape[1]
-    step = pl.program_id(0)
-    owner = lax.axis_index("lat") * groups_f + lax.axis_index("fld")
+    span = eh_ref.shape[1]
     eight = 8 * lats
-
-    @pl.when(step == 0)
-    def _():
-        for holder in range(holders):
-            lat = band_ref[holder]
-            for g in range(groups_f):
-                vs[pl.ds(pl.multiple_of((g * lats + lat) * 8, 8), 8), :] = msg_ref[holder * groups_f + g]
-        tall = []
-        for i8 in range(8):
-            tall.append(
-                jnp.concatenate(
-                    [vs[pl.ds(g * lats * 8 + i8, lats, stride=8), :] for g in range(groups_f)], axis=1
-                )
+    for holder in range(holders):
+        lat = band_ref[holder]
+        for g in range(groups_f):
+            vs[pl.ds(pl.multiple_of((g * lats + lat) * 8, 8), 8), :] = msg_ref[holder * groups_f + g]
+    tall = []
+    for i8 in range(8):
+        tall.append(
+            jnp.concatenate(
+                [vs[pl.ds(g * lats * 8 + i8, lats, stride=8), :] for g in range(groups_f)], axis=1
             )
-        v_high, v_low = split(jnp.concatenate(tall, axis=0))
-        pad_s[...] = jnp.zeros(pad_s.shape, F32)
-        pad_s[0:everyone, 0:everyone] = tm_ref[...]
-        m_high, m_low = split(pad_s[...])
-        shape = (LANES, LANES)
-        level = (lane_iota(shape) % wf) // 2
-        wide_h, wide_l = [], []
-        for g in range(groups_f):
-            pick = jnp.where(row_iota(shape) == fields * g + level, 1.0, 0.0).astype(BF16)
-            wide_h.append(dot(m_high, pick))
-            wide_l.append(dot(m_low, pick))
-        wide_h = jnp.concatenate(wide_h, axis=1)
-        wide_l = jnp.concatenate(wide_l, axis=1)
-        lane = lane_iota(wide_h.shape) % LANES
-        total_h, total_l = [], []
+        )
+    v_high, v_low = split(jnp.concatenate(tall, axis=0))
+    half = mix_ref.shape[0] // 2
+    mix_h = mix_ref[0:half, :]
+    fq[...] = dot_nt(mix_h, v_high) + dot_nt(mix_ref[half:, :], v_high) + dot_nt(mix_h, v_low)
+    tall_rows = 8 * KPAD
+
+    def quad_block(t, carry):
+        mixed = fq[pl.ds(pl.multiple_of(t * 4 * KPAD, 8), 4 * KPAD), :]
+        mixed = jnp.concatenate([mixed[0:2 * KPAD], mixed[2 * KPAD:4 * KPAD]], axis=1)
+        slot_pair = (lane_iota(mixed.shape) % eight) // (2 * lats)
+        left = jnp.concatenate([jnp.where(slot_pair == pp, mixed, 0.0) for pp in range(4)], axis=0)
+        left = jnp.concatenate(split(left), axis=0)
+        legs = pl.ds(pl.multiple_of(t * 2 * eight, 16), 2 * eight)
+        deep = pl.ds(pl.multiple_of(t * tall_rows, 16), tall_rows)
+        factor_at = pl.multiple_of(t * 4 * KPAD, 8)
+        for start in range(0, span, 2 * LANES):
+            size = min(2 * LANES, span - start)
+            modes = dot(left, eh_ref[legs, start:start + size])
+            modes = modes[0:tall_rows] + modes[tall_rows:]
+            damped = []
+            for pp in range(4):
+                factor = factor_ref[pl.ds(factor_at + pp * KPAD, KPAD), start:start + size]
+                at = 2 * pp * KPAD
+                damped.append(modes[at:at + KPAD] * factor)
+                damped.append(modes[at + KPAD:at + 2 * KPAD] * factor)
+            damped_ref[deep, start:start + size] = jnp.concatenate(damped, axis=0).astype(BF16)
+        sums[legs, :] = dot_nt(eh_ref[legs, :], damped_ref[deep, :])
+        return carry
+
+    lax.fori_loop(0, groups, quad_block, 0)
+
+    everything = sums[...]
+    own = (row_iota(everything.shape) // lats) % 8 // 2 == lane_iota(everything.shape) // (2 * KPAD)
+    own_h, own_l = split(jnp.where(own, everything, 0.0))
+    back_h = back_ref[0:FPAD, :]
+    cs[:, 0:FPAD] = dot_nt(own_h, back_h) + dot_nt(own_l, back_h) + dot_nt(own_h, back_ref[FPAD:, :])
+
+    lane = lane_iota((8, LANES))
+    for holder in range(holders):
+        lat = band_ref[holder]
+        tiles = [jnp.zeros((8, LANES), F32) for _ in range(groups_f)]
         for t in range(groups):
             for r in range(rows):
-                for c in range(2):
-                    keep = (lane // wf == t * rows + r) & (lane % 2 == c)
-                    total_h.append(jnp.where(keep, wide_h, 0.0))
-                    total_l.append(jnp.where(keep, wide_l, 0.0))
-        mix_h = jnp.concatenate(total_h, axis=0).astype(BF16)
-        mix_l = jnp.concatenate(total_l, axis=0).astype(BF16)
-        fq[...] = dot_nt(mix_h, v_high) + dot_nt(mix_l, v_high) + dot_nt(mix_h, v_low)
-
-        pad_s[...] = jnp.zeros(pad_s.shape, F32)
-        pad_s[0:everyone, 0:everyone] = bm_ref[...]
-        b_high, b_low = split(pad_s[...])
-        shape = (FPAD, KPAD)
-        expand = jnp.where(row_iota(shape) // 2 == lane_iota(shape), 1.0, 0.0).astype(BF16)
-        shape = (LANES, 8 * KPAD)
-        repeat = jnp.where(row_iota(shape) == lane_iota(shape) % KPAD, 1.0, 0.0).astype(BF16)
+                put = unit * t + wf * r
+                piece = cs[pl.ds((t * rows + r) * eight + lat, 8, stride=lats), :]
+                keep = (lane >= put) & (lane < put + wf)
+                for g in range(groups_f):
+                    moved = pltpu.roll(piece, (put - wf * g) % LANES, 1)
+                    tiles[g] = jnp.where(keep, moved, tiles[g])
+        for g in range(groups_f):
+            out_ref[holder * groups_f + g] = tiles[g]
+
+
+def output_kernel(damped_ref, back_ref, spec_ref, bk):
+    everyone, quad, _, places = spec_ref.shape
+    span = damped_ref.shape[1]
+
+    @pl.when(pl.program_id(0) == 0)
+    def _():
         shape = (FPAD, 8 * KPAD)
-        same = row_iota(shape) % 2 == (lane_iota(shape) // KPAD) % 2
         pair_of = lane_iota(shape) // (2 * KPAD)
-        for part, piece in enumerate((b_high, b_low)):
-            full = dot(dot(expand, piece).astype(BF16), repeat)
+        for part in range(2):
+            full = back_ref[part * FPAD:(part + 1) * FPAD, :].astype(F32)
             for pp in range(4):
-                bk[(4 * part + pp) * FPAD:(4 * part + pp + 1) * FPAD, :] = jnp.where(
-                    same & (pair_of == pp), full, 0.0
-                ).astype(BF16)
-
-    whole = places // LANES * LANES
-    waves, seconds, lasts = [], [], []
-    for pp in range(4):
-        pair = 4 * step + pp
-        there = pair < pairs
-        wave = fold_ref[owner, 2 * jnp.minimum(pair, pairs - 1)]
-        waves.append(wave)
-        seconds.append(jnp.where(there, cut_off - wave, -1))
-        lasts.append(jnp.where(there, places - 1, -1))
-    shape = (lats, span)
-    place = lane_iota(shape)
-    for pp in range(4):
-        leg = jnp.concatenate(
-            [
-                leg_ref[pp, :, 0:whole],
-                jnp.broadcast_to(leg_ref[pp, :, whole:places], (lats, span - whole)),
-            ],
-            axis=1,
-        )
-        first = place <= seconds[pp]
-        second = (place > seconds[pp]) & (place <= lasts[pp])
-        odd = ((place + jnp.where(first, 0, waves[pp])) & 1) == 1
-        signed = jnp.where(odd, -leg, leg)
-        for r, rowset in enumerate((leg, signed)):
-            start = r * eight + 2 * pp * lats
-            eh[start:start + 2 * lats, :] = jnp.concatenate(
-                [jnp.where(first, rowset, 0.0), jnp.where(second, rowset, 0.0)], axis=0
-            ).astype(BF16)
-
-    mixed = fq[pl.ds(pl.multiple_of(step * 4 * KPAD, 8), 4 * KPAD), :]
-    mixed = jnp.concatenate([mixed[0:2 * KPAD], mixed[2 * KPAD:4 * KPAD]], axis=1)
-    slot_pair = (lane_iota(mixed.shape) % eight) // (2 * lats)
-    left = jnp.concatenate([jnp.where(slot_pair == pp, mixed, 0.0) for pp in range(4)], axis=0)
-    left_h, left_l = split(left)
-    left = jnp.concatenate([left_h, left_l], axis=0)
-    tall_rows = 8 * KPAD
-
-    rate_shape = (KPAD, 2 * LANES)
-    rate_row = row_iota(rate_shape)
-    rate = jnp.zeros(rate_shape, F32)
-    for k in range(everyone):
-        rate = jnp.where(rate_row == k, rates_ref[k], rate)
+                at = (4 * part + pp) * FPAD
+                bk[at:at + FPAD, :] = jnp.where(pair_of == pp, full, 0.0).astype(BF16)
 
     for start in range(0, span, 2 * LANES):
         size = min(2 * LANES, span - start)
-        modes = dot(left, eh[:, start:start + size])
-        modes = modes[0:tall_rows] + modes[tall_rows:]
-        place = start + lane_iota((1, size))
-        damped = []
-        for pp in range(4):
-            degree = jnp.where(place > seconds[pp], place - 1, place + waves[pp])
-            tau = (degree * (degree + 1)).astype(F32) * (1.0 / float(cut_off * (cut_off + 1)))
-            factor = 1.0 / (1.0 + tau * rate[:, 0:size])
-            at = 2 * pp * KPAD
-            damped.append(modes[at:at + KPAD] * factor)
-            damped.append(modes[at + KPAD:at + 2 * KPAD] * factor)
-        damped = jnp.concatenate(damped, axis=0).astype(BF16)
-        spec = dot(bk[...], damped)
+        spec = dot(bk[...], damped_ref[:, start:start + size])
         spec = spec[0:4 * FPAD] + spec[4 * FPAD:]
-        sq[:, start:start + size] = spec.astype(BF16)
         kept = min(size, places - start)
         for pp in range(4):
             for f in range(everyone):
                 at = pp * FPAD + 2 * f
                 spec_ref[f, pp, :, start:start + kept] = spec[at:at + 2, 0:kept]
-
-    sums = dot_nt(eh[...], sq[...])
-    for r in range(rows):
-        for i8 in range(8):
-            at = (r * 8 + i8) * lats
-            pp = i8 // 2
-            tile = sums[at:at + lats, LANES * (pp // 2):LANES * (pp // 2 + 1)]
-            if pp % 2:
-                tile = pltpu.roll(tile, 64, 1)
-            cs[pl.ds(pl.multiple_of(step * 2 * eight + at, 8), lats), :] = tile
-
-    @pl.when(step == groups - 1)
-    def _():
-        lane = lane_iota((8, LANES))
-        for holder in range(holders):
-            lat = band_ref[holder]
-            tiles = [jnp.zeros((8, LANES), F32) for _ in range(groups_f)]
-            for t in range(groups):
-                for r in range(rows):
-                    put = unit * t + wf * r
-                    piece = cs[pl.ds((t * rows + r) * eight + lat, 8, stride=lats), :]
-                    keep = (lane >= put) & (lane < put + wf)
-                    for g in range(groups_f):
-                        moved = pltpu.roll(piece, (put - wf * g) % LANES, 1)
-                        tiles[g] = jnp.where(keep, moved, tiles[g])
-            for g in range(groups_f):
-                out_ref[holder * groups_f + g] = tiles[g]
 
 
 def per_device(grid, row_lengths, band_map, fold_map, legendre, to_modes, back_modes, mode_rates):
@@ -418,10 +469,13 @@
     chunks = -(-(width // 4) // LANES)
     across = chunks * LANES
     span = -(-places // LANES) * LANES
-    smem = pl.BlockSpec(memory_space=pltpu.SMEM)
+    hbm = pl.BlockSpec(memory_space=pltpu.HBM)
     vmem = pl.BlockSpec(memory_space=pltpu.VMEM)
-    room = pltpu.CompilerParams(vmem_limit_bytes=48 * 1024 * 1024)
+    room = pltpu.CompilerParams(vmem_limit_bytes=ROOM)
     message = jax.ShapeDtypeStruct((owners, 8, LANES), F32)
+    holders = band_map.shape[0]
+    groups_f = everyone // fields
+    dma = pltpu.SemaphoreType.DMA
 
     sending, cos_table, sin_table, first_factor, second_factor = pl.pallas_call(
         functools.partial(forward_kernel, cut_off, groups),
@@ -432,9 +486,14 @@
             jax.ShapeDtypeStruct((slots, LANES), F32),
             jax.ShapeDtypeStruct((slots, LANES), F32),
         ),
-        in_specs=[smem, smem, vmem, vmem],
+        in_specs=[hbm] * 4,
         out_specs=(vmem,) * 5,
         scratch_shapes=[
+            pltpu.SMEM(row_lengths.shape, jnp.int32),
+            pltpu.SMEM(band_map.shape, jnp.int32),
+            pltpu.VMEM(fold_map.shape, jnp.int32),
+            pltpu.VMEM(grid.shape, BF16),
+            dma((4,)),
             pltpu.VMEM((LANES, LANES), F32),
             pltpu.VMEM((slots, LANES), F32),
             pltpu.VMEM((slots, LANES), F32),
@@ -449,46 +508,75 @@
 
     arrived = lax.all_to_all(sending, ("lat", "fld"), split_axis=0, concat_axis=0, tiled=True)
 
-    spectral, leaving = pl.pallas_call(
-        functools.partial(spectral_kernel, cut_off, pairs, fields, rows),
-        grid=(groups,),
-        out_shape=(jax.ShapeDtypeStruct((everyone, pairs, 2, places), F32), message),
-        in_specs=[
-            smem,
-            smem,
-            smem,
-            pl.BlockSpec((owners, 8, LANES), lambda t: (0, 0, 0)),
-            pl.BlockSpec((4, lats, places), lambda t: (t, 0, 0)),
-            pl.BlockSpec((everyone, everyone), lambda t: (0, 0)),
-            pl.BlockSpec((everyone, everyone), lambda t: (0, 0)),
+    legs, factors, mix, back = pl.pallas_call(
+        functools.partial(prepare_kernel, cut_off, pairs, fields, rows),
+        out_shape=(
+            jax.ShapeDtypeStruct((groups * 16 * lats, span), BF16),
+            jax.ShapeDtypeStruct((groups * 4 * KPAD, span), F32),
+            jax.ShapeDtypeStruct((2 * groups * 4 * KPAD, groups_f * LANES), BF16),
+            jax.ShapeDtypeStruct((2 * FPAD, 8 * KPAD), BF16),
+        ),
+        in_specs=[hbm] * 5,
+        out_specs=(vmem,) * 4,
+        scratch_shapes=[
+            pltpu.SMEM(fold_map.shape, jnp.int32),
+            pltpu.SMEM(mode_rates.shape, F32),
+            pltpu.VMEM((pairs, lats, places), F32),
+            pltpu.VMEM(to_modes.shape, F32),
+            pltpu.VMEM(back_modes.shape, F32),
+            dma((5,)),
+            pltpu.VMEM((KPAD, LANES), F32),
         ],
-        out_specs=(
-            pl.BlockSpec((everyone, 4, 2, places), lambda t: (0, t, 0, 0)),
-            pl.BlockSpec((owners, 8, LANES), lambda t: (0, 0, 0)),
-        ),
+        compiler_params=room,
+        cost_estimate=pl.CostEstimate(flops=10**8, bytes_accessed=8 * 10**6, transcendentals=0),
+        name="prepare",
+    )(fold_map, mode_rates, jnp.transpose(legendre, (0, 2, 1)), to_modes, back_modes)
+
+    damped, leaving = pl.pallas_call(
+        functools.partial(solve_kernel, fields, rows),
+        out_shape=(jax.ShapeDtypeStruct((groups * 8 * KPAD, span), BF16), message),
+        in_specs=[hbm] + [vmem] * 5,
+        out_specs=(vmem,) * 2,
         scratch_shapes=[
+            pltpu.SMEM(band_map.shape, jnp.int32),
+            dma((1,)),
             pltpu.VMEM((owners * 8, LANES), F32),
             pltpu.VMEM((groups * 4 * KPAD, 8 * lats), F32),
-            pltpu.VMEM((8 * FPAD, 8 * KPAD), BF16),
-            pltpu.VMEM((KPAD, LANES), F32),
-            pltpu.VMEM((16 * lats, span), BF16),
-            pltpu.VMEM((4 * FPAD, span), BF16),
+            pltpu.VMEM((groups * 16 * lats, 8 * KPAD), F32),
             pltpu.VMEM((groups * 16 * lats, LANES), F32),
         ],
+        compiler_params=room,
+        name="solve",
+    )(band_map, arrived, legs, factors, mix, back)
+
+    returned = lax.all_to_all(leaving, ("lat", "fld"), split_axis=0, concat_axis=0, tiled=True)
+
+    spectral = pl.pallas_call(
+        output_kernel,
+        grid=(groups,),
+        out_shape=jax.ShapeDtypeStruct((everyone, pairs, 2, places), F32),
+        in_specs=[
+            pl.BlockSpec((8 * KPAD, span), lambda t: (t, 0)),
+            pl.BlockSpec((2 * FPAD, 8 * KPAD), lambda t: (0, 0)),
+        ],
+        out_specs=pl.BlockSpec((everyone, 4, 2, places), lambda t: (0, t, 0, 0)),
+        scratch_shapes=[pltpu.VMEM((8 * FPAD, 8 * KPAD), BF16)],
         compiler_params=pltpu.CompilerParams(
-            dimension_semantics=("arbitrary",), vmem_limit_bytes=48 * 1024 * 1024
+            dimension_semantics=("arbitrary",), vmem_limit_bytes=ROOM
         ),
-        name="spectral_solve",
-    )(band_map, fold_map, mode_rates, arrived, jnp.transpose(legendre, (0, 2, 1)), to_modes, back_modes)
-
-    returned = lax.all_to_all(leaving, ("lat", "fld"), split_axis=0, concat_axis=0, tiled=True)
+        cost_estimate=pl.CostEstimate(flops=10**8, bytes_accessed=8 * 10**6, transcendentals=0),
+        name="spectral_output",
+    )(damped, back)
 
     grid_out = pl.pallas_call(
         functools.partial(inverse_kernel, groups),
         out_shape=jax.ShapeDtypeStruct(grid.shape, BF16),
-        in_specs=[smem, smem, vmem, vmem, vmem, vmem, vmem],
+        in_specs=[hbm, hbm] + [vmem] * 5,
         out_specs=vmem,
         scratch_shapes=[
+            pltpu.SMEM(row_lengths.shape, jnp.int32),
+            pltpu.SMEM(band_map.shape, jnp.int32),
+            dma((2,)),
             pltpu.VMEM((owners, groups, 8, LANES), F32),
             pltpu.VMEM((16 * chunks, 4 * LANES), BF16),
         ],

time: 60.7 us -> 70.6 us (1.16)
  blocking collectives: 25.3 us -> 0 us
  local copies, waits for them, and re-layouts: 8.84 us -> 27.2 us
  starting transfers between devices: 0 us -> 13.1 us
  waiting for transfers between devices: 0 us -> 3.73 us
    all_to_all x2 -> x0, blocking collectives: 25.3 us -> none  [the longest x1 15.3 us: per_device(): lax.all_to_all(sending, ('lat', 'fld'), split_axis=0, concat_axis=0, tile...]
    unnamed x24 -> x50, local copies, waits for them, and re-layouts: 8.84 us -> 27.2 us
    all_to_all x0 -> x2, starting transfers between devices: none -> 13.1 us  [the longest x1 7.3 us: per_device(): lax.all_to_all(sending, ('lat', 'fld'), split_axis=0, concat_axis=0, tile...]
    all_to_all x0 -> x2, waiting for transfers between devices: none -> 3.73 us  [the longest x1 3.72 us: per_device(): lax.all_to_all(leaving, ('lat', 'fld'), split_axis=0, concat_axis=0, tile...]
    pallas_call x1, Pallas kernels: 4.31 us -> 2.85 us  [per_device(): pl.pallas_call(functools.partial(inverse_kernel, groups), out_shape=jax.S...]
    pallas_call x1 -> x3, Pallas kernels: 12.3 us -> 13.5 us  [the longest x1 6.13 us: per_device(): pl.pallas_call(functools.partial(solve_kernel, fields, rows), out_shape=(...]
  transfers between devices with their start and end apart: 0 -> 2, of which waited for: 0 -> 1; matrix products, arithmetic and copies ran while one was open for 0% -> 0% of each run, Pallas kernels for 0% -> 11%
where the time goes in v2:
time: 70.6 us; the launch traced here: 69.8 us
  local copies, waits for them, and re-layouts  27.2 us (39%)
  Pallas kernels  25 us (35%)
  starting transfers between devices  13.1 us (19%)
  waiting for transfers between devices  3.73 us (5%)
  between operations  0.73 us (1%)
    unnamed x50, local copies, waits for them, and re-layouts  27.2 us
    pallas_call x1, Pallas kernels, per_device(): pl.pallas_call(functools.partial(forward_kernel, cut_off, groups), out_sh...  8.63 us
    all_to_all x1, starting transfers between devices, per_device(): lax.all_to_all(sending, ('lat', 'fld'), split_axis=0, concat_axis=0, tile...  7.3 us
    pallas_call x1, Pallas kernels, per_device(): pl.pallas_call(functools.partial(solve_kernel, fields, rows), out_shape=(...  6.13 us
    all_to_all x1, starting transfers between devices, per_device(): lax.all_to_all(leaving, ('lat', 'fld'), split_axis=0, concat_axis=0, tile...  5.83 us
    pallas_call x1, Pallas kernels, per_device(): pl.pallas_call(output_kernel, grid=(groups,), out_shape=jax.ShapeDtypeStr...  4.5 us
    all_to_all x1, waiting for transfers between devices, per_device(): lax.all_to_all(leaving, ('lat', 'fld'), split_axis=0, concat_axis=0, tile...  3.72 us
    pallas_call x1, Pallas kernels, per_device(): pl.pallas_call(functools.partial(prepare_kernel, cut_off, pairs, fields,...  2.86 us
  transfers between devices with their start and end apart: 2, of which 1 were waited for; matrix products, arithmetic and copies ran while one was open for 0% of the time, Pallas kernels for 11%

profile of v2, /device:TPU:0, one launch (start us, length us, event | category | flops | bytes accessed | tf_op | source)
XLA Modules:
  0.0 69.8 jit_solution(3308613629822388717)
XLA Ops:
  0.6 0.9 %copy-done.14 = bf16[5,1,2,5248]{3,2,1,0:T(2,128)(2,1)S(1)} copy-done((bf16[5,1,2,5248]{3,2,1,0:T(2,128)(2,1)S(1)}, bf16[5,1,2,5248]{3,2,1,0:T(2,128)(2,1)}, u32[]{:S(2)}) %copy-start.14) | copy-done | bytes 104984
  1.5 0.7 %copy-done.15 = s32[32,40]{1,0:T(8,128)S(1)} copy-done((s32[32,40]{1,0:T(8,128)S(1)}, s32[32,40]{1,0:T(8,128)}, u32[]{:S(2)}) %copy-start.15) | copy-done | bytes 5144
  2.2 0.7 copy-done.19
  2.9 0.7 copy-done.22
  3.6 8.6 %forward_rows.1 = (f32[32,8,128]{2,1,0:T(8,128)}, bf16[1280,1408]{1,0:T(8,128)(2,1)S(1)}, bf16[1280,1408]{1,0:T(8,128)(2,1)S(1)}, f32[1280,128]{1,0:T(8,128)S(1)}, f32[1280,128]{1,0:T(8,128)S(1)}) custom-call(s32[8]{0:T(128)S(1)} %copy-done.22, s32[8]{0:T(128)S(1)} %copy-done.19, s32[32,40]{1,0:T(8,128)S(1)} %copy-done.15, bf16[5,1,2,5248]{3,2,1,0:T(2,128)(2,1)S(1)} %copy-done.14), custom_call_target="tpu_custom_call" | custom-call | tf_op jit(solution)/shard_map/forward_rows/pallas_call | solution.py:480
  12.2 1.8 %copy-done = bf16[1280,1408]{1,0:T(8,128)(2,1)} copy-done((bf16[1280,1408]{1,0:T(8,128)(2,1)}, bf16[1280,1408]{1,0:T(8,128)(2,1)S(1)}, u32[]{:S(2)}) %copy-start) | copy-done | bytes 3604504
  14.0 1.8 %copy-done.2 = bf16[1280,1408]{1,0:T(8,128)(2,1)} copy-done((bf16[1280,1408]{1,0:T(8,128)(2,1)}, bf16[1280,1408]{1,0:T(8,128)(2,1)S(1)}, u32[]{:S(2)}) %copy-start.2) | copy-done | bytes 3604504
  15.8 0.9 %copy-done.11 = f32[1280,128]{1,0:T(8,128)} copy-done((f32[1280,128]{1,0:T(8,128)}, f32[1280,128]{1,0:T(8,128)S(1)}, u32[]{:S(2)}) %copy-start.11) | copy-done | bytes 655384
  16.6 7.3 %all-to-all-start = ((f32[32,8,128]{2,1,0:T(8,128)}), f32[32,8,128]{2,1,0:T(8,128)S(1)}, u32[]{:S(2)}, u32[]{:S(2)}) async-start(f32[32,8,128]{2,1,0:T(8,128)} %get-tuple-element.13), calls=%async_computation | async-start | bytes 262144 | tf_op jit(solution)/shard_map/all_to_all | solution.py:509
  24.0 1.2 %copy-done.10 = f32[20,1281,8]{1,2,0:T(8,128)S(1)} copy-done((f32[20,1281,8]{1,2,0:T(8,128)S(1)}, f32[20,1281,8]{1,2,0:T(8,128)}, u32[]{:S(2)}) %copy-start.10) | copy-done | bytes 819864
  25.1 0.7 %copy-done.16 = s32[32,40]{1,0:T(8,128)S(1)} copy-done((s32[32,40]{1,0:T(8,128)S(1)}, s32[32,40]{1,0:T(8,128)}, u32[]{:S(2)}) %copy-start.16) | copy-done | bytes 5144
  25.8 0.7 %copy-done.17 = f32[20,20]{1,0:T(8,128)S(1)} copy-done((f32[20,20]{1,0:T(8,128)S(1)}, f32[20,20]{1,0:T(8,128)}, u32[]{:S(2)}) %copy-start.17) | copy-done | bytes 1624
  26.5 0.7 %copy-done.18 = f32[20,20]{1,0:T(8,128)S(1)} copy-done((f32[20,20]{1,0:T(8,128)S(1)}, f32[20,20]{1,0:T(8,128)}, u32[]{:S(2)}) %copy-start.18) | copy-done | bytes 1624
  27.3 0.7 copy-done.24
  27.9 2.9 %prepare.1 = (bf16[640,1408]{1,0:T(8,128)(2,1)S(1)}, f32[480,1408]{1,0:T(8,128)S(1)}, bf16[960,512]{1,0:T(8,128)(2,1)S(1)}, bf16[128,192]{1,0:T(8,128)(2,1)S(1)}) custom-call(s32[32,40]{1,0:T(8,128)S(1)} %copy-done.16, f32[20]{0:T(128)S(1)} %copy-done.24, f32[20,8,1281]{2,1,0:T(8,128)S(1)} %bitcast.2, f32[20,20]{1,0:T(8,128)S(1)} %copy-done.17, ...), custom_call_target="tpu_custom_call" | custom-call | flops 100000000 | bytes 8000000 | tf_op jit(solution)/shard_map/prepare/pallas_call | solution.py:511
  30.8 1.5 %copy-done.4 = f32[480,1408]{1,0:T(8,128)} copy-done((f32[480,1408]{1,0:T(8,128)}, f32[480,1408]{1,0:T(8,128)S(1)}, u32[]{:S(2)}) %copy-start.4) | copy-done | bytes 2703384
  32.3 1.3 %copy-done.6 = bf16[640,1408]{1,0:T(8,128)(2,1)} copy-done((bf16[640,1408]{1,0:T(8,128)(2,1)}, bf16[640,1408]{1,0:T(8,128)(2,1)S(1)}, u32[]{:S(2)}) %copy-start.6) | copy-done | bytes 1802264
  33.6 0.9 %copy-done.8 = bf16[960,512]{1,0:T(8,128)(2,1)} copy-done((bf16[960,512]{1,0:T(8,128)(2,1)}, bf16[960,512]{1,0:T(8,128)(2,1)S(1)}, u32[]{:S(2)}) %copy-start.8) | copy-done | bytes 983064
  34.5 1.8 %copy-done.5 = f32[480,1408]{1,0:T(8,128)S(1)} copy-done((f32[480,1408]{1,0:T(8,128)S(1)}, f32[480,1408]{1,0:T(8,128)}, u32[]{:S(2)}) %copy-start.5) | copy-done | bytes 2703384
  36.3 1.5 %copy-done.7 = bf16[640,1408]{1,0:T(8,128)(2,1)S(1)} copy-done((bf16[640,1408]{1,0:T(8,128)(2,1)S(1)}, bf16[640,1408]{1,0:T(8,128)(2,1)}, u32[]{:S(2)}) %copy-start.7) | copy-done | bytes 1802264
  37.8 1.2 %copy-done.9 = bf16[960,512]{1,0:T(8,128)(2,1)S(1)} copy-done((bf16[960,512]{1,0:T(8,128)(2,1)S(1)}, bf16[960,512]{1,0:T(8,128)(2,1)}, u32[]{:S(2)}) %copy-start.9) | copy-done | bytes 983064
  39.0 0.7 copy-done.20
  39.6 6.1 %solve.1 = (bf16[960,1408]{1,0:T(8,128)(2,1)S(1)}, f32[32,8,128]{2,1,0:T(8,128)S(1)}) custom-call(s32[8]{0:T(128)S(1)} %copy-done.20, f32[32,8,128]{2,1,0:T(8,128)S(1)} %all-to-all-done.msg_ref, bf16[640,1408]{1,0:T(8,128)(2,1)S(1)} %copy-done.7, f32[480,1408]{1,0:T(8,128)S(1)} %copy-done.5, bf16[960,512]{1,0:T(8,128)(2,1)S(1)} %copy-done.9, ...), custom_call_target="tpu_custom_call" | custom-call | tf_op jit(solution)/shard_map/solve/pallas_call | solution.py:535
  46.4 5.8 %all-to-all-start.1 = ((f32[32,8,128]{2,1,0:T(8,128)}), f32[32,8,128]{2,1,0:T(8,128)S(1)}, u32[]{:S(2)}, u32[]{:S(2)}) async-start(f32[32,8,128]{2,1,0:T(8,128)} %copy-done.13), calls=%async_computation.1 | async-start | bytes 262144 | tf_op jit(solution)/shard_map/all_to_all | solution.py:552
  52.3 4.5 %spectral_output.1 = f32[20,20,2,1281]{3,2,1,0:T(2,128)} custom-call(bf16[960,1408]{1,0:T(8,128)(2,1)S(1)} %get-tuple-element.18.damped_ref, bf16[128,192]{1,0:T(8,128)(2,1)S(1)} %get-tuple-element.17.back_ref), custom_call_target="tpu_custom_call" | custom-call | flops 100000000 | bytes 8000000 | tf_op jit(solution)/shard_map/spectral_output/pallas_call | solution.py:554
  56.8 3.7 %all-to-all-done.1.msg_ref = f32[32,8,128]{2,1,0:T(8,128)S(1)} async-done(((f32[32,8,128]{2,1,0:T(8,128)}), f32[32,8,128]{2,1,0:T(8,128)S(1)}, u32[]{:S(2)}, u32[]{:S(2)}) %all-to-all-start.1) | async-done | bytes 131104 | tf_op jit(solution)/shard_map/all_to_all | solution.py:552
  60.5 2.0 %copy-done.1 = bf16[1280,1408]{1,0:T(8,128)(2,1)S(1)} copy-done((bf16[1280,1408]{1,0:T(8,128)(2,1)S(1)}, bf16[1280,1408]{1,0:T(8,128)(2,1)}, u32[]{:S(2)}) %copy-start.1) | copy-done | bytes 3604504
  62.5 2.0 %copy-done.3 = bf16[1280,1408]{1,0:T(8,128)(2,1)S(1)} copy-done((bf16[1280,1408]{1,0:T(8,128)(2,1)S(1)}, bf16[1280,1408]{1,0:T(8,128)(2,1)}, u32[]{:S(2)}) %copy-start.3) | copy-done | bytes 3604504
  64.5 1.1 %copy-done.12 = f32[1280,128]{1,0:T(8,128)S(1)} copy-done((f32[1280,128]{1,0:T(8,128)S(1)}, f32[1280,128]{1,0:T(8,128)}, u32[]{:S(2)}) %copy-start.12) | copy-done | bytes 655384
  65.6 0.7 copy-done.21
  66.3 0.7 copy-done.23
  66.9 2.8 %inverse_rows.1 = bf16[5,1,2,5248]{3,2,1,0:T(2,128)(2,1)} custom-call(s32[8]{0:T(128)S(1)} %copy-done.23, s32[8]{0:T(128)S(1)} %copy-done.21, f32[32,8,128]{2,1,0:T(8,128)S(1)} %all-to-all-done.1.msg_ref, bf16[1280,1408]{1,0:T(8,128)(2,1)S(1)} %copy-done.1, bf16[1280,1408]{1,0:T(8,128)(2,1)S(1)} %copy-done.3, f32[1280,128]{1,0:T(8,128)S(1)} %get-tuple-element.22.k1_ref, ...), custom_call_target="tpu_custom_call" | custom-call | tf_op jit(solution)/shard_map/inverse_rows/pallas_call | solution.py:571
  (27 shorter events, 0.7 us)
Async XLA Ops:
  0.6 0.9 %copy-start.14 = (bf16[5,1,2,5248]{3,2,1,0:T(2,128)(2,1)S(1)}, bf16[5,1,2,5248]{3,2,1,0:T(2,128)(2,1)}, u32[]{:S(2)}) copy-start(bf16[5,1,2,5248]{3,2,1,0:T(2,128)(2,1)} %grid_hbm.1) | copy-start | bytes 314884
  1.5 0.7 %copy-start.15 = (s32[32,40]{1,0:T(8,128)S(1)}, s32[32,40]{1,0:T(8,128)}, u32[]{:S(2)}) copy-start(s32[32,40]{1,0:T(8,128)} %fold_hbm.3) | copy-start | bytes 15364
  2.2 0.7 copy-start.19
  2.9 0.7 copy-start.22
  12.2 1.8 %copy-start = (bf16[1280,1408]{1,0:T(8,128)(2,1)}, bf16[1280,1408]{1,0:T(8,128)(2,1)S(1)}, u32[]{:S(2)}) copy-start(bf16[1280,1408]{1,0:T(8,128)(2,1)S(1)} %get-tuple-element.20.cos_ref) | copy-start | bytes 10813444
  14.0 1.8 %copy-start.2 = (bf16[1280,1408]{1,0:T(8,128)(2,1)}, bf16[1280,1408]{1,0:T(8,128)(2,1)S(1)}, u32[]{:S(2)}) copy-start(bf16[1280,1408]{1,0:T(8,128)(2,1)S(1)} %get-tuple-element.21.sin_ref) | copy-start | bytes 10813444
  15.8 0.9 %copy-start.11 = (f32[1280,128]{1,0:T(8,128)}, f32[1280,128]{1,0:T(8,128)S(1)}, u32[]{:S(2)}) copy-start(f32[1280,128]{1,0:T(8,128)S(1)} %get-tuple-element.23.k2_ref) | copy-start | bytes 1966084
  16.6 17.9 %all-to-all-start = ((f32[32,8,128]{2,1,0:T(8,128)}), f32[32,8,128]{2,1,0:T(8,128)S(1)}, u32[]{:S(2)}, u32[]{:S(2)}) async-start(f32[32,8,128]{2,1,0:T(8,128)} %get-tuple-element.13), calls=%async_computation | async-start | bytes 262144 | tf_op jit(solution)/shard_map/all_to_all | solution.py:509
  23.9 1.2 %copy-start.10 = (f32[20,1281,8]{1,2,0:T(8,128)S(1)}, f32[20,1281,8]{1,2,0:T(8,128)}, u32[]{:S(2)}) copy-start(f32[20,1281,8]{1,2,0:T(8,128)} %param.12) | copy-start | bytes 2459524
  25.1 0.7 %copy-start.16 = (s32[32,40]{1,0:T(8,128)S(1)}, s32[32,40]{1,0:T(8,128)}, u32[]{:S(2)}) copy-start(s32[32,40]{1,0:T(8,128)} %fold_hbm.3) | copy-start | bytes 15364
  25.8 0.7 %copy-start.17 = (f32[20,20]{1,0:T(8,128)S(1)}, f32[20,20]{1,0:T(8,128)}, u32[]{:S(2)}) copy-start(f32[20,20]{1,0:T(8,128)} %tm_hbm.1) | copy-start | bytes 4804
  26.5 0.7 %copy-start.18 = (f32[20,20]{1,0:T(8,128)S(1)}, f32[20,20]{1,0:T(8,128)}, u32[]{:S(2)}) copy-start(f32[20,20]{1,0:T(8,128)} %bm_hbm.1) | copy-start | bytes 4804
  27.3 0.7 copy-start.24
  30.8 1.5 %copy-start.4 = (f32[480,1408]{1,0:T(8,128)}, f32[480,1408]{1,0:T(8,128)S(1)}, u32[]{:S(2)}) copy-start(f32[480,1408]{1,0:T(8,128)S(1)} %get-tuple-element.15.factor_ref) | copy-start | bytes 8110084
  32.3 1.3 %copy-start.6 = (bf16[640,1408]{1,0:T(8,128)(2,1)}, bf16[640,1408]{1,0:T(8,128)(2,1)S(1)}, u32[]{:S(2)}) copy-start(bf16[640,1408]{1,0:T(8,128)(2,1)S(1)} %get-tuple-element.14.eh_ref) | copy-start | bytes 5406724
  33.6 0.9 %copy-start.8 = (bf16[960,512]{1,0:T(8,128)(2,1)}, bf16[960,512]{1,0:T(8,128)(2,1)S(1)}, u32[]{:S(2)}) copy-start(bf16[960,512]{1,0:T(8,128)(2,1)S(1)} %get-tuple-element.16.mix_ref) | copy-start | bytes 2949124
  34.5 1.8 %copy-start.5 = (f32[480,1408]{1,0:T(8,128)S(1)}, f32[480,1408]{1,0:T(8,128)}, u32[]{:S(2)}) copy-start(f32[480,1408]{1,0:T(8,128)} %copy-done.4) | copy-start | bytes 8110084
  36.3 1.5 %copy-start.7 = (bf16[640,1408]{1,0:T(8,128)(2,1)S(1)}, bf16[640,1408]{1,0:T(8,128)(2,1)}, u32[]{:S(2)}) copy-start(bf16[640,1408]{1,0:T(8,128)(2,1)} %copy-done.6) | copy-start | bytes 5406724
  37.8 1.2 %copy-start.9 = (bf16[960,512]{1,0:T(8,128)(2,1)S(1)}, bf16[960,512]{1,0:T(8,128)(2,1)}, u32[]{:S(2)}) copy-start(bf16[960,512]{1,0:T(8,128)(2,1)} %copy-done.8) | copy-start | bytes 2949124
  39.0 0.7 copy-start.20
  45.8 0.6 copy-start.13
  46.4 14.1 %all-to-all-start.1 = ((f32[32,8,128]{2,1,0:T(8,128)}), f32[32,8,128]{2,1,0:T(8,128)S(1)}, u32[]{:S(2)}, u32[]{:S(2)}) async-start(f32[32,8,128]{2,1,0:T(8,128)} %copy-done.13), calls=%async_computation.1 | async-start | bytes 262144 | tf_op jit(solution)/shard_map/all_to_all | solution.py:552
  60.5 2.0 %copy-start.1 = (bf16[1280,1408]{1,0:T(8,128)(2,1)S(1)}, bf16[1280,1408]{1,0:T(8,128)(2,1)}, u32[]{:S(2)}) copy-start(bf16[1280,1408]{1,0:T(8,128)(2,1)} %copy-done) | copy-start | bytes 10813444
  62.5 2.0 %copy-start.3 = (bf16[1280,1408]{1,0:T(8,128)(2,1)S(1)}, bf16[1280,1408]{1,0:T(8,128)(2,1)}, u32[]{:S(2)}) copy-start(bf16[1280,1408]{1,0:T(8,128)(2,1)} %copy-done.2) | copy-start | bytes 10813444
  64.5 1.1 %copy-start.12 = (f32[1280,128]{1,0:T(8,128)S(1)}, f32[1280,128]{1,0:T(8,128)}, u32[]{:S(2)}) copy-start(f32[1280,128]{1,0:T(8,128)} %copy-done.11) | copy-start | bytes 1966084
  65.6 0.7 copy-start.21
  66.3 0.7 copy-start.23

commit v3 on v2

--- a/solution.py
+++ b/solution.py
@@ -472,19 +472,24 @@
     hbm = pl.BlockSpec(memory_space=pltpu.HBM)
     vmem = pl.BlockSpec(memory_space=pltpu.VMEM)
     room = pltpu.CompilerParams(vmem_limit_bytes=ROOM)
-    message = jax.ShapeDtypeStruct((owners, 8, LANES), F32)
+    message = pltpu.HBM((owners, 8, LANES), F32)
     holders = band_map.shape[0]
     groups_f = everyone // fields
     dma = pltpu.SemaphoreType.DMA
+    row_lengths, band_map, fold_map, to_modes, back_modes, mode_rates, grid = (
+        pltpu.with_memory_space_constraint(x, pltpu.HBM)
+        for x in (row_lengths, band_map, fold_map, to_modes, back_modes, mode_rates, grid)
+    )
+    legendre = pltpu.with_memory_space_constraint(jnp.transpose(legendre, (0, 2, 1)), pltpu.HBM)
 
     sending, cos_table, sin_table, first_factor, second_factor = pl.pallas_call(
         functools.partial(forward_kernel, cut_off, groups),
         out_shape=(
             message,
-            jax.ShapeDtypeStruct((slots, across), BF16),
-            jax.ShapeDtypeStruct((slots, across), BF16),
-            jax.ShapeDtypeStruct((slots, LANES), F32),
-            jax.ShapeDtypeStruct((slots, LANES), F32),
+            pltpu.VMEM((slots, across), BF16),
+            pltpu.VMEM((slots, across), BF16),
+            pltpu.VMEM((slots, LANES), F32),
+            pltpu.VMEM((slots, LANES), F32),
         ),
         in_specs=[hbm] * 4,
         out_specs=(vmem,) * 5,
@@ -506,15 +511,19 @@
         name="forward_rows",
     )(row_lengths, band_map, fold_map, grid)
 
+    cos_table, sin_table, first_factor, second_factor = (
+        pltpu.with_memory_space_constraint(x, pltpu.VMEM)
+        for x in (cos_table, sin_table, first_factor, second_factor)
+    )
     arrived = lax.all_to_all(sending, ("lat", "fld"), split_axis=0, concat_axis=0, tiled=True)
 
     legs, factors, mix, back = pl.pallas_call(
         functools.partial(prepare_kernel, cut_off, pairs, fields, rows),
         out_shape=(
-            jax.ShapeDtypeStruct((groups * 16 * lats, span), BF16),
-            jax.ShapeDtypeStruct((groups * 4 * KPAD, span), F32),
-            jax.ShapeDtypeStruct((2 * groups * 4 * KPAD, groups_f * LANES), BF16),
-            jax.ShapeDtypeStruct((2 * FPAD, 8 * KPAD), BF16),
+            pltpu.VMEM((groups * 16 * lats, span), BF16),
+            pltpu.VMEM((groups * 4 * KPAD, span), F32),
+            pltpu.VMEM((2 * groups * 4 * KPAD, groups_f * LANES), BF16),
+            pltpu.VMEM((2 * FPAD, 8 * KPAD), BF16),
         ),
         in_specs=[hbm] * 5,
         out_specs=(vmem,) * 4,
@@ -530,11 +539,14 @@
         compiler_params=room,
         cost_estimate=pl.CostEstimate(flops=10**8, bytes_accessed=8 * 10**6, transcendentals=0),
         name="prepare",
-    )(fold_map, mode_rates, jnp.transpose(legendre, (0, 2, 1)), to_modes, back_modes)
-
+    )(fold_map, mode_rates, legendre, to_modes, back_modes)
+
+    legs, factors, mix, back = (
+        pltpu.with_memory_space_constraint(x, pltpu.VMEM) for x in (legs, factors, mix, back)
+    )
     damped, leaving = pl.pallas_call(
         functools.partial(solve_kernel, fields, rows),
-        out_shape=(jax.ShapeDtypeStruct((groups * 8 * KPAD, span), BF16), message),
+        out_shape=(pltpu.VMEM((groups * 8 * KPAD, span), BF16), message),
         in_specs=[hbm] + [vmem] * 5,
         out_specs=(vmem,) * 2,
         scratch_shapes=[
@@ -551,6 +563,7 @@
 
     returned = lax.all_to_all(leaving, ("lat", "fld"), split_axis=0, concat_axis=0, tiled=True)
 
+    damped = pltpu.with_memory_space_constraint(damped, pltpu.VMEM)
     spectral = pl.pallas_call(
         output_kernel,
         grid=(groups,),

time: 70.6 us -> 62.4 us (0.88)
  local copies, waits for them, and re-layouts: 27.2 us -> 17.7 us
  Pallas kernels: 25 us -> 26.6 us
  waiting for transfers between devices: 3.73 us -> 4.96 us
  starting transfers between devices: 13.1 us -> 11.9 us
    unnamed x50 -> x24, local copies, waits for them, and re-layouts: 27.2 us -> 17.7 us
    all_to_all x1, waiting for transfers between devices: 0.01 us -> 1.24 us  [per_device(): lax.all_to_all(sending, ('lat', 'fld'), split_axis=0, concat_axis=0, tile...]
    all_to_all x1, starting transfers between devices: 5.83 us -> 4.61 us  [per_device(): lax.all_to_all(leaving, ('lat', 'fld'), split_axis=0, concat_axis=0, tile...]
    pallas_call x1, Pallas kernels: 6.13 us -> 6.9 us  [per_device(): pl.pallas_call(functools.partial(solve_kernel, fields, rows), out_shape=(...]
  transfers between devices with their start and end apart: 2 -> 2, of which waited for: 1 -> 2; matrix products, arithmetic and copies ran while one was open for 0% -> 0% of each run, Pallas kernels for 11% -> 13%
where the time goes in v3:
time: 62.4 us; the launch traced here: 61.9 us
  Pallas kernels  26.6 us (43%)
  local copies, waits for them, and re-layouts  17.7 us (28%)
  starting transfers between devices  11.9 us (19%)
  waiting for transfers between devices  4.96 us (8%)
  between operations  0.7 us (1%)
    unnamed x24, local copies, waits for them, and re-layouts  17.7 us
    pallas_call x1, Pallas kernels, per_device(): pl.pallas_call(functools.partial(forward_kernel, cut_off, groups), out_sh...  8.98 us
    all_to_all x1, starting transfers between devices, per_device(): lax.all_to_all(sending, ('lat', 'fld'), split_axis=0, concat_axis=0, tile...  7.3 us
    pallas_call x1, Pallas kernels, per_device(): pl.pallas_call(functools.partial(solve_kernel, fields, rows), out_shape=(...  6.9 us
    all_to_all x1, starting transfers between devices, per_device(): lax.all_to_all(leaving, ('lat', 'fld'), split_axis=0, concat_axis=0, tile...  4.61 us
    pallas_call x1, Pallas kernels, per_device(): pl.pallas_call(output_kernel, grid=(groups,), out_shape=jax.ShapeDtypeStr...  4.51 us
    all_to_all x1, waiting for transfers between devices, per_device(): lax.all_to_all(leaving, ('lat', 'fld'), split_axis=0, concat_axis=0, tile...  3.72 us
    pallas_call x1, Pallas kernels, per_device(): pl.pallas_call(functools.partial(prepare_kernel, cut_off, pairs, fields,...  3.24 us
  transfers between devices with their start and end apart: 2, of which 2 were waited for; matrix products, arithmetic and copies ran while one was open for 0% of the time, Pallas kernels for 13%

profile of v3, /device:TPU:0, one launch (start us, length us, event | category | flops | bytes accessed | tf_op | source)
XLA Modules:
  0.0 61.9 jit_solution(1567160278414997845)
XLA Ops:
  0.6 9.0 %forward_rows.1 = (f32[32,8,128]{2,1,0:T(8,128)}, bf16[1280,1408]{1,0:T(8,128)(2,1)S(1)}, bf16[1280,1408]{1,0:T(8,128)(2,1)S(1)}, f32[1280,128]{1,0:T(8,128)S(1)}, f32[1280,128]{1,0:T(8,128)S(1)}) custom-call(s32[8]{0:T(128)} %len_hbm.3, s32[8]{0:T(128)} %band_hbm.5, s32[32,40]{1,0:T(8,128)} %fold_hbm.3, bf16[5,1,2,5248]{3,2,1,0:T(2,128)(2,1)} %grid_hbm.1), custom_call_target="tpu_custom_call" | custom-call | tf_op jit(solution)/shard_map/forward_rows/pallas_call | solution.py:485
  9.6 0.0 copy-start
  9.6 1.8 %copy-done = bf16[1280,1408]{1,0:T(8,128)(2,1)} copy-done((bf16[1280,1408]{1,0:T(8,128)(2,1)}, bf16[1280,1408]{1,0:T(8,128)(2,1)S(1)}, u32[]{:S(2)}) %copy-start) | copy-done | bytes 3604504
  11.4 0.0 copy-start.2
  11.4 1.8 %copy-done.2 = bf16[1280,1408]{1,0:T(8,128)(2,1)} copy-done((bf16[1280,1408]{1,0:T(8,128)(2,1)}, bf16[1280,1408]{1,0:T(8,128)(2,1)S(1)}, u32[]{:S(2)}) %copy-start.2) | copy-done | bytes 3604504
  13.2 0.0 copy-start.10
  13.2 0.9 %copy-done.10 = f32[1280,128]{1,0:T(8,128)} copy-done((f32[1280,128]{1,0:T(8,128)}, f32[1280,128]{1,0:T(8,128)S(1)}, u32[]{:S(2)}) %copy-start.10) | copy-done | bytes 655384
  14.1 7.3 %all-to-all-start = ((f32[32,8,128]{2,1,0:T(8,128)}), f32[32,8,128]{2,1,0:T(8,128)S(1)}, u32[]{:S(2)}, u32[]{:S(2)}) async-start(f32[32,8,128]{2,1,0:T(8,128)} %get-tuple-element.13), calls=%async_computation | async-start | bytes 262144 | tf_op jit(solution)/shard_map/all_to_all | solution.py:518
  21.4 3.2 %prepare.1 = (bf16[640,1408]{1,0:T(8,128)(2,1)S(1)}, f32[480,1408]{1,0:T(8,128)S(1)}, bf16[960,512]{1,0:T(8,128)(2,1)S(1)}, bf16[128,192]{1,0:T(8,128)(2,1)S(1)}) custom-call(s32[32,40]{1,0:T(8,128)} %fold_hbm.3, f32[20]{0:T(128)} %rates_hbm.1, f32[20,8,1281]{2,1,0:T(8,128)} %bitcast.3, f32[20,20]{1,0:T(8,128)} %tm_hbm.1, f32[20,20]{1,0:T(8,128)} %bm_hbm.1), custom_call_target="tpu_custom_call" | custom-call | flops 100000000 | bytes 8000000 | tf_op jit(solution)/shard_map/prepare/pallas_call | solution.py:520
  24.6 0.0 copy-start.4
  24.6 1.5 %copy-done.4 = f32[480,1408]{1,0:T(8,128)} copy-done((f32[480,1408]{1,0:T(8,128)}, f32[480,1408]{1,0:T(8,128)S(1)}, u32[]{:S(2)}) %copy-start.4) | copy-done | bytes 2703384
  26.1 0.0 copy-start.6
  26.1 1.3 %copy-done.6 = bf16[640,1408]{1,0:T(8,128)(2,1)} copy-done((bf16[640,1408]{1,0:T(8,128)(2,1)}, bf16[640,1408]{1,0:T(8,128)(2,1)S(1)}, u32[]{:S(2)}) %copy-start.6) | copy-done | bytes 1802264
  27.4 0.0 copy-start.8
  27.4 0.9 %copy-done.8 = bf16[960,512]{1,0:T(8,128)(2,1)} copy-done((bf16[960,512]{1,0:T(8,128)(2,1)}, bf16[960,512]{1,0:T(8,128)(2,1)S(1)}, u32[]{:S(2)}) %copy-start.8) | copy-done | bytes 983064
  28.4 1.2 %all-to-all-done.msg_ref = f32[32,8,128]{2,1,0:T(8,128)S(1)} async-done(((f32[32,8,128]{2,1,0:T(8,128)}), f32[32,8,128]{2,1,0:T(8,128)S(1)}, u32[]{:S(2)}, u32[]{:S(2)}) %all-to-all-start) | async-done | bytes 131104 | tf_op jit(solution)/shard_map/all_to_all | solution.py:518
  29.6 0.0 copy-start.5
  29.6 1.8 %copy-done.5 = f32[480,1408]{1,0:T(8,128)S(1)} copy-done((f32[480,1408]{1,0:T(8,128)S(1)}, f32[480,1408]{1,0:T(8,128)}, u32[]{:S(2)}) %copy-start.5) | copy-done | bytes 2703384
  31.4 0.0 copy-start.7
  31.4 1.5 %copy-done.7 = bf16[640,1408]{1,0:T(8,128)(2,1)S(1)} copy-done((bf16[640,1408]{1,0:T(8,128)(2,1)S(1)}, bf16[640,1408]{1,0:T(8,128)(2,1)}, u32[]{:S(2)}) %copy-start.7) | copy-done | bytes 1802264
  32.8 0.0 copy-start.9
  32.8 1.2 %copy-done.9 = bf16[960,512]{1,0:T(8,128)(2,1)S(1)} copy-done((bf16[960,512]{1,0:T(8,128)(2,1)S(1)}, bf16[960,512]{1,0:T(8,128)(2,1)}, u32[]{:S(2)}) %copy-start.9) | copy-done | bytes 983064
  34.0 6.9 %solve.1 = (bf16[960,1408]{1,0:T(8,128)(2,1)S(1)}, f32[32,8,128]{2,1,0:T(8,128)}) custom-call(s32[8]{0:T(128)} %band_hbm.5, f32[32,8,128]{2,1,0:T(8,128)S(1)} %all-to-all-done.msg_ref, bf16[640,1408]{1,0:T(8,128)(2,1)S(1)} %copy-done.7, f32[480,1408]{1,0:T(8,128)S(1)} %copy-done.5, bf16[960,512]{1,0:T(8,128)(2,1)S(1)} %copy-done.9, ...), custom_call_target="tpu_custom_call" | custom-call | tf_op jit(solution)/shard_map/solve/pallas_call | solution.py:547
  41.0 4.6 %all-to-all-start.1 = ((f32[32,8,128]{2,1,0:T(8,128)}), f32[32,8,128]{2,1,0:T(8,128)S(1)}, u32[]{:S(2)}, u32[]{:S(2)}) async-start(f32[32,8,128]{2,1,0:T(8,128)} %get-tuple-element.19), calls=%async_computation.1 | async-start | bytes 262144 | tf_op jit(solution)/shard_map/all_to_all | solution.py:564
  45.6 4.5 %spectral_output.1 = f32[20,20,2,1281]{3,2,1,0:T(2,128)} custom-call(bf16[960,1408]{1,0:T(8,128)(2,1)S(1)} %get-tuple-element.18.damped_ref, bf16[128,192]{1,0:T(8,128)(2,1)S(1)} %get-tuple-element.17.back_ref), custom_call_target="tpu_custom_call" | custom-call | flops 100000000 | bytes 8000000 | tf_op jit(solution)/shard_map/spectral_output/pallas_call | solution.py:567
  50.1 3.7 %all-to-all-done.1.msg_ref = f32[32,8,128]{2,1,0:T(8,128)S(1)} async-done(((f32[32,8,128]{2,1,0:T(8,128)}), f32[32,8,128]{2,1,0:T(8,128)S(1)}, u32[]{:S(2)}, u32[]{:S(2)}) %all-to-all-start.1) | async-done | bytes 131104 | tf_op jit(solution)/shard_map/all_to_all | solution.py:564
  53.8 0.0 copy-start.1
  53.8 2.0 %copy-done.1 = bf16[1280,1408]{1,0:T(8,128)(2,1)S(1)} copy-done((bf16[1280,1408]{1,0:T(8,128)(2,1)S(1)}, bf16[1280,1408]{1,0:T(8,128)(2,1)}, u32[]{:S(2)}) %copy-start.1) | copy-done | bytes 3604504
  55.8 0.0 copy-start.3
  55.8 2.0 %copy-done.3 = bf16[1280,1408]{1,0:T(8,128)(2,1)S(1)} copy-done((bf16[1280,1408]{1,0:T(8,128)(2,1)S(1)}, bf16[1280,1408]{1,0:T(8,128)(2,1)}, u32[]{:S(2)}) %copy-start.3) | copy-done | bytes 3604504
  57.8 1.1 %copy-done.11 = f32[1280,128]{1,0:T(8,128)S(1)} copy-done((f32[1280,128]{1,0:T(8,128)S(1)}, f32[1280,128]{1,0:T(8,128)}, u32[]{:S(2)}) %copy-start.11) | copy-done | bytes 655384
  58.9 3.0 %inverse_rows.1 = bf16[5,1,2,5248]{3,2,1,0:T(2,128)(2,1)} custom-call(s32[8]{0:T(128)} %len_hbm.3, s32[8]{0:T(128)} %band_hbm.5, f32[32,8,128]{2,1,0:T(8,128)S(1)} %all-to-all-done.1.msg_ref, bf16[1280,1408]{1,0:T(8,128)(2,1)S(1)} %copy-done.1, bf16[1280,1408]{1,0:T(8,128)(2,1)S(1)} %copy-done.3, f32[1280,128]{1,0:T(8,128)S(1)} %get-tuple-element.22.k1_ref, ...), custom_call_target="tpu_custom_call" | custom-call | tf_op jit(solution)/shard_map/inverse_rows/pallas_call | solution.py:584
  (1 shorter events, 0.0 us)
Async XLA Ops:
  9.6 1.8 %copy-start = (bf16[1280,1408]{1,0:T(8,128)(2,1)}, bf16[1280,1408]{1,0:T(8,128)(2,1)S(1)}, u32[]{:S(2)}) copy-start(bf16[1280,1408]{1,0:T(8,128)(2,1)S(1)} %get-tuple-element.20.cos_ref) | copy-start | bytes 10813444
  11.4 1.8 %copy-start.2 = (bf16[1280,1408]{1,0:T(8,128)(2,1)}, bf16[1280,1408]{1,0:T(8,128)(2,1)S(1)}, u32[]{:S(2)}) copy-start(bf16[1280,1408]{1,0:T(8,128)(2,1)S(1)} %get-tuple-element.21.sin_ref) | copy-start | bytes 10813444
  13.2 0.9 %copy-start.10 = (f32[1280,128]{1,0:T(8,128)}, f32[1280,128]{1,0:T(8,128)S(1)}, u32[]{:S(2)}) copy-start(f32[1280,128]{1,0:T(8,128)S(1)} %get-tuple-element.23.k2_ref) | copy-start | bytes 1966084
  14.1 15.5 %all-to-all-start = ((f32[32,8,128]{2,1,0:T(8,128)}), f32[32,8,128]{2,1,0:T(8,128)S(1)}, u32[]{:S(2)}, u32[]{:S(2)}) async-start(f32[32,8,128]{2,1,0:T(8,128)} %get-tuple-element.13), calls=%async_computation | async-start | bytes 262144 | tf_op jit(solution)/shard_map/all_to_all | solution.py:518
  24.6 1.5 %copy-start.4 = (f32[480,1408]{1,0:T(8,128)}, f32[480,1408]{1,0:T(8,128)S(1)}, u32[]{:S(2)}) copy-start(f32[480,1408]{1,0:T(8,128)S(1)} %get-tuple-element.15.factor_ref) | copy-start | bytes 8110084
  26.1 1.3 %copy-start.6 = (bf16[640,1408]{1,0:T(8,128)(2,1)}, bf16[640,1408]{1,0:T(8,128)(2,1)S(1)}, u32[]{:S(2)}) copy-start(bf16[640,1408]{1,0:T(8,128)(2,1)S(1)} %get-tuple-element.14.eh_ref) | copy-start | bytes 5406724
  27.4 0.9 %copy-start.8 = (bf16[960,512]{1,0:T(8,128)(2,1)}, bf16[960,512]{1,0:T(8,128)(2,1)S(1)}, u32[]{:S(2)}) copy-start(bf16[960,512]{1,0:T(8,128)(2,1)S(1)} %get-tuple-element.16.mix_ref) | copy-start | bytes 2949124
  29.6 1.8 %copy-start.5 = (f32[480,1408]{1,0:T(8,128)S(1)}, f32[480,1408]{1,0:T(8,128)}, u32[]{:S(2)}) copy-start(f32[480,1408]{1,0:T(8,128)} %copy-done.4) | copy-start | bytes 8110084
  31.4 1.5 %copy-start.7 = (bf16[640,1408]{1,0:T(8,128)(2,1)S(1)}, bf16[640,1408]{1,0:T(8,128)(2,1)}, u32[]{:S(2)}) copy-start(bf16[640,1408]{1,0:T(8,128)(2,1)} %copy-done.6) | copy-start | bytes 5406724
  32.8 1.2 %copy-start.9 = (bf16[960,512]{1,0:T(8,128)(2,1)S(1)}, bf16[960,512]{1,0:T(8,128)(2,1)}, u32[]{:S(2)}) copy-start(bf16[960,512]{1,0:T(8,128)(2,1)} %copy-done.8) | copy-start | bytes 2949124
  41.0 12.8 %all-to-all-start.1 = ((f32[32,8,128]{2,1,0:T(8,128)}), f32[32,8,128]{2,1,0:T(8,128)S(1)}, u32[]{:S(2)}, u32[]{:S(2)}) async-start(f32[32,8,128]{2,1,0:T(8,128)} %get-tuple-element.19), calls=%async_computation.1 | async-start | bytes 262144 | tf_op jit(solution)/shard_map/all_to_all | solution.py:564
  53.8 2.0 %copy-start.1 = (bf16[1280,1408]{1,0:T(8,128)(2,1)S(1)}, bf16[1280,1408]{1,0:T(8,128)(2,1)}, u32[]{:S(2)}) copy-start(bf16[1280,1408]{1,0:T(8,128)(2,1)} %copy-done) | copy-start | bytes 10813444
  55.8 2.0 %copy-start.3 = (bf16[1280,1408]{1,0:T(8,128)(2,1)S(1)}, bf16[1280,1408]{1,0:T(8,128)(2,1)}, u32[]{:S(2)}) copy-start(bf16[1280,1408]{1,0:T(8,128)(2,1)} %copy-done.2) | copy-start | bytes 10813444
  57.8 1.1 %copy-start.11 = (f32[1280,128]{1,0:T(8,128)S(1)}, f32[1280,128]{1,0:T(8,128)}, u32[]{:S(2)}) copy-start(f32[1280,128]{1,0:T(8,128)} %copy-done.10) | copy-start | bytes 1966084

commit v4 on v3

--- a/solution.py
+++ b/solution.py
@@ -11,6 +11,7 @@
 LANES = 128
 KPAD = 24
 FPAD = 64
+DEEP = 256
 ROOM = 24 * 1024 * 1024
 F32 = jnp.float32
 BF16 = jnp.bfloat16
@@ -89,18 +90,27 @@
     return jnp.concatenate(picks, axis=1).astype(BF16)
 
 
+def phases_of(groups, wave, length, lanes):
+    shape = (groups + 16, lanes)
+    row = row_iota(shape)
+    steps = jnp.where(row < groups, (row // 4) * (4 * DEEP) + row % 4, 4 * (row - groups))
+    steps = jnp.where(row >= groups + 8, 32 << jnp.maximum(row - groups - 8, 0), steps)
+    period = jnp.full(shape, length, jnp.int32).astype(F32)
+    return turn(steps.astype(F32) * wave, period, 1.0 / period)
+
+
 def forward_kernel(
     cut_off, groups, len_hbm, band_hbm, fold_hbm, grid_hbm,
-    msg_ref, cos_ref, sin_ref, k1_ref, k2_ref,
-    len_ref, band_ref, fold_ref, grid_ref, sems, fold_s, mb, cb, sb, xs, xq, ys,
+    msg_ref, tc_hbm, ts_hbm, fc_hbm, fs_hbm,
+    len_ref, band_ref, fold_ref, grid_ref, sems, fold_s, wave_s, xs, xq, tc, ts, fc, fs, xt, ys,
 ):
     fetch_all(
         (len_hbm, band_hbm, fold_hbm, grid_hbm), (len_ref, band_ref, fold_ref, grid_ref), sems
     )
     fields, _, rows, width = grid_ref.shape
     owners, per_owner = fold_ref.shape
-    slots, across = cos_ref.shape
-    chunks = across // LANES
+    slots = tc.shape[1]
+    pieces = xq.shape[0] // 64
     padded = groups * 8
     unit = rows * fields * 2
     length = len_ref[band_ref[lax.axis_index("lat")]]
@@ -108,16 +118,17 @@
 
     fold_s[...] = jnp.full(fold_s.shape, -1.0, F32)
     fold_s[0:owners, 0:per_owner] = fold_ref[...].astype(F32)
-    waves = jnp.transpose(fold_s[...])[0:padded]
-    small = waves.shape
-    period = jnp.full(small, length // 4, jnp.int32).astype(F32)
-    step_c, step_s = turn(waves * float(LANES), period, 1.0 / period)
+    lane = lane_iota((1, LANES))
+    tiles = [jnp.full((1, LANES), -1.0, F32) for _ in range(slots // LANES)]
     for owner in range(owners):
-        put = pl.ds(owner * padded, padded)
-        wide = (padded, LANES)
-        mb[put, :] = jnp.broadcast_to(waves[:, owner:owner + 1], wide)
-        cb[put, :] = jnp.broadcast_to(step_c[:, owner:owner + 1], wide)
-        sb[put, :] = jnp.broadcast_to(step_s[:, owner:owner + 1], wide)
+        at, off = divmod(owner * padded, LANES)
+        line = fold_s[owner:owner + 1, :]
+        if off:
+            line = pltpu.roll(line, off, 1)
+        tiles[at] = jnp.where((lane >= off) & (lane < off + padded), line, tiles[at])
+        if off + padded > LANES:
+            tiles[at + 1] = jnp.where(lane < off + padded - LANES, line, tiles[at + 1])
+    wave_s[...] = jnp.broadcast_to(jnp.concatenate(tiles, axis=1), wave_s.shape)
 
     xs[...] = jnp.zeros(xs.shape, F32)
     inside = lane_iota((rows, width)) < length
@@ -125,127 +136,156 @@
         points = grid_ref[field, 0].astype(F32)
         xs[rows * field:rows * (field + 1), 0:width] = jnp.where(inside, points, 0.0)
     stacked = jnp.concatenate(
-        [xs[:, 4 * LANES * c:4 * LANES * (c + 1)] for c in range(chunks)], axis=0
+        [xs[:, 4 * LANES * c:4 * LANES * (c + 1)] for c in range(2 * pieces)], axis=0
     ).astype(BF16)
-    phases = dot(stacked, spread_matrix()).astype(BF16)
-    for c in range(chunks):
+    spread = dot(stacked, spread_matrix()).astype(BF16)
+    for c in range(2 * pieces):
         for phase in range(4):
-            piece = phases[16 * c:16 * (c + 1), LANES * phase:LANES * (phase + 1)]
-            for half in (0, 64):
-                xq[half + 16 * phase:half + 16 * (phase + 1), LANES * c:LANES * (c + 1)] = piece
-
-    block = 32
-    shape = (block, LANES)
-    lane = lane_iota(shape)
-    lane_f = lane.astype(F32)
-    phase_f = ((lane % 64) // 16).astype(F32)
-    quarter_v = jnp.full(shape, length // 4, jnp.int32).astype(F32)
-    quarter_i = 1.0 / quarter_v
-    length_v = jnp.full(shape, length, jnp.int32).astype(F32)
-    length_i = 1.0 / length_v
-    top_v = jnp.full(shape, top, jnp.int32).astype(F32)
-
-    def table_block(i, carry):
+            at = (4 * (c // 2) + phase) * 16
+            off = LANES * (c % 2)
+            xq[at:at + 16, off:off + LANES] = spread[
+                16 * c:16 * (c + 1), LANES * phase:LANES * (phase + 1)
+            ]
+
+    turns = 4 * pieces
+    block = 2 * LANES
+    xt[64:128, :] = jnp.zeros((64, slots), F32)
+    values = xq[...]
+
+    def lane_block(i, carry):
         at = pl.ds(pl.multiple_of(i * block, block), block)
-        wave = mb[at, :]
-        c1 = cb[at, :]
-        s1 = sb[at, :]
-        c_old, s_old = turn(wave * lane_f, quarter_v, quarter_i)
-        c_now = c_old * c1 - s_old * s1
-        s_now = s_old * c1 + c_old * s1
-        twice = c1 + c1
-        cos_ref[at, 0:LANES] = c_old.astype(BF16)
-        sin_ref[at, 0:LANES] = s_old.astype(BF16)
-        for c in range(1, chunks):
-            cos_ref[at, LANES * c:LANES * (c + 1)] = c_now.astype(BF16)
-            sin_ref[at, LANES * c:LANES * (c + 1)] = s_now.astype(BF16)
-            c_old, c_now = c_now, twice * c_now - c_old
-            s_old, s_now = s_now, twice * s_now - s_old
-        co, si = turn(wave * phase_f, length_v, length_i)
-        weight = jnp.where(wave == 0.0, 1.0, 2.0)
-        weight = jnp.where((wave >= 0.0) & (wave <= top_v), weight, 0.0)
-        upper = lane >= 64
-        k1_ref[at, :] = jnp.where(upper, -si, co) * weight
-        k2_ref[at, :] = jnp.where(upper, co, si) * weight
+        wave = wave_s[:, at]
+        wave = jnp.concatenate([wave] * ((turns + 16) // 8), axis=0)
+        co, si = phases_of(turns, wave, length, block)
+        one = wave[0:1]
+        weight = jnp.where(one == 0.0, 1.0, 2.0)
+        weight = jnp.where((one >= 0.0) & (one <= jnp.full(one.shape, top, jnp.int32).astype(F32)), weight, 0.0)
+        fc[:, at] = co[0:turns] * weight
+        fs[:, at] = si[0:turns] * weight
+        c_all = co[turns:turns + 8]
+        s_all = si[turns:turns + 8]
+        size, step = 8, turns + 8
+        while size < DEEP:
+            c1 = co[step:step + 1]
+            s1 = si[step:step + 1]
+            c_new = c_all * c1 - s_all * s1
+            s_new = s_all * c1 + c_all * s1
+            c_all = jnp.concatenate([c_all, c_new], axis=0)
+            s_all = jnp.concatenate([s_all, s_new], axis=0)
+            size, step = 2 * size, step + 1
+        c_all = c_all.astype(BF16)
+        s_all = s_all.astype(BF16)
+        tc[:, at] = c_all
+        ts[:, at] = s_all
+        inner_c = dot(values, c_all)
+        inner_s = dot(values, s_all)
+        real = jnp.zeros((16, block), F32)
+        imag = jnp.zeros((16, block), F32)
+        for g in range(turns):
+            c1 = fc[g:g + 1, at]
+            s1 = fs[g:g + 1, at]
+            part_c = inner_c[16 * g:16 * (g + 1)]
+            part_s = inner_s[16 * g:16 * (g + 1)]
+            real = real + (c1 * part_c - s1 * part_s)
+            imag = imag - (c1 * part_s + s1 * part_c)
+        both = jnp.concatenate([real, imag], axis=0) * jnp.where(one == 0.0, 1.0, 0.5)
+        high = both.astype(BF16).astype(F32)
+        xt[0:32, at] = high
+        xt[32:64, at] = both - high
         return carry
 
-    lax.fori_loop(0, slots // block, table_block, 0)
-
-    big = 256
-    values = xq[...]
-
-    def dot_block(i, carry):
-        at = pl.ds(pl.multiple_of(i * big, big), big)
-        both = jnp.concatenate([cos_ref[at, :], sin_ref[at, :]], axis=0)
-        inner = dot_nt(both, values)
-        fix = jnp.where(mb[at, :] == 0.0, 1.0, 0.5)
-        ys[at, :] = (inner[0:big] * k1_ref[at, :] - inner[big:2 * big] * k2_ref[at, :]) * fix
-        return carry
-
-    lax.fori_loop(0, slots // big, dot_block, 0)
-
+    lax.fori_loop(0, slots // block, lane_block, 0)
+    keeps = [
+        pltpu.make_async_copy(source, target, sems.at[i])
+        for i, (source, target) in enumerate(
+            ((tc, tc_hbm), (ts, ts_hbm), (fc, fc_hbm), (fs, fs_hbm))
+        )
+    ]
+    for keep in keeps:
+        keep.start()
+
+    for c in range(slots // LANES):
+        ys[LANES * c:LANES * (c + 1), :] = jnp.transpose(xt[:, LANES * c:LANES * (c + 1)])
     turned = ys[...].reshape(owners, groups, 8, LANES)
     shape = (LANES, LANES)
     source = row_iota(shape)
     target = lane_iota(shape)
     vec = source % 16
-    base = (vec % rows) * (fields * 2) + (vec // rows) * 2 + source // 64
+    base = (vec % rows) * (fields * 2) + (vec // rows) * 2 + (source // 16) % 2
+    used = (vec < rows * fields) & (source < 64)
     total = jnp.zeros((owners * 8, LANES), F32)
     for t in range(groups):
-        place = jnp.where((vec < rows * fields) & (target == base + unit * t), 1.0, 0.0).astype(BF16)
-        high, low = split(turned[:, t].reshape(owners * 8, LANES))
-        total = total + dot(
-            jnp.concatenate([high, low], axis=1), jnp.concatenate([place, place], axis=0)
-        )
+        place = jnp.where(used & (target == base + unit * t), 1.0, 0.0).astype(BF16)
+        total = total + dot(turned[:, t].reshape(owners * 8, LANES).astype(BF16), place)
     scale = 1.0 / jnp.sqrt(jnp.full((owners * 8, LANES), length, jnp.int32).astype(F32))
     msg_ref[...] = (total * scale).reshape(owners, 8, LANES)
+    for keep in keeps:
+        keep.wait()
 
 
 def inverse_kernel(
-    groups, len_hbm, band_hbm, msg_ref, cos_ref, sin_ref, k1_ref, k2_ref, grid_ref,
-    len_ref, band_ref, sems, zs, os,
+    groups, len_hbm, band_hbm, fc_hbm, fs_hbm, tc_hbm, ts_hbm, msg_ref, grid_ref,
+    len_ref, band_ref, fc, fs, tc, ts, sems, zs, xt, zr, zi, os,
 ):
-    fetch_all((len_hbm, band_hbm), (len_ref, band_ref), sems)
+    copies = [
+        pltpu.make_async_copy(source, target, sems.at[i])
+        for i, (source, target) in enumerate(
+            (
+                (len_hbm, len_ref), (band_hbm, band_ref), (fc_hbm, fc),
+                (fs_hbm, fs), (tc_hbm, tc), (ts_hbm, ts),
+            )
+        )
+    ]
+    for copy in copies:
+        copy.start()
     fields, _, rows, width = grid_ref.shape
     owners = msg_ref.shape[0]
-    slots, across = cos_ref.shape
-    chunks = across // LANES
+    slots = tc.shape[1]
+    turns = fc.shape[0]
     unit = rows * fields * 2
-    length = len_ref[band_ref[lax.axis_index("lat")]]
     high, low = split(msg_ref[...].reshape(owners * 8, LANES))
     pieces = jnp.concatenate([high, low], axis=1)
-    shape = (LANES, 2 * LANES)
+    shape = (LANES, LANES)
     source = row_iota(shape)
     target = lane_iota(shape)
     vec = target % 16
-    upper = (target % LANES) >= 64
-    imag = target >= LANES
-    base = (vec % rows) * (fields * 2) + (vec // rows) * 2 + jnp.where(imag, 1, 0)
-    sign = jnp.where(upper != imag, -1.0, 1.0)
-    factor_a = k1_ref[...].reshape(owners, groups, 8, LANES)
-    factor_b = k2_ref[...].reshape(owners, groups, 8, LANES)
+    base = (vec % rows) * (fields * 2) + (vec // rows) * 2 + target // 16
+    used = (vec < rows * fields) & (target < 32)
     for t in range(groups):
-        place = jnp.where((vec < rows * fields) & (source == base + unit * t), sign, 0.0).astype(BF16)
-        both = dot(pieces, jnp.concatenate([place, place], axis=0))
-        z = (
-            both[:, 0:LANES] * factor_a[:, t].reshape(owners * 8, LANES)
-            + both[:, LANES:] * factor_b[:, t].reshape(owners * 8, LANES)
-        )
-        zs[:, t] = z.reshape(owners, 8, LANES)
-    turned = jnp.transpose(zs[...].reshape(slots, LANES)).astype(BF16)
-    real = turned[0:64]
-    imag_part = turned[64:128]
-    scale = 1.0 / jnp.sqrt(jnp.full((64, 2 * LANES), length, jnp.int32).astype(F32))
-    for start in range(0, across, 2 * LANES):
-        size = min(2 * LANES, across - start)
-        total = dot(real, cos_ref[:, start:start + size]) - dot(imag_part, sin_ref[:, start:start + size])
-        out = total * scale[:, 0:size]
+        place = jnp.where(used & (source == base + unit * t), 1.0, 0.0).astype(BF16)
+        zs[:, t] = dot(pieces, jnp.concatenate([place, place], axis=0)).reshape(owners, 8, LANES)
+    turned = zs[...].reshape(slots, LANES)
+    for c in range(slots // LANES):
+        xt[:, LANES * c:LANES * (c + 1)] = jnp.transpose(turned[LANES * c:LANES * (c + 1)])[0:32]
+    for copy in copies[0:4]:
+        copy.wait()
+    length = len_ref[band_ref[lax.axis_index("lat")]]
+    block = 2 * LANES
+
+    def lane_block(i, carry):
+        at = pl.ds(pl.multiple_of(i * block, block), block)
+        real = xt[0:16, at]
+        imag = xt[16:32, at]
+        for g in range(turns):
+            c1 = fc[g:g + 1, at]
+            s1 = fs[g:g + 1, at]
+            zr[16 * g:16 * (g + 1), at] = (c1 * real - s1 * imag).astype(BF16)
+            zi[16 * g:16 * (g + 1), at] = (s1 * real + c1 * imag).astype(BF16)
+        return carry
+
+    lax.fori_loop(0, slots // block, lane_block, 0)
+    for copy in copies[4:]:
+        copy.wait()
+    out = dot_nt(zr[...], tc[...]) - dot_nt(zi[...], ts[...])
+    out = out * (1.0 / jnp.sqrt(jnp.full((16 * turns, DEEP), length, jnp.int32).astype(F32)))
+    chunks = os.shape[0] // 16
+    for c in range(chunks):
         for phase in range(4):
-            for sub in range(size // LANES):
-                c = start // LANES + sub
-                os[16 * c:16 * (c + 1), LANES * phase:LANES * (phase + 1)] = out[
-                    16 * phase:16 * (phase + 1), LANES * sub:LANES * (sub + 1)
-                ].astype(BF16)
+            at = (4 * (c // 2) + phase) * 16
+            off = LANES * (c % 2)
+            os[16 * c:16 * (c + 1), LANES * phase:LANES * (phase + 1)] = out[
+                at:at + 16, off:off + LANES
+            ].astype(BF16)
     merged = dot_nt(os[...], spread_matrix())
     for c in range(chunks):
         begin = 4 * LANES * c
@@ -262,8 +302,9 @@
 
 def prepare_kernel(
     cut_off, pairs, fields, rows, fold_hbm, rates_hbm, leg_hbm, tm_hbm, bm_hbm,
-    eh_ref, factor_ref, mix_ref, back_ref,
+    eh_hbm, factor_hbm, mix_hbm, back_ref,
     fold_ref, rates_ref, leg_ref, tm_ref, bm_ref, sems, pad_s,
+    eh_ref, factor_ref, mix_ref, out_sems, mix_sem,
 ):
     fetch_all(
         (fold_hbm, rates_hbm, leg_hbm, tm_hbm, bm_hbm),
@@ -301,6 +342,8 @@
                     total.append(jnp.where(keep, piece, 0.0))
             at = (part * groups + t) * 4 * KPAD
             mix_ref[at:at + 4 * KPAD, :] = jnp.concatenate(total, axis=0).astype(BF16)
+    keeps = [pltpu.make_async_copy(mix_ref, mix_hbm, mix_sem)]
+    keeps[0].start()
 
     pad_s[...] = jnp.zeros(pad_s.shape, F32)
     pad_s[0:everyone, 0:everyone] = bm_ref[...]
@@ -352,15 +395,45 @@
         factor_ref[pl.ds(pl.multiple_of(pair * KPAD, 8), KPAD), :] = 1.0 / (1.0 + tau * rate)
         return carry
 
-    lax.fori_loop(0, 4 * groups, pair_block, 0)
+    for t in range(groups):
+        lax.fori_loop(4 * t, 4 * t + 4, pair_block, 0)
+        part = pl.ds(4 * KPAD * t, 4 * KPAD)
+        legs = pl.ds(2 * eight * t, 2 * eight)
+        for keep in (
+            pltpu.make_async_copy(factor_ref.at[part], factor_hbm.at[part], out_sems.at[0, t]),
+            pltpu.make_async_copy(eh_ref.at[legs], eh_hbm.at[legs], out_sems.at[1, t]),
+        ):
+            keep.start()
+            keeps.append(keep)
+    for keep in keeps:
+        keep.wait()
 
 
 def solve_kernel(
-    fields, rows, band_hbm, msg_ref, eh_ref, factor_ref, mix_ref, back_ref,
+    fields, rows, band_hbm, factor_hbm, eh_hbm, mix_hbm, msg_ref, back_ref,
     damped_ref, out_ref,
-    band_ref, sems, vs, fq, sums, cs,
+    band_ref, sems, vs, fq, sums, cs, factor_ref, eh_ref, mix_ref, in_sems,
 ):
-    fetch_all((band_hbm,), (band_ref,), sems)
+    first = [
+        pltpu.make_async_copy(band_hbm, band_ref, sems.at[0]),
+        pltpu.make_async_copy(mix_hbm, mix_ref, sems.at[1]),
+    ]
+    for copy in first:
+        copy.start()
+    later = []
+    legs_rows = 16 * band_ref.shape[0]
+    for t in range(fq.shape[0] // (4 * KPAD)):
+        part = pl.ds(4 * KPAD * t, 4 * KPAD)
+        legs = pl.ds(legs_rows * t, legs_rows)
+        later.append(
+            (
+                pltpu.make_async_copy(eh_hbm.at[legs], eh_ref.at[legs], in_sems.at[0, t]),
+                pltpu.make_async_copy(factor_hbm.at[part], factor_ref.at[part], in_sems.at[1, t]),
+            )
+        )
+        for copy in later[-1]:
+            copy.start()
+    first[0].wait()
     holders = band_ref.shape[0]
     groups_f = msg_ref.shape[0] // holders
     lats = holders
@@ -381,6 +454,7 @@
             )
         )
     v_high, v_low = split(jnp.concatenate(tall, axis=0))
+    first[1].wait()
     half = mix_ref.shape[0] // 2
     mix_h = mix_ref[0:half, :]
     fq[...] = dot_nt(mix_h, v_high) + dot_nt(mix_ref[half:, :], v_high) + dot_nt(mix_h, v_low)
@@ -409,7 +483,10 @@
         sums[legs, :] = dot_nt(eh_ref[legs, :], damped_ref[deep, :])
         return carry
 
-    lax.fori_loop(0, groups, quad_block, 0)
+    for t in range(groups):
+        for copy in later[t]:
+            copy.wait()
+        quad_block(t, 0)
 
     everything = sums[...]
     own = (row_iota(everything.shape) // lats) % 8 // 2 == lane_iota(everything.shape) // (2 * KPAD)
@@ -466,8 +543,8 @@
     owners, per_owner = fold_map.shape
     groups = -(-per_owner // 8)
     slots = owners * groups * 8
-    chunks = -(-(width // 4) // LANES)
-    across = chunks * LANES
+    pieces = -(-(width // 4) // DEEP)
+    turns = 4 * pieces
     span = -(-places // LANES) * LANES
     hbm = pl.BlockSpec(memory_space=pltpu.HBM)
     vmem = pl.BlockSpec(memory_space=pltpu.VMEM)
@@ -482,51 +559,53 @@
     )
     legendre = pltpu.with_memory_space_constraint(jnp.transpose(legendre, (0, 2, 1)), pltpu.HBM)
 
-    sending, cos_table, sin_table, first_factor, second_factor = pl.pallas_call(
+    sending, cos_table, sin_table, cos_turn, sin_turn = pl.pallas_call(
         functools.partial(forward_kernel, cut_off, groups),
         out_shape=(
             message,
-            pltpu.VMEM((slots, across), BF16),
-            pltpu.VMEM((slots, across), BF16),
-            pltpu.VMEM((slots, LANES), F32),
-            pltpu.VMEM((slots, LANES), F32),
+            pltpu.HBM((DEEP, slots), BF16),
+            pltpu.HBM((DEEP, slots), BF16),
+            pltpu.HBM((turns, slots), F32),
+            pltpu.HBM((turns, slots), F32),
         ),
         in_specs=[hbm] * 4,
-        out_specs=(vmem,) * 5,
+        out_specs=(vmem,) + (hbm,) * 4,
         scratch_shapes=[
             pltpu.SMEM(row_lengths.shape, jnp.int32),
             pltpu.SMEM(band_map.shape, jnp.int32),
             pltpu.VMEM(fold_map.shape, jnp.int32),
             pltpu.VMEM(grid.shape, BF16),
             dma((4,)),
-            pltpu.VMEM((LANES, LANES), F32),
-            pltpu.VMEM((slots, LANES), F32),
-            pltpu.VMEM((slots, LANES), F32),
-            pltpu.VMEM((slots, LANES), F32),
-            pltpu.VMEM((16, 4 * across), F32),
-            pltpu.VMEM((LANES, across), BF16),
+            pltpu.VMEM((max(owners, 8), LANES), F32),
+            pltpu.VMEM((8, slots), F32),
+            pltpu.VMEM((16, 4 * DEEP * pieces), F32),
+            pltpu.VMEM((16 * turns, DEEP), BF16),
+            pltpu.VMEM((DEEP, slots), BF16),
+            pltpu.VMEM((DEEP, slots), BF16),
+            pltpu.VMEM((turns, slots), F32),
+            pltpu.VMEM((turns, slots), F32),
+            pltpu.VMEM((LANES, slots), F32),
             pltpu.VMEM((slots, LANES), F32),
         ],
         compiler_params=room,
         name="forward_rows",
     )(row_lengths, band_map, fold_map, grid)
-
-    cos_table, sin_table, first_factor, second_factor = (
-        pltpu.with_memory_space_constraint(x, pltpu.VMEM)
-        for x in (cos_table, sin_table, first_factor, second_factor)
-    )
+    tables = [
+        pltpu.with_memory_space_constraint(x, pltpu.HBM)
+        for x in (cos_turn, sin_turn, cos_table, sin_table)
+    ]
     arrived = lax.all_to_all(sending, ("lat", "fld"), split_axis=0, concat_axis=0, tiled=True)
 
     legs, factors, mix, back = pl.pallas_call(
         functools.partial(prepare_kernel, cut_off, pairs, fields, rows),
         out_shape=(
-            pltpu.VMEM((groups * 16 * lats, span), BF16),
-            pltpu.VMEM((groups * 4 * KPAD, span), F32),
-            pltpu.VMEM((2 * groups * 4 * KPAD, groups_f * LANES), BF16),
+            pltpu.HBM((groups * 16 * lats, span), BF16),
+            pltpu.HBM((groups * 4 * KPAD, span), F32),
+            pltpu.HBM((2 * groups * 4 * KPAD, groups_f * LANES), BF16),
             pltpu.VMEM((2 * FPAD, 8 * KPAD), BF16),
         ),
         in_specs=[hbm] * 5,
-        out_specs=(vmem,) * 4,
+        out_specs=(hbm, hbm, hbm, vmem),
         scratch_shapes=[
             pltpu.SMEM(fold_map.shape, jnp.int32),
             pltpu.SMEM(mode_rates.shape, F32),
@@ -535,31 +614,41 @@
             pltpu.VMEM(back_modes.shape, F32),
             dma((5,)),
             pltpu.VMEM((KPAD, LANES), F32),
+            pltpu.VMEM((groups * 16 * lats, span), BF16),
+            pltpu.VMEM((groups * 4 * KPAD, span), F32),
+            pltpu.VMEM((2 * groups * 4 * KPAD, groups_f * LANES), BF16),
+            dma((2, groups)),
+            dma,
         ],
         compiler_params=room,
         cost_estimate=pl.CostEstimate(flops=10**8, bytes_accessed=8 * 10**6, transcendentals=0),
         name="prepare",
     )(fold_map, mode_rates, legendre, to_modes, back_modes)
 
-    legs, factors, mix, back = (
-        pltpu.with_memory_space_constraint(x, pltpu.VMEM) for x in (legs, factors, mix, back)
+    legs, factors, mix = (
+        pltpu.with_memory_space_constraint(x, pltpu.HBM) for x in (legs, factors, mix)
     )
+    back = pltpu.with_memory_space_constraint(back, pltpu.VMEM)
     damped, leaving = pl.pallas_call(
         functools.partial(solve_kernel, fields, rows),
         out_shape=(pltpu.VMEM((groups * 8 * KPAD, span), BF16), message),
-        in_specs=[hbm] + [vmem] * 5,
+        in_specs=[hbm] * 4 + [vmem] * 2,
         out_specs=(vmem,) * 2,
         scratch_shapes=[
             pltpu.SMEM(band_map.shape, jnp.int32),
-            dma((1,)),
+            dma((2,)),
             pltpu.VMEM((owners * 8, LANES), F32),
             pltpu.VMEM((groups * 4 * KPAD, 8 * lats), F32),
             pltpu.VMEM((groups * 16 * lats, 8 * KPAD), F32),
             pltpu.VMEM((groups * 16 * lats, LANES), F32),
+            pltpu.VMEM((groups * 4 * KPAD, span), F32),
+            pltpu.VMEM((groups * 16 * lats, span), BF16),
+            pltpu.VMEM((2 * groups * 4 * KPAD, groups_f * LANES), BF16),
+            dma((2, groups)),
         ],
         compiler_params=room,
         name="solve",
-    )(band_map, arrived, legs, factors, mix, back)
+    )(band_map, factors, legs, mix, arrived, back)
 
     returned = lax.all_to_all(leaving, ("lat", "fld"), split_axis=0, concat_axis=0, tiled=True)
 
@@ -584,18 +673,25 @@
     grid_out = pl.pallas_call(
         functools.partial(inverse_kernel, groups),
         out_shape=jax.ShapeDtypeStruct(grid.shape, BF16),
-        in_specs=[hbm, hbm] + [vmem] * 5,
+        in_specs=[hbm] * 6 + [vmem],
         out_specs=vmem,
         scratch_shapes=[
             pltpu.SMEM(row_lengths.shape, jnp.int32),
             pltpu.SMEM(band_map.shape, jnp.int32),
-            dma((2,)),
+            pltpu.VMEM((turns, slots), F32),
+            pltpu.VMEM((turns, slots), F32),
+            pltpu.VMEM((DEEP, slots), BF16),
+            pltpu.VMEM((DEEP, slots), BF16),
+            dma((6,)),
             pltpu.VMEM((owners, groups, 8, LANES), F32),
-            pltpu.VMEM((16 * chunks, 4 * LANES), BF16),
+            pltpu.VMEM((32, slots), F32),
+            pltpu.VMEM((16 * turns, slots), BF16),
+            pltpu.VMEM((16 * turns, slots), BF16),
+            pltpu.VMEM((32 * pieces, 4 * LANES), BF16),
         ],
         compiler_params=room,
         name="inverse_rows",
-    )(row_lengths, band_map, returned, cos_table, sin_table, first_factor, second_factor)
+    )(row_lengths, band_map, *tables, returned)
     return (jnp.transpose(spectral, (0, 2, 1, 3)), grid_out)
 
 

time: 62.4 us -> 44.5 us (0.71)
  local copies, waits for them, and re-layouts: 17.7 us -> 0 us
  waiting for transfers between devices: 4.96 us -> 7.73 us
  starting transfers between devices: 11.9 us -> 9.88 us
  Pallas kernels: 26.6 us -> 25.9 us
    unnamed x24 -> x0, local copies, waits for them, and re-layouts: 17.7 us -> none
    pallas_call x1, Pallas kernels: 8.98 us -> 4.67 us  [per_device(): pl.pallas_call(functools.partial(forward_kernel, cut_off, groups), out_sh...]
    all_to_all x1, waiting for transfers between devices: 1.24 us -> 4.01 us  [per_device(): lax.all_to_all(sending, ('lat', 'fld'), split_axis=0, concat_axis=0, tile...]
    pallas_call x1, Pallas kernels: 6.9 us -> 9.42 us  [per_device(): pl.pallas_call(functools.partial(solve_kernel, fields, rows), out_shape=(...]
    all_to_all x1, starting transfers between devices: 4.61 us -> 2.58 us  [per_device(): lax.all_to_all(leaving, ('lat', 'fld'), split_axis=0, concat_axis=0, tile...]
    pallas_call x1, Pallas kernels: 3.24 us -> 4.21 us  [per_device(): pl.pallas_call(functools.partial(prepare_kernel, cut_off, pairs, fields,...]
  transfers between devices with their start and end apart: 2 -> 2, of which waited for: 2 -> 2; matrix products, arithmetic and copies ran while one was open for 0% -> 0% of each run, Pallas kernels for 13% -> 20%
where the time goes in v4:
time: 44.5 us; the launch traced here: 44.2 us
  Pallas kernels  25.9 us (58%)
  starting transfers between devices  9.88 us (22%)
  waiting for transfers between devices  7.73 us (17%)
  between operations  0.67 us (2%)
    pallas_call x1, Pallas kernels, per_device(): pl.pallas_call(functools.partial(solve_kernel, fields, rows), out_shape=(...  9.42 us
    all_to_all x1, starting transfers between devices, per_device(): lax.all_to_all(sending, ('lat', 'fld'), split_axis=0, concat_axis=0, tile...  7.3 us
    pallas_call x1, Pallas kernels, per_device(): pl.pallas_call(functools.partial(forward_kernel, cut_off, groups), out_sh...  4.67 us
    pallas_call x1, Pallas kernels, per_device(): pl.pallas_call(output_kernel, grid=(groups,), out_shape=jax.ShapeDtypeStr...  4.51 us
    pallas_call x1, Pallas kernels, per_device(): pl.pallas_call(functools.partial(prepare_kernel, cut_off, pairs, fields,...  4.21 us
    all_to_all x1, waiting for transfers between devices, per_device(): lax.all_to_all(sending, ('lat', 'fld'), split_axis=0, concat_axis=0, tile...  4.01 us
    all_to_all x1, waiting for transfers between devices, per_device(): lax.all_to_all(leaving, ('lat', 'fld'), split_axis=0, concat_axis=0, tile...  3.72 us
    pallas_call x1, Pallas kernels, per_device(): pl.pallas_call(functools.partial(inverse_kernel, groups), out_shape=jax.S...  3.07 us
  transfers between devices with their start and end apart: 2, of which 2 were waited for; matrix products, arithmetic and copies ran while one was open for 0% of the time, Pallas kernels for 20%

profile of v4, /device:TPU:0, one launch (start us, length us, event | category | flops | bytes accessed | tf_op | source)
XLA Modules:
  0.0 44.2 jit_solution(3947823899596467178)
XLA Ops:
  0.6 4.7 %forward_rows.1 = (f32[32,8,128]{2,1,0:T(8,128)}, bf16[256,1280]{1,0:T(8,128)(2,1)}, bf16[256,1280]{1,0:T(8,128)(2,1)}, f32[24,1280]{1,0:T(8,128)}, f32[24,1280]{1,0:T(8,128)}) custom-call(s32[8]{0:T(128)} %len_hbm.3, s32[8]{0:T(128)} %band_hbm.5, s32[32,40]{1,0:T(8,128)} %fold_hbm.3, bf16[5,1,2,5248]{3,2,1,0:T(2,128)(2,1)} %grid_hbm.1), custom_call_target="tpu_custom_call" | custom-call | tf_op jit(solution)/shard_map/forward_rows/pallas_call | solution.py:562
  5.3 7.3 %all-to-all-start = ((f32[32,8,128]{2,1,0:T(8,128)}), f32[32,8,128]{2,1,0:T(8,128)S(1)}, u32[]{:S(2)}, u32[]{:S(2)}) async-start(f32[32,8,128]{2,1,0:T(8,128)} %get-tuple-element.16), calls=%async_computation | async-start | bytes 262144 | tf_op jit(solution)/shard_map/all_to_all | solution.py:597
  12.6 4.2 %prepare.1 = (bf16[640,1408]{1,0:T(8,128)(2,1)}, f32[480,1408]{1,0:T(8,128)}, bf16[960,512]{1,0:T(8,128)(2,1)}, bf16[128,192]{1,0:T(8,128)(2,1)S(1)}) custom-call(s32[32,40]{1,0:T(8,128)} %fold_hbm.3, f32[20]{0:T(128)} %rates_hbm.1, f32[20,8,1281]{2,1,0:T(8,128)} %bitcast.3, f32[20,20]{1,0:T(8,128)} %tm_hbm.1, f32[20,20]{1,0:T(8,128)} %bm_hbm.1), custom_call_target="tpu_custom_call" | custom-call | flops 100000000 | bytes 8000000 | tf_op jit(solution)/shard_map/prepare/pallas_call | solution.py:599
  16.8 4.0 %all-to-all-done.msg_ref = f32[32,8,128]{2,1,0:T(8,128)S(1)} async-done(((f32[32,8,128]{2,1,0:T(8,128)}), f32[32,8,128]{2,1,0:T(8,128)S(1)}, u32[]{:S(2)}, u32[]{:S(2)}) %all-to-all-start) | async-done | bytes 131104 | tf_op jit(solution)/shard_map/all_to_all | solution.py:597
  20.9 9.4 %solve.1 = (bf16[960,1408]{1,0:T(8,128)(2,1)S(1)}, f32[32,8,128]{2,1,0:T(8,128)}) custom-call(s32[8]{0:T(128)} %band_hbm.5, f32[480,1408]{1,0:T(8,128)} %get-tuple-element.13.factor_hbm, bf16[640,1408]{1,0:T(8,128)(2,1)} %get-tuple-element.14.eh_hbm, bf16[960,512]{1,0:T(8,128)(2,1)} %get-tuple-element.15.mix_hbm, f32[32,8,128]{2,1,0:T(8,128)S(1)} %all-to-all-done.msg_ref, ...), custom_call_target="tpu_custom_call" | custom-call | tf_op jit(solution)/shard_map/solve/pallas_call | solution.py:632
  30.3 2.6 %all-to-all-start.1 = ((f32[32,8,128]{2,1,0:T(8,128)}), f32[32,8,128]{2,1,0:T(8,128)S(1)}, u32[]{:S(2)}, u32[]{:S(2)}) async-start(f32[32,8,128]{2,1,0:T(8,128)} %get-tuple-element.23), calls=%async_computation.1 | async-start | bytes 262144 | tf_op jit(solution)/shard_map/all_to_all | solution.py:653
  32.9 4.5 %spectral_output.1 = f32[20,20,2,1281]{3,2,1,0:T(2,128)} custom-call(bf16[960,1408]{1,0:T(8,128)(2,1)S(1)} %get-tuple-element.18.damped_ref, bf16[128,192]{1,0:T(8,128)(2,1)S(1)} %get-tuple-element.17.back_ref), custom_call_target="tpu_custom_call" | custom-call | flops 100000000 | bytes 8000000 | tf_op jit(solution)/shard_map/spectral_output/pallas_call | solution.py:656
  37.4 3.7 %all-to-all-done.1.msg_ref = f32[32,8,128]{2,1,0:T(8,128)S(1)} async-done(((f32[32,8,128]{2,1,0:T(8,128)}), f32[32,8,128]{2,1,0:T(8,128)S(1)}, u32[]{:S(2)}, u32[]{:S(2)}) %all-to-all-start.1) | async-done | bytes 131104 | tf_op jit(solution)/shard_map/all_to_all | solution.py:653
  41.1 3.1 %inverse_rows.1 = bf16[5,1,2,5248]{3,2,1,0:T(2,128)(2,1)} custom-call(s32[8]{0:T(128)} %len_hbm.3, s32[8]{0:T(128)} %band_hbm.5, f32[24,1280]{1,0:T(8,128)} %get-tuple-element.19.fc_hbm, f32[24,1280]{1,0:T(8,128)} %get-tuple-element.20.fs_hbm, bf16[256,1280]{1,0:T(8,128)(2,1)} %get-tuple-element.21.tc_hbm, bf16[256,1280]{1,0:T(8,128)(2,1)} %get-tuple-element.22.ts_hbm, ...), custom_call_target="tpu_custom_call" | custom-call | tf_op jit(solution)/shard_map/inverse_rows/pallas_call | solution.py:673
Async XLA Ops:
  5.3 15.5 %all-to-all-start = ((f32[32,8,128]{2,1,0:T(8,128)}), f32[32,8,128]{2,1,0:T(8,128)S(1)}, u32[]{:S(2)}, u32[]{:S(2)}) async-start(f32[32,8,128]{2,1,0:T(8,128)} %get-tuple-element.16), calls=%async_computation | async-start | bytes 262144 | tf_op jit(solution)/shard_map/all_to_all | solution.py:597
  30.3 10.8 %all-to-all-start.1 = ((f32[32,8,128]{2,1,0:T(8,128)}), f32[32,8,128]{2,1,0:T(8,128)S(1)}, u32[]{:S(2)}, u32[]{:S(2)}) async-start(f32[32,8,128]{2,1,0:T(8,128)} %get-tuple-element.23), calls=%async_computation.1 | async-start | bytes 262144 | tf_op jit(solution)/shard_map/all_to_all | solution.py:653

commit v5 on v4

--- a/solution.py
+++ b/solution.py
@@ -212,10 +212,11 @@
     target = lane_iota(shape)
     vec = source % 16
     base = (vec % rows) * (fields * 2) + (vec // rows) * 2 + (source // 16) % 2
+    mine = lax.axis_index("fld")
     used = (vec < rows * fields) & (source < 64)
     total = jnp.zeros((owners * 8, LANES), F32)
     for t in range(groups):
-        place = jnp.where(used & (target == base + unit * t), 1.0, 0.0).astype(BF16)
+        place = jnp.where(used & (target == (base + unit * (t + mine)) % LANES), 1.0, 0.0).astype(BF16)
         total = total + dot(turned[:, t].reshape(owners * 8, LANES).astype(BF16), place)
     scale = 1.0 / jnp.sqrt(jnp.full((owners * 8, LANES), length, jnp.int32).astype(F32))
     msg_ref[...] = (total * scale).reshape(owners, 8, LANES)
@@ -249,10 +250,10 @@
     source = row_iota(shape)
     target = lane_iota(shape)
     vec = target % 16
-    base = (vec % rows) * (fields * 2) + (vec // rows) * 2 + target // 16
+    base = (vec % rows + lax.axis_index("fld")) * (fields * 2) + (vec // rows) * 2 + target // 16
     used = (vec < rows * fields) & (target < 32)
     for t in range(groups):
-        place = jnp.where(used & (source == base + unit * t), 1.0, 0.0).astype(BF16)
+        place = jnp.where(used & (source == (base + unit * t) % LANES), 1.0, 0.0).astype(BF16)
         zs[:, t] = dot(pieces, jnp.concatenate([place, place], axis=0)).reshape(owners, 8, LANES)
     turned = zs[...].reshape(slots, LANES)
     for c in range(slots // LANES):
@@ -301,20 +302,18 @@
 
 
 def prepare_kernel(
-    cut_off, pairs, fields, rows, fold_hbm, rates_hbm, leg_hbm, tm_hbm, bm_hbm,
-    eh_hbm, factor_hbm, mix_hbm, back_ref,
-    fold_ref, rates_ref, leg_ref, tm_ref, bm_ref, sems, pad_s,
-    eh_ref, factor_ref, mix_ref, out_sems, mix_sem,
+    cut_off, pairs, fields, rows, fold_hbm, leg_hbm, tm_hbm, bm_hbm,
+    eh_hbm, mix_ref, back_ref, turn_ref,
+    fold_ref, leg_ref, tm_ref, bm_ref, sems, pad_s, eh_ref, out_sems,
 ):
     fetch_all(
-        (fold_hbm, rates_hbm, leg_hbm, tm_hbm, bm_hbm),
-        (fold_ref, rates_ref, leg_ref, tm_ref, bm_ref),
-        sems,
+        (fold_hbm, leg_hbm, tm_hbm, bm_hbm), (fold_ref, leg_ref, tm_ref, bm_ref), sems
     )
     everyone = tm_ref.shape[0]
     _, lats, places = leg_ref.shape
     groups_f = everyone // fields
     wf = fields * 2
+    unit = rows * wf
     span = eh_ref.shape[1]
     eight = 8 * lats
     groups = eh_ref.shape[0] // (2 * eight)
@@ -322,46 +321,39 @@
 
     pad_s[...] = jnp.zeros(pad_s.shape, F32)
     pad_s[0:everyone, 0:everyone] = tm_ref[...]
-    m_high, m_low = split(pad_s[...])
     shape = (LANES, LANES)
-    level = (lane_iota(shape) % wf) // 2
-    wide = []
-    for piece in (m_high, m_low):
-        parts = []
-        for g in range(groups_f):
-            pick = jnp.where(row_iota(shape) == fields * g + level, 1.0, 0.0).astype(BF16)
-            parts.append(dot(piece, pick))
-        wide.append(jnp.concatenate(parts, axis=1))
-    lane = lane_iota(wide[0].shape) % LANES
-    for part, piece in enumerate(wide):
-        for t in range(groups):
-            total = []
-            for r in range(rows):
-                for c in range(2):
-                    keep = (lane // wf == t * rows + r) & (lane % 2 == c)
-                    total.append(jnp.where(keep, piece, 0.0))
-            at = (part * groups + t) * 4 * KPAD
-            mix_ref[at:at + 4 * KPAD, :] = jnp.concatenate(total, axis=0).astype(BF16)
-    keeps = [pltpu.make_async_copy(mix_ref, mix_hbm, mix_sem)]
-    keeps[0].start()
+    level = (lane_iota(shape) // unit) * fields + (lane_iota(shape) % wf) // 2
+    pick = jnp.where(row_iota(shape) == level, 1.0, 0.0).astype(BF16)
+    lane = lane_iota((KPAD, LANES))
+    parts = []
+    for piece in split(pad_s[...]):
+        wide = dot(piece, pick)
+        total = []
+        for r in range(rows):
+            for c in range(2):
+                keep = ((lane % unit) // wf == r) & (lane % 2 == c) & (lane < unit * groups_f)
+                total.append(jnp.where(keep, wide, 0.0))
+        parts.append(jnp.concatenate(total, axis=0).astype(BF16))
+    mix_ref[...] = jnp.concatenate([parts[0], parts[1], parts[0]], axis=1)
 
     pad_s[...] = jnp.zeros(pad_s.shape, F32)
     pad_s[0:everyone, 0:everyone] = bm_ref[...]
     shape = (FPAD, KPAD)
     expand = jnp.where(row_iota(shape) // 2 == lane_iota(shape), 1.0, 0.0).astype(BF16)
-    shape = (LANES, 8 * KPAD)
+    shape = (LANES, 2 * LANES)
     repeat = jnp.where(row_iota(shape) == lane_iota(shape) % KPAD, 1.0, 0.0).astype(BF16)
-    shape = (FPAD, 8 * KPAD)
+    shape = (FPAD, 2 * LANES)
     same = row_iota(shape) % 2 == (lane_iota(shape) // KPAD) % 2
+    half = lane_iota((FPAD, LANES)) < 64
+    narrow = lane_iota((FPAD, LANES)) < 2 * KPAD
+    fulls = []
     for part, piece in enumerate(split(pad_s[...])):
-        full = dot(dot(expand, piece).astype(BF16), repeat)
-        back_ref[part * FPAD:(part + 1) * FPAD, :] = jnp.where(same, full, 0.0).astype(BF16)
-
-    rate_row = row_iota((KPAD, LANES))
-    rate = jnp.zeros((KPAD, LANES), F32)
-    for k in range(everyone):
-        rate = jnp.where(rate_row == k, rates_ref[k], rate)
-    rate = jnp.concatenate([rate] * (span // LANES), axis=1)
+        full = jnp.where(same, dot(dot(expand, piece).astype(BF16), repeat), 0.0)
+        back_ref[part * FPAD:(part + 1) * FPAD, :] = full[:, 0:8 * KPAD].astype(BF16)
+        fulls.append(jnp.where(narrow, full[:, 0:LANES], 0.0))
+    turn_ref[...] = jnp.concatenate(
+        [jnp.where(half, fulls[0], pltpu.roll(fulls[0], 64, 1)), fulls[1]], axis=1
+    ).astype(BF16)
 
     whole = places // LANES * LANES
     shape = (lats, span)
@@ -389,123 +381,134 @@
             eh_ref[pl.ds(pl.multiple_of(base + r * eight, 16), 2 * lats), :] = jnp.concatenate(
                 [jnp.where(first, rowset, 0.0), jnp.where(second, rowset, 0.0)], axis=0
             ).astype(BF16)
-        row = lane_iota((1, span))
-        degree = jnp.where(row > limit, row - 1, row + wave)
-        tau = (degree * (degree + 1)).astype(F32) * (1.0 / float(cut_off * (cut_off + 1)))
-        factor_ref[pl.ds(pl.multiple_of(pair * KPAD, 8), KPAD), :] = 1.0 / (1.0 + tau * rate)
         return carry
 
+    keeps = []
     for t in range(groups):
         lax.fori_loop(4 * t, 4 * t + 4, pair_block, 0)
-        part = pl.ds(4 * KPAD * t, 4 * KPAD)
-        legs = pl.ds(2 * eight * t, 2 * eight)
-        for keep in (
-            pltpu.make_async_copy(factor_ref.at[part], factor_hbm.at[part], out_sems.at[0, t]),
-            pltpu.make_async_copy(eh_ref.at[legs], eh_hbm.at[legs], out_sems.at[1, t]),
-        ):
-            keep.start()
-            keeps.append(keep)
+        part = pl.ds(2 * eight * t, 2 * eight)
+        keeps.append(pltpu.make_async_copy(eh_ref.at[part], eh_hbm.at[part], out_sems.at[t]))
+        keeps[-1].start()
     for keep in keeps:
         keep.wait()
 
 
 def solve_kernel(
-    fields, rows, band_hbm, factor_hbm, eh_hbm, mix_hbm, msg_ref, back_ref,
+    cut_off, pairs, fields, rows, band_hbm, fold_hbm, rates_hbm, eh_hbm, msg_ref, mix_ref, turn_ref,
     damped_ref, out_ref,
-    band_ref, sems, vs, fq, sums, cs, factor_ref, eh_ref, mix_ref, in_sems,
+    band_ref, fold_ref, rates_ref, sems, vs, cs, eh_ref, in_sems,
 ):
-    first = [
-        pltpu.make_async_copy(band_hbm, band_ref, sems.at[0]),
-        pltpu.make_async_copy(mix_hbm, mix_ref, sems.at[1]),
-    ]
-    for copy in first:
-        copy.start()
     later = []
-    legs_rows = 16 * band_ref.shape[0]
-    for t in range(fq.shape[0] // (4 * KPAD)):
-        part = pl.ds(4 * KPAD * t, 4 * KPAD)
-        legs = pl.ds(legs_rows * t, legs_rows)
-        later.append(
-            (
-                pltpu.make_async_copy(eh_hbm.at[legs], eh_ref.at[legs], in_sems.at[0, t]),
-                pltpu.make_async_copy(factor_hbm.at[part], factor_ref.at[part], in_sems.at[1, t]),
-            )
-        )
-        for copy in later[-1]:
-            copy.start()
-    first[0].wait()
-    holders = band_ref.shape[0]
-    groups_f = msg_ref.shape[0] // holders
-    lats = holders
-    groups = fq.shape[0] // (4 * KPAD)
+    for t in range(in_sems.shape[0]):
+        size = eh_ref.shape[0] // in_sems.shape[0]
+        part = pl.ds(size * t, size)
+        later.append(pltpu.make_async_copy(eh_hbm.at[part], eh_ref.at[part], in_sems.at[t]))
+        later[-1].start()
+    fetch_all((band_hbm, fold_hbm, rates_hbm), (band_ref, fold_ref, rates_ref), sems)
+    everyone = rates_ref.shape[0]
+    lats = band_ref.shape[0]
+    groups_f = msg_ref.shape[0] // lats
     wf = fields * 2
     unit = rows * wf
     span = eh_ref.shape[1]
     eight = 8 * lats
-    for holder in range(holders):
+    groups = eh_ref.shape[0] // (2 * eight)
+    deep = 8 * KPAD
+    owner = lax.axis_index("lat") * groups_f + lax.axis_index("fld")
+    for holder in range(lats):
         lat = band_ref[holder]
         for g in range(groups_f):
             vs[pl.ds(pl.multiple_of((g * lats + lat) * 8, 8), 8), :] = msg_ref[holder * groups_f + g]
+    lane = lane_iota((lats, LANES))
+    tiles = [
+        [vs[pl.ds(g * eight + i8, lats, stride=8), :] for g in range(groups_f)] for i8 in range(8)
+    ]
     tall = []
-    for i8 in range(8):
-        tall.append(
-            jnp.concatenate(
-                [vs[pl.ds(g * lats * 8 + i8, lats, stride=8), :] for g in range(groups_f)], axis=1
-            )
-        )
+    for t in range(groups):
+        for i8 in range(8):
+            line = tiles[i8][0]
+            for g in range(1, groups_f):
+                here = (lane - unit * (t + g)) % LANES < unit
+                line = jnp.where(here, tiles[i8][g], line)
+            if t:
+                line = pltpu.roll(line, LANES - unit * t, 1)
+            tall.append(line)
     v_high, v_low = split(jnp.concatenate(tall, axis=0))
-    first[1].wait()
-    half = mix_ref.shape[0] // 2
-    mix_h = mix_ref[0:half, :]
-    fq[...] = dot_nt(mix_h, v_high) + dot_nt(mix_ref[half:, :], v_high) + dot_nt(mix_h, v_low)
-    tall_rows = 8 * KPAD
-
-    def quad_block(t, carry):
-        mixed = fq[pl.ds(pl.multiple_of(t * 4 * KPAD, 8), 4 * KPAD), :]
-        mixed = jnp.concatenate([mixed[0:2 * KPAD], mixed[2 * KPAD:4 * KPAD]], axis=1)
-        slot_pair = (lane_iota(mixed.shape) % eight) // (2 * lats)
-        left = jnp.concatenate([jnp.where(slot_pair == pp, mixed, 0.0) for pp in range(4)], axis=0)
-        left = jnp.concatenate(split(left), axis=0)
-        legs = pl.ds(pl.multiple_of(t * 2 * eight, 16), 2 * eight)
-        deep = pl.ds(pl.multiple_of(t * tall_rows, 16), tall_rows)
-        factor_at = pl.multiple_of(t * 4 * KPAD, 8)
+    mixed = dot_nt(mix_ref[...], jnp.concatenate([v_high, v_high, v_low], axis=1))
+
+    rate_row = row_iota((KPAD, 2 * LANES))
+    rate = jnp.zeros((KPAD, 2 * LANES), F32)
+    for k in range(everyone):
+        rate = jnp.where(rate_row == k, rates_ref[k], rate)
+    slot_pair = (lane_iota((2 * KPAD, 2 * eight)) % eight) // (2 * lats)
+    blank = jnp.zeros((64 - 2 * KPAD, span), BF16)
+    front = lane_iota((lats, LANES)) < 64
+
+    for t in range(groups):
+        mine = mixed[:, eight * t:eight * (t + 1)]
+        mine = jnp.concatenate([mine[0:2 * KPAD], mine[2 * KPAD:4 * KPAD]], axis=1)
+        left = jnp.concatenate([jnp.where(slot_pair == pp, mine, 0.0) for pp in range(4)], axis=0)
+        left = jnp.concatenate(split(left), axis=1)
+        legs = pl.ds(2 * eight * t, 2 * eight)
+        later[t].wait()
+        waves, limits = [], []
+        for pp in range(4):
+            wave = fold_ref[owner, 2 * min(4 * t + pp, pairs - 1)]
+            waves.append(wave)
+            limits.append(cut_off - wave)
         for start in range(0, span, 2 * LANES):
             size = min(2 * LANES, span - start)
-            modes = dot(left, eh_ref[legs, start:start + size])
-            modes = modes[0:tall_rows] + modes[tall_rows:]
+            right = eh_ref[legs, start:start + size]
+            modes = dot(left, jnp.concatenate([right, right], axis=0))
+            place = start + lane_iota((1, size))
             damped = []
             for pp in range(4):
-                factor = factor_ref[pl.ds(factor_at + pp * KPAD, KPAD), start:start + size]
+                degree = jnp.where(place > limits[pp], place - 1, place + waves[pp])
+                tau = (degree * (degree + 1)).astype(F32) * (1.0 / float(cut_off * (cut_off + 1)))
+                below = 1.0 + tau * rate[:, 0:size]
+                factor = pl.reciprocal(below, approx=True)
+                factor = factor * (2.0 - below * factor)
                 at = 2 * pp * KPAD
                 damped.append(modes[at:at + KPAD] * factor)
                 damped.append(modes[at + KPAD:at + 2 * KPAD] * factor)
-            damped_ref[deep, start:start + size] = jnp.concatenate(damped, axis=0).astype(BF16)
-        sums[legs, :] = dot_nt(eh_ref[legs, :], damped_ref[deep, :])
-        return carry
-
-    for t in range(groups):
-        for copy in later[t]:
-            copy.wait()
-        quad_block(t, 0)
-
-    everything = sums[...]
-    own = (row_iota(everything.shape) // lats) % 8 // 2 == lane_iota(everything.shape) // (2 * KPAD)
-    own_h, own_l = split(jnp.where(own, everything, 0.0))
-    back_h = back_ref[0:FPAD, :]
-    cs[:, 0:FPAD] = dot_nt(own_h, back_h) + dot_nt(own_l, back_h) + dot_nt(own_h, back_ref[FPAD:, :])
+            damped_ref[deep * t:deep * (t + 1), start:start + size] = jnp.concatenate(
+                damped, axis=0
+            ).astype(BF16)
+        pieces = []
+        for pp in range(4):
+            at = deep * t + 2 * KPAD * pp
+            pieces += [damped_ref[at:at + 2 * KPAD, :], blank]
+        sums = dot_nt(eh_ref[legs, :], jnp.concatenate(pieces, axis=0))
+        highs, lows = [], []
+        for r in range(rows):
+            for i8 in range(8):
+                at = (r * 8 + i8) * lats
+                pp = i8 // 2
+                tile = sums[at:at + lats, LANES * (pp // 2):LANES * (pp // 2 + 1)]
+                if pp % 2:
+                    tile = pltpu.roll(tile, 64, 1)
+                high = tile.astype(BF16).astype(F32)
+                low = pltpu.roll(tile - high, 64, 1)
+                highs.append(jnp.where(front, high, low))
+                lows.append(jnp.where(front, high, 0.0))
+        own = jnp.concatenate(
+            [jnp.concatenate(highs, axis=0), jnp.concatenate(lows, axis=0)], axis=1
+        ).astype(BF16)
+        cs[2 * eight * t:2 * eight * (t + 1), 0:FPAD] = dot_nt(own, turn_ref[...])
 
     lane = lane_iota((8, LANES))
-    for holder in range(holders):
+    for holder in range(lats):
         lat = band_ref[holder]
         tiles = [jnp.zeros((8, LANES), F32) for _ in range(groups_f)]
         for t in range(groups):
             for r in range(rows):
-                put = unit * t + wf * r
+                put = wf * (rows * t + r)
                 piece = cs[pl.ds((t * rows + r) * eight + lat, 8, stride=lats), :]
-                keep = (lane >= put) & (lane < put + wf)
+                if put:
+                    piece = pltpu.roll(piece, put, 1)
                 for g in range(groups_f):
-                    moved = pltpu.roll(piece, (put - wf * g) % LANES, 1)
-                    tiles[g] = jnp.where(keep, moved, tiles[g])
+                    here = (lane - (put + wf * g)) % LANES < wf
+                    tiles[g] = jnp.where(here, piece, tiles[g])
         for g in range(groups_f):
             out_ref[holder * groups_f + g] = tiles[g]
 
@@ -596,59 +599,53 @@
     ]
     arrived = lax.all_to_all(sending, ("lat", "fld"), split_axis=0, concat_axis=0, tiled=True)
 
-    legs, factors, mix, back = pl.pallas_call(
+    legs, mix, back, turn_back = pl.pallas_call(
         functools.partial(prepare_kernel, cut_off, pairs, fields, rows),
         out_shape=(
             pltpu.HBM((groups * 16 * lats, span), BF16),
-            pltpu.HBM((groups * 4 * KPAD, span), F32),
-            pltpu.HBM((2 * groups * 4 * KPAD, groups_f * LANES), BF16),
+            pltpu.VMEM((2 * rows * KPAD, 3 * LANES), BF16),
             pltpu.VMEM((2 * FPAD, 8 * KPAD), BF16),
+            pltpu.VMEM((FPAD, 2 * LANES), BF16),
         ),
-        in_specs=[hbm] * 5,
-        out_specs=(hbm, hbm, hbm, vmem),
+        in_specs=[hbm] * 4,
+        out_specs=(hbm,) + (vmem,) * 3,
         scratch_shapes=[
             pltpu.SMEM(fold_map.shape, jnp.int32),
-            pltpu.SMEM(mode_rates.shape, F32),
             pltpu.VMEM((pairs, lats, places), F32),
             pltpu.VMEM(to_modes.shape, F32),
             pltpu.VMEM(back_modes.shape, F32),
-            dma((5,)),
+            dma((4,)),
             pltpu.VMEM((KPAD, LANES), F32),
             pltpu.VMEM((groups * 16 * lats, span), BF16),
-            pltpu.VMEM((groups * 4 * KPAD, span), F32),
-            pltpu.VMEM((2 * groups * 4 * KPAD, groups_f * LANES), BF16),
-            dma((2, groups)),
-            dma,
+            dma((groups,)),
         ],
         compiler_params=room,
         cost_estimate=pl.CostEstimate(flops=10**8, bytes_accessed=8 * 10**6, transcendentals=0),
         name="prepare",
-    )(fold_map, mode_rates, legendre, to_modes, back_modes)
-
-    legs, factors, mix = (
-        pltpu.with_memory_space_constraint(x, pltpu.HBM) for x in (legs, factors, mix)
+    )(fold_map, legendre, to_modes, back_modes)
+    legs = pltpu.with_memory_space_constraint(legs, pltpu.HBM)
+    mix, back, turn_back = (
+        pltpu.with_memory_space_constraint(x, pltpu.VMEM) for x in (mix, back, turn_back)
     )
-    back = pltpu.with_memory_space_constraint(back, pltpu.VMEM)
+
     damped, leaving = pl.pallas_call(
-        functools.partial(solve_kernel, fields, rows),
+        functools.partial(solve_kernel, cut_off, pairs, fields, rows),
         out_shape=(pltpu.VMEM((groups * 8 * KPAD, span), BF16), message),
-        in_specs=[hbm] * 4 + [vmem] * 2,
+        in_specs=[hbm] * 4 + [vmem] * 3,
         out_specs=(vmem,) * 2,
         scratch_shapes=[
             pltpu.SMEM(band_map.shape, jnp.int32),
-            dma((2,)),
+            pltpu.SMEM(fold_map.shape, jnp.int32),
+            pltpu.SMEM(mode_rates.shape, F32),
+            dma((3,)),
             pltpu.VMEM((owners * 8, LANES), F32),
-            pltpu.VMEM((groups * 4 * KPAD, 8 * lats), F32),
-            pltpu.VMEM((groups * 16 * lats, 8 * KPAD), F32),
             pltpu.VMEM((groups * 16 * lats, LANES), F32),
-            pltpu.VMEM((groups * 4 * KPAD, span), F32),
             pltpu.VMEM((groups * 16 * lats, span), BF16),
-            pltpu.VMEM((2 * groups * 4 * KPAD, groups_f * LANES), BF16),
-            dma((2, groups)),
+            dma((groups,)),
         ],
         compiler_params=room,
         name="solve",
-    )(band_map, factors, legs, mix, arrived, back)
+    )(band_map, fold_map, mode_rates, legs, arrived, mix, turn_back)
 
     returned = lax.all_to_all(leaving, ("lat", "fld"), split_axis=0, concat_axis=0, tiled=True)
 

time: 44.5 us -> 42.6 us (0.957)
  Pallas kernels: 25.9 us -> 23.6 us
    pallas_call x1, Pallas kernels: 9.42 us -> 7.46 us  [per_device(): pl.pallas_call(functools.partial(solve_kernel, cut_off, pairs, fields, ro...]
where the time goes in v5:
time: 42.6 us; the launch traced here: 42.2 us
  Pallas kernels  23.6 us (55%)
  starting transfers between devices  9.88 us (23%)
  waiting for transfers between devices  8.04 us (19%)
  between operations  0.67 us (2%)
    pallas_call x1, Pallas kernels, per_device(): pl.pallas_call(functools.partial(solve_kernel, cut_off, pairs, fields, ro...  7.46 us
    all_to_all x1, starting transfers between devices, per_device(): lax.all_to_all(sending, ('lat', 'fld'), split_axis=0, concat_axis=0, tile...  7.3 us
    pallas_call x1, Pallas kernels, per_device(): pl.pallas_call(functools.partial(forward_kernel, cut_off, groups), out_sh...  4.7 us
    pallas_call x1, Pallas kernels, per_device(): pl.pallas_call(output_kernel, grid=(groups,), out_shape=jax.ShapeDtypeStr...  4.5 us
    all_to_all x1, waiting for transfers between devices, per_device(): lax.all_to_all(sending, ('lat', 'fld'), split_axis=0, concat_axis=0, tile...  4.32 us
    pallas_call x1, Pallas kernels, per_device(): pl.pallas_call(functools.partial(prepare_kernel, cut_off, pairs, fields,...  3.9 us
    all_to_all x1, waiting for transfers between devices, per_device(): lax.all_to_all(leaving, ('lat', 'fld'), split_axis=0, concat_axis=0, tile...  3.72 us
    pallas_call x1, Pallas kernels, per_device(): pl.pallas_call(functools.partial(inverse_kernel, groups), out_shape=jax.S...  3.07 us
  transfers between devices with their start and end apart: 2, of which 2 were waited for; matrix products, arithmetic and copies ran while one was open for 0% of the time, Pallas kernels for 20%

profile of v5, /device:TPU:0, one launch (start us, length us, event | category | flops | bytes accessed | tf_op | source)
XLA Modules:
  0.0 42.2 jit_solution(12515967539759660341)
XLA Ops:
  0.6 4.7 %forward_rows.1 = (f32[32,8,128]{2,1,0:T(8,128)}, bf16[256,1280]{1,0:T(8,128)(2,1)}, bf16[256,1280]{1,0:T(8,128)(2,1)}, f32[24,1280]{1,0:T(8,128)}, f32[24,1280]{1,0:T(8,128)}) custom-call(s32[8]{0:T(128)} %len_hbm.3, s32[8]{0:T(128)} %band_hbm.5, s32[32,40]{1,0:T(8,128)} %fold_hbm.5, bf16[5,1,2,5248]{3,2,1,0:T(2,128)(2,1)} %grid_hbm.1), custom_call_target="tpu_custom_call" | custom-call | tf_op jit(solution)/shard_map/forward_rows/pallas_call | solution.py:565
  5.3 7.3 %all-to-all-start = ((f32[32,8,128]{2,1,0:T(8,128)}), f32[32,8,128]{2,1,0:T(8,128)S(1)}, u32[]{:S(2)}, u32[]{:S(2)}) async-start(f32[32,8,128]{2,1,0:T(8,128)} %get-tuple-element.14), calls=%async_computation | async-start | bytes 262144 | tf_op jit(solution)/shard_map/all_to_all | solution.py:600
  12.6 3.9 %prepare.1 = (bf16[640,1408]{1,0:T(8,128)(2,1)}, bf16[96,384]{1,0:T(8,128)(2,1)S(1)}, bf16[128,192]{1,0:T(8,128)(2,1)S(1)}, bf16[64,256]{1,0:T(8,128)(2,1)S(1)}) custom-call(s32[32,40]{1,0:T(8,128)} %fold_hbm.5, f32[20,8,1281]{2,1,0:T(8,128)} %bitcast.3, f32[20,20]{1,0:T(8,128)} %tm_hbm.1, f32[20,20]{1,0:T(8,128)} %bm_hbm.1), custom_call_target="tpu_custom_call" | custom-call | flops 100000000 | bytes 8000000 | tf_op jit(solution)/shard_map/prepare/pallas_call | solution.py:602
  16.6 4.3 %all-to-all-done.msg_ref = f32[32,8,128]{2,1,0:T(8,128)S(1)} async-done(((f32[32,8,128]{2,1,0:T(8,128)}), f32[32,8,128]{2,1,0:T(8,128)S(1)}, u32[]{:S(2)}, u32[]{:S(2)}) %all-to-all-start) | async-done | bytes 131104 | tf_op jit(solution)/shard_map/all_to_all | solution.py:600
  20.9 7.5 %solve.1 = (bf16[960,1408]{1,0:T(8,128)(2,1)S(1)}, f32[32,8,128]{2,1,0:T(8,128)}) custom-call(s32[8]{0:T(128)} %band_hbm.5, s32[32,40]{1,0:T(8,128)} %fold_hbm.5, f32[20]{0:T(128)} %rates_hbm.1, bf16[640,1408]{1,0:T(8,128)(2,1)} %get-tuple-element.13.eh_hbm, f32[32,8,128]{2,1,0:T(8,128)S(1)} %all-to-all-done.msg_ref, ...), custom_call_target="tpu_custom_call" | custom-call | tf_op jit(solution)/shard_map/solve/pallas_call | solution.py:631
  28.3 2.6 %all-to-all-start.1 = ((f32[32,8,128]{2,1,0:T(8,128)}), f32[32,8,128]{2,1,0:T(8,128)S(1)}, u32[]{:S(2)}, u32[]{:S(2)}) async-start(f32[32,8,128]{2,1,0:T(8,128)} %get-tuple-element.23), calls=%async_computation.1 | async-start | bytes 262144 | tf_op jit(solution)/shard_map/all_to_all | solution.py:650
  30.9 4.5 %spectral_output.1 = f32[20,20,2,1281]{3,2,1,0:T(2,128)} custom-call(bf16[960,1408]{1,0:T(8,128)(2,1)S(1)} %get-tuple-element.17.damped_ref, bf16[128,192]{1,0:T(8,128)(2,1)S(1)} %get-tuple-element.18.back_ref), custom_call_target="tpu_custom_call" | custom-call | flops 100000000 | bytes 8000000 | tf_op jit(solution)/shard_map/spectral_output/pallas_call | solution.py:653
  35.4 3.7 %all-to-all-done.1.msg_ref = f32[32,8,128]{2,1,0:T(8,128)S(1)} async-done(((f32[32,8,128]{2,1,0:T(8,128)}), f32[32,8,128]{2,1,0:T(8,128)S(1)}, u32[]{:S(2)}, u32[]{:S(2)}) %all-to-all-start.1) | async-done | bytes 131104 | tf_op jit(solution)/shard_map/all_to_all | solution.py:650
  39.2 3.1 %inverse_rows.1 = bf16[5,1,2,5248]{3,2,1,0:T(2,128)(2,1)} custom-call(s32[8]{0:T(128)} %len_hbm.3, s32[8]{0:T(128)} %band_hbm.5, f32[24,1280]{1,0:T(8,128)} %get-tuple-element.19.fc_hbm, f32[24,1280]{1,0:T(8,128)} %get-tuple-element.20.fs_hbm, bf16[256,1280]{1,0:T(8,128)(2,1)} %get-tuple-element.21.tc_hbm, bf16[256,1280]{1,0:T(8,128)(2,1)} %get-tuple-element.22.ts_hbm, ...), custom_call_target="tpu_custom_call" | custom-call | tf_op jit(solution)/shard_map/inverse_rows/pallas_call | solution.py:670
Async XLA Ops:
  5.3 15.5 %all-to-all-start = ((f32[32,8,128]{2,1,0:T(8,128)}), f32[32,8,128]{2,1,0:T(8,128)S(1)}, u32[]{:S(2)}, u32[]{:S(2)}) async-start(f32[32,8,128]{2,1,0:T(8,128)} %get-tuple-element.14), calls=%async_computation | async-start | bytes 262144 | tf_op jit(solution)/shard_map/all_to_all | solution.py:600
  28.3 10.8 %all-to-all-start.1 = ((f32[32,8,128]{2,1,0:T(8,128)}), f32[32,8,128]{2,1,0:T(8,128)S(1)}, u32[]{:S(2)}, u32[]{:S(2)}) async-start(f32[32,8,128]{2,1,0:T(8,128)} %get-tuple-element.23), calls=%async_computation.1 | async-start | bytes 262144 | tf_op jit(solution)/shard_map/all_to_all | solution.py:650

commit v6 on v5

--- a/solution.py
+++ b/solution.py
@@ -82,6 +82,13 @@
     return lax.broadcasted_iota(jnp.int32, shape, len(shape) - 2)
 
 
+def lanes_within(lane, start, size):
+    start %= LANES
+    if start + size <= LANES:
+        return (lane >= start) & (lane < start + size)
+    return (lane >= start) | (lane < start + size - LANES)
+
+
 def spread_matrix():
     shape = (4 * LANES, LANES)
     picks = []
@@ -101,8 +108,8 @@
 
 def forward_kernel(
     cut_off, groups, len_hbm, band_hbm, fold_hbm, grid_hbm,
-    msg_ref, tc_hbm, ts_hbm, fc_hbm, fs_hbm,
-    len_ref, band_ref, fold_ref, grid_ref, sems, fold_s, wave_s, xs, xq, tc, ts, fc, fs, xt, ys,
+    msg_ref, tc_hbm, ts_hbm, fc, fs,
+    len_ref, band_ref, fold_ref, grid_ref, sems, fold_s, wave_s, xs, xq, tc, ts, xt,
 ):
     fetch_all(
         (len_hbm, band_hbm, fold_hbm, grid_hbm), (len_ref, band_ref, fold_ref, grid_ref), sems
@@ -111,24 +118,23 @@
     owners, per_owner = fold_ref.shape
     slots = tc.shape[1]
     pieces = xq.shape[0] // 64
-    padded = groups * 8
     unit = rows * fields * 2
     length = len_ref[band_ref[lax.axis_index("lat")]]
     top = jnp.minimum(cut_off, (length - 1) // 2)
 
     fold_s[...] = jnp.full(fold_s.shape, -1.0, F32)
     fold_s[0:owners, 0:per_owner] = fold_ref[...].astype(F32)
-    lane = lane_iota((1, LANES))
-    tiles = [jnp.full((1, LANES), -1.0, F32) for _ in range(slots // LANES)]
-    for owner in range(owners):
-        at, off = divmod(owner * padded, LANES)
-        line = fold_s[owner:owner + 1, :]
-        if off:
-            line = pltpu.roll(line, off, 1)
-        tiles[at] = jnp.where((lane >= off) & (lane < off + padded), line, tiles[at])
-        if off + padded > LANES:
-            tiles[at + 1] = jnp.where(lane < off + padded - LANES, line, tiles[at + 1])
-    wave_s[...] = jnp.broadcast_to(jnp.concatenate(tiles, axis=1), wave_s.shape)
+    eights = jnp.floor(fold_s[...] * 0.125)
+    parts = jnp.concatenate([eights, fold_s[...] - 8.0 * eights], axis=1).astype(BF16)
+    shape = (owners * 8, fold_s.shape[0])
+    repeat = jnp.where(row_iota(shape) // 8 == lane_iota(shape), 1.0, 0.0).astype(BF16)
+    repeated = dot(repeat, parts)
+    lane = lane_iota(repeated.shape)
+    place = lane % LANES - row_iota(repeated.shape) % 8
+    weigh = jnp.where(lane_iota((8, 2 * LANES)) < LANES, 8.0, 1.0).astype(BF16)
+    for t in range(groups):
+        chosen = jnp.where(place == 8 * t, repeated, 0.0).astype(BF16)
+        wave_s[:, owners * 8 * t:owners * 8 * (t + 1)] = dot_nt(weigh, chosen)
 
     xs[...] = jnp.zeros(xs.shape, F32)
     inside = lane_iota((rows, width)) < length
@@ -149,11 +155,9 @@
 
     turns = 4 * pieces
     block = 2 * LANES
-    xt[64:128, :] = jnp.zeros((64, slots), F32)
     values = xq[...]
-
-    def lane_block(i, carry):
-        at = pl.ds(pl.multiple_of(i * block, block), block)
+    for i in range(slots // block):
+        at = pl.ds(i * block, block)
         wave = wave_s[:, at]
         wave = jnp.concatenate([wave] * ((turns + 16) // 8), axis=0)
         co, si = phases_of(turns, wave, length, block)
@@ -189,52 +193,40 @@
             real = real + (c1 * part_c - s1 * part_s)
             imag = imag - (c1 * part_s + s1 * part_c)
         both = jnp.concatenate([real, imag], axis=0) * jnp.where(one == 0.0, 1.0, 0.5)
-        high = both.astype(BF16).astype(F32)
-        xt[0:32, at] = high
-        xt[32:64, at] = both - high
-        return carry
-
-    lax.fori_loop(0, slots // block, lane_block, 0)
+        xt[:, at] = jnp.concatenate(split(both), axis=0)
     keeps = [
         pltpu.make_async_copy(source, target, sems.at[i])
         for i, (source, target) in enumerate(
-            ((tc, tc_hbm), (ts, ts_hbm), (fc, fc_hbm), (fs, fs_hbm))
+            ((tc, tc_hbm), (ts, ts_hbm))
         )
     ]
     for keep in keeps:
         keep.start()
 
-    for c in range(slots // LANES):
-        ys[LANES * c:LANES * (c + 1), :] = jnp.transpose(xt[:, LANES * c:LANES * (c + 1)])
-    turned = ys[...].reshape(owners, groups, 8, LANES)
-    shape = (LANES, LANES)
-    source = row_iota(shape)
-    target = lane_iota(shape)
+    turned = jnp.concatenate(
+        [xt[:, owners * 8 * t:owners * 8 * (t + 1)] for t in range(groups)], axis=0
+    )
+    shape = (LANES, 64 * groups)
+    source = lane_iota(shape)
     vec = source % 16
     base = (vec % rows) * (fields * 2) + (vec // rows) * 2 + (source // 16) % 2
-    mine = lax.axis_index("fld")
-    used = (vec < rows * fields) & (source < 64)
-    total = jnp.zeros((owners * 8, LANES), F32)
-    for t in range(groups):
-        place = jnp.where(used & (target == (base + unit * (t + mine)) % LANES), 1.0, 0.0).astype(BF16)
-        total = total + dot(turned[:, t].reshape(owners * 8, LANES).astype(BF16), place)
-    scale = 1.0 / jnp.sqrt(jnp.full((owners * 8, LANES), length, jnp.int32).astype(F32))
-    msg_ref[...] = (total * scale).reshape(owners, 8, LANES)
+    target = (base + unit * (source // 64 + lax.axis_index("fld"))) % LANES
+    place = jnp.where((vec < rows * fields) & (row_iota(shape) == target), 1.0, 0.0).astype(BF16)
+    total = dot(place, turned)
+    scale = 1.0 / jnp.sqrt(jnp.full(total.shape, length, jnp.int32).astype(F32))
+    msg_ref[...] = jnp.transpose(total * scale).reshape(owners, 8, LANES)
     for keep in keeps:
         keep.wait()
 
 
 def inverse_kernel(
-    groups, len_hbm, band_hbm, fc_hbm, fs_hbm, tc_hbm, ts_hbm, msg_ref, grid_ref,
-    len_ref, band_ref, fc, fs, tc, ts, sems, zs, xt, zr, zi, os,
+    groups, len_hbm, band_hbm, tc_hbm, ts_hbm, fc, fs, msg_ref, grid_ref,
+    len_ref, band_ref, tc, ts, sems, os,
 ):
     copies = [
         pltpu.make_async_copy(source, target, sems.at[i])
         for i, (source, target) in enumerate(
-            (
-                (len_hbm, len_ref), (band_hbm, band_ref), (fc_hbm, fc),
-                (fs_hbm, fs), (tc_hbm, tc), (ts_hbm, ts),
-            )
+            ((len_hbm, len_ref), (band_hbm, band_ref), (tc_hbm, tc), (ts_hbm, ts))
         )
     ]
     for copy in copies:
@@ -246,38 +238,34 @@
     unit = rows * fields * 2
     high, low = split(msg_ref[...].reshape(owners * 8, LANES))
     pieces = jnp.concatenate([high, low], axis=1)
-    shape = (LANES, LANES)
-    source = row_iota(shape)
-    target = lane_iota(shape)
+    shape = (32 * groups, 2 * LANES)
+    target = row_iota(shape) % 32
     vec = target % 16
-    base = (vec % rows + lax.axis_index("fld")) * (fields * 2) + (vec // rows) * 2 + target // 16
-    used = (vec < rows * fields) & (target < 32)
-    for t in range(groups):
-        place = jnp.where(used & (source == (base + unit * t) % LANES), 1.0, 0.0).astype(BF16)
-        zs[:, t] = dot(pieces, jnp.concatenate([place, place], axis=0)).reshape(owners, 8, LANES)
-    turned = zs[...].reshape(slots, LANES)
-    for c in range(slots // LANES):
-        xt[:, LANES * c:LANES * (c + 1)] = jnp.transpose(turned[LANES * c:LANES * (c + 1)])[0:32]
-    for copy in copies[0:4]:
+    base = (vec % rows) * (fields * 2) + (vec // rows) * 2 + target // 16
+    source = (base + unit * (row_iota(shape) // 32) + lax.axis_index("fld") * (fields * 2)) % LANES
+    place = jnp.where(
+        (vec < rows * fields) & (lane_iota(shape) % LANES == source), 1.0, 0.0
+    ).astype(BF16)
+    turned = dot_nt(place, pieces)
+    block = 2 * LANES
+    for copy in copies:
         copy.wait()
     length = len_ref[band_ref[lax.axis_index("lat")]]
-    block = 2 * LANES
-
-    def lane_block(i, carry):
-        at = pl.ds(pl.multiple_of(i * block, block), block)
-        real = xt[0:16, at]
-        imag = xt[16:32, at]
+    out = jnp.zeros((16 * turns, DEEP), F32)
+    for i in range(slots // block):
+        t, off = divmod(i * block, owners * 8)
+        real = turned[32 * t:32 * t + 16, off:off + block]
+        imag = turned[32 * t + 16:32 * t + 32, off:off + block]
+        at = pl.ds(i * block, block)
+        reals, imags = [], []
         for g in range(turns):
             c1 = fc[g:g + 1, at]
             s1 = fs[g:g + 1, at]
-            zr[16 * g:16 * (g + 1), at] = (c1 * real - s1 * imag).astype(BF16)
-            zi[16 * g:16 * (g + 1), at] = (s1 * real + c1 * imag).astype(BF16)
-        return carry
-
-    lax.fori_loop(0, slots // block, lane_block, 0)
-    for copy in copies[4:]:
-        copy.wait()
-    out = dot_nt(zr[...], tc[...]) - dot_nt(zi[...], ts[...])
+            reals.append(c1 * real - s1 * imag)
+            imags.append(s1 * real + c1 * imag)
+        reals = jnp.concatenate(reals, axis=0).astype(BF16)
+        imags = jnp.concatenate(imags, axis=0).astype(BF16)
+        out = out + (dot_nt(reals, tc[:, at]) - dot_nt(imags, ts[:, at]))
     out = out * (1.0 / jnp.sqrt(jnp.full((16 * turns, DEEP), length, jnp.int32).astype(F32)))
     chunks = os.shape[0] // 16
     for c in range(chunks):
@@ -302,12 +290,14 @@
 
 
 def prepare_kernel(
-    cut_off, pairs, fields, rows, fold_hbm, leg_hbm, tm_hbm, bm_hbm,
-    eh_hbm, mix_ref, back_ref, turn_ref,
-    fold_ref, leg_ref, tm_ref, bm_ref, sems, pad_s, eh_ref, out_sems,
+    cut_off, pairs, fields, rows, fold_hbm, band_hbm, rates_hbm, leg_hbm, tm_hbm, bm_hbm,
+    eh_hbm, mix_ref, back_ref, turn_ref, tau_ref, rate_ref,
+    fold_ref, band_ref, rates_ref, leg_ref, tm_ref, bm_ref, sems, pad_s, eh_ref, out_sems,
 ):
     fetch_all(
-        (fold_hbm, leg_hbm, tm_hbm, bm_hbm), (fold_ref, leg_ref, tm_ref, bm_ref), sems
+        (fold_hbm, band_hbm, rates_hbm, leg_hbm, tm_hbm, bm_hbm),
+        (fold_ref, band_ref, rates_ref, leg_ref, tm_ref, bm_ref),
+        sems,
     )
     everyone = tm_ref.shape[0]
     _, lats, places = leg_ref.shape
@@ -353,6 +343,29 @@
         fulls.append(jnp.where(narrow, full[:, 0:LANES], 0.0))
     turn_ref[...] = jnp.concatenate(
         [jnp.where(half, fulls[0], pltpu.roll(fulls[0], 64, 1)), fulls[1]], axis=1
+    ).astype(BF16)
+
+    row = row_iota((KPAD, 2 * LANES))
+    rate = jnp.zeros((KPAD, 2 * LANES), F32)
+    for k in range(everyone):
+        rate = jnp.where(row == k, rates_ref[k], rate)
+    rate_ref[...] = rate
+    line = lane_iota((1, span))
+    for pair in range(4 * groups):
+        wave = fold_ref[owner, 2 * min(pair, pairs - 1)]
+        degree = jnp.where(line > cut_off - wave, line - 1, line + wave)
+        tau_ref[pair:pair + 1, :] = (degree * (degree + 1)).astype(F32) * (
+            1.0 / float(cut_off * (cut_off + 1))
+        )
+
+    shape = (2 * eight, 2 * eight)
+    band = jnp.zeros(shape, jnp.int32)
+    for holder in range(lats):
+        band = jnp.where(row_iota(shape) % lats == holder, band_ref[holder], band)
+    order = jnp.where(
+        (row_iota(shape) // lats == lane_iota(shape) // lats) & (lane_iota(shape) % lats == band),
+        1.0,
+        0.0,
     ).astype(BF16)
 
     whole = places // LANES * LANES
@@ -387,6 +400,7 @@
     for t in range(groups):
         lax.fori_loop(4 * t, 4 * t + 4, pair_block, 0)
         part = pl.ds(2 * eight * t, 2 * eight)
+        eh_ref[part, :] = dot(order, eh_ref[part, :]).astype(BF16)
         keeps.append(pltpu.make_async_copy(eh_ref.at[part], eh_hbm.at[part], out_sems.at[t]))
         keeps[-1].start()
     for keep in keeps:
@@ -394,52 +408,40 @@
 
 
 def solve_kernel(
-    cut_off, pairs, fields, rows, band_hbm, fold_hbm, rates_hbm, eh_hbm, msg_ref, mix_ref, turn_ref,
-    damped_ref, out_ref,
-    band_ref, fold_ref, rates_ref, sems, vs, cs, eh_ref, in_sems,
+    fields, rows, lats, eh_hbm, msg_ref, mix_ref, turn_ref, tau_ref, rate_ref,
+    damped_ref, out_ref, cs, eh_ref, in_sems,
 ):
+    groups = in_sems.shape[0]
+    eight = 8 * lats
     later = []
-    for t in range(in_sems.shape[0]):
-        size = eh_ref.shape[0] // in_sems.shape[0]
-        part = pl.ds(size * t, size)
+    for t in range(groups):
+        part = pl.ds(2 * eight * t, 2 * eight)
         later.append(pltpu.make_async_copy(eh_hbm.at[part], eh_ref.at[part], in_sems.at[t]))
         later[-1].start()
-    fetch_all((band_hbm, fold_hbm, rates_hbm), (band_ref, fold_ref, rates_ref), sems)
-    everyone = rates_ref.shape[0]
-    lats = band_ref.shape[0]
-    groups_f = msg_ref.shape[0] // lats
+    groups_f = msg_ref.shape[0] // eight
     wf = fields * 2
     unit = rows * wf
     span = eh_ref.shape[1]
-    eight = 8 * lats
-    groups = eh_ref.shape[0] // (2 * eight)
     deep = 8 * KPAD
-    owner = lax.axis_index("lat") * groups_f + lax.axis_index("fld")
-    for holder in range(lats):
-        lat = band_ref[holder]
-        for g in range(groups_f):
-            vs[pl.ds(pl.multiple_of((g * lats + lat) * 8, 8), 8), :] = msg_ref[holder * groups_f + g]
     lane = lane_iota((lats, LANES))
     tiles = [
-        [vs[pl.ds(g * eight + i8, lats, stride=8), :] for g in range(groups_f)] for i8 in range(8)
+        [msg_ref[pl.ds(8 * g + i8, lats, stride=8 * groups_f), :] for g in range(groups_f)]
+        for i8 in range(8)
     ]
     tall = []
     for t in range(groups):
+        here = [lanes_within(lane, unit * (t + g), unit) for g in range(groups_f)]
         for i8 in range(8):
             line = tiles[i8][0]
             for g in range(1, groups_f):
-                here = (lane - unit * (t + g)) % LANES < unit
-                line = jnp.where(here, tiles[i8][g], line)
+                line = jnp.where(here[g], tiles[i8][g], line)
             if t:
                 line = pltpu.roll(line, LANES - unit * t, 1)
             tall.append(line)
     v_high, v_low = split(jnp.concatenate(tall, axis=0))
     mixed = dot_nt(mix_ref[...], jnp.concatenate([v_high, v_high, v_low], axis=1))
 
-    rate_row = row_iota((KPAD, 2 * LANES))
-    rate = jnp.zeros((KPAD, 2 * LANES), F32)
-    for k in range(everyone):
-        rate = jnp.where(rate_row == k, rates_ref[k], rate)
+    rate = rate_ref[...]
     slot_pair = (lane_iota((2 * KPAD, 2 * eight)) % eight) // (2 * lats)
     blank = jnp.zeros((64 - 2 * KPAD, span), BF16)
     front = lane_iota((lats, LANES)) < 64
@@ -451,20 +453,13 @@
         left = jnp.concatenate(split(left), axis=1)
         legs = pl.ds(2 * eight * t, 2 * eight)
         later[t].wait()
-        waves, limits = [], []
-        for pp in range(4):
-            wave = fold_ref[owner, 2 * min(4 * t + pp, pairs - 1)]
-            waves.append(wave)
-            limits.append(cut_off - wave)
         for start in range(0, span, 2 * LANES):
             size = min(2 * LANES, span - start)
             right = eh_ref[legs, start:start + size]
             modes = dot(left, jnp.concatenate([right, right], axis=0))
-            place = start + lane_iota((1, size))
             damped = []
             for pp in range(4):
-                degree = jnp.where(place > limits[pp], place - 1, place + waves[pp])
-                tau = (degree * (degree + 1)).astype(F32) * (1.0 / float(cut_off * (cut_off + 1)))
+                tau = tau_ref[4 * t + pp:4 * t + pp + 1, start:start + size]
                 below = 1.0 + tau * rate[:, 0:size]
                 factor = pl.reciprocal(below, approx=True)
                 factor = factor * (2.0 - below * factor)
@@ -497,20 +492,20 @@
         cs[2 * eight * t:2 * eight * (t + 1), 0:FPAD] = dot_nt(own, turn_ref[...])
 
     lane = lane_iota((8, LANES))
+    here = [
+        lanes_within(lane, wf * u, wf) for u in range(rows * groups + groups_f - 1)
+    ]
     for holder in range(lats):
-        lat = band_ref[holder]
         tiles = [jnp.zeros((8, LANES), F32) for _ in range(groups_f)]
-        for t in range(groups):
-            for r in range(rows):
-                put = wf * (rows * t + r)
-                piece = cs[pl.ds((t * rows + r) * eight + lat, 8, stride=lats), :]
-                if put:
-                    piece = pltpu.roll(piece, put, 1)
-                for g in range(groups_f):
-                    here = (lane - (put + wf * g)) % LANES < wf
-                    tiles[g] = jnp.where(here, piece, tiles[g])
+        for u in range(rows * groups):
+            piece = cs[pl.ds(u * eight + holder, 8, stride=lats), :]
+            if u:
+                piece = pltpu.roll(piece, wf * u, 1)
+            for g in range(groups_f):
+                tiles[g] = jnp.where(here[u + g], piece, tiles[g])
         for g in range(groups_f):
-            out_ref[holder * groups_f + g] = tiles[g]
+            at = (holder * groups_f + g) * 8
+            out_ref[at:at + 8, :] = tiles[g]
 
 
 def output_kernel(damped_ref, back_ref, spec_ref, bk):
@@ -568,53 +563,53 @@
             message,
             pltpu.HBM((DEEP, slots), BF16),
             pltpu.HBM((DEEP, slots), BF16),
-            pltpu.HBM((turns, slots), F32),
-            pltpu.HBM((turns, slots), F32),
+            pltpu.VMEM((turns, slots), F32),
+            pltpu.VMEM((turns, slots), F32),
         ),
         in_specs=[hbm] * 4,
-        out_specs=(vmem,) + (hbm,) * 4,
+        out_specs=(vmem, hbm, hbm, vmem, vmem),
         scratch_shapes=[
             pltpu.SMEM(row_lengths.shape, jnp.int32),
             pltpu.SMEM(band_map.shape, jnp.int32),
             pltpu.VMEM(fold_map.shape, jnp.int32),
             pltpu.VMEM(grid.shape, BF16),
             dma((4,)),
-            pltpu.VMEM((max(owners, 8), LANES), F32),
+            pltpu.VMEM((LANES, LANES), F32),
             pltpu.VMEM((8, slots), F32),
             pltpu.VMEM((16, 4 * DEEP * pieces), F32),
             pltpu.VMEM((16 * turns, DEEP), BF16),
             pltpu.VMEM((DEEP, slots), BF16),
             pltpu.VMEM((DEEP, slots), BF16),
-            pltpu.VMEM((turns, slots), F32),
-            pltpu.VMEM((turns, slots), F32),
-            pltpu.VMEM((LANES, slots), F32),
-            pltpu.VMEM((slots, LANES), F32),
+            pltpu.VMEM((64, slots), BF16),
         ],
         compiler_params=room,
         name="forward_rows",
     )(row_lengths, band_map, fold_map, grid)
     tables = [
-        pltpu.with_memory_space_constraint(x, pltpu.HBM)
-        for x in (cos_turn, sin_turn, cos_table, sin_table)
-    ]
+        pltpu.with_memory_space_constraint(x, pltpu.HBM) for x in (cos_table, sin_table)
+    ] + [pltpu.with_memory_space_constraint(x, pltpu.VMEM) for x in (cos_turn, sin_turn)]
     arrived = lax.all_to_all(sending, ("lat", "fld"), split_axis=0, concat_axis=0, tiled=True)
 
-    legs, mix, back, turn_back = pl.pallas_call(
+    legs, mix, back, turn_back, tau, rate = pl.pallas_call(
         functools.partial(prepare_kernel, cut_off, pairs, fields, rows),
         out_shape=(
             pltpu.HBM((groups * 16 * lats, span), BF16),
             pltpu.VMEM((2 * rows * KPAD, 3 * LANES), BF16),
             pltpu.VMEM((2 * FPAD, 8 * KPAD), BF16),
             pltpu.VMEM((FPAD, 2 * LANES), BF16),
+            pltpu.VMEM((groups * 4, span), F32),
+            pltpu.VMEM((KPAD, 2 * LANES), F32),
         ),
-        in_specs=[hbm] * 4,
-        out_specs=(hbm,) + (vmem,) * 3,
+        in_specs=[hbm] * 6,
+        out_specs=(hbm,) + (vmem,) * 5,
         scratch_shapes=[
             pltpu.SMEM(fold_map.shape, jnp.int32),
+            pltpu.SMEM(band_map.shape, jnp.int32),
+            pltpu.SMEM(mode_rates.shape, F32),
             pltpu.VMEM((pairs, lats, places), F32),
             pltpu.VMEM(to_modes.shape, F32),
             pltpu.VMEM(back_modes.shape, F32),
-            dma((4,)),
+            dma((6,)),
             pltpu.VMEM((KPAD, LANES), F32),
             pltpu.VMEM((groups * 16 * lats, span), BF16),
             dma((groups,)),
@@ -622,30 +617,30 @@
         compiler_params=room,
         cost_estimate=pl.CostEstimate(flops=10**8, bytes_accessed=8 * 10**6, transcendentals=0),
         name="prepare",
-    )(fold_map, legendre, to_modes, back_modes)
+    )(fold_map, band_map, mode_rates, legendre, to_modes, back_modes)
     legs = pltpu.with_memory_space_constraint(legs, pltpu.HBM)
-    mix, back, turn_back = (
-        pltpu.with_memory_space_constraint(x, pltpu.VMEM) for x in (mix, back, turn_back)
+    mix, back, turn_back, tau, rate = (
+        pltpu.with_memory_space_constraint(x, pltpu.VMEM)
+        for x in (mix, back, turn_back, tau, rate)
     )
 
     damped, leaving = pl.pallas_call(
-        functools.partial(solve_kernel, cut_off, pairs, fields, rows),
-        out_shape=(pltpu.VMEM((groups * 8 * KPAD, span), BF16), message),
-        in_specs=[hbm] * 4 + [vmem] * 3,
+        functools.partial(solve_kernel, fields, rows, lats),
+        out_shape=(
+            pltpu.VMEM((groups * 8 * KPAD, span), BF16),
+            pltpu.HBM((owners * 8, LANES), F32),
+        ),
+        in_specs=[hbm] + [vmem] * 5,
         out_specs=(vmem,) * 2,
         scratch_shapes=[
-            pltpu.SMEM(band_map.shape, jnp.int32),
-            pltpu.SMEM(fold_map.shape, jnp.int32),
-            pltpu.SMEM(mode_rates.shape, F32),
-            dma((3,)),
-            pltpu.VMEM((owners * 8, LANES), F32),
             pltpu.VMEM((groups * 16 * lats, LANES), F32),
             pltpu.VMEM((groups * 16 * lats, span), BF16),
             dma((groups,)),
         ],
         compiler_params=room,
         name="solve",
-    )(band_map, fold_map, mode_rates, legs, arrived, mix, turn_back)
+    )(legs, arrived.reshape(owners * 8, LANES), mix, turn_back, tau, rate)
+    leaving = leaving.reshape(owners, 8, LANES)
 
     returned = lax.all_to_all(leaving, ("lat", "fld"), split_axis=0, concat_axis=0, tiled=True)
 
@@ -670,20 +665,14 @@
     grid_out = pl.pallas_call(
         functools.partial(inverse_kernel, groups),
         out_shape=jax.ShapeDtypeStruct(grid.shape, BF16),
-        in_specs=[hbm] * 6 + [vmem],
+        in_specs=[hbm] * 4 + [vmem] * 3,
         out_specs=vmem,
         scratch_shapes=[
             pltpu.SMEM(row_lengths.shape, jnp.int32),
             pltpu.SMEM(band_map.shape, jnp.int32),
-            pltpu.VMEM((turns, slots), F32),
-            pltpu.VMEM((turns, slots), F32),
             pltpu.VMEM((DEEP, slots), BF16),
             pltpu.VMEM((DEEP, slots), BF16),
-            dma((6,)),
-            pltpu.VMEM((owners, groups, 8, LANES), F32),
-            pltpu.VMEM((32, slots), F32),
-            pltpu.VMEM((16 * turns, slots), BF16),
-            pltpu.VMEM((16 * turns, slots), BF16),
+            dma((4,)),
             pltpu.VMEM((32 * pieces, 4 * LANES), BF16),
         ],
         compiler_params=room,

time: 42.6 us -> 42.5 us (level)
  waiting for transfers between devices: 8.04 us -> 6.47 us
  Pallas kernels: 23.6 us -> 24.6 us
  starting transfers between devices: 9.88 us -> 10.4 us
    all_to_all x1, waiting for transfers between devices: 4.32 us -> 2.75 us  [per_device(): lax.all_to_all(sending, ('lat', 'fld'), split_axis=0, concat_axis=0, tile...]
    pallas_call x1, Pallas kernels: 3.9 us -> 5.47 us  [per_device(): pl.pallas_call(functools.partial(prepare_kernel, cut_off, pairs, fields,...]
    all_to_all x1, starting transfers between devices: 2.58 us -> 3.1 us  [per_device(): lax.all_to_all(leaving, ('lat', 'fld'), split_axis=0, concat_axis=0, tile...]
    pallas_call x1, Pallas kernels: 7.46 us -> 6.94 us  [per_device(): pl.pallas_call(functools.partial(solve_kernel, fields, rows, lats), out_s...]
  transfers between devices with their start and end apart: 2 -> 2, of which waited for: 2 -> 2; matrix products, arithmetic and copies ran while one was open for 0% -> 0% of each run, Pallas kernels for 20% -> 24%
where the time goes in v6:
time: 42.5 us; the launch traced here: 42.1 us
  Pallas kernels  24.6 us (58%)
  starting transfers between devices  10.4 us (24%)
  waiting for transfers between devices  6.47 us (15%)
  between operations  0.67 us (2%)
    all_to_all x1, starting transfers between devices, per_device(): lax.all_to_all(sending, ('lat', 'fld'), split_axis=0, concat_axis=0, tile...  7.3 us
    pallas_call x1, Pallas kernels, per_device(): pl.pallas_call(functools.partial(solve_kernel, fields, rows, lats), out_s...  6.94 us
    pallas_call x1, Pallas kernels, per_device(): pl.pallas_call(functools.partial(prepare_kernel, cut_off, pairs, fields,...  5.47 us
    pallas_call x1, Pallas kernels, per_device(): pl.pallas_call(functools.partial(forward_kernel, cut_off, groups), out_sh...  4.62 us
    pallas_call x1, Pallas kernels, per_device(): pl.pallas_call(output_kernel, grid=(groups,), out_shape=jax.ShapeDtypeStr...  4.51 us
    all_to_all x1, waiting for transfers between devices, per_device(): lax.all_to_all(leaving, ('lat', 'fld'), split_axis=0, concat_axis=0, tile...  3.72 us
    all_to_all x1, starting transfers between devices, per_device(): lax.all_to_all(leaving, ('lat', 'fld'), split_axis=0, concat_axis=0, tile...  3.1 us
    pallas_call x1, Pallas kernels, per_device(): pl.pallas_call(functools.partial(inverse_kernel, groups), out_shape=jax.S...  3.03 us
  transfers between devices with their start and end apart: 2, of which 2 were waited for; matrix products, arithmetic and copies ran while one was open for 0% of the time, Pallas kernels for 24%

profile of v6, /device:TPU:0, one launch (start us, length us, event | category | flops | bytes accessed | tf_op | source)
XLA Modules:
  0.0 42.1 jit_solution(12647361472069041624)
XLA Ops:
  0.6 4.6 %forward_rows.1 = (f32[32,8,128]{2,1,0:T(8,128)}, bf16[256,1280]{1,0:T(8,128)(2,1)}, bf16[256,1280]{1,0:T(8,128)(2,1)}, f32[24,1280]{1,0:T(8,128)S(1)}, f32[24,1280]{1,0:T(8,128)S(1)}) custom-call(s32[8]{0:T(128)} %len_hbm.3, s32[8]{0:T(128)} %band_hbm.5, s32[32,40]{1,0:T(8,128)} %fold_hbm.3, bf16[5,1,2,5248]{3,2,1,0:T(2,128)(2,1)} %grid_hbm.1), custom_call_target="tpu_custom_call" | custom-call | tf_op jit(solution)/shard_map/forward_rows/pallas_call | solution.py:560
  5.3 7.3 %all-to-all-start = ((f32[32,8,128]{2,1,0:T(8,128)}), f32[32,8,128]{2,1,0:T(8,128)S(1)}, u32[]{:S(2)}, u32[]{:S(2)}) async-start(f32[32,8,128]{2,1,0:T(8,128)} %get-tuple-element.16), calls=%async_computation | async-start | bytes 262144 | tf_op jit(solution)/shard_map/all_to_all | solution.py:591
  12.6 5.5 %prepare.1 = (bf16[640,1408]{1,0:T(8,128)(2,1)}, bf16[96,384]{1,0:T(8,128)(2,1)S(1)}, bf16[128,192]{1,0:T(8,128)(2,1)S(1)}, bf16[64,256]{1,0:T(8,128)(2,1)S(1)},...) custom-call(s32[32,40]{1,0:T(8,128)} %fold_hbm.3, s32[8]{0:T(128)} %band_hbm.5, f32[20]{0:T(128)} %rates_hbm.1, ...), custom_call_target="tpu_custom_call" | custom-call | flops 100000000 | bytes 8000000 | tf_op jit(solution)/shard_map/prepare/pallas_call | solution.py:593
  18.1 2.8 %all-to-all-done = f32[32,8,128]{2,1,0:T(8,128)S(1)} async-done(((f32[32,8,128]{2,1,0:T(8,128)}), f32[32,8,128]{2,1,0:T(8,128)S(1)}, u32[]{:S(2)}, u32[]{:S(2)}) %all-to-all-start) | async-done | bytes 131104 | tf_op jit(solution)/shard_map/all_to_all | solution.py:591
  20.8 6.9 %solve.1 = (bf16[960,1408]{1,0:T(8,128)(2,1)S(1)}, f32[256,128]{1,0:T(8,128)}) custom-call(bf16[640,1408]{1,0:T(8,128)(2,1)} %get-tuple-element.15.eh_hbm, f32[256,128]{1,0:T(8,128)S(1)} %bitcast.4, bf16[96,384]{1,0:T(8,128)(2,1)S(1)} %get-tuple-element.17.mix_ref, bf16[64,256]{1,0:T(8,128)(2,1)S(1)} %get-tuple-element.18.turn_ref, ...), custom_call_target="tpu_custom_call" | custom-call | tf_op jit(solution)/shard_map/solve/pallas_call | solution.py:627
  27.8 3.1 %all-to-all-start.1 = ((f32[32,8,128]{2,1,0:T(8,128)}), f32[32,8,128]{2,1,0:T(8,128)S(1)}, u32[]{:S(2)}, u32[]{:S(2)}) async-start(f32[32,8,128]{2,1,0:T(8,128)} %bitcast.7), calls=%async_computation.1 | async-start | bytes 262144 | tf_op jit(solution)/shard_map/all_to_all | solution.py:645
  30.9 4.5 %spectral_output.1 = f32[20,20,2,1281]{3,2,1,0:T(2,128)} custom-call(bf16[960,1408]{1,0:T(8,128)(2,1)S(1)} %get-tuple-element.21.damped_ref, bf16[128,192]{1,0:T(8,128)(2,1)S(1)} %get-tuple-element.22.back_ref), custom_call_target="tpu_custom_call" | custom-call | flops 100000000 | bytes 8000000 | tf_op jit(solution)/shard_map/spectral_output/pallas_call | solution.py:648
  35.4 3.7 %all-to-all-done.1.msg_ref = f32[32,8,128]{2,1,0:T(8,128)S(1)} async-done(((f32[32,8,128]{2,1,0:T(8,128)}), f32[32,8,128]{2,1,0:T(8,128)S(1)}, u32[]{:S(2)}, u32[]{:S(2)}) %all-to-all-start.1) | async-done | bytes 131104 | tf_op jit(solution)/shard_map/all_to_all | solution.py:645
  39.1 3.0 %inverse_rows.1 = bf16[5,1,2,5248]{3,2,1,0:T(2,128)(2,1)} custom-call(s32[8]{0:T(128)} %len_hbm.3, s32[8]{0:T(128)} %band_hbm.5, bf16[256,1280]{1,0:T(8,128)(2,1)} %get-tuple-element.23.tc_hbm, bf16[256,1280]{1,0:T(8,128)(2,1)} %get-tuple-element.24.ts_hbm, f32[24,1280]{1,0:T(8,128)S(1)} %get-tuple-element.25.fc, f32[24,1280]{1,0:T(8,128)S(1)} %get-tuple-element.26.fs, ...), custom_call_target="tpu_custom_call" | custom-call | tf_op jit(solution)/shard_map/inverse_rows/pallas_call | solution.py:665
Async XLA Ops:
  5.3 15.5 %all-to-all-start = ((f32[32,8,128]{2,1,0:T(8,128)}), f32[32,8,128]{2,1,0:T(8,128)S(1)}, u32[]{:S(2)}, u32[]{:S(2)}) async-start(f32[32,8,128]{2,1,0:T(8,128)} %get-tuple-element.16), calls=%async_computation | async-start | bytes 262144 | tf_op jit(solution)/shard_map/all_to_all | solution.py:591
  27.8 11.3 %all-to-all-start.1 = ((f32[32,8,128]{2,1,0:T(8,128)}), f32[32,8,128]{2,1,0:T(8,128)S(1)}, u32[]{:S(2)}, u32[]{:S(2)}) async-start(f32[32,8,128]{2,1,0:T(8,128)} %bitcast.7), calls=%async_computation.1 | async-start | bytes 262144 | tf_op jit(solution)/shard_map/all_to_all | solution.py:645

commit v7 on v6

--- a/solution.py
+++ b/solution.py
@@ -63,13 +63,17 @@
     return horner(COS_POLY, z), part * horner(SIN_POLY, z)
 
 
-def fetch_all(sources, targets, sems):
+def start_all(sources, targets, sems):
     copies = [
         pltpu.make_async_copy(source, target, sems.at[i])
         for i, (source, target) in enumerate(zip(sources, targets))
     ]
     for copy in copies:
         copy.start()
+    return copies
+
+
+def wait_all(copies):
     for copy in copies:
         copy.wait()
 
@@ -108,10 +112,10 @@
 
 def forward_kernel(
     cut_off, groups, len_hbm, band_hbm, fold_hbm, grid_hbm,
-    msg_ref, tc_hbm, ts_hbm, fc, fs,
-    len_ref, band_ref, fold_ref, grid_ref, sems, fold_s, wave_s, xs, xq, tc, ts, xt,
+    msg_ref, tc, ts, fc, fs,
+    len_ref, band_ref, fold_ref, grid_ref, sems, fold_s, wave_s, xs, xq, xt,
 ):
-    fetch_all(
+    copies = start_all(
         (len_hbm, band_hbm, fold_hbm, grid_hbm), (len_ref, band_ref, fold_ref, grid_ref), sems
     )
     fields, _, rows, width = grid_ref.shape
@@ -119,32 +123,40 @@
     slots = tc.shape[1]
     pieces = xq.shape[0] // 64
     unit = rows * fields * 2
+    spread_s = spread_matrix()
+    shape = (owners * 8, fold_s.shape[0])
+    repeat = jnp.where(row_iota(shape) // 8 == lane_iota(shape), 1.0, 0.0).astype(BF16)
+    weigh = jnp.where(lane_iota((8, 2 * LANES)) < LANES, 8.0, 1.0).astype(BF16)
+    shape = (LANES, 64 * groups)
+    source = lane_iota(shape)
+    vec = source % 16
+    base = (vec % rows) * (fields * 2) + (vec // rows) * 2 + (source // 16) % 2
+    target = (base + unit * (source // 64 + lax.axis_index("fld"))) % LANES
+    packing = jnp.where((vec < rows * fields) & (row_iota(shape) == target), 1.0, 0.0).astype(BF16)
+    fold_s[...] = jnp.full(fold_s.shape, -1.0, F32)
+    xs[...] = jnp.zeros(xs.shape, F32)
+    wait_all(copies)
     length = len_ref[band_ref[lax.axis_index("lat")]]
     top = jnp.minimum(cut_off, (length - 1) // 2)
 
-    fold_s[...] = jnp.full(fold_s.shape, -1.0, F32)
     fold_s[0:owners, 0:per_owner] = fold_ref[...].astype(F32)
     eights = jnp.floor(fold_s[...] * 0.125)
     parts = jnp.concatenate([eights, fold_s[...] - 8.0 * eights], axis=1).astype(BF16)
-    shape = (owners * 8, fold_s.shape[0])
-    repeat = jnp.where(row_iota(shape) // 8 == lane_iota(shape), 1.0, 0.0).astype(BF16)
     repeated = dot(repeat, parts)
     lane = lane_iota(repeated.shape)
     place = lane % LANES - row_iota(repeated.shape) % 8
-    weigh = jnp.where(lane_iota((8, 2 * LANES)) < LANES, 8.0, 1.0).astype(BF16)
     for t in range(groups):
         chosen = jnp.where(place == 8 * t, repeated, 0.0).astype(BF16)
         wave_s[:, owners * 8 * t:owners * 8 * (t + 1)] = dot_nt(weigh, chosen)
 
-    xs[...] = jnp.zeros(xs.shape, F32)
-    inside = lane_iota((rows, width)) < length
     for field in range(fields):
-        points = grid_ref[field, 0].astype(F32)
-        xs[rows * field:rows * (field + 1), 0:width] = jnp.where(inside, points, 0.0)
+        xs[rows * field:rows * (field + 1), 0:width] = grid_ref[field, 0].astype(F32)
     stacked = jnp.concatenate(
         [xs[:, 4 * LANES * c:4 * LANES * (c + 1)] for c in range(2 * pieces)], axis=0
     ).astype(BF16)
-    spread = dot(stacked, spread_matrix()).astype(BF16)
+    spread = dot(stacked, spread_s)
+    across = (row_iota(spread.shape) // 16) * LANES + lane_iota(spread.shape) % LANES
+    spread = jnp.where(across < length // 4, spread, 0.0).astype(BF16)
     for c in range(2 * pieces):
         for phase in range(4):
             at = (4 * (c // 2) + phase) * 16
@@ -194,43 +206,20 @@
             imag = imag - (c1 * part_s + s1 * part_c)
         both = jnp.concatenate([real, imag], axis=0) * jnp.where(one == 0.0, 1.0, 0.5)
         xt[:, at] = jnp.concatenate(split(both), axis=0)
-    keeps = [
-        pltpu.make_async_copy(source, target, sems.at[i])
-        for i, (source, target) in enumerate(
-            ((tc, tc_hbm), (ts, ts_hbm))
-        )
-    ]
-    for keep in keeps:
-        keep.start()
-
     turned = jnp.concatenate(
         [xt[:, owners * 8 * t:owners * 8 * (t + 1)] for t in range(groups)], axis=0
     )
-    shape = (LANES, 64 * groups)
-    source = lane_iota(shape)
-    vec = source % 16
-    base = (vec % rows) * (fields * 2) + (vec // rows) * 2 + (source // 16) % 2
-    target = (base + unit * (source // 64 + lax.axis_index("fld"))) % LANES
-    place = jnp.where((vec < rows * fields) & (row_iota(shape) == target), 1.0, 0.0).astype(BF16)
-    total = dot(place, turned)
+    total = dot(packing, turned)
     scale = 1.0 / jnp.sqrt(jnp.full(total.shape, length, jnp.int32).astype(F32))
     msg_ref[...] = jnp.transpose(total * scale).reshape(owners, 8, LANES)
-    for keep in keeps:
-        keep.wait()
 
 
 def inverse_kernel(
-    groups, len_hbm, band_hbm, tc_hbm, ts_hbm, fc, fs, msg_ref, grid_ref,
-    len_ref, band_ref, tc, ts, sems, os,
+    groups, len_hbm, band_hbm, tc, ts, fc, fs, msg_ref, grid_ref,
+    len_ref, band_ref, sems, os,
 ):
-    copies = [
-        pltpu.make_async_copy(source, target, sems.at[i])
-        for i, (source, target) in enumerate(
-            ((len_hbm, len_ref), (band_hbm, band_ref), (tc_hbm, tc), (ts_hbm, ts))
-        )
-    ]
-    for copy in copies:
-        copy.start()
+    copies = start_all((len_hbm, band_hbm), (len_ref, band_ref), sems)
+    spread_s = spread_matrix()
     fields, _, rows, width = grid_ref.shape
     owners = msg_ref.shape[0]
     slots = tc.shape[1]
@@ -248,9 +237,6 @@
     ).astype(BF16)
     turned = dot_nt(place, pieces)
     block = 2 * LANES
-    for copy in copies:
-        copy.wait()
-    length = len_ref[band_ref[lax.axis_index("lat")]]
     out = jnp.zeros((16 * turns, DEEP), F32)
     for i in range(slots // block):
         t, off = divmod(i * block, owners * 8)
@@ -266,6 +252,8 @@
         reals = jnp.concatenate(reals, axis=0).astype(BF16)
         imags = jnp.concatenate(imags, axis=0).astype(BF16)
         out = out + (dot_nt(reals, tc[:, at]) - dot_nt(imags, ts[:, at]))
+    wait_all(copies)
+    length = len_ref[band_ref[lax.axis_index("lat")]]
     out = out * (1.0 / jnp.sqrt(jnp.full((16 * turns, DEEP), length, jnp.int32).astype(F32)))
     chunks = os.shape[0] // 16
     for c in range(chunks):
@@ -275,7 +263,7 @@
             os[16 * c:16 * (c + 1), LANES * phase:LANES * (phase + 1)] = out[
                 at:at + 16, off:off + LANES
             ].astype(BF16)
-    merged = dot_nt(os[...], spread_matrix())
+    merged = dot_nt(os[...], spread_s)
     for c in range(chunks):
         begin = 4 * LANES * c
         size = min(4 * LANES, width - begin)
@@ -294,11 +282,12 @@
     eh_hbm, mix_ref, back_ref, turn_ref, tau_ref, rate_ref,
     fold_ref, band_ref, rates_ref, leg_ref, tm_ref, bm_ref, sems, pad_s, eh_ref, out_sems,
 ):
-    fetch_all(
-        (fold_hbm, band_hbm, rates_hbm, leg_hbm, tm_hbm, bm_hbm),
-        (fold_ref, band_ref, rates_ref, leg_ref, tm_ref, bm_ref),
+    copies = start_all(
+        (fold_hbm, band_hbm, rates_hbm, tm_hbm, bm_hbm, leg_hbm),
+        (fold_ref, band_ref, rates_ref, tm_ref, bm_ref, leg_ref),
         sems,
     )
+    wait_all(copies[:-1])
     everyone = tm_ref.shape[0]
     _, lats, places = leg_ref.shape
     groups_f = everyone // fields
@@ -350,15 +339,20 @@
     for k in range(everyone):
         rate = jnp.where(row == k, rates_ref[k], rate)
     rate_ref[...] = rate
-    line = lane_iota((1, span))
+    paired = tau_ref.shape[0]
+    row = row_iota((paired, LANES))
+    waves = []
+    wave = jnp.zeros((paired, LANES), jnp.int32)
     for pair in range(4 * groups):
-        wave = fold_ref[owner, 2 * min(pair, pairs - 1)]
-        degree = jnp.where(line > cut_off - wave, line - 1, line + wave)
-        tau_ref[pair:pair + 1, :] = (degree * (degree + 1)).astype(F32) * (
-            1.0 / float(cut_off * (cut_off + 1))
-        )
-
-    shape = (2 * eight, 2 * eight)
+        waves.append(fold_ref[owner, 2 * min(pair, pairs - 1)])
+        wave = jnp.where(row == pair, waves[pair], wave)
+    wave = jnp.concatenate([wave] * (span // LANES), axis=1)
+    line = lane_iota((paired, span))
+    degree = jnp.where(line > cut_off - wave, line - 1, line + wave)
+    tau_ref[...] = (degree * (degree + 1)).astype(F32) * (1.0 / float(cut_off * (cut_off + 1)))
+
+    quad_rows = 4 * lats
+    shape = (quad_rows, quad_rows)
     band = jnp.zeros(shape, jnp.int32)
     for holder in range(lats):
         band = jnp.where(row_iota(shape) % lats == holder, band_ref[holder], band)
@@ -369,55 +363,60 @@
     ).astype(BF16)
 
     whole = places // LANES * LANES
-    shape = (lats, span)
-    place = lane_iota(shape)
-
-    def pair_block(pair, carry):
-        there = pair < pairs
-        index = jnp.minimum(pair, pairs - 1)
-        wave = fold_ref[owner, 2 * index]
-        limit = jnp.where(there, cut_off - wave, -1)
-        last = jnp.where(there, places - 1, -1)
-        leg = jnp.concatenate(
-            [
-                leg_ref[index, :, 0:whole],
-                jnp.broadcast_to(leg_ref[index, :, whole:places], (lats, span - whole)),
-            ],
-            axis=1,
-        )
-        first = place <= limit
-        second = (place > limit) & (place <= last)
-        odd = ((place + jnp.where(first, 0, wave)) & 1) == 1
-        signed = jnp.where(odd, -leg, leg)
-        base = (pair // 4) * 2 * eight + (pair % 4) * 2 * lats
-        for r, rowset in enumerate((leg, signed)):
-            eh_ref[pl.ds(pl.multiple_of(base + r * eight, 16), 2 * lats), :] = jnp.concatenate(
-                [jnp.where(first, rowset, 0.0), jnp.where(second, rowset, 0.0)], axis=0
-            ).astype(BF16)
-        return carry
-
+    line = lane_iota((quad_rows, span))
+    row = row_iota((quad_rows, LANES)) // lats
+    copies[-1].wait()
     keeps = []
     for t in range(groups):
-        lax.fori_loop(4 * t, 4 * t + 4, pair_block, 0)
+        wave = jnp.zeros((quad_rows, LANES), jnp.int32)
+        last = jnp.zeros((quad_rows, LANES), jnp.int32)
+        stack = []
+        for pp in range(4):
+            there = 4 * t + pp < pairs
+            index = min(4 * t + pp, pairs - 1)
+            wave = jnp.where(row == pp, waves[4 * t + pp], wave)
+            last = jnp.where(row == pp, places - 1 if there else -1, last)
+            stack.append(
+                jnp.concatenate(
+                    [
+                        leg_ref[index, :, 0:whole],
+                        jnp.broadcast_to(leg_ref[index, :, whole:places], (lats, span - whole)),
+                    ],
+                    axis=1,
+                )
+            )
+        wave = jnp.concatenate([wave] * (span // LANES), axis=1)
+        last = jnp.concatenate([last] * (span // LANES), axis=1)
+        leg = dot(order, jnp.concatenate(stack, axis=0).astype(BF16))
+        before = line <= cut_off - wave
+        first = before & (line <= last)
+        second = jnp.logical_not(before) & (line <= last)
+        odd = ((line + jnp.where(before, 0, wave)) & 1) == 1
+        signed = jnp.where(odd, -leg, leg)
+        for r, rowset in enumerate((leg, signed)):
+            near = jnp.where(first, rowset, 0.0)
+            far = jnp.where(second, rowset, 0.0)
+            for pp in range(4):
+                at = 2 * eight * t + r * eight + 2 * pp * lats
+                eh_ref[at:at + 2 * lats, :] = jnp.concatenate(
+                    [near[pp * lats:(pp + 1) * lats], far[pp * lats:(pp + 1) * lats]], axis=0
+                ).astype(BF16)
         part = pl.ds(2 * eight * t, 2 * eight)
-        eh_ref[part, :] = dot(order, eh_ref[part, :]).astype(BF16)
         keeps.append(pltpu.make_async_copy(eh_ref.at[part], eh_hbm.at[part], out_sems.at[t]))
         keeps[-1].start()
-    for keep in keeps:
-        keep.wait()
+    wait_all(keeps)
 
 
 def solve_kernel(
     fields, rows, lats, eh_hbm, msg_ref, mix_ref, turn_ref, tau_ref, rate_ref,
-    damped_ref, out_ref, cs, eh_ref, in_sems,
+    damped_hbm, out_ref, cs, eh_ref, damped_ref, in_sems, out_sems,
 ):
-    groups = in_sems.shape[0]
     eight = 8 * lats
-    later = []
-    for t in range(groups):
-        part = pl.ds(2 * eight * t, 2 * eight)
-        later.append(pltpu.make_async_copy(eh_hbm.at[part], eh_ref.at[part], in_sems.at[t]))
-        later[-1].start()
+    groups = eh_ref.shape[0] // (2 * eight)
+    parts = [pl.ds(0, 2 * eight), pl.ds(2 * eight, 2 * eight * (groups - 1))]
+    later = start_all(
+        [eh_hbm.at[part] for part in parts], [eh_ref.at[part] for part in parts], in_sems
+    )
     groups_f = msg_ref.shape[0] // eight
     wf = fields * 2
     unit = rows * wf
@@ -446,13 +445,19 @@
     blank = jnp.zeros((64 - 2 * KPAD, span), BF16)
     front = lane_iota((lats, LANES)) < 64
 
+    lefts = []
     for t in range(groups):
         mine = mixed[:, eight * t:eight * (t + 1)]
         mine = jnp.concatenate([mine[0:2 * KPAD], mine[2 * KPAD:4 * KPAD]], axis=1)
         left = jnp.concatenate([jnp.where(slot_pair == pp, mine, 0.0) for pp in range(4)], axis=0)
-        left = jnp.concatenate(split(left), axis=1)
+        lefts.append(jnp.concatenate(split(left), axis=1))
+
+    keeps = []
+    for t in range(groups):
+        left = lefts[t]
         legs = pl.ds(2 * eight * t, 2 * eight)
-        later[t].wait()
+        if t < 2:
+            later[t].wait()
         for start in range(0, span, 2 * LANES):
             size = min(2 * LANES, span - start)
             right = eh_ref[legs, start:start + size]
@@ -469,12 +474,23 @@
             damped_ref[deep * t:deep * (t + 1), start:start + size] = jnp.concatenate(
                 damped, axis=0
             ).astype(BF16)
+        part = pl.ds(deep * t, deep)
+        keeps.append(
+            pltpu.make_async_copy(damped_ref.at[part], damped_hbm.at[part], out_sems.at[t])
+        )
+        keeps[-1].start()
+
+    products = []
+    for t in range(groups):
+        legs = pl.ds(2 * eight * t, 2 * eight)
         pieces = []
         for pp in range(4):
             at = deep * t + 2 * KPAD * pp
             pieces += [damped_ref[at:at + 2 * KPAD, :], blank]
-        sums = dot_nt(eh_ref[legs, :], jnp.concatenate(pieces, axis=0))
-        highs, lows = [], []
+        products.append(dot_nt(eh_ref[legs, :], jnp.concatenate(pieces, axis=0)))
+
+    highs, lows = [], []
+    for sums in products:
         for r in range(rows):
             for i8 in range(8):
                 at = (r * 8 + i8) * lats
@@ -486,10 +502,10 @@
                 low = pltpu.roll(tile - high, 64, 1)
                 highs.append(jnp.where(front, high, low))
                 lows.append(jnp.where(front, high, 0.0))
-        own = jnp.concatenate(
-            [jnp.concatenate(highs, axis=0), jnp.concatenate(lows, axis=0)], axis=1
-        ).astype(BF16)
-        cs[2 * eight * t:2 * eight * (t + 1), 0:FPAD] = dot_nt(own, turn_ref[...])
+    own = jnp.concatenate(
+        [jnp.concatenate(highs, axis=0), jnp.concatenate(lows, axis=0)], axis=1
+    ).astype(BF16)
+    cs[:, 0:FPAD] = dot_nt(own, turn_ref[...])
 
     lane = lane_iota((8, LANES))
     here = [
@@ -506,6 +522,7 @@
         for g in range(groups_f):
             at = (holder * groups_f + g) * 8
             out_ref[at:at + 8, :] = tiles[g]
+    wait_all(keeps)
 
 
 def output_kernel(damped_ref, back_ref, spec_ref, bk):
@@ -561,13 +578,13 @@
         functools.partial(forward_kernel, cut_off, groups),
         out_shape=(
             message,
-            pltpu.HBM((DEEP, slots), BF16),
-            pltpu.HBM((DEEP, slots), BF16),
+            pltpu.VMEM((DEEP, slots), BF16),
+            pltpu.VMEM((DEEP, slots), BF16),
             pltpu.VMEM((turns, slots), F32),
             pltpu.VMEM((turns, slots), F32),
         ),
         in_specs=[hbm] * 4,
-        out_specs=(vmem, hbm, hbm, vmem, vmem),
+        out_specs=(vmem,) * 5,
         scratch_shapes=[
             pltpu.SMEM(row_lengths.shape, jnp.int32),
             pltpu.SMEM(band_map.shape, jnp.int32),
@@ -578,16 +595,15 @@
             pltpu.VMEM((8, slots), F32),
             pltpu.VMEM((16, 4 * DEEP * pieces), F32),
             pltpu.VMEM((16 * turns, DEEP), BF16),
-            pltpu.VMEM((DEEP, slots), BF16),
-            pltpu.VMEM((DEEP, slots), BF16),
             pltpu.VMEM((64, slots), BF16),
         ],
         compiler_params=room,
         name="forward_rows",
     )(row_lengths, band_map, fold_map, grid)
     tables = [
-        pltpu.with_memory_space_constraint(x, pltpu.HBM) for x in (cos_table, sin_table)
-    ] + [pltpu.with_memory_space_constraint(x, pltpu.VMEM) for x in (cos_turn, sin_turn)]
+        pltpu.with_memory_space_constraint(x, pltpu.VMEM)
+        for x in (cos_table, sin_table, cos_turn, sin_turn)
+    ]
     arrived = lax.all_to_all(sending, ("lat", "fld"), split_axis=0, concat_axis=0, tiled=True)
 
     legs, mix, back, turn_back, tau, rate = pl.pallas_call(
@@ -597,7 +613,7 @@
             pltpu.VMEM((2 * rows * KPAD, 3 * LANES), BF16),
             pltpu.VMEM((2 * FPAD, 8 * KPAD), BF16),
             pltpu.VMEM((FPAD, 2 * LANES), BF16),
-            pltpu.VMEM((groups * 4, span), F32),
+            pltpu.VMEM((-(-groups * 4 // 8) * 8, span), F32),
             pltpu.VMEM((KPAD, 2 * LANES), F32),
         ),
         in_specs=[hbm] * 6,
@@ -627,14 +643,16 @@
     damped, leaving = pl.pallas_call(
         functools.partial(solve_kernel, fields, rows, lats),
         out_shape=(
-            pltpu.VMEM((groups * 8 * KPAD, span), BF16),
+            pltpu.HBM((groups * 8 * KPAD, span), BF16),
             pltpu.HBM((owners * 8, LANES), F32),
         ),
         in_specs=[hbm] + [vmem] * 5,
-        out_specs=(vmem,) * 2,
+        out_specs=(hbm, vmem),
         scratch_shapes=[
             pltpu.VMEM((groups * 16 * lats, LANES), F32),
             pltpu.VMEM((groups * 16 * lats, span), BF16),
+            pltpu.VMEM((groups * 8 * KPAD, span), BF16),
+            dma((2,)),
             dma((groups,)),
         ],
         compiler_params=room,
@@ -644,7 +662,7 @@
 
     returned = lax.all_to_all(leaving, ("lat", "fld"), split_axis=0, concat_axis=0, tiled=True)
 
-    damped = pltpu.with_memory_space_constraint(damped, pltpu.VMEM)
+    damped = pltpu.with_memory_space_constraint(damped, pltpu.HBM)
     spectral = pl.pallas_call(
         output_kernel,
         grid=(groups,),
@@ -665,14 +683,12 @@
     grid_out = pl.pallas_call(
         functools.partial(inverse_kernel, groups),
         out_shape=jax.ShapeDtypeStruct(grid.shape, BF16),
-        in_specs=[hbm] * 4 + [vmem] * 3,
+        in_specs=[hbm] * 2 + [vmem] * 5,
         out_specs=vmem,
         scratch_shapes=[
             pltpu.SMEM(row_lengths.shape, jnp.int32),
             pltpu.SMEM(band_map.shape, jnp.int32),
-            pltpu.VMEM((DEEP, slots), BF16),
-            pltpu.VMEM((DEEP, slots), BF16),
-            dma((4,)),
+            dma((2,)),
             pltpu.VMEM((32 * pieces, 4 * LANES), BF16),
         ],
         compiler_params=room,

time: 42.5 us -> 38.6 us (0.908)
  Pallas kernels: 24.6 us -> 20.6 us
  waiting for transfers between devices: 6.47 us -> 7.06 us
  starting transfers between devices: 10.4 us -> 9.89 us
    pallas_call x1, Pallas kernels: 5.47 us -> 2.9 us  [per_device(): pl.pallas_call(functools.partial(prepare_kernel, cut_off, pairs, fields,...]
    all_to_all x1, waiting for transfers between devices: 2.75 us -> 5.32 us  [per_device(): lax.all_to_all(sending, ('lat', 'fld'), split_axis=0, concat_axis=0, tile...]
    pallas_call x1, Pallas kernels: 6.94 us -> 4.86 us  [per_device(): pl.pallas_call(functools.partial(solve_kernel, fields, rows, lats), out_s...]
    pallas_call x1, Pallas kernels: 4.51 us -> 6.49 us  [per_device(): pl.pallas_call(output_kernel, grid=(groups,), out_shape=jax.ShapeDtypeStr...]
    all_to_all x1, waiting for transfers between devices: 3.72 us -> 1.74 us  [per_device(): lax.all_to_all(leaving, ('lat', 'fld'), split_axis=0, concat_axis=0, tile...]
    pallas_call x1, Pallas kernels: 4.62 us -> 3.73 us  [per_device(): pl.pallas_call(functools.partial(forward_kernel, cut_off, groups), out_sh...]
    all_to_all x1, starting transfers between devices: 3.1 us -> 2.58 us  [per_device(): lax.all_to_all(leaving, ('lat', 'fld'), split_axis=0, concat_axis=0, tile...]
    pallas_call x1, Pallas kernels: 3.03 us -> 2.58 us  [per_device(): pl.pallas_call(functools.partial(inverse_kernel, groups), out_shape=jax.S...]
  transfers between devices with their start and end apart: 2 -> 2, of which waited for: 2 -> 2; matrix products, arithmetic and copies ran while one was open for 0% -> 0% of each run, Pallas kernels for 24% -> 25%
where the time goes in v7:
time: 38.6 us; the launch traced here: 38.2 us
  Pallas kernels  20.6 us (53%)
  starting transfers between devices  9.89 us (26%)
  waiting for transfers between devices  7.06 us (18%)
  between operations  0.67 us (2%)
    all_to_all x1, starting transfers between devices, per_device(): lax.all_to_all(sending, ('lat', 'fld'), split_axis=0, concat_axis=0, tile...  7.3 us
    pallas_call x1, Pallas kernels, per_device(): pl.pallas_call(output_kernel, grid=(groups,), out_shape=jax.ShapeDtypeStr...  6.49 us
    all_to_all x1, waiting for transfers between devices, per_device(): lax.all_to_all(sending, ('lat', 'fld'), split_axis=0, concat_axis=0, tile...  5.32 us
    pallas_call x1, Pallas kernels, per_device(): pl.pallas_call(functools.partial(solve_kernel, fields, rows, lats), out_s...  4.86 us
    pallas_call x1, Pallas kernels, per_device(): pl.pallas_call(functools.partial(forward_kernel, cut_off, groups), out_sh...  3.73 us
    pallas_call x1, Pallas kernels, per_device(): pl.pallas_call(functools.partial(prepare_kernel, cut_off, pairs, fields,...  2.9 us
    all_to_all x1, starting transfers between devices, per_device(): lax.all_to_all(leaving, ('lat', 'fld'), split_axis=0, concat_axis=0, tile...  2.58 us
    pallas_call x1, Pallas kernels, per_device(): pl.pallas_call(functools.partial(inverse_kernel, groups), out_shape=jax.S...  2.58 us
  transfers between devices with their start and end apart: 2, of which 2 were waited for; matrix products, arithmetic and copies ran while one was open for 0% of the time, Pallas kernels for 25%

profile of v7, /device:TPU:0, one launch (start us, length us, event | category | flops | bytes accessed | tf_op | source)
XLA Modules:
  0.0 38.2 jit_solution(13731894178788211866)
XLA Ops:
  0.6 3.7 %forward_rows.1 = (f32[32,8,128]{2,1,0:T(8,128)}, bf16[256,1280]{1,0:T(8,128)(2,1)S(1)}, bf16[256,1280]{1,0:T(8,128)(2,1)S(1)}, f32[24,1280]{1,0:T(8,128)S(1)}, f32[24,1280]{1,0:T(8,128)S(1)}) custom-call(s32[8]{0:T(128)} %len_hbm.3, s32[8]{0:T(128)} %band_hbm.5, s32[32,40]{1,0:T(8,128)} %fold_hbm.3, bf16[5,1,2,5248]{3,2,1,0:T(2,128)(2,1)} %grid_hbm.1), custom_call_target="tpu_custom_call" | custom-call | tf_op jit(solution)/shard_map/forward_rows/pallas_call | solution.py:577
  4.4 7.3 %all-to-all-start = ((f32[32,8,128]{2,1,0:T(8,128)}), f32[32,8,128]{2,1,0:T(8,128)S(1)}, u32[]{:S(2)}, u32[]{:S(2)}) async-start(f32[32,8,128]{2,1,0:T(8,128)} %get-tuple-element.16), calls=%async_computation | async-start | bytes 262144 | tf_op jit(solution)/shard_map/all_to_all | solution.py:607
  11.7 2.9 %prepare.1 = (bf16[640,1408]{1,0:T(8,128)(2,1)}, bf16[96,384]{1,0:T(8,128)(2,1)S(1)}, bf16[128,192]{1,0:T(8,128)(2,1)S(1)}, bf16[64,256]{1,0:T(8,128)(2,1)S(1)},...) custom-call(s32[32,40]{1,0:T(8,128)} %fold_hbm.3, s32[8]{0:T(128)} %band_hbm.5, f32[20]{0:T(128)} %rates_hbm.1, ...), custom_call_target="tpu_custom_call" | custom-call | flops 100000000 | bytes 8000000 | tf_op jit(solution)/shard_map/prepare/pallas_call | solution.py:609
  14.6 5.3 %all-to-all-done = f32[32,8,128]{2,1,0:T(8,128)S(1)} async-done(((f32[32,8,128]{2,1,0:T(8,128)}), f32[32,8,128]{2,1,0:T(8,128)S(1)}, u32[]{:S(2)}, u32[]{:S(2)}) %all-to-all-start) | async-done | bytes 131104 | tf_op jit(solution)/shard_map/all_to_all | solution.py:607
  19.9 4.9 %solve.1 = (bf16[960,1408]{1,0:T(8,128)(2,1)}, f32[256,128]{1,0:T(8,128)}) custom-call(bf16[640,1408]{1,0:T(8,128)(2,1)} %get-tuple-element.15.eh_hbm, f32[256,128]{1,0:T(8,128)S(1)} %bitcast.4, bf16[96,384]{1,0:T(8,128)(2,1)S(1)} %get-tuple-element.17.mix_ref, bf16[64,256]{1,0:T(8,128)(2,1)S(1)} %get-tuple-element.18.turn_ref, ...), custom_call_target="tpu_custom_call" | custom-call | tf_op jit(solution)/shard_map/solve/pallas_call | solution.py:643
  24.8 2.6 %all-to-all-start.1 = ((f32[32,8,128]{2,1,0:T(8,128)}), f32[32,8,128]{2,1,0:T(8,128)S(1)}, u32[]{:S(2)}, u32[]{:S(2)}) async-start(f32[32,8,128]{2,1,0:T(8,128)} %bitcast.7), calls=%async_computation.1 | async-start | bytes 262144 | tf_op jit(solution)/shard_map/all_to_all | solution.py:663
  27.4 6.5 %spectral_output.1 = f32[20,20,2,1281]{3,2,1,0:T(2,128)} custom-call(bf16[960,1408]{1,0:T(8,128)(2,1)} %get-tuple-element.21.damped_ref, bf16[128,192]{1,0:T(8,128)(2,1)S(1)} %get-tuple-element.22.back_ref), custom_call_target="tpu_custom_call" | custom-call | flops 100000000 | bytes 8000000 | tf_op jit(solution)/shard_map/spectral_output/pallas_call | solution.py:666
  33.9 1.7 %all-to-all-done.1.msg_ref = f32[32,8,128]{2,1,0:T(8,128)S(1)} async-done(((f32[32,8,128]{2,1,0:T(8,128)}), f32[32,8,128]{2,1,0:T(8,128)S(1)}, u32[]{:S(2)}, u32[]{:S(2)}) %all-to-all-start.1) | async-done | bytes 131104 | tf_op jit(solution)/shard_map/all_to_all | solution.py:663
  35.6 2.6 %inverse_rows.1 = bf16[5,1,2,5248]{3,2,1,0:T(2,128)(2,1)} custom-call(s32[8]{0:T(128)} %len_hbm.3, s32[8]{0:T(128)} %band_hbm.5, bf16[256,1280]{1,0:T(8,128)(2,1)S(1)} %get-tuple-element.23.tc, bf16[256,1280]{1,0:T(8,128)(2,1)S(1)} %get-tuple-element.24.ts, f32[24,1280]{1,0:T(8,128)S(1)} %get-tuple-element.25.fc, f32[24,1280]{1,0:T(8,128)S(1)} %get-tuple-element.26.fs, ...), custom_call_target="tpu_custom_call" | custom-call | tf_op jit(solution)/shard_map/inverse_rows/pallas_call | solution.py:683
Async XLA Ops:
  4.4 15.5 %all-to-all-start = ((f32[32,8,128]{2,1,0:T(8,128)}), f32[32,8,128]{2,1,0:T(8,128)S(1)}, u32[]{:S(2)}, u32[]{:S(2)}) async-start(f32[32,8,128]{2,1,0:T(8,128)} %get-tuple-element.16), calls=%async_computation | async-start | bytes 262144 | tf_op jit(solution)/shard_map/all_to_all | solution.py:607
  24.8 10.8 %all-to-all-start.1 = ((f32[32,8,128]{2,1,0:T(8,128)}), f32[32,8,128]{2,1,0:T(8,128)S(1)}, u32[]{:S(2)}, u32[]{:S(2)}) async-start(f32[32,8,128]{2,1,0:T(8,128)} %bitcast.7), calls=%async_computation.1 | async-start | bytes 262144 | tf_op jit(solution)/shard_map/all_to_all | solution.py:663

commit v8 on v7

--- a/solution.py
+++ b/solution.py
@@ -409,7 +409,7 @@
 
 def solve_kernel(
     fields, rows, lats, eh_hbm, msg_ref, mix_ref, turn_ref, tau_ref, rate_ref,
-    damped_hbm, out_ref, cs, eh_ref, damped_ref, in_sems, out_sems,
+    near_ref, far_hbm, out_ref, cs, eh_ref, far_ref, in_sems, out_sems,
 ):
     eight = 8 * lats
     groups = eh_ref.shape[0] // (2 * eight)
@@ -422,6 +422,9 @@
     unit = rows * wf
     span = eh_ref.shape[1]
     deep = 8 * KPAD
+    near = near_ref.shape[0] // deep
+    holds = [(near_ref, deep * t) for t in range(near)]
+    holds += [(far_ref, deep * t) for t in range(groups - near)]
     lane = lane_iota((lats, LANES))
     tiles = [
         [msg_ref[pl.ds(8 * g + i8, lats, stride=8 * groups_f), :] for g in range(groups_f)]
@@ -471,22 +474,23 @@
                 at = 2 * pp * KPAD
                 damped.append(modes[at:at + KPAD] * factor)
                 damped.append(modes[at + KPAD:at + 2 * KPAD] * factor)
-            damped_ref[deep * t:deep * (t + 1), start:start + size] = jnp.concatenate(
-                damped, axis=0
-            ).astype(BF16)
-        part = pl.ds(deep * t, deep)
-        keeps.append(
-            pltpu.make_async_copy(damped_ref.at[part], damped_hbm.at[part], out_sems.at[t])
-        )
-        keeps[-1].start()
+            hold, at = holds[t]
+            hold[at:at + deep, start:start + size] = jnp.concatenate(damped, axis=0).astype(BF16)
+        if t >= near:
+            part = pl.ds(deep * (t - near), deep)
+            keeps.append(
+                pltpu.make_async_copy(far_ref.at[part], far_hbm.at[part], out_sems.at[t - near])
+            )
+            keeps[-1].start()
 
     products = []
     for t in range(groups):
         legs = pl.ds(2 * eight * t, 2 * eight)
         pieces = []
+        hold, base = holds[t]
         for pp in range(4):
-            at = deep * t + 2 * KPAD * pp
-            pieces += [damped_ref[at:at + 2 * KPAD, :], blank]
+            at = base + 2 * KPAD * pp
+            pieces += [hold[at:at + 2 * KPAD, :], blank]
         products.append(dot_nt(eh_ref[legs, :], jnp.concatenate(pieces, axis=0)))
 
     highs, lows = [], []
@@ -525,29 +529,49 @@
     wait_all(keeps)
 
 
-def output_kernel(damped_ref, back_ref, spec_ref, bk):
+def output_kernel(near_ref, far_hbm, back_ref, spec_ref, bk, far_s, sems):
     everyone, quad, _, places = spec_ref.shape
-    span = damped_ref.shape[1]
-
-    @pl.when(pl.program_id(0) == 0)
+    span = near_ref.shape[1]
+    deep = 8 * KPAD
+    near = near_ref.shape[0] // deep
+    tall = 2 * everyone
+    step = pl.program_id(0)
+
+    def far_copy(t):
+        part = pl.ds(pl.multiple_of(deep * t, deep), deep)
+        return pltpu.make_async_copy(far_hbm.at[part], far_s.at[part], sems.at[t])
+
+    @pl.when(step == 0)
     def _():
-        shape = (FPAD, 8 * KPAD)
-        pair_of = lane_iota(shape) // (2 * KPAD)
+        for t in range(sems.shape[0]):
+            far_copy(t).start()
+        pair_of = lane_iota((tall, deep)) // (2 * KPAD)
+        rows = []
         for part in range(2):
-            full = back_ref[part * FPAD:(part + 1) * FPAD, :].astype(F32)
+            full = back_ref[part * FPAD:part * FPAD + tall, :].astype(F32)
             for pp in range(4):
-                at = (4 * part + pp) * FPAD
-                bk[at:at + FPAD, :] = jnp.where(pair_of == pp, full, 0.0).astype(BF16)
-
-    for start in range(0, span, 2 * LANES):
-        size = min(2 * LANES, span - start)
-        spec = dot(bk[...], damped_ref[:, start:start + size])
-        spec = spec[0:4 * FPAD] + spec[4 * FPAD:]
-        kept = min(size, places - start)
-        for pp in range(4):
-            for f in range(everyone):
-                at = pp * FPAD + 2 * f
-                spec_ref[f, pp, :, start:start + kept] = spec[at:at + 2, 0:kept]
+                rows.append(jnp.where(pair_of == pp, full, 0.0))
+        bk[...] = jnp.concatenate(rows, axis=0).astype(BF16)
+
+    def write(source, at):
+        for start in range(0, span, 2 * LANES):
+            size = min(2 * LANES, span - start)
+            spec = dot(bk[...], source[pl.ds(at, deep), start:start + size])
+            spec = spec[0:4 * tall] + spec[4 * tall:]
+            kept = min(size, places - start)
+            for pp in range(4):
+                for f in range(everyone):
+                    row = pp * tall + 2 * f
+                    spec_ref[f, pp, :, start:start + kept] = spec[row:row + 2, 0:kept]
+
+    @pl.when(step < near)
+    def _():
+        write(near_ref, pl.multiple_of(deep * step, deep))
+
+    @pl.when(step >= near)
+    def _():
+        far_copy(step - near).wait()
+        write(far_s, pl.multiple_of(deep * (step - near), deep))
 
 
 def per_device(grid, row_lengths, band_map, fold_map, legendre, to_modes, back_modes, mode_rates):
@@ -640,20 +664,22 @@
         for x in (mix, back, turn_back, tau, rate)
     )
 
-    damped, leaving = pl.pallas_call(
+    near = groups // 2
+    damped_near, damped_far, leaving = pl.pallas_call(
         functools.partial(solve_kernel, fields, rows, lats),
         out_shape=(
-            pltpu.HBM((groups * 8 * KPAD, span), BF16),
+            pltpu.VMEM((near * 8 * KPAD, span), BF16),
+            pltpu.HBM(((groups - near) * 8 * KPAD, span), BF16),
             pltpu.HBM((owners * 8, LANES), F32),
         ),
         in_specs=[hbm] + [vmem] * 5,
-        out_specs=(hbm, vmem),
+        out_specs=(vmem, hbm, vmem),
         scratch_shapes=[
             pltpu.VMEM((groups * 16 * lats, LANES), F32),
             pltpu.VMEM((groups * 16 * lats, span), BF16),
-            pltpu.VMEM((groups * 8 * KPAD, span), BF16),
+            pltpu.VMEM(((groups - near) * 8 * KPAD, span), BF16),
             dma((2,)),
-            dma((groups,)),
+            dma((groups - near,)),
         ],
         compiler_params=room,
         name="solve",
@@ -662,23 +688,29 @@
 
     returned = lax.all_to_all(leaving, ("lat", "fld"), split_axis=0, concat_axis=0, tiled=True)
 
-    damped = pltpu.with_memory_space_constraint(damped, pltpu.HBM)
+    damped_near = pltpu.with_memory_space_constraint(damped_near, pltpu.VMEM)
+    damped_far = pltpu.with_memory_space_constraint(damped_far, pltpu.HBM)
     spectral = pl.pallas_call(
         output_kernel,
         grid=(groups,),
         out_shape=jax.ShapeDtypeStruct((everyone, pairs, 2, places), F32),
         in_specs=[
-            pl.BlockSpec((8 * KPAD, span), lambda t: (t, 0)),
+            pl.BlockSpec((near * 8 * KPAD, span), lambda t: (0, 0)),
+            hbm,
             pl.BlockSpec((2 * FPAD, 8 * KPAD), lambda t: (0, 0)),
         ],
         out_specs=pl.BlockSpec((everyone, 4, 2, places), lambda t: (0, t, 0, 0)),
-        scratch_shapes=[pltpu.VMEM((8 * FPAD, 8 * KPAD), BF16)],
+        scratch_shapes=[
+            pltpu.VMEM((16 * everyone, 8 * KPAD), BF16),
+            pltpu.VMEM(((groups - near) * 8 * KPAD, span), BF16),
+            dma((groups - near,)),
+        ],
         compiler_params=pltpu.CompilerParams(
             dimension_semantics=("arbitrary",), vmem_limit_bytes=ROOM
         ),
         cost_estimate=pl.CostEstimate(flops=10**8, bytes_accessed=8 * 10**6, transcendentals=0),
         name="spectral_output",
-    )(damped, back)
+    )(damped_near, damped_far, back)
 
     grid_out = pl.pallas_call(
         functools.partial(inverse_kernel, groups),

time: 38.6 us -> 38.6 us (level)
  Pallas kernels: 20.6 us -> 18.2 us
  waiting for transfers between devices: 7.06 us -> 9.44 us
    pallas_call x1, Pallas kernels: 6.49 us -> 4.11 us  [per_device(): pl.pallas_call(output_kernel, grid=(groups,), out_shape=jax.ShapeDtypeStr...]
    all_to_all x1, waiting for transfers between devices: 1.74 us -> 4.11 us  [per_device(): lax.all_to_all(leaving, ('lat', 'fld'), split_axis=0, concat_axis=0, tile...]
  transfers between devices with their start and end apart: 2 -> 2, of which waited for: 2 -> 2; matrix products, arithmetic and copies ran while one was open for 0% -> 0% of each run, Pallas kernels for 25% -> 18%
where the time goes in v8:
time: 38.6 us; the launch traced here: 38.2 us
  Pallas kernels  18.2 us (47%)
  starting transfers between devices  9.89 us (26%)
  waiting for transfers between devices  9.44 us (24%)
  between operations  0.68 us (2%)
    all_to_all x1, starting transfers between devices, per_device(): lax.all_to_all(sending, ('lat', 'fld'), split_axis=0, concat_axis=0, tile...  7.3 us
    all_to_all x1, waiting for transfers between devices, per_device(): lax.all_to_all(sending, ('lat', 'fld'), split_axis=0, concat_axis=0, tile...  5.32 us
    pallas_call x1, Pallas kernels, per_device(): pl.pallas_call(functools.partial(solve_kernel, fields, rows, lats), out_s...  4.92 us
    all_to_all x1, waiting for transfers between devices, per_device(): lax.all_to_all(leaving, ('lat', 'fld'), split_axis=0, concat_axis=0, tile...  4.11 us
    pallas_call x1, Pallas kernels, per_device(): pl.pallas_call(output_kernel, grid=(groups,), out_shape=jax.ShapeDtypeStr...  4.11 us
    pallas_call x1, Pallas kernels, per_device(): pl.pallas_call(functools.partial(forward_kernel, cut_off, groups), out_sh...  3.73 us
    pallas_call x1, Pallas kernels, per_device(): pl.pallas_call(functools.partial(prepare_kernel, cut_off, pairs, fields,...  2.9 us
    all_to_all x1, starting transfers between devices, per_device(): lax.all_to_all(leaving, ('lat', 'fld'), split_axis=0, concat_axis=0, tile...  2.58 us
  transfers between devices with their start and end apart: 2, of which 2 were waited for; matrix products, arithmetic and copies ran while one was open for 0% of the time, Pallas kernels for 18%

profile of v8, /device:TPU:0, one launch (start us, length us, event | category | flops | bytes accessed | tf_op | source)
XLA Modules:
  0.0 38.2 jit_solution(4272859367724790478)
XLA Ops:
  0.6 3.7 %forward_rows.1 = (f32[32,8,128]{2,1,0:T(8,128)}, bf16[256,1280]{1,0:T(8,128)(2,1)S(1)}, bf16[256,1280]{1,0:T(8,128)(2,1)S(1)}, f32[24,1280]{1,0:T(8,128)S(1)}, f32[24,1280]{1,0:T(8,128)S(1)}) custom-call(s32[8]{0:T(128)} %len_hbm.3, s32[8]{0:T(128)} %band_hbm.5, s32[32,40]{1,0:T(8,128)} %fold_hbm.3, bf16[5,1,2,5248]{3,2,1,0:T(2,128)(2,1)} %grid_hbm.1), custom_call_target="tpu_custom_call" | custom-call | tf_op jit(solution)/shard_map/forward_rows/pallas_call | solution.py:601
  4.4 7.3 %all-to-all-start = ((f32[32,8,128]{2,1,0:T(8,128)}), f32[32,8,128]{2,1,0:T(8,128)S(1)}, u32[]{:S(2)}, u32[]{:S(2)}) async-start(f32[32,8,128]{2,1,0:T(8,128)} %get-tuple-element.17), calls=%async_computation | async-start | bytes 262144 | tf_op jit(solution)/shard_map/all_to_all | solution.py:631
  11.7 2.9 %prepare.1 = (bf16[640,1408]{1,0:T(8,128)(2,1)}, bf16[96,384]{1,0:T(8,128)(2,1)S(1)}, bf16[128,192]{1,0:T(8,128)(2,1)S(1)}, bf16[64,256]{1,0:T(8,128)(2,1)S(1)},...) custom-call(s32[32,40]{1,0:T(8,128)} %fold_hbm.3, s32[8]{0:T(128)} %band_hbm.5, f32[20]{0:T(128)} %rates_hbm.1, ...), custom_call_target="tpu_custom_call" | custom-call | flops 100000000 | bytes 8000000 | tf_op jit(solution)/shard_map/prepare/pallas_call | solution.py:633
  14.6 5.3 %all-to-all-done = f32[32,8,128]{2,1,0:T(8,128)S(1)} async-done(((f32[32,8,128]{2,1,0:T(8,128)}), f32[32,8,128]{2,1,0:T(8,128)S(1)}, u32[]{:S(2)}, u32[]{:S(2)}) %all-to-all-start) | async-done | bytes 131104 | tf_op jit(solution)/shard_map/all_to_all | solution.py:631
  19.9 4.9 %solve.1 = (bf16[384,1408]{1,0:T(8,128)(2,1)S(1)}, bf16[576,1408]{1,0:T(8,128)(2,1)}, f32[256,128]{1,0:T(8,128)}) custom-call(bf16[640,1408]{1,0:T(8,128)(2,1)} %get-tuple-element.16.eh_hbm, f32[256,128]{1,0:T(8,128)S(1)} %bitcast.4, bf16[96,384]{1,0:T(8,128)(2,1)S(1)} %get-tuple-element.18.mix_ref, bf16[64,256]{1,0:T(8,128)(2,1)S(1)} %get-tuple-element.19.turn_ref, ...), custom_call_target="tpu_custom_call" | custom-call | tf_op jit(solution)/shard_map/solve/pallas_call | solution.py:668
  24.8 2.6 %all-to-all-start.1 = ((f32[32,8,128]{2,1,0:T(8,128)}), f32[32,8,128]{2,1,0:T(8,128)S(1)}, u32[]{:S(2)}, u32[]{:S(2)}) async-start(f32[32,8,128]{2,1,0:T(8,128)} %bitcast.7), calls=%async_computation.1 | async-start | bytes 262144 | tf_op jit(solution)/shard_map/all_to_all | solution.py:689
  27.4 4.1 %spectral_output.1 = f32[20,20,2,1281]{3,2,1,0:T(2,128)} custom-call(bf16[384,1408]{1,0:T(8,128)(2,1)S(1)} %get-tuple-element.22.near_ref, bf16[576,1408]{1,0:T(8,128)(2,1)} %get-tuple-element.23.far_hbm, bf16[128,192]{1,0:T(8,128)(2,1)S(1)} %get-tuple-element.24.back_ref), custom_call_target="tpu_custom_call" | custom-call | flops 100000000 | bytes 8000000 | tf_op jit(solution)/shard_map/spectral_output/pallas_call | solution.py:693
  31.5 4.1 %all-to-all-done.1.msg_ref = f32[32,8,128]{2,1,0:T(8,128)S(1)} async-done(((f32[32,8,128]{2,1,0:T(8,128)}), f32[32,8,128]{2,1,0:T(8,128)S(1)}, u32[]{:S(2)}, u32[]{:S(2)}) %all-to-all-start.1) | async-done | bytes 131104 | tf_op jit(solution)/shard_map/all_to_all | solution.py:689
  35.7 2.6 %inverse_rows.1 = bf16[5,1,2,5248]{3,2,1,0:T(2,128)(2,1)} custom-call(s32[8]{0:T(128)} %len_hbm.3, s32[8]{0:T(128)} %band_hbm.5, bf16[256,1280]{1,0:T(8,128)(2,1)S(1)} %get-tuple-element.25.tc, bf16[256,1280]{1,0:T(8,128)(2,1)S(1)} %get-tuple-element.26.ts, f32[24,1280]{1,0:T(8,128)S(1)} %get-tuple-element.27.fc, f32[24,1280]{1,0:T(8,128)S(1)} %get-tuple-element.28.fs, ...), custom_call_target="tpu_custom_call" | custom-call | tf_op jit(solution)/shard_map/inverse_rows/pallas_call | solution.py:715
Async XLA Ops:
  4.4 15.5 %all-to-all-start = ((f32[32,8,128]{2,1,0:T(8,128)}), f32[32,8,128]{2,1,0:T(8,128)S(1)}, u32[]{:S(2)}, u32[]{:S(2)}) async-start(f32[32,8,128]{2,1,0:T(8,128)} %get-tuple-element.17), calls=%async_computation | async-start | bytes 262144 | tf_op jit(solution)/shard_map/all_to_all | solution.py:631
  24.8 10.8 %all-to-all-start.1 = ((f32[32,8,128]{2,1,0:T(8,128)}), f32[32,8,128]{2,1,0:T(8,128)S(1)}, u32[]{:S(2)}, u32[]{:S(2)}) async-start(f32[32,8,128]{2,1,0:T(8,128)} %bitcast.7), calls=%async_computation.1 | async-start | bytes 262144 | tf_op jit(solution)/shard_map/all_to_all | solution.py:689

commit v9 on v8

--- a/solution.py
+++ b/solution.py
@@ -237,21 +237,23 @@
     ).astype(BF16)
     turned = dot_nt(place, pieces)
     block = 2 * LANES
-    out = jnp.zeros((16 * turns, DEEP), F32)
+    lefts, rights = [], []
     for i in range(slots // block):
         t, off = divmod(i * block, owners * 8)
         real = turned[32 * t:32 * t + 16, off:off + block]
         imag = turned[32 * t + 16:32 * t + 32, off:off + block]
+        less_real = -real
+        less_imag = -imag
         at = pl.ds(i * block, block)
         reals, imags = [], []
         for g in range(turns):
             c1 = fc[g:g + 1, at]
             s1 = fs[g:g + 1, at]
-            reals.append(c1 * real - s1 * imag)
-            imags.append(s1 * real + c1 * imag)
-        reals = jnp.concatenate(reals, axis=0).astype(BF16)
-        imags = jnp.concatenate(imags, axis=0).astype(BF16)
-        out = out + (dot_nt(reals, tc[:, at]) - dot_nt(imags, ts[:, at]))
+            reals.append(c1 * real + s1 * less_imag)
+            imags.append(s1 * less_real + c1 * less_imag)
+        lefts += [jnp.concatenate(reals, axis=0).astype(BF16), jnp.concatenate(imags, axis=0).astype(BF16)]
+        rights += [tc[:, at], ts[:, at]]
+    out = dot_nt(jnp.concatenate(lefts, axis=1), jnp.concatenate(rights, axis=1))
     wait_all(copies)
     length = len_ref[band_ref[lax.axis_index("lat")]]
     out = out * (1.0 / jnp.sqrt(jnp.full((16 * turns, DEEP), length, jnp.int32).astype(F32)))
@@ -323,16 +325,13 @@
     repeat = jnp.where(row_iota(shape) == lane_iota(shape) % KPAD, 1.0, 0.0).astype(BF16)
     shape = (FPAD, 2 * LANES)
     same = row_iota(shape) % 2 == (lane_iota(shape) // KPAD) % 2
-    half = lane_iota((FPAD, LANES)) < 64
-    narrow = lane_iota((FPAD, LANES)) < 2 * KPAD
     fulls = []
     for part, piece in enumerate(split(pad_s[...])):
         full = jnp.where(same, dot(dot(expand, piece).astype(BF16), repeat), 0.0)
         back_ref[part * FPAD:(part + 1) * FPAD, :] = full[:, 0:8 * KPAD].astype(BF16)
-        fulls.append(jnp.where(narrow, full[:, 0:LANES], 0.0))
-    turn_ref[...] = jnp.concatenate(
-        [jnp.where(half, fulls[0], pltpu.roll(fulls[0], 64, 1)), fulls[1]], axis=1
-    ).astype(BF16)
+        fulls.append(full)
+    turn = jnp.where(lane_iota(shape) < 4 * KPAD, fulls[0], fulls[1])
+    turn_ref[...] = turn[:, 0:6 * KPAD].astype(BF16)
 
     row = row_iota((KPAD, 2 * LANES))
     rate = jnp.zeros((KPAD, 2 * LANES), F32)
@@ -445,9 +444,6 @@
 
     rate = rate_ref[...]
     slot_pair = (lane_iota((2 * KPAD, 2 * eight)) % eight) // (2 * lats)
-    blank = jnp.zeros((64 - 2 * KPAD, span), BF16)
-    front = lane_iota((lats, LANES)) < 64
-
     lefts = []
     for t in range(groups):
         mine = mixed[:, eight * t:eight * (t + 1)]
@@ -483,33 +479,19 @@
             )
             keeps[-1].start()
 
-    products = []
+    picks = []
     for t in range(groups):
-        legs = pl.ds(2 * eight * t, 2 * eight)
-        pieces = []
-        hold, base = holds[t]
-        for pp in range(4):
-            at = base + 2 * KPAD * pp
-            pieces += [hold[at:at + 2 * KPAD, :], blank]
-        products.append(dot_nt(eh_ref[legs, :], jnp.concatenate(pieces, axis=0)))
-
-    highs, lows = [], []
-    for sums in products:
-        for r in range(rows):
-            for i8 in range(8):
-                at = (r * 8 + i8) * lats
-                pp = i8 // 2
-                tile = sums[at:at + lats, LANES * (pp // 2):LANES * (pp // 2 + 1)]
-                if pp % 2:
-                    tile = pltpu.roll(tile, 64, 1)
-                high = tile.astype(BF16).astype(F32)
-                low = pltpu.roll(tile - high, 64, 1)
-                highs.append(jnp.where(front, high, low))
-                lows.append(jnp.where(front, high, 0.0))
-    own = jnp.concatenate(
-        [jnp.concatenate(highs, axis=0), jnp.concatenate(lows, axis=0)], axis=1
-    ).astype(BF16)
-    cs[:, 0:FPAD] = dot_nt(own, turn_ref[...])
+        hold, at = holds[t]
+        product = dot_nt(hold[at:at + deep, :], eh_ref[pl.ds(2 * eight * t, 2 * eight), :])
+        pick = product[0:2 * KPAD]
+        for pp in range(1, 4):
+            pick = jnp.where(slot_pair == pp, product[2 * KPAD * pp:2 * KPAD * (pp + 1)], pick)
+        picks.append(pick)
+    high, low = split(jnp.concatenate(picks, axis=1))
+    back = dot(turn_ref[...], jnp.concatenate([high, low, high], axis=0))
+    back = jnp.concatenate([back, jnp.zeros((LANES - FPAD, back.shape[1]), F32)], axis=0)
+    for at in range(0, back.shape[1], LANES):
+        cs[at:at + LANES, :] = jnp.transpose(back[:, at:at + LANES])
 
     lane = lane_iota((8, LANES))
     here = [
@@ -636,7 +618,7 @@
             pltpu.HBM((groups * 16 * lats, span), BF16),
             pltpu.VMEM((2 * rows * KPAD, 3 * LANES), BF16),
             pltpu.VMEM((2 * FPAD, 8 * KPAD), BF16),
-            pltpu.VMEM((FPAD, 2 * LANES), BF16),
+            pltpu.VMEM((FPAD, 6 * KPAD), BF16),
             pltpu.VMEM((-(-groups * 4 // 8) * 8, span), F32),
             pltpu.VMEM((KPAD, 2 * LANES), F32),
         ),

time: 38.6 us -> 38.2 us (0.990)
  Pallas kernels: 18.2 us -> 17.7 us
    pallas_call x1, Pallas kernels: 4.92 us -> 4.33 us  [per_device(): pl.pallas_call(functools.partial(solve_kernel, fields, rows, lats), out_s...]
where the time goes in v9:
time: 38.2 us; the launch traced here: 37.8 us
  Pallas kernels  17.7 us (46%)
  starting transfers between devices  9.89 us (26%)
  waiting for transfers between devices  9.5 us (25%)
  between operations  0.68 us (2%)
    all_to_all x1, starting transfers between devices, per_device(): lax.all_to_all(sending, ('lat', 'fld'), split_axis=0, concat_axis=0, tile...  7.3 us
    all_to_all x1, waiting for transfers between devices, per_device(): lax.all_to_all(sending, ('lat', 'fld'), split_axis=0, concat_axis=0, tile...  5.38 us
    pallas_call x1, Pallas kernels, per_device(): pl.pallas_call(functools.partial(solve_kernel, fields, rows, lats), out_s...  4.33 us
    all_to_all x1, waiting for transfers between devices, per_device(): lax.all_to_all(leaving, ('lat', 'fld'), split_axis=0, concat_axis=0, tile...  4.11 us
    pallas_call x1, Pallas kernels, per_device(): pl.pallas_call(output_kernel, grid=(groups,), out_shape=jax.ShapeDtypeStr...  4.11 us
    pallas_call x1, Pallas kernels, per_device(): pl.pallas_call(functools.partial(forward_kernel, cut_off, groups), out_sh...  3.73 us
    pallas_call x1, Pallas kernels, per_device(): pl.pallas_call(functools.partial(prepare_kernel, cut_off, pairs, fields,...  2.84 us
    pallas_call x1, Pallas kernels, per_device(): pl.pallas_call(functools.partial(inverse_kernel, groups), out_shape=jax.S...  2.74 us
  transfers between devices with their start and end apart: 2, of which 2 were waited for; matrix products, arithmetic and copies ran while one was open for 0% of the time, Pallas kernels for 18%

profile of v9, /device:TPU:0, one launch (start us, length us, event | category | flops | bytes accessed | tf_op | source)
XLA Modules:
  0.0 37.8 jit_solution(8837860707339440913)
XLA Ops:
  0.6 3.7 %forward_rows.1 = (f32[32,8,128]{2,1,0:T(8,128)}, bf16[256,1280]{1,0:T(8,128)(2,1)S(1)}, bf16[256,1280]{1,0:T(8,128)(2,1)S(1)}, f32[24,1280]{1,0:T(8,128)S(1)}, f32[24,1280]{1,0:T(8,128)S(1)}) custom-call(s32[8]{0:T(128)} %len_hbm.3, s32[8]{0:T(128)} %band_hbm.5, s32[32,40]{1,0:T(8,128)} %fold_hbm.3, bf16[5,1,2,5248]{3,2,1,0:T(2,128)(2,1)} %grid_hbm.1), custom_call_target="tpu_custom_call" | custom-call | tf_op jit(solution)/shard_map/forward_rows/pallas_call | solution.py:583
  4.4 7.3 %all-to-all-start = ((f32[32,8,128]{2,1,0:T(8,128)}), f32[32,8,128]{2,1,0:T(8,128)S(1)}, u32[]{:S(2)}, u32[]{:S(2)}) async-start(f32[32,8,128]{2,1,0:T(8,128)} %get-tuple-element.17), calls=%async_computation | async-start | bytes 262144 | tf_op jit(solution)/shard_map/all_to_all | solution.py:613
  11.7 2.8 %prepare.1 = (bf16[640,1408]{1,0:T(8,128)(2,1)}, bf16[96,384]{1,0:T(8,128)(2,1)S(1)}, bf16[128,192]{1,0:T(8,128)(2,1)S(1)}, bf16[64,144]{1,0:T(8,128)(2,1)S(1)},...) custom-call(s32[32,40]{1,0:T(8,128)} %fold_hbm.3, s32[8]{0:T(128)} %band_hbm.5, f32[20]{0:T(128)} %rates_hbm.1, ...), custom_call_target="tpu_custom_call" | custom-call | flops 100000000 | bytes 8000000 | tf_op jit(solution)/shard_map/prepare/pallas_call | solution.py:615
  14.5 5.4 %all-to-all-done = f32[32,8,128]{2,1,0:T(8,128)S(1)} async-done(((f32[32,8,128]{2,1,0:T(8,128)}), f32[32,8,128]{2,1,0:T(8,128)S(1)}, u32[]{:S(2)}, u32[]{:S(2)}) %all-to-all-start) | async-done | bytes 131104 | tf_op jit(solution)/shard_map/all_to_all | solution.py:613
  19.9 4.3 %solve.1 = (bf16[384,1408]{1,0:T(8,128)(2,1)S(1)}, bf16[576,1408]{1,0:T(8,128)(2,1)}, f32[256,128]{1,0:T(8,128)}) custom-call(bf16[640,1408]{1,0:T(8,128)(2,1)} %get-tuple-element.16.eh_hbm, f32[256,128]{1,0:T(8,128)S(1)} %bitcast.4, bf16[96,384]{1,0:T(8,128)(2,1)S(1)} %get-tuple-element.18.mix_ref, bf16[64,144]{1,0:T(8,128)(2,1)S(1)} %get-tuple-element.19.turn_ref, ...), custom_call_target="tpu_custom_call" | custom-call | tf_op jit(solution)/shard_map/solve/pallas_call | solution.py:650
  24.2 2.6 %all-to-all-start.1 = ((f32[32,8,128]{2,1,0:T(8,128)}), f32[32,8,128]{2,1,0:T(8,128)S(1)}, u32[]{:S(2)}, u32[]{:S(2)}) async-start(f32[32,8,128]{2,1,0:T(8,128)} %bitcast.7), calls=%async_computation.1 | async-start | bytes 262144 | tf_op jit(solution)/shard_map/all_to_all | solution.py:671
  26.8 4.1 %spectral_output.1 = f32[20,20,2,1281]{3,2,1,0:T(2,128)} custom-call(bf16[384,1408]{1,0:T(8,128)(2,1)S(1)} %get-tuple-element.22.near_ref, bf16[576,1408]{1,0:T(8,128)(2,1)} %get-tuple-element.23.far_hbm, bf16[128,192]{1,0:T(8,128)(2,1)S(1)} %get-tuple-element.24.back_ref), custom_call_target="tpu_custom_call" | custom-call | flops 100000000 | bytes 8000000 | tf_op jit(solution)/shard_map/spectral_output/pallas_call | solution.py:675
  30.9 4.1 %all-to-all-done.1.msg_ref = f32[32,8,128]{2,1,0:T(8,128)S(1)} async-done(((f32[32,8,128]{2,1,0:T(8,128)}), f32[32,8,128]{2,1,0:T(8,128)S(1)}, u32[]{:S(2)}, u32[]{:S(2)}) %all-to-all-start.1) | async-done | bytes 131104 | tf_op jit(solution)/shard_map/all_to_all | solution.py:671
  35.1 2.7 %inverse_rows.1 = bf16[5,1,2,5248]{3,2,1,0:T(2,128)(2,1)} custom-call(s32[8]{0:T(128)} %len_hbm.3, s32[8]{0:T(128)} %band_hbm.5, bf16[256,1280]{1,0:T(8,128)(2,1)S(1)} %get-tuple-element.25.tc, bf16[256,1280]{1,0:T(8,128)(2,1)S(1)} %get-tuple-element.26.ts, f32[24,1280]{1,0:T(8,128)S(1)} %get-tuple-element.27.fc, f32[24,1280]{1,0:T(8,128)S(1)} %get-tuple-element.28.fs, ...), custom_call_target="tpu_custom_call" | custom-call | tf_op jit(solution)/shard_map/inverse_rows/pallas_call | solution.py:697
Async XLA Ops:
  4.4 15.5 %all-to-all-start = ((f32[32,8,128]{2,1,0:T(8,128)}), f32[32,8,128]{2,1,0:T(8,128)S(1)}, u32[]{:S(2)}, u32[]{:S(2)}) async-start(f32[32,8,128]{2,1,0:T(8,128)} %get-tuple-element.17), calls=%async_computation | async-start | bytes 262144 | tf_op jit(solution)/shard_map/all_to_all | solution.py:613
  24.2 10.8 %all-to-all-start.1 = ((f32[32,8,128]{2,1,0:T(8,128)}), f32[32,8,128]{2,1,0:T(8,128)S(1)}, u32[]{:S(2)}, u32[]{:S(2)}) async-start(f32[32,8,128]{2,1,0:T(8,128)} %bitcast.7), calls=%async_computation.1 | async-start | bytes 262144 | tf_op jit(solution)/shard_map/all_to_all | solution.py:671

commit v10 on v9

--- a/solution.py
+++ b/solution.py
@@ -214,30 +214,40 @@
     msg_ref[...] = jnp.transpose(total * scale).reshape(owners, 8, LANES)
 
 
+def inverse_prepare_kernel(
+    groups, fields, rows, tc, ts, after_hbm, right_ref, place_ref,
+):
+    del after_hbm
+    unit = rows * fields * 2
+    shape = place_ref.shape
+    target = row_iota(shape) % 32
+    vec = target % 16
+    base = (vec % rows) * (fields * 2) + (vec // rows) * 2 + target // 16
+    source = (base + unit * (row_iota(shape) // 32) + lax.axis_index("fld") * (fields * 2)) % LANES
+    place_ref[...] = jnp.where(
+        (vec < rows * fields) & (lane_iota(shape) % LANES == source), 1.0, 0.0
+    ).astype(BF16)
+    block = 2 * LANES
+    for i in range(tc.shape[1] // block):
+        at = pl.ds(i * block, block)
+        for part, table in enumerate((tc, ts)):
+            put = (2 * i + part) * block
+            right_ref[put:put + block, :] = jnp.transpose(table[:, at].astype(F32)).astype(BF16)
+
+
 def inverse_kernel(
-    groups, len_hbm, band_hbm, tc, ts, fc, fs, msg_ref, grid_ref,
+    groups, len_hbm, band_hbm, right_ref, place_ref, fc, fs, msg_ref, grid_ref,
     len_ref, band_ref, sems, os,
 ):
     copies = start_all((len_hbm, band_hbm), (len_ref, band_ref), sems)
     spread_s = spread_matrix()
     fields, _, rows, width = grid_ref.shape
     owners = msg_ref.shape[0]
-    slots = tc.shape[1]
-    turns = fc.shape[0]
-    unit = rows * fields * 2
+    slots, turns = fc.shape[1], fc.shape[0]
     high, low = split(msg_ref[...].reshape(owners * 8, LANES))
-    pieces = jnp.concatenate([high, low], axis=1)
-    shape = (32 * groups, 2 * LANES)
-    target = row_iota(shape) % 32
-    vec = target % 16
-    base = (vec % rows) * (fields * 2) + (vec // rows) * 2 + target // 16
-    source = (base + unit * (row_iota(shape) // 32) + lax.axis_index("fld") * (fields * 2)) % LANES
-    place = jnp.where(
-        (vec < rows * fields) & (lane_iota(shape) % LANES == source), 1.0, 0.0
-    ).astype(BF16)
-    turned = dot_nt(place, pieces)
+    turned = dot_nt(place_ref[...], jnp.concatenate([high, low], axis=1))
     block = 2 * LANES
-    lefts, rights = [], []
+    out = jnp.zeros((16 * turns, DEEP), F32)
     for i in range(slots // block):
         t, off = divmod(i * block, owners * 8)
         real = turned[32 * t:32 * t + 16, off:off + block]
@@ -251,9 +261,14 @@
             s1 = fs[g:g + 1, at]
             reals.append(c1 * real + s1 * less_imag)
             imags.append(s1 * less_real + c1 * less_imag)
-        lefts += [jnp.concatenate(reals, axis=0).astype(BF16), jnp.concatenate(imags, axis=0).astype(BF16)]
-        rights += [tc[:, at], ts[:, at]]
-    out = dot_nt(jnp.concatenate(lefts, axis=1), jnp.concatenate(rights, axis=1))
+        left = jnp.concatenate(
+            [
+                jnp.concatenate(reals, axis=0).astype(BF16),
+                jnp.concatenate(imags, axis=0).astype(BF16),
+            ],
+            axis=1,
+        )
+        out = out + dot(left, right_ref[2 * block * i:2 * block * (i + 1), :])
     wait_all(copies)
     length = len_ref[band_ref[lax.axis_index("lat")]]
     out = out * (1.0 / jnp.sqrt(jnp.full((16 * turns, DEEP), length, jnp.int32).astype(F32)))
@@ -408,7 +423,7 @@
 
 def solve_kernel(
     fields, rows, lats, eh_hbm, msg_ref, mix_ref, turn_ref, tau_ref, rate_ref,
-    near_ref, far_hbm, out_ref, cs, eh_ref, far_ref, in_sems, out_sems,
+    damped_hbm, out_ref, cs, eh_ref, damped_ref, in_sems, out_sems,
 ):
     eight = 8 * lats
     groups = eh_ref.shape[0] // (2 * eight)
@@ -421,9 +436,6 @@
     unit = rows * wf
     span = eh_ref.shape[1]
     deep = 8 * KPAD
-    near = near_ref.shape[0] // deep
-    holds = [(near_ref, deep * t) for t in range(near)]
-    holds += [(far_ref, deep * t) for t in range(groups - near)]
     lane = lane_iota((lats, LANES))
     tiles = [
         [msg_ref[pl.ds(8 * g + i8, lats, stride=8 * groups_f), :] for g in range(groups_f)]
@@ -470,19 +482,18 @@
                 at = 2 * pp * KPAD
                 damped.append(modes[at:at + KPAD] * factor)
                 damped.append(modes[at + KPAD:at + 2 * KPAD] * factor)
-            hold, at = holds[t]
-            hold[at:at + deep, start:start + size] = jnp.concatenate(damped, axis=0).astype(BF16)
-        if t >= near:
-            part = pl.ds(deep * (t - near), deep)
-            keeps.append(
-                pltpu.make_async_copy(far_ref.at[part], far_hbm.at[part], out_sems.at[t - near])
-            )
-            keeps[-1].start()
+            damped_ref[deep * t:deep * (t + 1), start:start + size] = jnp.concatenate(
+                damped, axis=0
+            ).astype(BF16)
+        part = pl.ds(deep * t, deep)
+        keeps.append(
+            pltpu.make_async_copy(damped_ref.at[part], damped_hbm.at[part], out_sems.at[t])
+        )
+        keeps[-1].start()
 
     picks = []
     for t in range(groups):
-        hold, at = holds[t]
-        product = dot_nt(hold[at:at + deep, :], eh_ref[pl.ds(2 * eight * t, 2 * eight), :])
+        product = dot_nt(damped_ref[deep * t:deep * (t + 1), :], eh_ref[pl.ds(2 * eight * t, 2 * eight), :])
         pick = product[0:2 * KPAD]
         for pp in range(1, 4):
             pick = jnp.where(slot_pair == pp, product[2 * KPAD * pp:2 * KPAD * (pp + 1)], pick)
@@ -511,22 +522,21 @@
     wait_all(keeps)
 
 
-def output_kernel(near_ref, far_hbm, back_ref, spec_ref, bk, far_s, sems):
+def output_kernel(damped_hbm, back_ref, spec_ref, bk, damped_s, sems):
     everyone, quad, _, places = spec_ref.shape
-    span = near_ref.shape[1]
+    span = damped_s.shape[1]
     deep = 8 * KPAD
-    near = near_ref.shape[0] // deep
     tall = 2 * everyone
     step = pl.program_id(0)
 
-    def far_copy(t):
+    def fetch(t):
         part = pl.ds(pl.multiple_of(deep * t, deep), deep)
-        return pltpu.make_async_copy(far_hbm.at[part], far_s.at[part], sems.at[t])
+        return pltpu.make_async_copy(damped_hbm.at[part], damped_s.at[part], sems.at[t])
 
     @pl.when(step == 0)
     def _():
         for t in range(sems.shape[0]):
-            far_copy(t).start()
+            fetch(t).start()
         pair_of = lane_iota((tall, deep)) // (2 * KPAD)
         rows = []
         for part in range(2):
@@ -535,25 +545,17 @@
                 rows.append(jnp.where(pair_of == pp, full, 0.0))
         bk[...] = jnp.concatenate(rows, axis=0).astype(BF16)
 
-    def write(source, at):
-        for start in range(0, span, 2 * LANES):
-            size = min(2 * LANES, span - start)
-            spec = dot(bk[...], source[pl.ds(at, deep), start:start + size])
-            spec = spec[0:4 * tall] + spec[4 * tall:]
-            kept = min(size, places - start)
-            for pp in range(4):
-                for f in range(everyone):
-                    row = pp * tall + 2 * f
-                    spec_ref[f, pp, :, start:start + kept] = spec[row:row + 2, 0:kept]
-
-    @pl.when(step < near)
-    def _():
-        write(near_ref, pl.multiple_of(deep * step, deep))
-
-    @pl.when(step >= near)
-    def _():
-        far_copy(step - near).wait()
-        write(far_s, pl.multiple_of(deep * (step - near), deep))
+    fetch(step).wait()
+    at = pl.multiple_of(deep * step, deep)
+    for start in range(0, span, 2 * LANES):
+        size = min(2 * LANES, span - start)
+        spec = dot(bk[...], damped_s[pl.ds(at, deep), start:start + size])
+        spec = spec[0:4 * tall] + spec[4 * tall:]
+        kept = min(size, places - start)
+        for pp in range(4):
+            for f in range(everyone):
+                row = pp * tall + 2 * f
+                spec_ref[f, pp, :, start:start + kept] = spec[row:row + 2, 0:kept]
 
 
 def per_device(grid, row_lengths, band_map, fold_map, legendre, to_modes, back_modes, mode_rates):
@@ -646,22 +648,20 @@
         for x in (mix, back, turn_back, tau, rate)
     )
 
-    near = groups // 2
-    damped_near, damped_far, leaving = pl.pallas_call(
+    damped, leaving = pl.pallas_call(
         functools.partial(solve_kernel, fields, rows, lats),
         out_shape=(
-            pltpu.VMEM((near * 8 * KPAD, span), BF16),
-            pltpu.HBM(((groups - near) * 8 * KPAD, span), BF16),
+            pltpu.HBM((groups * 8 * KPAD, span), BF16),
             pltpu.HBM((owners * 8, LANES), F32),
         ),
         in_specs=[hbm] + [vmem] * 5,
-        out_specs=(vmem, hbm, vmem),
+        out_specs=(hbm, vmem),
         scratch_shapes=[
             pltpu.VMEM((groups * 16 * lats, LANES), F32),
             pltpu.VMEM((groups * 16 * lats, span), BF16),
-            pltpu.VMEM(((groups - near) * 8 * KPAD, span), BF16),
+            pltpu.VMEM((groups * 8 * KPAD, span), BF16),
             dma((2,)),
-            dma((groups - near,)),
+            dma((groups,)),
         ],
         compiler_params=room,
         name="solve",
@@ -670,29 +670,41 @@
 
     returned = lax.all_to_all(leaving, ("lat", "fld"), split_axis=0, concat_axis=0, tiled=True)
 
-    damped_near = pltpu.with_memory_space_constraint(damped_near, pltpu.VMEM)
-    damped_far = pltpu.with_memory_space_constraint(damped_far, pltpu.HBM)
+    damped = pltpu.with_memory_space_constraint(damped, pltpu.HBM)
     spectral = pl.pallas_call(
         output_kernel,
         grid=(groups,),
         out_shape=jax.ShapeDtypeStruct((everyone, pairs, 2, places), F32),
         in_specs=[
-            pl.BlockSpec((near * 8 * KPAD, span), lambda t: (0, 0)),
             hbm,
             pl.BlockSpec((2 * FPAD, 8 * KPAD), lambda t: (0, 0)),
         ],
         out_specs=pl.BlockSpec((everyone, 4, 2, places), lambda t: (0, t, 0, 0)),
         scratch_shapes=[
             pltpu.VMEM((16 * everyone, 8 * KPAD), BF16),
-            pltpu.VMEM(((groups - near) * 8 * KPAD, span), BF16),
-            dma((groups - near,)),
+            pltpu.VMEM((groups * 8 * KPAD, span), BF16),
+            dma((groups,)),
         ],
         compiler_params=pltpu.CompilerParams(
             dimension_semantics=("arbitrary",), vmem_limit_bytes=ROOM
         ),
         cost_estimate=pl.CostEstimate(flops=10**8, bytes_accessed=8 * 10**6, transcendentals=0),
         name="spectral_output",
-    )(damped_near, damped_far, back)
+    )(damped, back)
+
+    right, place = pl.pallas_call(
+        functools.partial(inverse_prepare_kernel, groups, fields, rows),
+        out_shape=(
+            pltpu.VMEM((2 * slots, DEEP), BF16),
+            pltpu.VMEM((32 * groups, 2 * LANES), BF16),
+        ),
+        in_specs=[vmem, vmem, hbm],
+        out_specs=(vmem,) * 2,
+        compiler_params=room,
+        cost_estimate=pl.CostEstimate(flops=10**8, bytes_accessed=8 * 10**6, transcendentals=0),
+        name="inverse_prepare",
+    )(tables[0], tables[1], damped)
+    right, place = (pltpu.with_memory_space_constraint(x, pltpu.VMEM) for x in (right, place))
 
     grid_out = pl.pallas_call(
         functools.partial(inverse_kernel, groups),
@@ -707,7 +719,7 @@
         ],
         compiler_params=room,
         name="inverse_rows",
-    )(row_lengths, band_map, *tables, returned)
+    )(row_lengths, band_map, right, place, *tables[2:], returned)
     return (jnp.transpose(spectral, (0, 2, 1, 3)), grid_out)
 
 

time: 38.2 us -> 38.1 us (level)
  waiting for transfers between devices: 9.5 us -> 7.97 us
  Pallas kernels: 17.7 us -> 19.2 us
    all_to_all x1, waiting for transfers between devices: 4.11 us -> 2.58 us  [per_device(): lax.all_to_all(leaving, ('lat', 'fld'), split_axis=0, concat_axis=0, tile...]
    pallas_call x1, Pallas kernels: 4.11 us -> 5.14 us  [per_device(): pl.pallas_call(output_kernel, grid=(groups,), out_shape=jax.ShapeDtypeStr...]
    pallas_call x0 -> x1, Pallas kernels: none -> 0.49 us  [per_device(): pl.pallas_call(functools.partial(inverse_prepare_kernel, groups, fields,...]
  transfers between devices with their start and end apart: 2 -> 2, of which waited for: 2 -> 2; matrix products, arithmetic and copies ran while one was open for 0% -> 0% of each run, Pallas kernels for 18% -> 22%
where the time goes in v10:
time: 38.1 us; the launch traced here: 37.8 us
  Pallas kernels  19.2 us (50%)
  starting transfers between devices  9.88 us (26%)
  waiting for transfers between devices  7.97 us (21%)
  between operations  0.69 us (2%)
    all_to_all x1, starting transfers between devices, per_device(): lax.all_to_all(sending, ('lat', 'fld'), split_axis=0, concat_axis=0, tile...  7.3 us
    all_to_all x1, waiting for transfers between devices, per_device(): lax.all_to_all(sending, ('lat', 'fld'), split_axis=0, concat_axis=0, tile...  5.39 us
    pallas_call x1, Pallas kernels, per_device(): pl.pallas_call(output_kernel, grid=(groups,), out_shape=jax.ShapeDtypeStr...  5.14 us
    pallas_call x1, Pallas kernels, per_device(): pl.pallas_call(functools.partial(solve_kernel, fields, rows, lats), out_s...  4.33 us
    pallas_call x1, Pallas kernels, per_device(): pl.pallas_call(functools.partial(forward_kernel, cut_off, groups), out_sh...  3.73 us
    pallas_call x1, Pallas kernels, per_device(): pl.pallas_call(functools.partial(prepare_kernel, cut_off, pairs, fields,...  2.83 us
    pallas_call x1, Pallas kernels, per_device(): pl.pallas_call(functools.partial(inverse_kernel, groups), out_shape=jax.S...  2.72 us
    all_to_all x1, waiting for transfers between devices, per_device(): lax.all_to_all(leaving, ('lat', 'fld'), split_axis=0, concat_axis=0, tile...  2.58 us
  transfers between devices with their start and end apart: 2, of which 2 were waited for; matrix products, arithmetic and copies ran while one was open for 0% of the time, Pallas kernels for 22%

profile of v10, /device:TPU:0, one launch (start us, length us, event | category | flops | bytes accessed | tf_op | source)
XLA Modules:
  0.0 37.8 jit_solution(11559635249943906911)
XLA Ops:
  0.6 3.7 %forward_rows.1 = (f32[32,8,128]{2,1,0:T(8,128)}, bf16[256,1280]{1,0:T(8,128)(2,1)S(1)}, bf16[256,1280]{1,0:T(8,128)(2,1)S(1)}, f32[24,1280]{1,0:T(8,128)S(1)}, f32[24,1280]{1,0:T(8,128)S(1)}) custom-call(s32[8]{0:T(128)} %len_hbm.3, s32[8]{0:T(128)} %band_hbm.5, s32[32,40]{1,0:T(8,128)} %fold_hbm.3, bf16[5,1,2,5248]{3,2,1,0:T(2,128)(2,1)} %grid_hbm.1), custom_call_target="tpu_custom_call" | custom-call | tf_op jit(solution)/shard_map/forward_rows/pallas_call | solution.py:585
  4.4 7.3 %all-to-all-start = ((f32[32,8,128]{2,1,0:T(8,128)}), f32[32,8,128]{2,1,0:T(8,128)S(1)}, u32[]{:S(2)}, u32[]{:S(2)}) async-start(f32[32,8,128]{2,1,0:T(8,128)} %get-tuple-element.18), calls=%async_computation | async-start | bytes 262144 | tf_op jit(solution)/shard_map/all_to_all | solution.py:615
  11.7 2.8 %prepare.1 = (bf16[640,1408]{1,0:T(8,128)(2,1)}, bf16[96,384]{1,0:T(8,128)(2,1)S(1)}, bf16[128,192]{1,0:T(8,128)(2,1)S(1)}, bf16[64,144]{1,0:T(8,128)(2,1)S(1)},...) custom-call(s32[32,40]{1,0:T(8,128)} %fold_hbm.3, s32[8]{0:T(128)} %band_hbm.5, f32[20]{0:T(128)} %rates_hbm.1, ...), custom_call_target="tpu_custom_call" | custom-call | flops 100000000 | bytes 8000000 | tf_op jit(solution)/shard_map/prepare/pallas_call | solution.py:617
  14.5 5.4 %all-to-all-done = f32[32,8,128]{2,1,0:T(8,128)S(1)} async-done(((f32[32,8,128]{2,1,0:T(8,128)}), f32[32,8,128]{2,1,0:T(8,128)S(1)}, u32[]{:S(2)}, u32[]{:S(2)}) %all-to-all-start) | async-done | bytes 131104 | tf_op jit(solution)/shard_map/all_to_all | solution.py:615
  19.9 4.3 %solve.1 = (bf16[960,1408]{1,0:T(8,128)(2,1)}, f32[256,128]{1,0:T(8,128)}) custom-call(bf16[640,1408]{1,0:T(8,128)(2,1)} %get-tuple-element.17.eh_hbm, f32[256,128]{1,0:T(8,128)S(1)} %bitcast.4, bf16[96,384]{1,0:T(8,128)(2,1)S(1)} %get-tuple-element.19.mix_ref, bf16[64,144]{1,0:T(8,128)(2,1)S(1)} %get-tuple-element.20.turn_ref, ...), custom_call_target="tpu_custom_call" | custom-call | tf_op jit(solution)/shard_map/solve/pallas_call | solution.py:651
  24.2 2.6 %all-to-all-start.1 = ((f32[32,8,128]{2,1,0:T(8,128)}), f32[32,8,128]{2,1,0:T(8,128)S(1)}, u32[]{:S(2)}, u32[]{:S(2)}) async-start(f32[32,8,128]{2,1,0:T(8,128)} %bitcast.7), calls=%async_computation.1 | async-start | bytes 262144 | tf_op jit(solution)/shard_map/all_to_all | solution.py:671
  26.8 5.1 %spectral_output.1 = f32[20,20,2,1281]{3,2,1,0:T(2,128)} custom-call(bf16[960,1408]{1,0:T(8,128)(2,1)} %get-tuple-element.23.damped_hbm.after_hbm, bf16[128,192]{1,0:T(8,128)(2,1)S(1)} %get-tuple-element.24.back_ref), custom_call_target="tpu_custom_call" | custom-call | flops 100000000 | bytes 8000000 | tf_op jit(solution)/shard_map/spectral_output/pallas_call | solution.py:674
  32.0 0.5 %inverse_prepare.1 = (bf16[2560,256]{1,0:T(8,128)(2,1)S(1)}, bf16[160,256]{1,0:T(8,128)(2,1)S(1)}) custom-call(bf16[256,1280]{1,0:T(8,128)(2,1)S(1)} %get-tuple-element.25.tc, bf16[256,1280]{1,0:T(8,128)(2,1)S(1)} %get-tuple-element.26.ts, bf16[960,1408]{1,0:T(8,128)(2,1)} %get-tuple-element.23.damped_hbm.after_hbm), custom_call_target="tpu_custom_call" | custom-call | flops 100000000 | bytes 8000000 | tf_op jit(solution)/shard_map/inverse_prepare/pallas_call | solution.py:695
  32.5 2.6 %all-to-all-done.1.msg_ref = f32[32,8,128]{2,1,0:T(8,128)S(1)} async-done(((f32[32,8,128]{2,1,0:T(8,128)}), f32[32,8,128]{2,1,0:T(8,128)S(1)}, u32[]{:S(2)}, u32[]{:S(2)}) %all-to-all-start.1) | async-done | bytes 131104 | tf_op jit(solution)/shard_map/all_to_all | solution.py:671
  35.1 2.7 %inverse_rows.1 = bf16[5,1,2,5248]{3,2,1,0:T(2,128)(2,1)} custom-call(s32[8]{0:T(128)} %len_hbm.3, s32[8]{0:T(128)} %band_hbm.5, bf16[2560,256]{1,0:T(8,128)(2,1)S(1)} %get-tuple-element.27.right_ref, bf16[160,256]{1,0:T(8,128)(2,1)S(1)} %get-tuple-element.28.place_ref, f32[24,1280]{1,0:T(8,128)S(1)} %get-tuple-element.29.fc, ...), custom_call_target="tpu_custom_call" | custom-call | tf_op jit(solution)/shard_map/inverse_rows/pallas_call | solution.py:709
Async XLA Ops:
  4.4 15.5 %all-to-all-start = ((f32[32,8,128]{2,1,0:T(8,128)}), f32[32,8,128]{2,1,0:T(8,128)S(1)}, u32[]{:S(2)}, u32[]{:S(2)}) async-start(f32[32,8,128]{2,1,0:T(8,128)} %get-tuple-element.18), calls=%async_computation | async-start | bytes 262144 | tf_op jit(solution)/shard_map/all_to_all | solution.py:615
  24.2 10.8 %all-to-all-start.1 = ((f32[32,8,128]{2,1,0:T(8,128)}), f32[32,8,128]{2,1,0:T(8,128)S(1)}, u32[]{:S(2)}, u32[]{:S(2)}) async-start(f32[32,8,128]{2,1,0:T(8,128)} %bitcast.7), calls=%async_computation.1 | async-start | bytes 262144 | tf_op jit(solution)/shard_map/all_to_all | solution.py:671

commit v11 on v9

--- a/solution.py
+++ b/solution.py
@@ -12,6 +12,7 @@
 KPAD = 24
 FPAD = 64
 DEEP = 256
+TWICE = 24
 ROOM = 24 * 1024 * 1024
 F32 = jnp.float32
 BF16 = jnp.bfloat16
@@ -110,10 +111,24 @@
     return turn(steps.astype(F32) * wave, period, 1.0 / period)
 
 
+def two_phases(ref, g, at, used, block):
+    first = ref[2 * g:2 * g + 1, at]
+    second = ref[2 * g + 1:2 * g + 2, at]
+    tiles = []
+    for low in range(0, TWICE, 8):
+        if low + 8 <= used:
+            tiles.append(jnp.broadcast_to(first, (8, block)))
+        elif low >= used:
+            tiles.append(jnp.broadcast_to(second, (8, block)))
+        else:
+            tiles.append(jnp.where(low + row_iota((8, block)) < used, first, second))
+    return jnp.concatenate(tiles, axis=0)
+
+
 def forward_kernel(
     cut_off, groups, len_hbm, band_hbm, fold_hbm, grid_hbm,
     msg_ref, tc, ts, fc, fs,
-    len_ref, band_ref, fold_ref, grid_ref, sems, fold_s, wave_s, xs, xq, xt,
+    len_ref, band_ref, fold_ref, grid_ref, sems, fold_s, wave_s, xs, xt,
 ):
     copies = start_all(
         (len_hbm, band_hbm, fold_hbm, grid_hbm), (len_ref, band_ref, fold_ref, grid_ref), sems
@@ -121,18 +136,26 @@
     fields, _, rows, width = grid_ref.shape
     owners, per_owner = fold_ref.shape
     slots = tc.shape[1]
-    pieces = xq.shape[0] // 64
+    pieces = xs.shape[1] // (4 * DEEP)
     unit = rows * fields * 2
+    used = rows * fields
     spread_s = spread_matrix()
-    shape = (owners * 8, fold_s.shape[0])
-    repeat = jnp.where(row_iota(shape) // 8 == lane_iota(shape), 1.0, 0.0).astype(BF16)
-    weigh = jnp.where(lane_iota((8, 2 * LANES)) < LANES, 8.0, 1.0).astype(BF16)
-    shape = (LANES, 64 * groups)
+    shape = (LANES, owners * 8)
+    repeat = jnp.where(row_iota(shape) == lane_iota(shape) // 8, 1.0, 0.0).astype(BF16)
+    shape = (8 * groups, 16 * groups)
+    weigh = jnp.where(
+        lane_iota(shape) % (8 * groups) // 8 == row_iota(shape) // 8,
+        jnp.where(lane_iota(shape) < 8 * groups, 8.0, 1.0),
+        0.0,
+    ).astype(BF16)
+    tall = 4 * TWICE
+    shape = (LANES, tall * groups)
     source = lane_iota(shape)
-    vec = source % 16
-    base = (vec % rows) * (fields * 2) + (vec // rows) * 2 + (source // 16) % 2
-    target = (base + unit * (source // 64 + lax.axis_index("fld"))) % LANES
-    packing = jnp.where((vec < rows * fields) & (row_iota(shape) == target), 1.0, 0.0).astype(BF16)
+    row = source % TWICE
+    vec = row % used
+    base = (vec % rows) * (fields * 2) + (vec // rows) * 2 + (source // TWICE) % 2
+    target = (base + unit * (source // tall + lax.axis_index("fld"))) % LANES
+    packing = jnp.where((row < 2 * used) & (row_iota(shape) == target), 1.0, 0.0).astype(BF16)
     fold_s[...] = jnp.full(fold_s.shape, -1.0, F32)
     xs[...] = jnp.zeros(xs.shape, F32)
     wait_all(copies)
@@ -140,34 +163,44 @@
     top = jnp.minimum(cut_off, (length - 1) // 2)
 
     fold_s[0:owners, 0:per_owner] = fold_ref[...].astype(F32)
-    eights = jnp.floor(fold_s[...] * 0.125)
-    parts = jnp.concatenate([eights, fold_s[...] - 8.0 * eights], axis=1).astype(BF16)
-    repeated = dot(repeat, parts)
-    lane = lane_iota(repeated.shape)
-    place = lane % LANES - row_iota(repeated.shape) % 8
+    turned = jnp.transpose(fold_s[...])[0:8 * groups]
+    eights = jnp.floor(turned * 0.125)
+    parts = jnp.concatenate([eights, turned - 8.0 * eights], axis=0).astype(BF16)
+    repeated = dot(parts, repeat)
+    own = lane_iota(repeated.shape) % 8 == row_iota(repeated.shape) % 8
+    waves = dot(weigh, jnp.where(own, repeated, 0.0).astype(BF16))
     for t in range(groups):
-        chosen = jnp.where(place == 8 * t, repeated, 0.0).astype(BF16)
-        wave_s[:, owners * 8 * t:owners * 8 * (t + 1)] = dot_nt(weigh, chosen)
+        wave_s[:, owners * 8 * t:owners * 8 * (t + 1)] = waves[8 * t:8 * t + 8]
 
     for field in range(fields):
-        xs[rows * field:rows * (field + 1), 0:width] = grid_ref[field, 0].astype(F32)
+        points = grid_ref[field, 0].astype(F32)
+        for copy in (0, used):
+            at = copy + rows * field
+            xs[at:at + rows, 0:width] = points
     stacked = jnp.concatenate(
         [xs[:, 4 * LANES * c:4 * LANES * (c + 1)] for c in range(2 * pieces)], axis=0
     ).astype(BF16)
     spread = dot(stacked, spread_s)
-    across = (row_iota(spread.shape) // 16) * LANES + lane_iota(spread.shape) % LANES
-    spread = jnp.where(across < length // 4, spread, 0.0).astype(BF16)
-    for c in range(2 * pieces):
-        for phase in range(4):
-            at = (4 * (c // 2) + phase) * 16
-            off = LANES * (c % 2)
-            xq[at:at + 16, off:off + LANES] = spread[
-                16 * c:16 * (c + 1), LANES * phase:LANES * (phase + 1)
-            ]
+    shape = (TWICE, LANES)
+    front = row_iota(shape) < used
+    values = []
+    for k in range(pieces):
+        for pair in range(2):
+            halves = []
+            for half in range(2):
+                c = 2 * k + half
+                rows_c = spread[TWICE * c:TWICE * (c + 1)]
+                off = 2 * LANES * pair
+                both = jnp.where(
+                    front, rows_c[:, off:off + LANES], rows_c[:, off + LANES:off + 2 * LANES]
+                )
+                inside = c * LANES + lane_iota(shape) < length // 4
+                halves.append(jnp.where(inside, both, 0.0))
+            values.append(jnp.concatenate(halves, axis=1))
+    values = jnp.concatenate(values, axis=0).astype(BF16)
 
     turns = 4 * pieces
     block = 2 * LANES
-    values = xq[...]
     for i in range(slots // block):
         at = pl.ds(i * block, block)
         wave = wave_s[:, at]
@@ -195,17 +228,18 @@
         ts[:, at] = s_all
         inner_c = dot(values, c_all)
         inner_s = dot(values, s_all)
-        real = jnp.zeros((16, block), F32)
-        imag = jnp.zeros((16, block), F32)
-        for g in range(turns):
-            c1 = fc[g:g + 1, at]
-            s1 = fs[g:g + 1, at]
-            part_c = inner_c[16 * g:16 * (g + 1)]
-            part_s = inner_s[16 * g:16 * (g + 1)]
+        real = jnp.zeros((TWICE, block), F32)
+        imag = jnp.zeros((TWICE, block), F32)
+        for g in range(turns // 2):
+            c1 = two_phases(fc, g, at, used, block)
+            s1 = two_phases(fs, g, at, used, block)
+            part_c = inner_c[TWICE * g:TWICE * (g + 1)]
+            part_s = inner_s[TWICE * g:TWICE * (g + 1)]
             real = real + (c1 * part_c - s1 * part_s)
             imag = imag - (c1 * part_s + s1 * part_c)
         both = jnp.concatenate([real, imag], axis=0) * jnp.where(one == 0.0, 1.0, 0.5)
         xt[:, at] = jnp.concatenate(split(both), axis=0)
+
     turned = jnp.concatenate(
         [xt[:, owners * 8 * t:owners * 8 * (t + 1)] for t in range(groups)], axis=0
     )
@@ -227,44 +261,46 @@
     unit = rows * fields * 2
     high, low = split(msg_ref[...].reshape(owners * 8, LANES))
     pieces = jnp.concatenate([high, low], axis=1)
-    shape = (32 * groups, 2 * LANES)
-    target = row_iota(shape) % 32
-    vec = target % 16
-    base = (vec % rows) * (fields * 2) + (vec // rows) * 2 + target // 16
-    source = (base + unit * (row_iota(shape) // 32) + lax.axis_index("fld") * (fields * 2)) % LANES
+    used = rows * fields
+    tall = 2 * TWICE
+    shape = (tall * groups, 2 * LANES)
+    target = row_iota(shape) % tall
+    row = target % TWICE
+    vec = row % used
+    base = (vec % rows) * (fields * 2) + (vec // rows) * 2 + target // TWICE
+    source = (base + unit * (row_iota(shape) // tall) + lax.axis_index("fld") * (fields * 2)) % LANES
     place = jnp.where(
-        (vec < rows * fields) & (lane_iota(shape) % LANES == source), 1.0, 0.0
+        (row < 2 * used) & (lane_iota(shape) % LANES == source), 1.0, 0.0
     ).astype(BF16)
     turned = dot_nt(place, pieces)
     block = 2 * LANES
-    lefts, rights = [], []
+    out = jnp.zeros((TWICE * turns // 2, DEEP), F32)
     for i in range(slots // block):
         t, off = divmod(i * block, owners * 8)
-        real = turned[32 * t:32 * t + 16, off:off + block]
-        imag = turned[32 * t + 16:32 * t + 32, off:off + block]
-        less_real = -real
-        less_imag = -imag
+        real = turned[tall * t:tall * t + TWICE, off:off + block]
+        imag = turned[tall * t + TWICE:tall * (t + 1), off:off + block]
         at = pl.ds(i * block, block)
         reals, imags = [], []
-        for g in range(turns):
-            c1 = fc[g:g + 1, at]
-            s1 = fs[g:g + 1, at]
-            reals.append(c1 * real + s1 * less_imag)
-            imags.append(s1 * less_real + c1 * less_imag)
-        lefts += [jnp.concatenate(reals, axis=0).astype(BF16), jnp.concatenate(imags, axis=0).astype(BF16)]
-        rights += [tc[:, at], ts[:, at]]
-    out = dot_nt(jnp.concatenate(lefts, axis=1), jnp.concatenate(rights, axis=1))
+        for g in range(turns // 2):
+            c1 = two_phases(fc, g, at, used, block)
+            s1 = two_phases(fs, g, at, used, block)
+            reals.append(c1 * real - s1 * imag)
+            imags.append(s1 * real + c1 * imag)
+        reals = jnp.concatenate(reals, axis=0).astype(BF16)
+        imags = jnp.concatenate(imags, axis=0).astype(BF16)
+        out = out + (dot_nt(reals, tc[:, at]) - dot_nt(imags, ts[:, at]))
     wait_all(copies)
     length = len_ref[band_ref[lax.axis_index("lat")]]
-    out = out * (1.0 / jnp.sqrt(jnp.full((16 * turns, DEEP), length, jnp.int32).astype(F32)))
+    out = out * (1.0 / jnp.sqrt(jnp.full(out.shape, length, jnp.int32).astype(F32)))
     chunks = os.shape[0] // 16
     for c in range(chunks):
+        off = LANES * (c % 2)
         for phase in range(4):
-            at = (4 * (c // 2) + phase) * 16
-            off = LANES * (c % 2)
-            os[16 * c:16 * (c + 1), LANES * phase:LANES * (phase + 1)] = out[
-                at:at + 16, off:off + LANES
-            ].astype(BF16)
+            at = (2 * (c // 2) + phase // 2) * TWICE
+            piece = out[at:at + TWICE, off:off + LANES]
+            if phase % 2:
+                piece = pltpu.roll(piece, TWICE - used, 0)
+            os[16 * c:16 * (c + 1), LANES * phase:LANES * (phase + 1)] = piece[0:16].astype(BF16)
     merged = dot_nt(os[...], spread_s)
     for c in range(chunks):
         begin = 4 * LANES * c
@@ -466,7 +502,6 @@
                 tau = tau_ref[4 * t + pp:4 * t + pp + 1, start:start + size]
                 below = 1.0 + tau * rate[:, 0:size]
                 factor = pl.reciprocal(below, approx=True)
-                factor = factor * (2.0 - below * factor)
                 at = 2 * pp * KPAD
                 damped.append(modes[at:at + KPAD] * factor)
                 damped.append(modes[at + KPAD:at + 2 * KPAD] * factor)
@@ -599,9 +634,8 @@
             dma((4,)),
             pltpu.VMEM((LANES, LANES), F32),
             pltpu.VMEM((8, slots), F32),
-            pltpu.VMEM((16, 4 * DEEP * pieces), F32),
-            pltpu.VMEM((16 * turns, DEEP), BF16),
-            pltpu.VMEM((64, slots), BF16),
+            pltpu.VMEM((TWICE, 4 * DEEP * pieces), F32),
+            pltpu.VMEM((4 * TWICE, slots), BF16),
         ],
         compiler_params=room,
         name="forward_rows",

time: 38.2 us -> 37.9 us (level)
  transfers between devices with their start and end apart: 2 -> 2, of which waited for: 2 -> 2; matrix products, arithmetic and copies ran while one was open for 0% -> 0% of each run, Pallas kernels for 18% -> 19%
where the time goes in v11:
time: 37.9 us; the launch traced here: 37.5 us
  Pallas kernels  17.5 us (46%)
  starting transfers between devices  9.89 us (26%)
  waiting for transfers between devices  9.5 us (25%)
  between operations  0.68 us (2%)
    all_to_all x1, starting transfers between devices, per_device(): lax.all_to_all(sending, ('lat', 'fld'), split_axis=0, concat_axis=0, tile...  7.3 us
    all_to_all x1, waiting for transfers between devices, per_device(): lax.all_to_all(sending, ('lat', 'fld'), split_axis=0, concat_axis=0, tile...  5.38 us
    pallas_call x1, Pallas kernels, per_device(): pl.pallas_call(functools.partial(solve_kernel, fields, rows, lats), out_s...  4.25 us
    all_to_all x1, waiting for transfers between devices, per_device(): lax.all_to_all(leaving, ('lat', 'fld'), split_axis=0, concat_axis=0, tile...  4.11 us
    pallas_call x1, Pallas kernels, per_device(): pl.pallas_call(output_kernel, grid=(groups,), out_shape=jax.ShapeDtypeStr...  4.11 us
    pallas_call x1, Pallas kernels, per_device(): pl.pallas_call(functools.partial(forward_kernel, cut_off, groups), out_sh...  3.54 us
    pallas_call x1, Pallas kernels, per_device(): pl.pallas_call(functools.partial(prepare_kernel, cut_off, pairs, fields,...  2.84 us
    pallas_call x1, Pallas kernels, per_device(): pl.pallas_call(functools.partial(inverse_kernel, groups), out_shape=jax.S...  2.74 us
  transfers between devices with their start and end apart: 2, of which 2 were waited for; matrix products, arithmetic and copies ran while one was open for 0% of the time, Pallas kernels for 19%

profile of v11, /device:TPU:0, one launch (start us, length us, event | category | flops | bytes accessed | tf_op | source)
XLA Modules:
  0.0 37.5 jit_solution(14097517952190011882)
XLA Ops:
  0.6 3.5 %forward_rows.1 = (f32[32,8,128]{2,1,0:T(8,128)}, bf16[256,1280]{1,0:T(8,128)(2,1)S(1)}, bf16[256,1280]{1,0:T(8,128)(2,1)S(1)}, f32[24,1280]{1,0:T(8,128)S(1)}, f32[24,1280]{1,0:T(8,128)S(1)}) custom-call(s32[8]{0:T(128)} %len_hbm.3, s32[8]{0:T(128)} %band_hbm.5, s32[32,40]{1,0:T(8,128)} %fold_hbm.3, bf16[5,1,2,5248]{3,2,1,0:T(2,128)(2,1)} %grid_hbm.1), custom_call_target="tpu_custom_call" | custom-call | tf_op jit(solution)/shard_map/forward_rows/pallas_call | solution.py:618
  4.2 7.3 %all-to-all-start = ((f32[32,8,128]{2,1,0:T(8,128)}), f32[32,8,128]{2,1,0:T(8,128)S(1)}, u32[]{:S(2)}, u32[]{:S(2)}) async-start(f32[32,8,128]{2,1,0:T(8,128)} %get-tuple-element.17), calls=%async_computation | async-start | bytes 262144 | tf_op jit(solution)/shard_map/all_to_all | solution.py:647
  11.5 2.8 %prepare.1 = (bf16[640,1408]{1,0:T(8,128)(2,1)}, bf16[96,384]{1,0:T(8,128)(2,1)S(1)}, bf16[128,192]{1,0:T(8,128)(2,1)S(1)}, bf16[64,144]{1,0:T(8,128)(2,1)S(1)},...) custom-call(s32[32,40]{1,0:T(8,128)} %fold_hbm.3, s32[8]{0:T(128)} %band_hbm.5, f32[20]{0:T(128)} %rates_hbm.1, ...), custom_call_target="tpu_custom_call" | custom-call | flops 100000000 | bytes 8000000 | tf_op jit(solution)/shard_map/prepare/pallas_call | solution.py:649
  14.3 5.4 %all-to-all-done = f32[32,8,128]{2,1,0:T(8,128)S(1)} async-done(((f32[32,8,128]{2,1,0:T(8,128)}), f32[32,8,128]{2,1,0:T(8,128)S(1)}, u32[]{:S(2)}, u32[]{:S(2)}) %all-to-all-start) | async-done | bytes 131104 | tf_op jit(solution)/shard_map/all_to_all | solution.py:647
  19.7 4.3 %solve.1 = (bf16[384,1408]{1,0:T(8,128)(2,1)S(1)}, bf16[576,1408]{1,0:T(8,128)(2,1)}, f32[256,128]{1,0:T(8,128)}) custom-call(bf16[640,1408]{1,0:T(8,128)(2,1)} %get-tuple-element.16.eh_hbm, f32[256,128]{1,0:T(8,128)S(1)} %bitcast.4, bf16[96,384]{1,0:T(8,128)(2,1)S(1)} %get-tuple-element.18.mix_ref, bf16[64,144]{1,0:T(8,128)(2,1)S(1)} %get-tuple-element.19.turn_ref, ...), custom_call_target="tpu_custom_call" | custom-call | tf_op jit(solution)/shard_map/solve/pallas_call | solution.py:684
  24.0 2.6 %all-to-all-start.1 = ((f32[32,8,128]{2,1,0:T(8,128)}), f32[32,8,128]{2,1,0:T(8,128)S(1)}, u32[]{:S(2)}, u32[]{:S(2)}) async-start(f32[32,8,128]{2,1,0:T(8,128)} %bitcast.7), calls=%async_computation.1 | async-start | bytes 262144 | tf_op jit(solution)/shard_map/all_to_all | solution.py:705
  26.6 4.1 %spectral_output.1 = f32[20,20,2,1281]{3,2,1,0:T(2,128)} custom-call(bf16[384,1408]{1,0:T(8,128)(2,1)S(1)} %get-tuple-element.22.near_ref, bf16[576,1408]{1,0:T(8,128)(2,1)} %get-tuple-element.23.far_hbm, bf16[128,192]{1,0:T(8,128)(2,1)S(1)} %get-tuple-element.24.back_ref), custom_call_target="tpu_custom_call" | custom-call | flops 100000000 | bytes 8000000 | tf_op jit(solution)/shard_map/spectral_output/pallas_call | solution.py:709
  30.7 4.1 %all-to-all-done.1.msg_ref = f32[32,8,128]{2,1,0:T(8,128)S(1)} async-done(((f32[32,8,128]{2,1,0:T(8,128)}), f32[32,8,128]{2,1,0:T(8,128)S(1)}, u32[]{:S(2)}, u32[]{:S(2)}) %all-to-all-start.1) | async-done | bytes 131104 | tf_op jit(solution)/shard_map/all_to_all | solution.py:705
  34.8 2.7 %inverse_rows.1 = bf16[5,1,2,5248]{3,2,1,0:T(2,128)(2,1)} custom-call(s32[8]{0:T(128)} %len_hbm.3, s32[8]{0:T(128)} %band_hbm.5, bf16[256,1280]{1,0:T(8,128)(2,1)S(1)} %get-tuple-element.25.tc, bf16[256,1280]{1,0:T(8,128)(2,1)S(1)} %get-tuple-element.26.ts, f32[24,1280]{1,0:T(8,128)S(1)} %get-tuple-element.27.fc, f32[24,1280]{1,0:T(8,128)S(1)} %get-tuple-element.28.fs, ...), custom_call_target="tpu_custom_call" | custom-call | tf_op jit(solution)/shard_map/inverse_rows/pallas_call | solution.py:731
Async XLA Ops:
  4.2 15.5 %all-to-all-start = ((f32[32,8,128]{2,1,0:T(8,128)}), f32[32,8,128]{2,1,0:T(8,128)S(1)}, u32[]{:S(2)}, u32[]{:S(2)}) async-start(f32[32,8,128]{2,1,0:T(8,128)} %get-tuple-element.17), calls=%async_computation | async-start | bytes 262144 | tf_op jit(solution)/shard_map/all_to_all | solution.py:647
  24.0 10.8 %all-to-all-start.1 = ((f32[32,8,128]{2,1,0:T(8,128)}), f32[32,8,128]{2,1,0:T(8,128)S(1)}, u32[]{:S(2)}, u32[]{:S(2)}) async-start(f32[32,8,128]{2,1,0:T(8,128)} %bitcast.7), calls=%async_computation.1 | async-start | bytes 262144 | tf_op jit(solution)/shard_map/all_to_all | solution.py:705

commit v12 on v11

--- a/solution.py
+++ b/solution.py
@@ -102,13 +102,20 @@
     return jnp.concatenate(picks, axis=1).astype(BF16)
 
 
-def phases_of(groups, wave, length, lanes):
-    shape = (groups + 16, lanes)
-    row = row_iota(shape)
-    steps = jnp.where(row < groups, (row // 4) * (4 * DEEP) + row % 4, 4 * (row - groups))
+def phase_steps(groups, lanes):
+    row = row_iota((groups + 16, lanes))
+    steps = jnp.where(row < groups, (row >> 2) * (4 * DEEP) + (row & 3), 4 * (row - groups))
     steps = jnp.where(row >= groups + 8, 32 << jnp.maximum(row - groups - 8, 0), steps)
-    period = jnp.full(shape, length, jnp.int32).astype(F32)
-    return turn(steps.astype(F32) * wave, period, 1.0 / period)
+    return steps.astype(F32)
+
+
+def slot_lane(index, fields, rows):
+    used = rows * fields
+    part = (index >= TWICE).astype(jnp.int32)
+    row = index - TWICE * part
+    vec = jnp.where(row >= used, row - used, row)
+    lane = lax.rem(vec, rows) * (fields * 2) + lax.div(vec, rows) * 2 + part
+    return jnp.where(row < 2 * used, lane, -LANES)
 
 
 def two_phases(ref, g, at, used, block):
@@ -141,21 +148,25 @@
     used = rows * fields
     spread_s = spread_matrix()
     shape = (LANES, owners * 8)
-    repeat = jnp.where(row_iota(shape) == lane_iota(shape) // 8, 1.0, 0.0).astype(BF16)
+    repeat = jnp.where(row_iota(shape) == lane_iota(shape) >> 3, 1.0, 0.0).astype(BF16)
     shape = (8 * groups, 16 * groups)
     weigh = jnp.where(
-        lane_iota(shape) % (8 * groups) // 8 == row_iota(shape) // 8,
+        jnp.where(lane_iota(shape) < 8 * groups, lane_iota(shape), lane_iota(shape) - 8 * groups) >> 3
+        == row_iota(shape) >> 3,
         jnp.where(lane_iota(shape) < 8 * groups, 8.0, 1.0),
         0.0,
     ).astype(BF16)
     tall = 4 * TWICE
     shape = (LANES, tall * groups)
-    source = lane_iota(shape)
-    row = source % TWICE
-    vec = row % used
-    base = (vec % rows) * (fields * 2) + (vec // rows) * 2 + (source // TWICE) % 2
-    target = (base + unit * (source // tall + lax.axis_index("fld"))) % LANES
-    packing = jnp.where((row < 2 * used) & (row_iota(shape) == target), 1.0, 0.0).astype(BF16)
+    one = (1, 2 * TWICE)
+    base = slot_lane(lane_iota(one), fields, rows)
+    targets = []
+    for t in range(groups):
+        target = base + unit * (t + lax.axis_index("fld"))
+        target = jnp.where(base < 0, base, target & (LANES - 1))
+        targets += [target, target]
+    target = jnp.concatenate(targets, axis=1)
+    packing = jnp.where(row_iota(shape) == target, 1.0, 0.0).astype(BF16)
     fold_s[...] = jnp.full(fold_s.shape, -1.0, F32)
     xs[...] = jnp.zeros(xs.shape, F32)
     wait_all(copies)
@@ -167,7 +178,7 @@
     eights = jnp.floor(turned * 0.125)
     parts = jnp.concatenate([eights, turned - 8.0 * eights], axis=0).astype(BF16)
     repeated = dot(parts, repeat)
-    own = lane_iota(repeated.shape) % 8 == row_iota(repeated.shape) % 8
+    own = (lane_iota(repeated.shape) & 7) == (row_iota(repeated.shape) & 7)
     waves = dot(weigh, jnp.where(own, repeated, 0.0).astype(BF16))
     for t in range(groups):
         wave_s[:, owners * 8 * t:owners * 8 * (t + 1)] = waves[8 * t:8 * t + 8]
@@ -201,11 +212,14 @@
 
     turns = 4 * pieces
     block = 2 * LANES
+    steps = phase_steps(turns, block)
+    period = jnp.full(steps.shape, length, jnp.int32).astype(F32)
+    inverse = 1.0 / period
     for i in range(slots // block):
         at = pl.ds(i * block, block)
         wave = wave_s[:, at]
         wave = jnp.concatenate([wave] * ((turns + 16) // 8), axis=0)
-        co, si = phases_of(turns, wave, length, block)
+        co, si = turn(steps * wave, period, inverse)
         one = wave[0:1]
         weight = jnp.where(one == 0.0, 1.0, 2.0)
         weight = jnp.where((one >= 0.0) & (one <= jnp.full(one.shape, top, jnp.int32).astype(F32)), weight, 0.0)
@@ -263,15 +277,15 @@
     pieces = jnp.concatenate([high, low], axis=1)
     used = rows * fields
     tall = 2 * TWICE
-    shape = (tall * groups, 2 * LANES)
-    target = row_iota(shape) % tall
-    row = target % TWICE
-    vec = row % used
-    base = (vec % rows) * (fields * 2) + (vec // rows) * 2 + target // TWICE
-    source = (base + unit * (row_iota(shape) // tall) + lax.axis_index("fld") * (fields * 2)) % LANES
-    place = jnp.where(
-        (row < 2 * used) & (lane_iota(shape) % LANES == source), 1.0, 0.0
-    ).astype(BF16)
+    shape = (tall, LANES)
+    base = slot_lane(row_iota(shape), fields, rows)
+    places = []
+    for t in range(groups):
+        source = (base + unit * t + lax.axis_index("fld") * (fields * 2)) & (LANES - 1)
+        source = jnp.where(base < 0, base, source)
+        places.append(jnp.where(lane_iota(shape) == source, 1.0, 0.0))
+    place = jnp.concatenate(places, axis=0).astype(BF16)
+    place = jnp.concatenate([place, place], axis=1)
     turned = dot_nt(place, pieces)
     block = 2 * LANES
     out = jnp.zeros((TWICE * turns // 2, DEEP), F32)

time: 37.9 us -> 37.8 us (level)
  no operation moved by 1% of the time
where the time goes in v12:
time: 37.8 us; the launch traced here: 37.4 us
  Pallas kernels  17.3 us (46%)
  starting transfers between devices  9.89 us (26%)
  waiting for transfers between devices  9.5 us (25%)
  between operations  0.68 us (2%)
    all_to_all x1, starting transfers between devices, per_device(): lax.all_to_all(sending, ('lat', 'fld'), split_axis=0, concat_axis=0, tile...  7.3 us
    all_to_all x1, waiting for transfers between devices, per_device(): lax.all_to_all(sending, ('lat', 'fld'), split_axis=0, concat_axis=0, tile...  5.38 us
    pallas_call x1, Pallas kernels, per_device(): pl.pallas_call(functools.partial(solve_kernel, fields, rows, lats), out_s...  4.25 us
    all_to_all x1, waiting for transfers between devices, per_device(): lax.all_to_all(leaving, ('lat', 'fld'), split_axis=0, concat_axis=0, tile...  4.12 us
    pallas_call x1, Pallas kernels, per_device(): pl.pallas_call(output_kernel, grid=(groups,), out_shape=jax.ShapeDtypeStr...  4.1 us
    pallas_call x1, Pallas kernels, per_device(): pl.pallas_call(functools.partial(forward_kernel, cut_off, groups), out_sh...  3.65 us
    pallas_call x1, Pallas kernels, per_device(): pl.pallas_call(functools.partial(prepare_kernel, cut_off, pairs, fields,...  2.84 us
    all_to_all x1, starting transfers between devices, per_device(): lax.all_to_all(leaving, ('lat', 'fld'), split_axis=0, concat_axis=0, tile...  2.58 us
  transfers between devices with their start and end apart: 2, of which 2 were waited for; matrix products, arithmetic and copies ran while one was open for 0% of the time, Pallas kernels for 19%

profile of v12, /device:TPU:0, one launch (start us, length us, event | category | flops | bytes accessed | tf_op | source)
XLA Modules:
  0.0 37.4 jit_solution(16965027218405289881)
XLA Ops:
  0.6 3.6 %forward_rows.1 = (f32[32,8,128]{2,1,0:T(8,128)}, bf16[256,1280]{1,0:T(8,128)(2,1)S(1)}, bf16[256,1280]{1,0:T(8,128)(2,1)S(1)}, f32[24,1280]{1,0:T(8,128)S(1)}, f32[24,1280]{1,0:T(8,128)S(1)}) custom-call(s32[8]{0:T(128)} %len_hbm.3, s32[8]{0:T(128)} %band_hbm.5, s32[32,40]{1,0:T(8,128)} %fold_hbm.3, bf16[5,1,2,5248]{3,2,1,0:T(2,128)(2,1)} %grid_hbm.1), custom_call_target="tpu_custom_call" | custom-call | tf_op jit(solution)/shard_map/forward_rows/pallas_call | solution.py:632
  4.3 7.3 %all-to-all-start = ((f32[32,8,128]{2,1,0:T(8,128)}), f32[32,8,128]{2,1,0:T(8,128)S(1)}, u32[]{:S(2)}, u32[]{:S(2)}) async-start(f32[32,8,128]{2,1,0:T(8,128)} %get-tuple-element.17), calls=%async_computation | async-start | bytes 262144 | tf_op jit(solution)/shard_map/all_to_all | solution.py:661
  11.6 2.8 %prepare.1 = (bf16[640,1408]{1,0:T(8,128)(2,1)}, bf16[96,384]{1,0:T(8,128)(2,1)S(1)}, bf16[128,192]{1,0:T(8,128)(2,1)S(1)}, bf16[64,144]{1,0:T(8,128)(2,1)S(1)},...) custom-call(s32[32,40]{1,0:T(8,128)} %fold_hbm.3, s32[8]{0:T(128)} %band_hbm.5, f32[20]{0:T(128)} %rates_hbm.1, ...), custom_call_target="tpu_custom_call" | custom-call | flops 100000000 | bytes 8000000 | tf_op jit(solution)/shard_map/prepare/pallas_call | solution.py:663
  14.4 5.4 %all-to-all-done = f32[32,8,128]{2,1,0:T(8,128)S(1)} async-done(((f32[32,8,128]{2,1,0:T(8,128)}), f32[32,8,128]{2,1,0:T(8,128)S(1)}, u32[]{:S(2)}, u32[]{:S(2)}) %all-to-all-start) | async-done | bytes 131104 | tf_op jit(solution)/shard_map/all_to_all | solution.py:661
  19.8 4.3 %solve.1 = (bf16[384,1408]{1,0:T(8,128)(2,1)S(1)}, bf16[576,1408]{1,0:T(8,128)(2,1)}, f32[256,128]{1,0:T(8,128)}) custom-call(bf16[640,1408]{1,0:T(8,128)(2,1)} %get-tuple-element.16.eh_hbm, f32[256,128]{1,0:T(8,128)S(1)} %bitcast.4, bf16[96,384]{1,0:T(8,128)(2,1)S(1)} %get-tuple-element.18.mix_ref, bf16[64,144]{1,0:T(8,128)(2,1)S(1)} %get-tuple-element.19.turn_ref, ...), custom_call_target="tpu_custom_call" | custom-call | tf_op jit(solution)/shard_map/solve/pallas_call | solution.py:698
  24.1 2.6 %all-to-all-start.1 = ((f32[32,8,128]{2,1,0:T(8,128)}), f32[32,8,128]{2,1,0:T(8,128)S(1)}, u32[]{:S(2)}, u32[]{:S(2)}) async-start(f32[32,8,128]{2,1,0:T(8,128)} %bitcast.7), calls=%async_computation.1 | async-start | bytes 262144 | tf_op jit(solution)/shard_map/all_to_all | solution.py:719
  26.7 4.1 %spectral_output.1 = f32[20,20,2,1281]{3,2,1,0:T(2,128)} custom-call(bf16[384,1408]{1,0:T(8,128)(2,1)S(1)} %get-tuple-element.22.near_ref, bf16[576,1408]{1,0:T(8,128)(2,1)} %get-tuple-element.23.far_hbm, bf16[128,192]{1,0:T(8,128)(2,1)S(1)} %get-tuple-element.24.back_ref), custom_call_target="tpu_custom_call" | custom-call | flops 100000000 | bytes 8000000 | tf_op jit(solution)/shard_map/spectral_output/pallas_call | solution.py:723
  30.8 4.1 %all-to-all-done.1.msg_ref = f32[32,8,128]{2,1,0:T(8,128)S(1)} async-done(((f32[32,8,128]{2,1,0:T(8,128)}), f32[32,8,128]{2,1,0:T(8,128)S(1)}, u32[]{:S(2)}, u32[]{:S(2)}) %all-to-all-start.1) | async-done | bytes 131104 | tf_op jit(solution)/shard_map/all_to_all | solution.py:719
  34.9 2.5 %inverse_rows.1 = bf16[5,1,2,5248]{3,2,1,0:T(2,128)(2,1)} custom-call(s32[8]{0:T(128)} %len_hbm.3, s32[8]{0:T(128)} %band_hbm.5, bf16[256,1280]{1,0:T(8,128)(2,1)S(1)} %get-tuple-element.25.tc, bf16[256,1280]{1,0:T(8,128)(2,1)S(1)} %get-tuple-element.26.ts, f32[24,1280]{1,0:T(8,128)S(1)} %get-tuple-element.27.fc, f32[24,1280]{1,0:T(8,128)S(1)} %get-tuple-element.28.fs, ...), custom_call_target="tpu_custom_call" | custom-call | tf_op jit(solution)/shard_map/inverse_rows/pallas_call | solution.py:745
Async XLA Ops:
  4.3 15.5 %all-to-all-start = ((f32[32,8,128]{2,1,0:T(8,128)}), f32[32,8,128]{2,1,0:T(8,128)S(1)}, u32[]{:S(2)}, u32[]{:S(2)}) async-start(f32[32,8,128]{2,1,0:T(8,128)} %get-tuple-element.17), calls=%async_computation | async-start | bytes 262144 | tf_op jit(solution)/shard_map/all_to_all | solution.py:661
  24.1 10.8 %all-to-all-start.1 = ((f32[32,8,128]{2,1,0:T(8,128)}), f32[32,8,128]{2,1,0:T(8,128)S(1)}, u32[]{:S(2)}, u32[]{:S(2)}) async-start(f32[32,8,128]{2,1,0:T(8,128)} %bitcast.7), calls=%async_computation.1 | async-start | bytes 262144 | tf_op jit(solution)/shard_map/all_to_all | solution.py:719

commit v13 on v12

--- a/solution.py
+++ b/solution.py
@@ -184,36 +184,33 @@
         wave_s[:, owners * 8 * t:owners * 8 * (t + 1)] = waves[8 * t:8 * t + 8]
 
     for field in range(fields):
-        points = grid_ref[field, 0].astype(F32)
-        for copy in (0, used):
-            at = copy + rows * field
-            xs[at:at + rows, 0:width] = points
+        xs[rows * field:rows * (field + 1), 0:width] = grid_ref[field, 0].astype(F32)
     stacked = jnp.concatenate(
         [xs[:, 4 * LANES * c:4 * LANES * (c + 1)] for c in range(2 * pieces)], axis=0
     ).astype(BF16)
     spread = dot(stacked, spread_s)
-    shape = (TWICE, LANES)
-    front = row_iota(shape) < used
+    blank = jnp.zeros((TWICE - 16, LANES), F32)
     values = []
     for k in range(pieces):
         for pair in range(2):
             halves = []
             for half in range(2):
                 c = 2 * k + half
-                rows_c = spread[TWICE * c:TWICE * (c + 1)]
                 off = 2 * LANES * pair
-                both = jnp.where(
-                    front, rows_c[:, off:off + LANES], rows_c[:, off + LANES:off + 2 * LANES]
+                rows_c = spread[16 * c:16 * (c + 1)]
+                inside = c * LANES + lane_iota((16, LANES)) < length // 4
+                first, second = (
+                    jnp.concatenate([jnp.where(inside, rows_c[:, o:o + LANES], 0.0), blank], axis=0)
+                    for o in (off, off + LANES)
                 )
-                inside = c * LANES + lane_iota(shape) < length // 4
-                halves.append(jnp.where(inside, both, 0.0))
+                halves.append(first + pltpu.roll(second, used, 0))
             values.append(jnp.concatenate(halves, axis=1))
     values = jnp.concatenate(values, axis=0).astype(BF16)
 
     turns = 4 * pieces
     block = 2 * LANES
     steps = phase_steps(turns, block)
-    period = jnp.full(steps.shape, length, jnp.int32).astype(F32)
+    period = jnp.full((1, block), length, jnp.int32).astype(F32)
     inverse = 1.0 / period
     for i in range(slots // block):
         at = pl.ds(i * block, block)
@@ -331,8 +328,8 @@
 
 def prepare_kernel(
     cut_off, pairs, fields, rows, fold_hbm, band_hbm, rates_hbm, leg_hbm, tm_hbm, bm_hbm,
-    eh_hbm, mix_ref, back_ref, turn_ref, tau_ref, rate_ref,
-    fold_ref, band_ref, rates_ref, leg_ref, tm_ref, bm_ref, sems, pad_s, eh_ref, out_sems,
+    near_ref, far_hbm, mix_ref, back_ref, turn_ref, tau_ref, rate_ref,
+    fold_ref, band_ref, rates_ref, leg_ref, tm_ref, bm_ref, sems, pad_s, far_ref, out_sems,
 ):
     copies = start_all(
         (fold_hbm, band_hbm, rates_hbm, tm_hbm, bm_hbm, leg_hbm),
@@ -345,9 +342,10 @@
     groups_f = everyone // fields
     wf = fields * 2
     unit = rows * wf
-    span = eh_ref.shape[1]
+    span = near_ref.shape[1]
     eight = 8 * lats
-    groups = eh_ref.shape[0] // (2 * eight)
+    close = near_ref.shape[0] // (2 * eight)
+    groups = close + far_ref.shape[0] // (2 * eight)
     owner = lax.axis_index("lat") * groups_f + lax.axis_index("fld")
 
     pad_s[...] = jnp.zeros(pad_s.shape, F32)
@@ -446,30 +444,35 @@
             near = jnp.where(first, rowset, 0.0)
             far = jnp.where(second, rowset, 0.0)
             for pp in range(4):
-                at = 2 * eight * t + r * eight + 2 * pp * lats
-                eh_ref[at:at + 2 * lats, :] = jnp.concatenate(
+                at = 2 * eight * (t if t < close else t - close) + r * eight + 2 * pp * lats
+                hold = near_ref if t < close else far_ref
+                hold[at:at + 2 * lats, :] = jnp.concatenate(
                     [near[pp * lats:(pp + 1) * lats], far[pp * lats:(pp + 1) * lats]], axis=0
                 ).astype(BF16)
-        part = pl.ds(2 * eight * t, 2 * eight)
-        keeps.append(pltpu.make_async_copy(eh_ref.at[part], eh_hbm.at[part], out_sems.at[t]))
-        keeps[-1].start()
+        if t >= close:
+            part = pl.ds(2 * eight * (t - close), 2 * eight)
+            keeps.append(
+                pltpu.make_async_copy(far_ref.at[part], far_hbm.at[part], out_sems.at[t - close])
+            )
+            keeps[-1].start()
     wait_all(keeps)
 
 
 def solve_kernel(
-    fields, rows, lats, eh_hbm, msg_ref, mix_ref, turn_ref, tau_ref, rate_ref,
-    near_ref, far_hbm, out_ref, cs, eh_ref, far_ref, in_sems, out_sems,
+    fields, rows, lats, legs_hbm, legs_ref, msg_ref, mix_ref, turn_ref, tau_ref, rate_ref,
+    near_ref, far_hbm, out_ref, cs, eh_ref, far_ref, in_sem, out_sems,
 ):
     eight = 8 * lats
-    groups = eh_ref.shape[0] // (2 * eight)
-    parts = [pl.ds(0, 2 * eight), pl.ds(2 * eight, 2 * eight * (groups - 1))]
-    later = start_all(
-        [eh_hbm.at[part] for part in parts], [eh_ref.at[part] for part in parts], in_sems
-    )
+    close = legs_ref.shape[0] // (2 * eight)
+    groups = close + eh_ref.shape[0] // (2 * eight)
+    fetch = pltpu.make_async_copy(legs_hbm, eh_ref, in_sem)
+    fetch.start()
+    quads = [legs_ref.at[pl.ds(2 * eight * t, 2 * eight)] for t in range(close)]
+    quads += [eh_ref.at[pl.ds(2 * eight * t, 2 * eight)] for t in range(groups - close)]
     groups_f = msg_ref.shape[0] // eight
     wf = fields * 2
     unit = rows * wf
-    span = eh_ref.shape[1]
+    span = legs_ref.shape[1]
     deep = 8 * KPAD
     near = near_ref.shape[0] // deep
     holds = [(near_ref, deep * t) for t in range(near)]
@@ -504,12 +507,11 @@
     keeps = []
     for t in range(groups):
         left = lefts[t]
-        legs = pl.ds(2 * eight * t, 2 * eight)
-        if t < 2:
-            later[t].wait()
+        if t == close:
+            fetch.wait()
         for start in range(0, span, 2 * LANES):
             size = min(2 * LANES, span - start)
-            right = eh_ref[legs, start:start + size]
+            right = quads[t][:, start:start + size]
             modes = dot(left, jnp.concatenate([right, right], axis=0))
             damped = []
             for pp in range(4):
@@ -531,7 +533,7 @@
     picks = []
     for t in range(groups):
         hold, at = holds[t]
-        product = dot_nt(hold[at:at + deep, :], eh_ref[pl.ds(2 * eight * t, 2 * eight), :])
+        product = dot_nt(hold[at:at + deep, :], quads[t][...])
         pick = product[0:2 * KPAD]
         for pp in range(1, 4):
             pick = jnp.where(slot_pair == pp, product[2 * KPAD * pp:2 * KPAD * (pp + 1)], pick)
@@ -648,7 +650,7 @@
             dma((4,)),
             pltpu.VMEM((LANES, LANES), F32),
             pltpu.VMEM((8, slots), F32),
-            pltpu.VMEM((TWICE, 4 * DEEP * pieces), F32),
+            pltpu.VMEM((16, 4 * DEEP * pieces), F32),
             pltpu.VMEM((4 * TWICE, slots), BF16),
         ],
         compiler_params=room,
@@ -660,10 +662,12 @@
     ]
     arrived = lax.all_to_all(sending, ("lat", "fld"), split_axis=0, concat_axis=0, tiled=True)
 
-    legs, mix, back, turn_back, tau, rate = pl.pallas_call(
+    close = 1
+    legs, legs_far, mix, back, turn_back, tau, rate = pl.pallas_call(
         functools.partial(prepare_kernel, cut_off, pairs, fields, rows),
         out_shape=(
-            pltpu.HBM((groups * 16 * lats, span), BF16),
+            pltpu.VMEM((close * 16 * lats, span), BF16),
+            pltpu.HBM(((groups - close) * 16 * lats, span), BF16),
             pltpu.VMEM((2 * rows * KPAD, 3 * LANES), BF16),
             pltpu.VMEM((2 * FPAD, 8 * KPAD), BF16),
             pltpu.VMEM((FPAD, 6 * KPAD), BF16),
@@ -671,7 +675,7 @@
             pltpu.VMEM((KPAD, 2 * LANES), F32),
         ),
         in_specs=[hbm] * 6,
-        out_specs=(hbm,) + (vmem,) * 5,
+        out_specs=(vmem, hbm) + (vmem,) * 5,
         scratch_shapes=[
             pltpu.SMEM(fold_map.shape, jnp.int32),
             pltpu.SMEM(band_map.shape, jnp.int32),
@@ -681,17 +685,17 @@
             pltpu.VMEM(back_modes.shape, F32),
             dma((6,)),
             pltpu.VMEM((KPAD, LANES), F32),
-            pltpu.VMEM((groups * 16 * lats, span), BF16),
-            dma((groups,)),
+            pltpu.VMEM(((groups - close) * 16 * lats, span), BF16),
+            dma((groups - close,)),
         ],
         compiler_params=room,
         cost_estimate=pl.CostEstimate(flops=10**8, bytes_accessed=8 * 10**6, transcendentals=0),
         name="prepare",
     )(fold_map, band_map, mode_rates, legendre, to_modes, back_modes)
-    legs = pltpu.with_memory_space_constraint(legs, pltpu.HBM)
-    mix, back, turn_back, tau, rate = (
+    legs_far = pltpu.with_memory_space_constraint(legs_far, pltpu.HBM)
+    legs, mix, back, turn_back, tau, rate = (
         pltpu.with_memory_space_constraint(x, pltpu.VMEM)
-        for x in (mix, back, turn_back, tau, rate)
+        for x in (legs, mix, back, turn_back, tau, rate)
     )
 
     near = groups // 2
@@ -702,18 +706,18 @@
             pltpu.HBM(((groups - near) * 8 * KPAD, span), BF16),
             pltpu.HBM((owners * 8, LANES), F32),
         ),
-        in_specs=[hbm] + [vmem] * 5,
+        in_specs=[hbm] + [vmem] * 6,
         out_specs=(vmem, hbm, vmem),
         scratch_shapes=[
             pltpu.VMEM((groups * 16 * lats, LANES), F32),
-            pltpu.VMEM((groups * 16 * lats, span), BF16),
+            pltpu.VMEM(((groups - close) * 16 * lats, span), BF16),
             pltpu.VMEM(((groups - near) * 8 * KPAD, span), BF16),
-            dma((2,)),
+            dma,
             dma((groups - near,)),
         ],
         compiler_params=room,
         name="solve",
-    )(legs, arrived.reshape(owners * 8, LANES), mix, turn_back, tau, rate)
+    )(legs_far, legs, arrived.reshape(owners * 8, LANES), mix, turn_back, tau, rate)
     leaving = leaving.reshape(owners, 8, LANES)
 
     returned = lax.all_to_all(leaving, ("lat", "fld"), split_axis=0, concat_axis=0, tiled=True)

time: 37.8 us -> 37.6 us (level)
  no operation moved by 1% of the time
where the time goes in v13:
time: 37.6 us; the launch traced here: 37.2 us
  Pallas kernels  17.1 us (45%)
  starting transfers between devices  9.87 us (26%)
  waiting for transfers between devices  9.56 us (25%)
  between operations  0.68 us (2%)
    all_to_all x1, starting transfers between devices, per_device(): lax.all_to_all(sending, ('lat', 'fld'), split_axis=0, concat_axis=0, tile...  7.29 us
    all_to_all x1, waiting for transfers between devices, per_device(): lax.all_to_all(sending, ('lat', 'fld'), split_axis=0, concat_axis=0, tile...  5.44 us
    pallas_call x1, Pallas kernels, per_device(): pl.pallas_call(functools.partial(solve_kernel, fields, rows, lats), out_s...  4.12 us
    all_to_all x1, waiting for transfers between devices, per_device(): lax.all_to_all(leaving, ('lat', 'fld'), split_axis=0, concat_axis=0, tile...  4.12 us
    pallas_call x1, Pallas kernels, per_device(): pl.pallas_call(output_kernel, grid=(groups,), out_shape=jax.ShapeDtypeStr...  4.1 us
    pallas_call x1, Pallas kernels, per_device(): pl.pallas_call(functools.partial(forward_kernel, cut_off, groups), out_sh...  3.64 us
    pallas_call x1, Pallas kernels, per_device(): pl.pallas_call(functools.partial(prepare_kernel, cut_off, pairs, fields,...  2.78 us
    all_to_all x1, starting transfers between devices, per_device(): lax.all_to_all(leaving, ('lat', 'fld'), split_axis=0, concat_axis=0, tile...  2.58 us
  transfers between devices with their start and end apart: 2, of which 2 were waited for; matrix products, arithmetic and copies ran while one was open for 0% of the time, Pallas kernels for 19%

profile of v13, /device:TPU:0, one launch (start us, length us, event | category | flops | bytes accessed | tf_op | source)
XLA Modules:
  0.0 37.2 jit_solution(15443399083303876209)
XLA Ops:
  0.6 3.6 %forward_rows.1 = (f32[32,8,128]{2,1,0:T(8,128)}, bf16[256,1280]{1,0:T(8,128)(2,1)S(1)}, bf16[256,1280]{1,0:T(8,128)(2,1)S(1)}, f32[24,1280]{1,0:T(8,128)S(1)}, f32[24,1280]{1,0:T(8,128)S(1)}) custom-call(s32[8]{0:T(128)} %len_hbm.3, s32[8]{0:T(128)} %band_hbm.5, s32[32,40]{1,0:T(8,128)} %fold_hbm.3, bf16[5,1,2,5248]{3,2,1,0:T(2,128)(2,1)} %grid_hbm.1), custom_call_target="tpu_custom_call" | custom-call | tf_op jit(solution)/shard_map/forward_rows/pallas_call | solution.py:634
  4.3 7.3 %all-to-all-start = ((f32[32,8,128]{2,1,0:T(8,128)}), f32[32,8,128]{2,1,0:T(8,128)S(1)}, u32[]{:S(2)}, u32[]{:S(2)}) async-start(f32[32,8,128]{2,1,0:T(8,128)} %get-tuple-element.19), calls=%async_computation | async-start | bytes 262144 | tf_op jit(solution)/shard_map/all_to_all | solution.py:663
  11.6 2.8 %prepare.1 = (bf16[128,1408]{1,0:T(8,128)(2,1)S(1)}, bf16[512,1408]{1,0:T(8,128)(2,1)}, bf16[96,384]{1,0:T(8,128)(2,1)S(1)}, bf16[128,192]{1,0:T(8,128)(2,1)S(1)...) custom-call(s32[32,40]{1,0:T(8,128)} %fold_hbm.3, s32[8]{0:T(128)} %band_hbm.5, ...), custom_call_target="tpu_custom_call" | custom-call | flops 100000000 | bytes 8000000 | tf_op jit(solution)/shard_map/prepare/pallas_call | solution.py:666
  14.4 5.4 %all-to-all-done = f32[32,8,128]{2,1,0:T(8,128)S(1)} async-done(((f32[32,8,128]{2,1,0:T(8,128)}), f32[32,8,128]{2,1,0:T(8,128)S(1)}, u32[]{:S(2)}, u32[]{:S(2)}) %all-to-all-start) | async-done | bytes 131104 | tf_op jit(solution)/shard_map/all_to_all | solution.py:663
  19.8 4.1 %solve.1 = (bf16[384,1408]{1,0:T(8,128)(2,1)S(1)}, bf16[576,1408]{1,0:T(8,128)(2,1)}, f32[256,128]{1,0:T(8,128)}) custom-call(bf16[512,1408]{1,0:T(8,128)(2,1)} %get-tuple-element.17.legs_hbm, bf16[128,1408]{1,0:T(8,128)(2,1)S(1)} %get-tuple-element.18.legs_ref, f32[256,128]{1,0:T(8,128)S(1)} %bitcast.4, bf16[96,384]{1,0:T(8,128)(2,1)S(1)} %get-tuple-element.20.mix_ref, ...), custom_call_target="tpu_custom_call" | custom-call | tf_op jit(solution)/shard_map/solve/pallas_call | solution.py:702
  23.9 2.6 %all-to-all-start.1 = ((f32[32,8,128]{2,1,0:T(8,128)}), f32[32,8,128]{2,1,0:T(8,128)S(1)}, u32[]{:S(2)}, u32[]{:S(2)}) async-start(f32[32,8,128]{2,1,0:T(8,128)} %bitcast.7), calls=%async_computation.1 | async-start | bytes 262144 | tf_op jit(solution)/shard_map/all_to_all | solution.py:723
  26.5 4.1 %spectral_output.1 = f32[20,20,2,1281]{3,2,1,0:T(2,128)} custom-call(bf16[384,1408]{1,0:T(8,128)(2,1)S(1)} %get-tuple-element.24.near_ref, bf16[576,1408]{1,0:T(8,128)(2,1)} %get-tuple-element.25.far_hbm, bf16[128,192]{1,0:T(8,128)(2,1)S(1)} %get-tuple-element.26.back_ref), custom_call_target="tpu_custom_call" | custom-call | flops 100000000 | bytes 8000000 | tf_op jit(solution)/shard_map/spectral_output/pallas_call | solution.py:727
  30.6 4.1 %all-to-all-done.1.msg_ref = f32[32,8,128]{2,1,0:T(8,128)S(1)} async-done(((f32[32,8,128]{2,1,0:T(8,128)}), f32[32,8,128]{2,1,0:T(8,128)S(1)}, u32[]{:S(2)}, u32[]{:S(2)}) %all-to-all-start.1) | async-done | bytes 131104 | tf_op jit(solution)/shard_map/all_to_all | solution.py:723
  34.7 2.5 %inverse_rows.1 = bf16[5,1,2,5248]{3,2,1,0:T(2,128)(2,1)} custom-call(s32[8]{0:T(128)} %len_hbm.3, s32[8]{0:T(128)} %band_hbm.5, bf16[256,1280]{1,0:T(8,128)(2,1)S(1)} %get-tuple-element.27.tc, bf16[256,1280]{1,0:T(8,128)(2,1)S(1)} %get-tuple-element.28.ts, f32[24,1280]{1,0:T(8,128)S(1)} %get-tuple-element.29.fc, f32[24,1280]{1,0:T(8,128)S(1)} %get-tuple-element.30.fs, ...), custom_call_target="tpu_custom_call" | custom-call | tf_op jit(solution)/shard_map/inverse_rows/pallas_call | solution.py:749
Async XLA Ops:
  4.3 15.5 %all-to-all-start = ((f32[32,8,128]{2,1,0:T(8,128)}), f32[32,8,128]{2,1,0:T(8,128)S(1)}, u32[]{:S(2)}, u32[]{:S(2)}) async-start(f32[32,8,128]{2,1,0:T(8,128)} %get-tuple-element.19), calls=%async_computation | async-start | bytes 262144 | tf_op jit(solution)/shard_map/all_to_all | solution.py:663
  23.9 10.8 %all-to-all-start.1 = ((f32[32,8,128]{2,1,0:T(8,128)}), f32[32,8,128]{2,1,0:T(8,128)S(1)}, u32[]{:S(2)}, u32[]{:S(2)}) async-start(f32[32,8,128]{2,1,0:T(8,128)} %bitcast.7), calls=%async_computation.1 | async-start | bytes 262144 | tf_op jit(solution)/shard_map/all_to_all | solution.py:723

commit v14 on v13

--- a/solution.py
+++ b/solution.py
@@ -212,14 +212,15 @@
     steps = phase_steps(turns, block)
     period = jnp.full((1, block), length, jnp.int32).astype(F32)
     inverse = 1.0 / period
-    for i in range(slots // block):
+    def make_tables(i):
         at = pl.ds(i * block, block)
         wave = wave_s[:, at]
         wave = jnp.concatenate([wave] * ((turns + 16) // 8), axis=0)
         co, si = turn(steps * wave, period, inverse)
         one = wave[0:1]
         weight = jnp.where(one == 0.0, 1.0, 2.0)
-        weight = jnp.where((one >= 0.0) & (one <= jnp.full(one.shape, top, jnp.int32).astype(F32)), weight, 0.0)
+        limit = jnp.full(one.shape, top, jnp.int32).astype(F32)
+        weight = jnp.where((one >= 0.0) & (one <= limit), weight, 0.0)
         fc[:, at] = co[0:turns] * weight
         fs[:, at] = si[0:turns] * weight
         c_all = co[turns:turns + 8]
@@ -237,8 +238,10 @@
         s_all = s_all.astype(BF16)
         tc[:, at] = c_all
         ts[:, at] = s_all
-        inner_c = dot(values, c_all)
-        inner_s = dot(values, s_all)
+        return c_all, s_all
+
+    def finish(i, inner_c, inner_s):
+        at = pl.ds(i * block, block)
         real = jnp.zeros((TWICE, block), F32)
         imag = jnp.zeros((TWICE, block), F32)
         for g in range(turns // 2):
@@ -248,8 +251,18 @@
             part_s = inner_s[TWICE * g:TWICE * (g + 1)]
             real = real + (c1 * part_c - s1 * part_s)
             imag = imag - (c1 * part_s + s1 * part_c)
-        both = jnp.concatenate([real, imag], axis=0) * jnp.where(one == 0.0, 1.0, 0.5)
+        fix = jnp.where(wave_s[0:1, at] == 0.0, 1.0, 0.5)
+        both = jnp.concatenate([real, imag], axis=0) * fix
         xt[:, at] = jnp.concatenate(split(both), axis=0)
+
+    blocks = slots // block
+    ready = make_tables(0)
+    for i in range(blocks):
+        inner_c = dot(values, ready[0])
+        inner_s = dot(values, ready[1])
+        if i + 1 < blocks:
+            ready = make_tables(i + 1)
+        finish(i, inner_c, inner_s)
 
     turned = jnp.concatenate(
         [xt[:, owners * 8 * t:owners * 8 * (t + 1)] for t in range(groups)], axis=0
@@ -286,7 +299,7 @@
     turned = dot_nt(place, pieces)
     block = 2 * LANES
     out = jnp.zeros((TWICE * turns // 2, DEEP), F32)
-    for i in range(slots // block):
+    def twisted(i):
         t, off = divmod(i * block, owners * 8)
         real = turned[tall * t:tall * t + TWICE, off:off + block]
         imag = turned[tall * t + TWICE:tall * (t + 1), off:off + block]
@@ -297,9 +310,20 @@
             s1 = two_phases(fs, g, at, used, block)
             reals.append(c1 * real - s1 * imag)
             imags.append(s1 * real + c1 * imag)
-        reals = jnp.concatenate(reals, axis=0).astype(BF16)
-        imags = jnp.concatenate(imags, axis=0).astype(BF16)
-        out = out + (dot_nt(reals, tc[:, at]) - dot_nt(imags, ts[:, at]))
+        return (
+            jnp.concatenate(reals, axis=0).astype(BF16),
+            jnp.concatenate(imags, axis=0).astype(BF16),
+        )
+
+    blocks = slots // block
+    ready = twisted(0)
+    for i in range(blocks):
+        at = pl.ds(i * block, block)
+        part_r = dot_nt(ready[0], tc[:, at])
+        part_i = dot_nt(ready[1], ts[:, at])
+        if i + 1 < blocks:
+            ready = twisted(i + 1)
+        out = out + (part_r - part_i)
     wait_all(copies)
     length = len_ref[band_ref[lax.axis_index("lat")]]
     out = out * (1.0 / jnp.sqrt(jnp.full(out.shape, length, jnp.int32).astype(F32)))
@@ -505,39 +529,53 @@
         lefts.append(jnp.concatenate(split(left), axis=1))
 
     keeps = []
+
+    def damp(t, start, modes):
+        size = modes.shape[1]
+        damped = []
+        for pp in range(4):
+            tau = tau_ref[4 * t + pp:4 * t + pp + 1, start:start + size]
+            factor = pl.reciprocal(1.0 + tau * rate[:, 0:size], approx=True)
+            at = 2 * pp * KPAD
+            damped.append(modes[at:at + KPAD] * factor)
+            damped.append(modes[at + KPAD:at + 2 * KPAD] * factor)
+        hold, at = holds[t]
+        hold[at:at + deep, start:start + size] = jnp.concatenate(damped, axis=0).astype(BF16)
+        if t >= near and start + size == span:
+            part = pl.ds(deep * (t - near), deep)
+            keeps.append(
+                pltpu.make_async_copy(far_ref.at[part], far_hbm.at[part], out_sems.at[t - near])
+            )
+            keeps[-1].start()
+
+    waiting = None
     for t in range(groups):
-        left = lefts[t]
         if t == close:
             fetch.wait()
         for start in range(0, span, 2 * LANES):
             size = min(2 * LANES, span - start)
             right = quads[t][:, start:start + size]
-            modes = dot(left, jnp.concatenate([right, right], axis=0))
-            damped = []
-            for pp in range(4):
-                tau = tau_ref[4 * t + pp:4 * t + pp + 1, start:start + size]
-                below = 1.0 + tau * rate[:, 0:size]
-                factor = pl.reciprocal(below, approx=True)
-                at = 2 * pp * KPAD
-                damped.append(modes[at:at + KPAD] * factor)
-                damped.append(modes[at + KPAD:at + 2 * KPAD] * factor)
-            hold, at = holds[t]
-            hold[at:at + deep, start:start + size] = jnp.concatenate(damped, axis=0).astype(BF16)
-        if t >= near:
-            part = pl.ds(deep * (t - near), deep)
-            keeps.append(
-                pltpu.make_async_copy(far_ref.at[part], far_hbm.at[part], out_sems.at[t - near])
-            )
-            keeps[-1].start()
+            modes = dot(lefts[t], jnp.concatenate([right, right], axis=0))
+            if waiting is not None:
+                damp(*waiting)
+            waiting = (t, start, modes)
+    damp(*waiting)
+
+    def choose(product):
+        pick = product[0:2 * KPAD]
+        for pp in range(1, 4):
+            pick = jnp.where(slot_pair == pp, product[2 * KPAD * pp:2 * KPAD * (pp + 1)], pick)
+        return pick
 
     picks = []
+    waiting = None
     for t in range(groups):
         hold, at = holds[t]
         product = dot_nt(hold[at:at + deep, :], quads[t][...])
-        pick = product[0:2 * KPAD]
-        for pp in range(1, 4):
-            pick = jnp.where(slot_pair == pp, product[2 * KPAD * pp:2 * KPAD * (pp + 1)], pick)
-        picks.append(pick)
+        if waiting is not None:
+            picks.append(choose(waiting))
+        waiting = product
+    picks.append(choose(waiting))
     high, low = split(jnp.concatenate(picks, axis=1))
     back = dot(turn_ref[...], jnp.concatenate([high, low, high], axis=0))
     back = jnp.concatenate([back, jnp.zeros((LANES - FPAD, back.shape[1]), F32)], axis=0)

time: 37.6 us -> 37.6 us (level)
  no operation moved by 1% of the time
where the time goes in v14:
time: 37.6 us; the launch traced here: 37.2 us
  Pallas kernels  17.1 us (45%)
  starting transfers between devices  9.89 us (26%)
  waiting for transfers between devices  9.55 us (25%)
  between operations  0.68 us (2%)
    all_to_all x1, starting transfers between devices, per_device(): lax.all_to_all(sending, ('lat', 'fld'), split_axis=0, concat_axis=0, tile...  7.31 us
    all_to_all x1, waiting for transfers between devices, per_device(): lax.all_to_all(sending, ('lat', 'fld'), split_axis=0, concat_axis=0, tile...  5.44 us
    pallas_call x1, Pallas kernels, per_device(): pl.pallas_call(functools.partial(solve_kernel, fields, rows, lats), out_s...  4.12 us
    pallas_call x1, Pallas kernels, per_device(): pl.pallas_call(output_kernel, grid=(groups,), out_shape=jax.ShapeDtypeStr...  4.11 us
    all_to_all x1, waiting for transfers between devices, per_device(): lax.all_to_all(leaving, ('lat', 'fld'), split_axis=0, concat_axis=0, tile...  4.11 us
    pallas_call x1, Pallas kernels, per_device(): pl.pallas_call(functools.partial(forward_kernel, cut_off, groups), out_sh...  3.61 us
    pallas_call x1, Pallas kernels, per_device(): pl.pallas_call(functools.partial(prepare_kernel, cut_off, pairs, fields,...  2.78 us
    all_to_all x1, starting transfers between devices, per_device(): lax.all_to_all(leaving, ('lat', 'fld'), split_axis=0, concat_axis=0, tile...  2.58 us
  transfers between devices with their start and end apart: 2, of which 2 were waited for; matrix products, arithmetic and copies ran while one was open for 0% of the time, Pallas kernels for 19%

profile of v14, /device:TPU:0, one launch (start us, length us, event | category | flops | bytes accessed | tf_op | source)
XLA Modules:
  0.0 37.2 jit_solution(16104323707739689282)
XLA Ops:
  0.6 3.6 %forward_rows.1 = (f32[32,8,128]{2,1,0:T(8,128)}, bf16[256,1280]{1,0:T(8,128)(2,1)S(1)}, bf16[256,1280]{1,0:T(8,128)(2,1)S(1)}, f32[24,1280]{1,0:T(8,128)S(1)}, f32[24,1280]{1,0:T(8,128)S(1)}) custom-call(s32[8]{0:T(128)} %len_hbm.3, s32[8]{0:T(128)} %band_hbm.5, s32[32,40]{1,0:T(8,128)} %fold_hbm.3, bf16[5,1,2,5248]{3,2,1,0:T(2,128)(2,1)} %grid_hbm.1), custom_call_target="tpu_custom_call" | custom-call | tf_op jit(solution)/shard_map/forward_rows/pallas_call | solution.py:672
  4.2 7.3 %all-to-all-start = ((f32[32,8,128]{2,1,0:T(8,128)}), f32[32,8,128]{2,1,0:T(8,128)S(1)}, u32[]{:S(2)}, u32[]{:S(2)}) async-start(f32[32,8,128]{2,1,0:T(8,128)} %get-tuple-element.19), calls=%async_computation | async-start | bytes 262144 | tf_op jit(solution)/shard_map/all_to_all | solution.py:701
  11.6 2.8 %prepare.1 = (bf16[128,1408]{1,0:T(8,128)(2,1)S(1)}, bf16[512,1408]{1,0:T(8,128)(2,1)}, bf16[96,384]{1,0:T(8,128)(2,1)S(1)}, bf16[128,192]{1,0:T(8,128)(2,1)S(1)...) custom-call(s32[32,40]{1,0:T(8,128)} %fold_hbm.3, s32[8]{0:T(128)} %band_hbm.5, ...), custom_call_target="tpu_custom_call" | custom-call | flops 100000000 | bytes 8000000 | tf_op jit(solution)/shard_map/prepare/pallas_call | solution.py:704
  14.4 5.4 %all-to-all-done = f32[32,8,128]{2,1,0:T(8,128)S(1)} async-done(((f32[32,8,128]{2,1,0:T(8,128)}), f32[32,8,128]{2,1,0:T(8,128)S(1)}, u32[]{:S(2)}, u32[]{:S(2)}) %all-to-all-start) | async-done | bytes 131104 | tf_op jit(solution)/shard_map/all_to_all | solution.py:701
  19.8 4.1 %solve.1 = (bf16[384,1408]{1,0:T(8,128)(2,1)S(1)}, bf16[576,1408]{1,0:T(8,128)(2,1)}, f32[256,128]{1,0:T(8,128)}) custom-call(bf16[512,1408]{1,0:T(8,128)(2,1)} %get-tuple-element.17.legs_hbm, bf16[128,1408]{1,0:T(8,128)(2,1)S(1)} %get-tuple-element.18.legs_ref, f32[256,128]{1,0:T(8,128)S(1)} %bitcast.4, bf16[96,384]{1,0:T(8,128)(2,1)S(1)} %get-tuple-element.20.mix_ref, ...), custom_call_target="tpu_custom_call" | custom-call | tf_op jit(solution)/shard_map/solve/pallas_call | solution.py:740
  23.9 2.6 %all-to-all-start.1 = ((f32[32,8,128]{2,1,0:T(8,128)}), f32[32,8,128]{2,1,0:T(8,128)S(1)}, u32[]{:S(2)}, u32[]{:S(2)}) async-start(f32[32,8,128]{2,1,0:T(8,128)} %bitcast.7), calls=%async_computation.1 | async-start | bytes 262144 | tf_op jit(solution)/shard_map/all_to_all | solution.py:761
  26.5 4.1 %spectral_output.1 = f32[20,20,2,1281]{3,2,1,0:T(2,128)} custom-call(bf16[384,1408]{1,0:T(8,128)(2,1)S(1)} %get-tuple-element.24.near_ref, bf16[576,1408]{1,0:T(8,128)(2,1)} %get-tuple-element.25.far_hbm, bf16[128,192]{1,0:T(8,128)(2,1)S(1)} %get-tuple-element.26.back_ref), custom_call_target="tpu_custom_call" | custom-call | flops 100000000 | bytes 8000000 | tf_op jit(solution)/shard_map/spectral_output/pallas_call | solution.py:765
  30.6 4.1 %all-to-all-done.1.msg_ref = f32[32,8,128]{2,1,0:T(8,128)S(1)} async-done(((f32[32,8,128]{2,1,0:T(8,128)}), f32[32,8,128]{2,1,0:T(8,128)S(1)}, u32[]{:S(2)}, u32[]{:S(2)}) %all-to-all-start.1) | async-done | bytes 131104 | tf_op jit(solution)/shard_map/all_to_all | solution.py:761
  34.7 2.5 %inverse_rows.1 = bf16[5,1,2,5248]{3,2,1,0:T(2,128)(2,1)} custom-call(s32[8]{0:T(128)} %len_hbm.3, s32[8]{0:T(128)} %band_hbm.5, bf16[256,1280]{1,0:T(8,128)(2,1)S(1)} %get-tuple-element.27.tc, bf16[256,1280]{1,0:T(8,128)(2,1)S(1)} %get-tuple-element.28.ts, f32[24,1280]{1,0:T(8,128)S(1)} %get-tuple-element.29.fc, f32[24,1280]{1,0:T(8,128)S(1)} %get-tuple-element.30.fs, ...), custom_call_target="tpu_custom_call" | custom-call | tf_op jit(solution)/shard_map/inverse_rows/pallas_call | solution.py:787
Async XLA Ops:
  4.2 15.5 %all-to-all-start = ((f32[32,8,128]{2,1,0:T(8,128)}), f32[32,8,128]{2,1,0:T(8,128)S(1)}, u32[]{:S(2)}, u32[]{:S(2)}) async-start(f32[32,8,128]{2,1,0:T(8,128)} %get-tuple-element.19), calls=%async_computation | async-start | bytes 262144 | tf_op jit(solution)/shard_map/all_to_all | solution.py:701
  23.9 10.8 %all-to-all-start.1 = ((f32[32,8,128]{2,1,0:T(8,128)}), f32[32,8,128]{2,1,0:T(8,128)S(1)}, u32[]{:S(2)}, u32[]{:S(2)}) async-start(f32[32,8,128]{2,1,0:T(8,128)} %bitcast.7), calls=%async_computation.1 | async-start | bytes 262144 | tf_op jit(solution)/shard_map/all_to_all | solution.py:761

commit v15 on v14

--- a/solution.py
+++ b/solution.py
@@ -352,8 +352,8 @@
 
 def prepare_kernel(
     cut_off, pairs, fields, rows, fold_hbm, band_hbm, rates_hbm, leg_hbm, tm_hbm, bm_hbm,
-    near_ref, far_hbm, mix_ref, back_ref, turn_ref, tau_ref, rate_ref,
-    fold_ref, band_ref, rates_ref, leg_ref, tm_ref, bm_ref, sems, pad_s, far_ref, out_sems,
+    eh_hbm, round_ref, mix_ref, back_ref, turn_ref, tau_ref, rate_ref,
+    fold_ref, band_ref, rates_ref, leg_ref, tm_ref, bm_ref, sems, pad_s, eh_ref, out_sems,
 ):
     copies = start_all(
         (fold_hbm, band_hbm, rates_hbm, tm_hbm, bm_hbm, leg_hbm),
@@ -366,10 +366,9 @@
     groups_f = everyone // fields
     wf = fields * 2
     unit = rows * wf
-    span = near_ref.shape[1]
+    span = eh_ref.shape[1]
     eight = 8 * lats
-    close = near_ref.shape[0] // (2 * eight)
-    groups = close + far_ref.shape[0] // (2 * eight)
+    groups = eh_ref.shape[0] // (2 * eight)
     owner = lax.axis_index("lat") * groups_f + lax.axis_index("fld")
 
     pad_s[...] = jnp.zeros(pad_s.shape, F32)
@@ -382,10 +381,12 @@
     for piece in split(pad_s[...]):
         wide = dot(piece, pick)
         total = []
-        for r in range(rows):
+        for parity in range(2):
             for c in range(2):
-                keep = ((lane % unit) // wf == r) & (lane % 2 == c) & (lane < unit * groups_f)
-                total.append(jnp.where(keep, wide, 0.0))
+                keep = (lane % 2 == c) & (lane < unit * groups_f)
+                flip = (lane % unit) // wf >= 1 if parity else lane < 0
+                total.append(jnp.where(keep, jnp.where(flip, -wide, wide), 0.0))
+        total.append(jnp.zeros((LANES - 4 * KPAD, LANES), F32))
         parts.append(jnp.concatenate(total, axis=0).astype(BF16))
     mix_ref[...] = jnp.concatenate([parts[0], parts[1], parts[0]], axis=1)
 
@@ -397,26 +398,38 @@
     repeat = jnp.where(row_iota(shape) == lane_iota(shape) % KPAD, 1.0, 0.0).astype(BF16)
     shape = (FPAD, 2 * LANES)
     same = row_iota(shape) % 2 == (lane_iota(shape) // KPAD) % 2
-    fulls = []
     for part, piece in enumerate(split(pad_s[...])):
         full = jnp.where(same, dot(dot(expand, piece).astype(BF16), repeat), 0.0)
         back_ref[part * FPAD:(part + 1) * FPAD, :] = full[:, 0:8 * KPAD].astype(BF16)
-        fulls.append(full)
-    turn = jnp.where(lane_iota(shape) < 4 * KPAD, fulls[0], fulls[1])
-    turn_ref[...] = turn[:, 0:6 * KPAD].astype(BF16)
+    shape = (LANES, LANES)
+    row, lane = row_iota(shape), lane_iota(shape)
+    width = 2 * everyone
+    south = lane >= width
+    level = jnp.where(south, lane - width, lane)
+    pick = jnp.where(row == (level >> 1), 1.0, 0.0).astype(BF16)
+    part = lax.div(row, KPAD)
+    keep = ((part & 1) == (level & 1)) & (part < 4) & (lane < 2 * width)
+    flip = south & (part >= 2)
+    wide = []
+    for piece in split(jnp.transpose(jnp.concatenate([pad_s[...], jnp.zeros((LANES - KPAD, LANES), F32)], axis=0))):
+        small = dot(piece, pick)[0:KPAD]
+        tall = jnp.concatenate([small] * 5 + [jnp.zeros((LANES - 5 * KPAD, LANES), F32)], axis=0)
+        wide.append(jnp.where(keep, jnp.where(flip, -tall, tall), 0.0).astype(BF16))
+    turn_ref[...] = jnp.concatenate([wide[0], wide[0], wide[1]], axis=0)
 
     row = row_iota((KPAD, 2 * LANES))
     rate = jnp.zeros((KPAD, 2 * LANES), F32)
     for k in range(everyone):
         rate = jnp.where(row == k, rates_ref[k], rate)
     rate_ref[...] = rate
+    wide_rate = jnp.concatenate([rate[:, 0:LANES]] * (span // LANES), axis=1)
     paired = tau_ref.shape[0]
     row = row_iota((paired, LANES))
     waves = []
     wave = jnp.zeros((paired, LANES), jnp.int32)
     for pair in range(4 * groups):
         waves.append(fold_ref[owner, 2 * min(pair, pairs - 1)])
-        wave = jnp.where(row == pair, waves[pair], wave)
+        wave = jnp.where(row == 8 * (pair // 4) + pair % 4, waves[pair], wave)
     wave = jnp.concatenate([wave] * (span // LANES), axis=1)
     line = lane_iota((paired, span))
     degree = jnp.where(line > cut_off - wave, line - 1, line + wave)
@@ -463,44 +476,49 @@
         first = before & (line <= last)
         second = jnp.logical_not(before) & (line <= last)
         odd = ((line + jnp.where(before, 0, wave)) & 1) == 1
-        signed = jnp.where(odd, -leg, leg)
-        for r, rowset in enumerate((leg, signed)):
-            near = jnp.where(first, rowset, 0.0)
-            far = jnp.where(second, rowset, 0.0)
+        masks = [
+            [jnp.where(side & odd, 1.0, 0.0) if par else jnp.where(odd, 0.0, jnp.where(side, 1.0, 0.0)) for par in range(2)]
+            for side in (first, second)
+        ]
+        for par in range(2):
+            near = leg * masks[0][par]
+            far = leg * masks[1][par]
             for pp in range(4):
-                at = 2 * eight * (t if t < close else t - close) + r * eight + 2 * pp * lats
-                hold = near_ref if t < close else far_ref
-                hold[at:at + 2 * lats, :] = jnp.concatenate(
+                at = 2 * eight * t + par * eight + 2 * pp * lats
+                eh_ref[at:at + 2 * lats, :] = jnp.concatenate(
                     [near[pp * lats:(pp + 1) * lats], far[pp * lats:(pp + 1) * lats]], axis=0
                 ).astype(BF16)
-        if t >= close:
-            part = pl.ds(2 * eight * (t - close), 2 * eight)
-            keeps.append(
-                pltpu.make_async_copy(far_ref.at[part], far_hbm.at[part], out_sems.at[t - close])
-            )
-            keeps[-1].start()
+        part = pl.ds(2 * eight * t, 2 * eight)
+        keeps.append(pltpu.make_async_copy(eh_ref.at[part], eh_hbm.at[part], out_sems.at[t]))
+        keeps[-1].start()
+
+        for pp in range(4):
+            own = leg[pp * lats:(pp + 1) * lats]
+            pairs_of = jnp.concatenate([own * own[j:j + 1] for j in range(lats)], axis=0)
+            pair = 4 * t + pp
+            factor = pl.reciprocal(1.0 + tau_ref[8 * t + pp:8 * t + pp + 1, :] * wide_rate, approx=True)
+            damp = []
+            for side in range(2):
+                for par in range(2):
+                    mask = masks[side][par][pp * lats:pp * lats + 8]
+                    part = (factor * jnp.concatenate([mask] * (KPAD // 8), axis=0)).astype(BF16)
+                    damp += [part, part]
+                damp.append(jnp.zeros((LANES - 4 * KPAD, span), BF16))
+            both = dot_nt(pairs_of.astype(BF16), jnp.concatenate([jnp.concatenate(damp[0:2], axis=0), jnp.concatenate(damp[2:4], axis=0), damp[4], jnp.concatenate(damp[5:7], axis=0), jnp.concatenate(damp[7:9], axis=0), damp[9]], axis=0))
+            for side in range(2):
+                at = (2 * pair + side) * lats * lats
+                round_ref[at:at + lats * lats, :] = both[:, LANES * side:LANES * (side + 1)]
     wait_all(keeps)
 
 
 def solve_kernel(
-    fields, rows, lats, legs_hbm, legs_ref, msg_ref, mix_ref, turn_ref, tau_ref, rate_ref,
-    near_ref, far_hbm, out_ref, cs, eh_ref, far_ref, in_sem, out_sems,
+    fields, rows, lats, msg_ref, round_ref, mix_ref, turn_ref, mixed_ref, out_ref, cs,
 ):
     eight = 8 * lats
-    close = legs_ref.shape[0] // (2 * eight)
-    groups = close + eh_ref.shape[0] // (2 * eight)
-    fetch = pltpu.make_async_copy(legs_hbm, eh_ref, in_sem)
-    fetch.start()
-    quads = [legs_ref.at[pl.ds(2 * eight * t, 2 * eight)] for t in range(close)]
-    quads += [eh_ref.at[pl.ds(2 * eight * t, 2 * eight)] for t in range(groups - close)]
+    groups = mixed_ref.shape[0] // eight
     groups_f = msg_ref.shape[0] // eight
     wf = fields * 2
     unit = rows * wf
-    span = legs_ref.shape[1]
-    deep = 8 * KPAD
-    near = near_ref.shape[0] // deep
-    holds = [(near_ref, deep * t) for t in range(near)]
-    holds += [(far_ref, deep * t) for t in range(groups - near)]
     lane = lane_iota((lats, LANES))
     tiles = [
         [msg_ref[pl.ds(8 * g + i8, lats, stride=8 * groups_f), :] for g in range(groups_f)]
@@ -517,70 +535,18 @@
                 line = pltpu.roll(line, LANES - unit * t, 1)
             tall.append(line)
     v_high, v_low = split(jnp.concatenate(tall, axis=0))
-    mixed = dot_nt(mix_ref[...], jnp.concatenate([v_high, v_high, v_low], axis=1))
-
-    rate = rate_ref[...]
-    slot_pair = (lane_iota((2 * KPAD, 2 * eight)) % eight) // (2 * lats)
-    lefts = []
-    for t in range(groups):
-        mine = mixed[:, eight * t:eight * (t + 1)]
-        mine = jnp.concatenate([mine[0:2 * KPAD], mine[2 * KPAD:4 * KPAD]], axis=1)
-        left = jnp.concatenate([jnp.where(slot_pair == pp, mine, 0.0) for pp in range(4)], axis=0)
-        lefts.append(jnp.concatenate(split(left), axis=1))
-
-    keeps = []
-
-    def damp(t, start, modes):
-        size = modes.shape[1]
-        damped = []
-        for pp in range(4):
-            tau = tau_ref[4 * t + pp:4 * t + pp + 1, start:start + size]
-            factor = pl.reciprocal(1.0 + tau * rate[:, 0:size], approx=True)
-            at = 2 * pp * KPAD
-            damped.append(modes[at:at + KPAD] * factor)
-            damped.append(modes[at + KPAD:at + 2 * KPAD] * factor)
-        hold, at = holds[t]
-        hold[at:at + deep, start:start + size] = jnp.concatenate(damped, axis=0).astype(BF16)
-        if t >= near and start + size == span:
-            part = pl.ds(deep * (t - near), deep)
-            keeps.append(
-                pltpu.make_async_copy(far_ref.at[part], far_hbm.at[part], out_sems.at[t - near])
-            )
-            keeps[-1].start()
-
-    waiting = None
-    for t in range(groups):
-        if t == close:
-            fetch.wait()
-        for start in range(0, span, 2 * LANES):
-            size = min(2 * LANES, span - start)
-            right = quads[t][:, start:start + size]
-            modes = dot(lefts[t], jnp.concatenate([right, right], axis=0))
-            if waiting is not None:
-                damp(*waiting)
-            waiting = (t, start, modes)
-    damp(*waiting)
-
-    def choose(product):
-        pick = product[0:2 * KPAD]
-        for pp in range(1, 4):
-            pick = jnp.where(slot_pair == pp, product[2 * KPAD * pp:2 * KPAD * (pp + 1)], pick)
-        return pick
-
-    picks = []
-    waiting = None
-    for t in range(groups):
-        hold, at = holds[t]
-        product = dot_nt(hold[at:at + deep, :], quads[t][...])
-        if waiting is not None:
-            picks.append(choose(waiting))
-        waiting = product
-    picks.append(choose(waiting))
-    high, low = split(jnp.concatenate(picks, axis=1))
-    back = dot(turn_ref[...], jnp.concatenate([high, low, high], axis=0))
-    back = jnp.concatenate([back, jnp.zeros((LANES - FPAD, back.shape[1]), F32)], axis=0)
-    for at in range(0, back.shape[1], LANES):
-        cs[at:at + LANES, :] = jnp.transpose(back[:, at:at + LANES])
+    mixed_ref[...] = dot_nt(jnp.concatenate([v_high, v_high, v_low], axis=1), mix_ref[...])
+
+    sums = []
+    for slot in range(8 * groups):
+        mine = mixed_ref[slot * lats:(slot + 1) * lats, :]
+        total = jnp.zeros((lats, LANES), F32)
+        for j in range(lats):
+            at = (slot * lats + j) * lats
+            total = total + mine[j:j + 1] * round_ref[at:at + lats, :]
+        sums.append(total)
+    high, low = split(jnp.concatenate(sums, axis=0))
+    cs[...] = dot(jnp.concatenate([high, low, high], axis=1), turn_ref[...])
 
     lane = lane_iota((8, LANES))
     here = [
@@ -588,61 +554,76 @@
     ]
     for holder in range(lats):
         tiles = [jnp.zeros((8, LANES), F32) for _ in range(groups_f)]
-        for u in range(rows * groups):
-            piece = cs[pl.ds(u * eight + holder, 8, stride=lats), :]
-            if u:
-                piece = pltpu.roll(piece, wf * u, 1)
-            for g in range(groups_f):
-                tiles[g] = jnp.where(here[u + g], piece, tiles[g])
+        for t in range(groups):
+            piece = cs[pl.ds(t * eight + holder, 8, stride=lats), :]
+            for r in range(rows):
+                u = rows * t + r
+                moved = pltpu.roll(piece, (wf * u - wf * groups_f * r) % LANES, 1)
+                for g in range(groups_f):
+                    tiles[g] = jnp.where(here[u + g], moved, tiles[g])
         for g in range(groups_f):
             at = (holder * groups_f + g) * 8
             out_ref[at:at + 8, :] = tiles[g]
-    wait_all(keeps)
-
-
-def output_kernel(near_ref, far_hbm, back_ref, spec_ref, bk, far_s, sems):
+
+
+def output_kernel(
+    lats, eh_hbm, mixed_ref, tau_ref, rate_ref, back_ref, spec_ref, bk, eh_s, sems,
+):
     everyone, quad, _, places = spec_ref.shape
-    span = near_ref.shape[1]
-    deep = 8 * KPAD
-    near = near_ref.shape[0] // deep
+    span = eh_s.shape[1]
+    eight = 8 * lats
     tall = 2 * everyone
     step = pl.program_id(0)
 
-    def far_copy(t):
-        part = pl.ds(pl.multiple_of(deep * t, deep), deep)
-        return pltpu.make_async_copy(far_hbm.at[part], far_s.at[part], sems.at[t])
+    def fetch(t):
+        part = pl.ds(pl.multiple_of(2 * eight * t, 16), 2 * eight)
+        return pltpu.make_async_copy(eh_hbm.at[part], eh_s.at[part], sems.at[t])
 
     @pl.when(step == 0)
     def _():
         for t in range(sems.shape[0]):
-            far_copy(t).start()
-        pair_of = lane_iota((tall, deep)) // (2 * KPAD)
-        rows = []
+            fetch(t).start()
+        pair_of = lane_iota((tall, 8 * KPAD)) // (2 * KPAD)
+        parts = []
         for part in range(2):
             full = back_ref[part * FPAD:part * FPAD + tall, :].astype(F32)
             for pp in range(4):
-                rows.append(jnp.where(pair_of == pp, full, 0.0))
-        bk[...] = jnp.concatenate(rows, axis=0).astype(BF16)
-
-    def write(source, at):
-        for start in range(0, span, 2 * LANES):
-            size = min(2 * LANES, span - start)
-            spec = dot(bk[...], source[pl.ds(at, deep), start:start + size])
-            spec = spec[0:4 * tall] + spec[4 * tall:]
-            kept = min(size, places - start)
-            for pp in range(4):
-                for f in range(everyone):
-                    row = pp * tall + 2 * f
-                    spec_ref[f, pp, :, start:start + kept] = spec[row:row + 2, 0:kept]
-
-    @pl.when(step < near)
-    def _():
-        write(near_ref, pl.multiple_of(deep * step, deep))
-
-    @pl.when(step >= near)
-    def _():
-        far_copy(step - near).wait()
-        write(far_s, pl.multiple_of(deep * (step - near), deep))
+                parts.append(jnp.where(pair_of == pp, full, 0.0))
+        bk[...] = jnp.concatenate(parts, axis=0).astype(BF16)
+
+    rate = rate_ref[...]
+    taus = tau_ref[pl.ds(pl.multiple_of(8 * step, 8), 8), :]
+    mine = mixed_ref[pl.ds(pl.multiple_of(eight * step, 8), eight), :]
+    if eight < LANES:
+        mine = jnp.concatenate([mine, jnp.zeros((LANES - eight, LANES), F32)], axis=0)
+    mine = [
+        jnp.transpose(mine[at:at + LANES])[:, 0:min(eight, LANES)] for at in range(0, eight, LANES)
+    ]
+    mine = jnp.concatenate(mine, axis=1) if len(mine) > 1 else mine[0]
+    mine = jnp.concatenate([mine[0:2 * KPAD], mine[2 * KPAD:4 * KPAD]], axis=1)
+    slot_pair = (lane_iota((2 * KPAD, 2 * eight)) & (eight - 1)) // (2 * lats)
+    left = jnp.concatenate([jnp.where(slot_pair == pp, mine, 0.0) for pp in range(4)], axis=0)
+    left = jnp.concatenate(split(left), axis=1)
+    fetch(step).wait()
+    legs = pl.ds(pl.multiple_of(2 * eight * step, 16), 2 * eight)
+    for start in range(0, span, 2 * LANES):
+        size = min(2 * LANES, span - start)
+        right = eh_s[legs, start:start + size]
+        modes = dot(left, jnp.concatenate([right, right], axis=0))
+        damped = []
+        for pp in range(4):
+            tau = taus[pp:pp + 1, start:start + size]
+            factor = pl.reciprocal(1.0 + tau * rate[:, 0:size], approx=True)
+            at = 2 * pp * KPAD
+            damped.append(modes[at:at + KPAD] * factor)
+            damped.append(modes[at + KPAD:at + 2 * KPAD] * factor)
+        spec = dot(bk[...], jnp.concatenate(damped, axis=0).astype(BF16))
+        spec = spec[0:4 * tall] + spec[4 * tall:]
+        kept = min(size, places - start)
+        for pp in range(4):
+            for f in range(everyone):
+                row = pp * tall + 2 * f
+                spec_ref[f, pp, :, start:start + kept] = spec[row:row + 2, 0:kept]
 
 
 def per_device(grid, row_lengths, band_map, fold_map, legendre, to_modes, back_modes, mode_rates):
@@ -700,20 +681,19 @@
     ]
     arrived = lax.all_to_all(sending, ("lat", "fld"), split_axis=0, concat_axis=0, tiled=True)
 
-    close = 1
-    legs, legs_far, mix, back, turn_back, tau, rate = pl.pallas_call(
+    legs, rounds, mix, back, turn_back, tau, rate = pl.pallas_call(
         functools.partial(prepare_kernel, cut_off, pairs, fields, rows),
         out_shape=(
-            pltpu.VMEM((close * 16 * lats, span), BF16),
-            pltpu.HBM(((groups - close) * 16 * lats, span), BF16),
-            pltpu.VMEM((2 * rows * KPAD, 3 * LANES), BF16),
-            pltpu.VMEM((2 * FPAD, 8 * KPAD), BF16),
-            pltpu.VMEM((FPAD, 6 * KPAD), BF16),
-            pltpu.VMEM((-(-groups * 4 // 8) * 8, span), F32),
-            pltpu.VMEM((KPAD, 2 * LANES), F32),
+            pltpu.HBM((groups * 16 * lats, span), BF16),
+            pltpu.VMEM((groups * 8 * lats * lats, LANES), F32),
+            pltpu.VMEM((LANES, 3 * LANES), BF16),
+            pltpu.HBM((2 * FPAD, 8 * KPAD), BF16),
+            pltpu.VMEM((3 * LANES, LANES), BF16),
+            pltpu.HBM((8 * groups, span), F32),
+            pltpu.HBM((KPAD, 2 * LANES), F32),
         ),
         in_specs=[hbm] * 6,
-        out_specs=(vmem, hbm) + (vmem,) * 5,
+        out_specs=(hbm,) + (vmem,) * 6,
         scratch_shapes=[
             pltpu.SMEM(fold_map.shape, jnp.int32),
             pltpu.SMEM(band_map.shape, jnp.int32),
@@ -723,66 +703,60 @@
             pltpu.VMEM(back_modes.shape, F32),
             dma((6,)),
             pltpu.VMEM((KPAD, LANES), F32),
-            pltpu.VMEM(((groups - close) * 16 * lats, span), BF16),
-            dma((groups - close,)),
+            pltpu.VMEM((groups * 16 * lats, span), BF16),
+            dma((groups,)),
         ],
         compiler_params=room,
         cost_estimate=pl.CostEstimate(flops=10**8, bytes_accessed=8 * 10**6, transcendentals=0),
         name="prepare",
     )(fold_map, band_map, mode_rates, legendre, to_modes, back_modes)
-    legs_far = pltpu.with_memory_space_constraint(legs_far, pltpu.HBM)
-    legs, mix, back, turn_back, tau, rate = (
-        pltpu.with_memory_space_constraint(x, pltpu.VMEM)
-        for x in (legs, mix, back, turn_back, tau, rate)
+    legs, back, tau, rate = (
+        pltpu.with_memory_space_constraint(x, pltpu.HBM) for x in (legs, back, tau, rate)
     )
-
-    near = groups // 2
-    damped_near, damped_far, leaving = pl.pallas_call(
+    rounds, mix, turn_back = (
+        pltpu.with_memory_space_constraint(x, pltpu.VMEM) for x in (rounds, mix, turn_back)
+    )
+
+    mixed, leaving = pl.pallas_call(
         functools.partial(solve_kernel, fields, rows, lats),
         out_shape=(
-            pltpu.VMEM((near * 8 * KPAD, span), BF16),
-            pltpu.HBM(((groups - near) * 8 * KPAD, span), BF16),
+            pltpu.VMEM((groups * 8 * lats, LANES), F32),
             pltpu.HBM((owners * 8, LANES), F32),
         ),
-        in_specs=[hbm] + [vmem] * 6,
-        out_specs=(vmem, hbm, vmem),
-        scratch_shapes=[
-            pltpu.VMEM((groups * 16 * lats, LANES), F32),
-            pltpu.VMEM(((groups - close) * 16 * lats, span), BF16),
-            pltpu.VMEM(((groups - near) * 8 * KPAD, span), BF16),
-            dma,
-            dma((groups - near,)),
-        ],
+        in_specs=[vmem] * 4,
+        out_specs=(vmem,) * 2,
+        scratch_shapes=[pltpu.VMEM((groups * 8 * lats, LANES), F32)],
         compiler_params=room,
         name="solve",
-    )(legs_far, legs, arrived.reshape(owners * 8, LANES), mix, turn_back, tau, rate)
+    )(arrived.reshape(owners * 8, LANES), rounds, mix, turn_back)
     leaving = leaving.reshape(owners, 8, LANES)
 
     returned = lax.all_to_all(leaving, ("lat", "fld"), split_axis=0, concat_axis=0, tiled=True)
 
-    damped_near = pltpu.with_memory_space_constraint(damped_near, pltpu.VMEM)
-    damped_far = pltpu.with_memory_space_constraint(damped_far, pltpu.HBM)
+    mixed = pltpu.with_memory_space_constraint(mixed, pltpu.VMEM)
     spectral = pl.pallas_call(
-        output_kernel,
+        functools.partial(output_kernel, lats),
         grid=(groups,),
         out_shape=jax.ShapeDtypeStruct((everyone, pairs, 2, places), F32),
         in_specs=[
-            pl.BlockSpec((near * 8 * KPAD, span), lambda t: (0, 0)),
             hbm,
-            pl.BlockSpec((2 * FPAD, 8 * KPAD), lambda t: (0, 0)),
+            vmem,
+            vmem,
+            vmem,
+            vmem,
         ],
         out_specs=pl.BlockSpec((everyone, 4, 2, places), lambda t: (0, t, 0, 0)),
         scratch_shapes=[
             pltpu.VMEM((16 * everyone, 8 * KPAD), BF16),
-            pltpu.VMEM(((groups - near) * 8 * KPAD, span), BF16),
-            dma((groups - near,)),
+            pltpu.VMEM((groups * 16 * lats, span), BF16),
+            dma((groups,)),
         ],
         compiler_params=pltpu.CompilerParams(
             dimension_semantics=("arbitrary",), vmem_limit_bytes=ROOM
         ),
         cost_estimate=pl.CostEstimate(flops=10**8, bytes_accessed=8 * 10**6, transcendentals=0),
         name="spectral_output",
-    )(damped_near, damped_far, back)
+    )(legs, mixed, tau, rate, back)
 
     grid_out = pl.pallas_call(
         functools.partial(inverse_kernel, groups),

time: 37.6 us -> 37.5 us (level)
  waiting for transfers between devices: 9.55 us -> 0.97 us
  Pallas kernels: 17.1 us -> 23.3 us
  starting transfers between devices: 9.89 us -> 12.2 us
    pallas_call x1, Pallas kernels: 4.11 us -> 8.72 us  [per_device(): pl.pallas_call(functools.partial(output_kernel, lats), grid=(groups,), ou...]
    all_to_all x1, waiting for transfers between devices: 5.44 us -> 0.97 us  [per_device(): lax.all_to_all(sending, ('lat', 'fld'), split_axis=0, concat_axis=0, tile...]
    pallas_call x1, Pallas kernels: 2.78 us -> 7.25 us  [per_device(): pl.pallas_call(functools.partial(prepare_kernel, cut_off, pairs, fields,...]
    all_to_all x1, waiting for transfers between devices: 4.11 us -> 0.01 us  [per_device(): lax.all_to_all(leaving, ('lat', 'fld'), split_axis=0, concat_axis=0, tile...]
    pallas_call x1, Pallas kernels: 4.12 us -> 1.26 us  [per_device(): pl.pallas_call(functools.partial(solve_kernel, fields, rows, lats), out_s...]
    all_to_all x1, starting transfers between devices: 2.58 us -> 4.88 us  [per_device(): lax.all_to_all(leaving, ('lat', 'fld'), split_axis=0, concat_axis=0, tile...]
  transfers between devices with their start and end apart: 2 -> 2, of which waited for: 2 -> 1; matrix products, arithmetic and copies ran while one was open for 0% -> 0% of each run, Pallas kernels for 19% -> 43%
where the time goes in v15:
time: 37.5 us; the launch traced here: 37.2 us
  Pallas kernels  23.3 us (62%)
  starting transfers between devices  12.2 us (33%)
  waiting for transfers between devices  0.97 us (3%)
  between operations  0.68 us (2%)
    pallas_call x1, Pallas kernels, per_device(): pl.pallas_call(functools.partial(output_kernel, lats), grid=(groups,), ou...  8.72 us
    all_to_all x1, starting transfers between devices, per_device(): lax.all_to_all(sending, ('lat', 'fld'), split_axis=0, concat_axis=0, tile...  7.31 us
    pallas_call x1, Pallas kernels, per_device(): pl.pallas_call(functools.partial(prepare_kernel, cut_off, pairs, fields,...  7.25 us
    all_to_all x1, starting transfers between devices, per_device(): lax.all_to_all(leaving, ('lat', 'fld'), split_axis=0, concat_axis=0, tile...  4.88 us
    pallas_call x1, Pallas kernels, per_device(): pl.pallas_call(functools.partial(forward_kernel, cut_off, groups), out_sh...  3.62 us
    pallas_call x1, Pallas kernels, per_device(): pl.pallas_call(functools.partial(inverse_kernel, groups), out_shape=jax.S...  2.49 us
    pallas_call x1, Pallas kernels, per_device(): pl.pallas_call(functools.partial(solve_kernel, fields, rows, lats), out_s...  1.26 us
    all_to_all x1, waiting for transfers between devices, per_device(): lax.all_to_all(sending, ('lat', 'fld'), split_axis=0, concat_axis=0, tile...  0.97 us
  transfers between devices with their start and end apart: 2, of which 1 were waited for; matrix products, arithmetic and copies ran while one was open for 0% of the time, Pallas kernels for 43%

profile of v15, /device:TPU:0, one launch (start us, length us, event | category | flops | bytes accessed | tf_op | source)
XLA Modules:
  0.0 37.2 jit_solution(1249037320772878511)
XLA Ops:
  0.6 3.6 %forward_rows.1 = (f32[32,8,128]{2,1,0:T(8,128)}, bf16[256,1280]{1,0:T(8,128)(2,1)S(1)}, bf16[256,1280]{1,0:T(8,128)(2,1)S(1)}, f32[24,1280]{1,0:T(8,128)S(1)}, f32[24,1280]{1,0:T(8,128)S(1)}) custom-call(s32[8]{0:T(128)} %len_hbm.3, s32[8]{0:T(128)} %band_hbm.5, s32[32,40]{1,0:T(8,128)} %fold_hbm.3, bf16[5,1,2,5248]{3,2,1,0:T(2,128)(2,1)} %grid_hbm.1), custom_call_target="tpu_custom_call" | custom-call | tf_op jit(solution)/shard_map/forward_rows/pallas_call | solution.py:653
  4.3 7.3 %all-to-all-start = ((f32[32,8,128]{2,1,0:T(8,128)}), f32[32,8,128]{2,1,0:T(8,128)S(1)}, u32[]{:S(2)}, u32[]{:S(2)}) async-start(f32[32,8,128]{2,1,0:T(8,128)} %get-tuple-element.17), calls=%async_computation | async-start | bytes 262144 | tf_op jit(solution)/shard_map/all_to_all | solution.py:682
  11.6 7.3 %prepare.1 = (bf16[640,1408]{1,0:T(8,128)(2,1)}, f32[2560,128]{1,0:T(8,128)S(1)}, bf16[128,384]{1,0:T(8,128)(2,1)S(1)}, bf16[128,192]{1,0:T(8,128)(2,1)}, bf16[3...) custom-call(s32[32,40]{1,0:T(8,128)} %fold_hbm.3, s32[8]{0:T(128)} %band_hbm.5, f32[20]{0:T(128)} %rates_hbm.1, ...), custom_call_target="tpu_custom_call" | custom-call | flops 100000000 | bytes 8000000 | tf_op jit(solution)/shard_map/prepare/pallas_call | solution.py:684
  18.8 1.0 %all-to-all-done = f32[32,8,128]{2,1,0:T(8,128)S(1)} async-done(((f32[32,8,128]{2,1,0:T(8,128)}), f32[32,8,128]{2,1,0:T(8,128)S(1)}, u32[]{:S(2)}, u32[]{:S(2)}) %all-to-all-start) | async-done | bytes 131104 | tf_op jit(solution)/shard_map/all_to_all | solution.py:682
  19.8 1.3 %solve.1 = (f32[320,128]{1,0:T(8,128)S(1)}, f32[256,128]{1,0:T(8,128)}) custom-call(f32[256,128]{1,0:T(8,128)S(1)} %bitcast.4, f32[2560,128]{1,0:T(8,128)S(1)} %get-tuple-element.18.round_ref, bf16[128,384]{1,0:T(8,128)(2,1)S(1)} %get-tuple-element.19.mix_ref, bf16[384,128]{1,0:T(8,128)(2,1)S(1)} %get-tuple-element.20.turn_ref), custom_call_target="tpu_custom_call" | custom-call | tf_op jit(solution)/shard_map/solve/pallas_call | solution.py:720
  21.1 4.9 %all-to-all-start.1 = ((f32[32,8,128]{2,1,0:T(8,128)}), f32[32,8,128]{2,1,0:T(8,128)S(1)}, u32[]{:S(2)}, u32[]{:S(2)}) async-start(f32[32,8,128]{2,1,0:T(8,128)} %bitcast.7), calls=%async_computation.1 | async-start | bytes 262144 | tf_op jit(solution)/shard_map/all_to_all | solution.py:734
  25.9 8.7 %spectral_output.1 = f32[20,20,2,1281]{3,2,1,0:T(2,128)} custom-call(bf16[640,1408]{1,0:T(8,128)(2,1)} %get-tuple-element.16.eh_hbm, f32[320,128]{1,0:T(8,128)S(1)} %get-tuple-element.21.mixed_ref, f32[40,1408]{1,0:T(8,128)} %get-tuple-element.22.tau_ref, f32[24,256]{1,0:T(8,128)} %get-tuple-element.23.rate_ref, bf16[128,192]{1,0:T(8,128)(2,1)} %get-tuple-element.24.back_ref), custom_call_target="tpu_custom_call" | custom-call | flops 100000000 | bytes 8000000 | tf_op jit(solution)/shard_map/spectral_output/pallas_call | solution.py:737
  34.7 0.0 all-to-all-done.1.msg_ref
  34.7 2.5 %inverse_rows.1 = bf16[5,1,2,5248]{3,2,1,0:T(2,128)(2,1)} custom-call(s32[8]{0:T(128)} %len_hbm.3, s32[8]{0:T(128)} %band_hbm.5, bf16[256,1280]{1,0:T(8,128)(2,1)S(1)} %get-tuple-element.25.tc, bf16[256,1280]{1,0:T(8,128)(2,1)S(1)} %get-tuple-element.26.ts, f32[24,1280]{1,0:T(8,128)S(1)} %get-tuple-element.27.fc, f32[24,1280]{1,0:T(8,128)S(1)} %get-tuple-element.28.fs, ...), custom_call_target="tpu_custom_call" | custom-call | tf_op jit(solution)/shard_map/inverse_rows/pallas_call | solution.py:761
Async XLA Ops:
  4.3 15.5 %all-to-all-start = ((f32[32,8,128]{2,1,0:T(8,128)}), f32[32,8,128]{2,1,0:T(8,128)S(1)}, u32[]{:S(2)}, u32[]{:S(2)}) async-start(f32[32,8,128]{2,1,0:T(8,128)} %get-tuple-element.17), calls=%async_computation | async-start | bytes 262144 | tf_op jit(solution)/shard_map/all_to_all | solution.py:682
  21.1 13.6 %all-to-all-start.1 = ((f32[32,8,128]{2,1,0:T(8,128)}), f32[32,8,128]{2,1,0:T(8,128)S(1)}, u32[]{:S(2)}, u32[]{:S(2)}) async-start(f32[32,8,128]{2,1,0:T(8,128)} %bitcast.7), calls=%async_computation.1 | async-start | bytes 262144 | tf_op jit(solution)/shard_map/all_to_all | solution.py:734

commit v16 on v15

--- a/solution.py
+++ b/solution.py
@@ -381,8 +381,8 @@
     for piece in split(pad_s[...]):
         wide = dot(piece, pick)
         total = []
-        for parity in range(2):
-            for c in range(2):
+        for c in range(2):
+            for parity in range(2):
                 keep = (lane % 2 == c) & (lane < unit * groups_f)
                 flip = (lane % unit) // wf >= 1 if parity else lane < 0
                 total.append(jnp.where(keep, jnp.where(flip, -wide, wide), 0.0))
@@ -408,8 +408,8 @@
     level = jnp.where(south, lane - width, lane)
     pick = jnp.where(row == (level >> 1), 1.0, 0.0).astype(BF16)
     part = lax.div(row, KPAD)
-    keep = ((part & 1) == (level & 1)) & (part < 4) & (lane < 2 * width)
-    flip = south & (part >= 2)
+    keep = ((part >> 1) == (level & 1)) & (part < 4) & (lane < 2 * width)
+    flip = south & ((part & 1) == 1)
     wide = []
     for piece in split(jnp.transpose(jnp.concatenate([pad_s[...], jnp.zeros((LANES - KPAD, LANES), F32)], axis=0))):
         small = dot(piece, pick)[0:KPAD]
@@ -451,6 +451,7 @@
     row = row_iota((quad_rows, LANES)) // lats
     copies[-1].wait()
     keeps = []
+    todo = []
     for t in range(groups):
         wave = jnp.zeros((quad_rows, LANES), jnp.int32)
         last = jnp.zeros((quad_rows, LANES), jnp.int32)
@@ -492,6 +493,10 @@
         keeps.append(pltpu.make_async_copy(eh_ref.at[part], eh_hbm.at[part], out_sems.at[t]))
         keeps[-1].start()
 
+        todo.append((leg, masks))
+
+    rest = jnp.zeros((LANES - 4 * KPAD, span), F32)
+    for t, (leg, masks) in enumerate(todo):
         for pp in range(4):
             own = leg[pp * lats:(pp + 1) * lats]
             pairs_of = jnp.concatenate([own * own[j:j + 1] for j in range(lats)], axis=0)
@@ -501,13 +506,10 @@
             for side in range(2):
                 for par in range(2):
                     mask = masks[side][par][pp * lats:pp * lats + 8]
-                    part = (factor * jnp.concatenate([mask] * (KPAD // 8), axis=0)).astype(BF16)
-                    damp += [part, part]
-                damp.append(jnp.zeros((LANES - 4 * KPAD, span), BF16))
-            both = dot_nt(pairs_of.astype(BF16), jnp.concatenate([jnp.concatenate(damp[0:2], axis=0), jnp.concatenate(damp[2:4], axis=0), damp[4], jnp.concatenate(damp[5:7], axis=0), jnp.concatenate(damp[7:9], axis=0), damp[9]], axis=0))
-            for side in range(2):
-                at = (2 * pair + side) * lats * lats
-                round_ref[at:at + lats * lats, :] = both[:, LANES * side:LANES * (side + 1)]
+                    damp.append(factor * jnp.concatenate([mask] * (KPAD // 8), axis=0))
+            damp = jnp.concatenate(damp + [rest], axis=0).astype(BF16)
+            at = pair * lats * lats
+            round_ref[at:at + lats * lats, :] = dot_nt(pairs_of.astype(BF16), damp)
     wait_all(keeps)
 
 
@@ -537,14 +539,25 @@
     v_high, v_low = split(jnp.concatenate(tall, axis=0))
     mixed_ref[...] = dot_nt(jnp.concatenate([v_high, v_high, v_low], axis=1), mix_ref[...])
 
+    lane = lane_iota((lats, LANES))
+    front = lane < 2 * KPAD
     sums = []
-    for slot in range(8 * groups):
-        mine = mixed_ref[slot * lats:(slot + 1) * lats, :]
-        total = jnp.zeros((lats, LANES), F32)
+    for pair in range(4 * groups):
+        one = mixed_ref[2 * pair * lats:(2 * pair + 1) * lats, :]
+        two = mixed_ref[(2 * pair + 1) * lats:(2 * pair + 2) * lats, :]
+        parts = (
+            jnp.where(front, one, pltpu.roll(two, 2 * KPAD, 1)),
+            jnp.where(front, pltpu.roll(one, LANES - 2 * KPAD, 1), two),
+        )
+        totals = [jnp.zeros((lats, LANES), F32) for _ in parts]
         for j in range(lats):
-            at = (slot * lats + j) * lats
-            total = total + mine[j:j + 1] * round_ref[at:at + lats, :]
-        sums.append(total)
+            at = (pair * lats + j) * lats
+            matrix = round_ref[at:at + lats, :]
+            totals = [
+                total + part[j:j + 1] * matrix for total, part in zip(totals, parts)
+            ]
+        sums.append(jnp.where(front, totals[0], pltpu.roll(totals[1], 2 * KPAD, 1)))
+        sums.append(jnp.where(front, pltpu.roll(totals[0], LANES - 2 * KPAD, 1), totals[1]))
     high, low = split(jnp.concatenate(sums, axis=0))
     cs[...] = dot(jnp.concatenate([high, low, high], axis=1), turn_ref[...])
 
@@ -600,7 +613,15 @@
         jnp.transpose(mine[at:at + LANES])[:, 0:min(eight, LANES)] for at in range(0, eight, LANES)
     ]
     mine = jnp.concatenate(mine, axis=1) if len(mine) > 1 else mine[0]
-    mine = jnp.concatenate([mine[0:2 * KPAD], mine[2 * KPAD:4 * KPAD]], axis=1)
+    mine = jnp.concatenate(
+        [
+            jnp.concatenate(
+                [mine[par * KPAD:(par + 1) * KPAD], mine[(par + 2) * KPAD:(par + 3) * KPAD]], axis=0
+            )
+            for par in range(2)
+        ],
+        axis=1,
+    )
     slot_pair = (lane_iota((2 * KPAD, 2 * eight)) & (eight - 1)) // (2 * lats)
     left = jnp.concatenate([jnp.where(slot_pair == pp, mine, 0.0) for pp in range(4)], axis=0)
     left = jnp.concatenate(split(left), axis=1)
@@ -685,7 +706,7 @@
         functools.partial(prepare_kernel, cut_off, pairs, fields, rows),
         out_shape=(
             pltpu.HBM((groups * 16 * lats, span), BF16),
-            pltpu.VMEM((groups * 8 * lats * lats, LANES), F32),
+            pltpu.VMEM((groups * 4 * lats * lats, LANES), F32),
             pltpu.VMEM((LANES, 3 * LANES), BF16),
             pltpu.HBM((2 * FPAD, 8 * KPAD), BF16),
             pltpu.VMEM((3 * LANES, LANES), BF16),
@@ -706,7 +727,7 @@
             pltpu.VMEM((groups * 16 * lats, span), BF16),
             dma((groups,)),
         ],
-        compiler_params=room,
+        compiler_params=pltpu.CompilerParams(vmem_limit_bytes=2 * ROOM),
         cost_estimate=pl.CostEstimate(flops=10**8, bytes_accessed=8 * 10**6, transcendentals=0),
         name="prepare",
     )(fold_map, band_map, mode_rates, legendre, to_modes, back_modes)

time: 37.5 us -> 36 us (0.960)
  waiting for transfers between devices: 0.97 us -> 2.58 us
  starting transfers between devices: 12.2 us -> 10.6 us
  Pallas kernels: 23.3 us -> 21.9 us
    all_to_all x1, starting transfers between devices: 4.88 us -> 3.26 us  [per_device(): lax.all_to_all(leaving, ('lat', 'fld'), split_axis=0, concat_axis=0, tile...]
    all_to_all x1, waiting for transfers between devices: 0.97 us -> 2.58 us  [per_device(): lax.all_to_all(sending, ('lat', 'fld'), split_axis=0, concat_axis=0, tile...]
    pallas_call x1, Pallas kernels: 7.25 us -> 5.64 us  [per_device(): pl.pallas_call(functools.partial(prepare_kernel, cut_off, pairs, fields,...]
  transfers between devices with their start and end apart: 2 -> 2, of which waited for: 1 -> 1; matrix products, arithmetic and copies ran while one was open for 0% -> 0% of each run, Pallas kernels for 43% -> 40%
where the time goes in v16:
time: 36 us; the launch traced here: 35.7 us
  Pallas kernels  21.9 us (61%)
  starting transfers between devices  10.6 us (29%)
  waiting for transfers between devices  2.58 us (7%)
  between operations  0.68 us (2%)
    pallas_call x1, Pallas kernels, per_device(): pl.pallas_call(functools.partial(output_kernel, lats), grid=(groups,), ou...  8.72 us
    all_to_all x1, starting transfers between devices, per_device(): lax.all_to_all(sending, ('lat', 'fld'), split_axis=0, concat_axis=0, tile...  7.31 us
    pallas_call x1, Pallas kernels, per_device(): pl.pallas_call(functools.partial(prepare_kernel, cut_off, pairs, fields,...  5.64 us
    pallas_call x1, Pallas kernels, per_device(): pl.pallas_call(functools.partial(forward_kernel, cut_off, groups), out_sh...  3.62 us
    all_to_all x1, starting transfers between devices, per_device(): lax.all_to_all(leaving, ('lat', 'fld'), split_axis=0, concat_axis=0, tile...  3.26 us
    all_to_all x1, waiting for transfers between devices, per_device(): lax.all_to_all(sending, ('lat', 'fld'), split_axis=0, concat_axis=0, tile...  2.58 us
    pallas_call x1, Pallas kernels, per_device(): pl.pallas_call(functools.partial(inverse_kernel, groups), out_shape=jax.S...  2.49 us
    pallas_call x1, Pallas kernels, per_device(): pl.pallas_call(functools.partial(solve_kernel, fields, rows, lats), out_s...  1.41 us
  transfers between devices with their start and end apart: 2, of which 1 were waited for; matrix products, arithmetic and copies ran while one was open for 0% of the time, Pallas kernels for 40%

profile of v16, /device:TPU:0, one launch (start us, length us, event | category | flops | bytes accessed | tf_op | source)
XLA Modules:
  0.0 35.7 jit_solution(15324401023048516114)
XLA Ops:
  0.6 3.6 %forward_rows.1 = (f32[32,8,128]{2,1,0:T(8,128)}, bf16[256,1280]{1,0:T(8,128)(2,1)S(1)}, bf16[256,1280]{1,0:T(8,128)(2,1)S(1)}, f32[24,1280]{1,0:T(8,128)S(1)}, f32[24,1280]{1,0:T(8,128)S(1)}) custom-call(s32[8]{0:T(128)} %len_hbm.3, s32[8]{0:T(128)} %band_hbm.5, s32[32,40]{1,0:T(8,128)} %fold_hbm.3, bf16[5,1,2,5248]{3,2,1,0:T(2,128)(2,1)} %grid_hbm.1), custom_call_target="tpu_custom_call" | custom-call | tf_op jit(solution)/shard_map/forward_rows/pallas_call | solution.py:674
  4.3 7.3 %all-to-all-start = ((f32[32,8,128]{2,1,0:T(8,128)}), f32[32,8,128]{2,1,0:T(8,128)S(1)}, u32[]{:S(2)}, u32[]{:S(2)}) async-start(f32[32,8,128]{2,1,0:T(8,128)} %get-tuple-element.17), calls=%async_computation | async-start | bytes 262144 | tf_op jit(solution)/shard_map/all_to_all | solution.py:703
  11.6 5.6 %prepare.1 = (bf16[640,1408]{1,0:T(8,128)(2,1)}, f32[1280,128]{1,0:T(8,128)S(1)}, bf16[128,384]{1,0:T(8,128)(2,1)S(1)}, bf16[128,192]{1,0:T(8,128)(2,1)}, bf16[3...) custom-call(s32[32,40]{1,0:T(8,128)} %fold_hbm.3, s32[8]{0:T(128)} %band_hbm.5, f32[20]{0:T(128)} %rates_hbm.1, ...), custom_call_target="tpu_custom_call" | custom-call | flops 100000000 | bytes 8000000 | tf_op jit(solution)/shard_map/prepare/pallas_call | solution.py:705
  17.2 2.6 %all-to-all-done = f32[32,8,128]{2,1,0:T(8,128)S(1)} async-done(((f32[32,8,128]{2,1,0:T(8,128)}), f32[32,8,128]{2,1,0:T(8,128)S(1)}, u32[]{:S(2)}, u32[]{:S(2)}) %all-to-all-start) | async-done | bytes 131104 | tf_op jit(solution)/shard_map/all_to_all | solution.py:703
  19.8 1.4 %solve.1 = (f32[320,128]{1,0:T(8,128)S(1)}, f32[256,128]{1,0:T(8,128)}) custom-call(f32[256,128]{1,0:T(8,128)S(1)} %bitcast.4, f32[1280,128]{1,0:T(8,128)S(1)} %get-tuple-element.18.round_ref, bf16[128,384]{1,0:T(8,128)(2,1)S(1)} %get-tuple-element.19.mix_ref, bf16[384,128]{1,0:T(8,128)(2,1)S(1)} %get-tuple-element.20.turn_ref), custom_call_target="tpu_custom_call" | custom-call | tf_op jit(solution)/shard_map/solve/pallas_call | solution.py:741
  21.2 3.3 %all-to-all-start.1 = ((f32[32,8,128]{2,1,0:T(8,128)}), f32[32,8,128]{2,1,0:T(8,128)S(1)}, u32[]{:S(2)}, u32[]{:S(2)}) async-start(f32[32,8,128]{2,1,0:T(8,128)} %bitcast.7), calls=%async_computation.1 | async-start | bytes 262144 | tf_op jit(solution)/shard_map/all_to_all | solution.py:755
  24.5 8.7 %spectral_output.1 = f32[20,20,2,1281]{3,2,1,0:T(2,128)} custom-call(bf16[640,1408]{1,0:T(8,128)(2,1)} %get-tuple-element.16.eh_hbm, f32[320,128]{1,0:T(8,128)S(1)} %get-tuple-element.21.mixed_ref, f32[40,1408]{1,0:T(8,128)} %get-tuple-element.22.tau_ref, f32[24,256]{1,0:T(8,128)} %get-tuple-element.23.rate_ref, bf16[128,192]{1,0:T(8,128)(2,1)} %get-tuple-element.24.back_ref), custom_call_target="tpu_custom_call" | custom-call | flops 100000000 | bytes 8000000 | tf_op jit(solution)/shard_map/spectral_output/pallas_call | solution.py:758
  33.2 0.0 all-to-all-done.1.msg_ref
  33.2 2.5 %inverse_rows.1 = bf16[5,1,2,5248]{3,2,1,0:T(2,128)(2,1)} custom-call(s32[8]{0:T(128)} %len_hbm.3, s32[8]{0:T(128)} %band_hbm.5, bf16[256,1280]{1,0:T(8,128)(2,1)S(1)} %get-tuple-element.25.tc, bf16[256,1280]{1,0:T(8,128)(2,1)S(1)} %get-tuple-element.26.ts, f32[24,1280]{1,0:T(8,128)S(1)} %get-tuple-element.27.fc, f32[24,1280]{1,0:T(8,128)S(1)} %get-tuple-element.28.fs, ...), custom_call_target="tpu_custom_call" | custom-call | tf_op jit(solution)/shard_map/inverse_rows/pallas_call | solution.py:782
Async XLA Ops:
  4.3 15.5 %all-to-all-start = ((f32[32,8,128]{2,1,0:T(8,128)}), f32[32,8,128]{2,1,0:T(8,128)S(1)}, u32[]{:S(2)}, u32[]{:S(2)}) async-start(f32[32,8,128]{2,1,0:T(8,128)} %get-tuple-element.17), calls=%async_computation | async-start | bytes 262144 | tf_op jit(solution)/shard_map/all_to_all | solution.py:703
  21.2 12.0 %all-to-all-start.1 = ((f32[32,8,128]{2,1,0:T(8,128)}), f32[32,8,128]{2,1,0:T(8,128)S(1)}, u32[]{:S(2)}, u32[]{:S(2)}) async-start(f32[32,8,128]{2,1,0:T(8,128)} %bitcast.7), calls=%async_computation.1 | async-start | bytes 262144 | tf_op jit(solution)/shard_map/all_to_all | solution.py:755

commit v17 on v16

--- a/solution.py
+++ b/solution.py
@@ -352,8 +352,9 @@
 
 def prepare_kernel(
     cut_off, pairs, fields, rows, fold_hbm, band_hbm, rates_hbm, leg_hbm, tm_hbm, bm_hbm,
-    eh_hbm, round_ref, mix_ref, back_ref, turn_ref, tau_ref, rate_ref,
+    eh_hbm, round_ref, mix_ref, back_hbm, turn_ref, tau_hbm, rate_hbm,
     fold_ref, band_ref, rates_ref, leg_ref, tm_ref, bm_ref, sems, pad_s, eh_ref, out_sems,
+    back_ref, tau_ref, rate_ref, small_sems,
 ):
     copies = start_all(
         (fold_hbm, band_hbm, rates_hbm, tm_hbm, bm_hbm, leg_hbm),
@@ -450,7 +451,7 @@
     line = lane_iota((quad_rows, span))
     row = row_iota((quad_rows, LANES)) // lats
     copies[-1].wait()
-    keeps = []
+    keeps = start_all((back_ref, tau_ref, rate_ref), (back_hbm, tau_hbm, rate_hbm), small_sems)
     todo = []
     for t in range(groups):
         wave = jnp.zeros((quad_rows, LANES), jnp.int32)
@@ -580,7 +581,8 @@
 
 
 def output_kernel(
-    lats, eh_hbm, mixed_ref, tau_ref, rate_ref, back_ref, spec_ref, bk, eh_s, sems,
+    lats, eh_hbm, tau_hbm, rate_hbm, back_hbm, mixed_ref, spec_ref,
+    bk, eh_s, sems, tau_ref, rate_ref, back_ref, small_sems,
 ):
     everyone, quad, _, places = spec_ref.shape
     span = eh_s.shape[1]
@@ -594,14 +596,13 @@
 
     @pl.when(step == 0)
     def _():
+        small = start_all((back_hbm, tau_hbm, rate_hbm), (back_ref, tau_ref, rate_ref), small_sems)
         for t in range(sems.shape[0]):
             fetch(t).start()
+        wait_all(small)
         pair_of = lane_iota((tall, 8 * KPAD)) // (2 * KPAD)
-        parts = []
-        for part in range(2):
-            full = back_ref[part * FPAD:part * FPAD + tall, :].astype(F32)
-            for pp in range(4):
-                parts.append(jnp.where(pair_of == pp, full, 0.0))
+        full = back_ref[0:tall, :].astype(F32)
+        parts = [jnp.where(pair_of == pp, full, 0.0) for pp in range(4)]
         bk[...] = jnp.concatenate(parts, axis=0).astype(BF16)
 
     rate = rate_ref[...]
@@ -624,13 +625,12 @@
     )
     slot_pair = (lane_iota((2 * KPAD, 2 * eight)) & (eight - 1)) // (2 * lats)
     left = jnp.concatenate([jnp.where(slot_pair == pp, mine, 0.0) for pp in range(4)], axis=0)
-    left = jnp.concatenate(split(left), axis=1)
+    left = left.astype(BF16)
     fetch(step).wait()
     legs = pl.ds(pl.multiple_of(2 * eight * step, 16), 2 * eight)
     for start in range(0, span, 2 * LANES):
         size = min(2 * LANES, span - start)
-        right = eh_s[legs, start:start + size]
-        modes = dot(left, jnp.concatenate([right, right], axis=0))
+        modes = dot(left, eh_s[legs, start:start + size])
         damped = []
         for pp in range(4):
             tau = taus[pp:pp + 1, start:start + size]
@@ -639,7 +639,6 @@
             damped.append(modes[at:at + KPAD] * factor)
             damped.append(modes[at + KPAD:at + 2 * KPAD] * factor)
         spec = dot(bk[...], jnp.concatenate(damped, axis=0).astype(BF16))
-        spec = spec[0:4 * tall] + spec[4 * tall:]
         kept = min(size, places - start)
         for pp in range(4):
             for f in range(everyone):
@@ -714,7 +713,7 @@
             pltpu.HBM((KPAD, 2 * LANES), F32),
         ),
         in_specs=[hbm] * 6,
-        out_specs=(hbm,) + (vmem,) * 6,
+        out_specs=(hbm, vmem, vmem, hbm, vmem, hbm, hbm),
         scratch_shapes=[
             pltpu.SMEM(fold_map.shape, jnp.int32),
             pltpu.SMEM(band_map.shape, jnp.int32),
@@ -726,6 +725,10 @@
             pltpu.VMEM((KPAD, LANES), F32),
             pltpu.VMEM((groups * 16 * lats, span), BF16),
             dma((groups,)),
+            pltpu.VMEM((2 * FPAD, 8 * KPAD), BF16),
+            pltpu.VMEM((8 * groups, span), F32),
+            pltpu.VMEM((KPAD, 2 * LANES), F32),
+            dma((3,)),
         ],
         compiler_params=pltpu.CompilerParams(vmem_limit_bytes=2 * ROOM),
         cost_estimate=pl.CostEstimate(flops=10**8, bytes_accessed=8 * 10**6, transcendentals=0),
@@ -761,23 +764,27 @@
         out_shape=jax.ShapeDtypeStruct((everyone, pairs, 2, places), F32),
         in_specs=[
             hbm,
-            vmem,
-            vmem,
-            vmem,
+            hbm,
+            hbm,
+            hbm,
             vmem,
         ],
         out_specs=pl.BlockSpec((everyone, 4, 2, places), lambda t: (0, t, 0, 0)),
         scratch_shapes=[
-            pltpu.VMEM((16 * everyone, 8 * KPAD), BF16),
+            pltpu.VMEM((8 * everyone, 8 * KPAD), BF16),
             pltpu.VMEM((groups * 16 * lats, span), BF16),
             dma((groups,)),
+            pltpu.VMEM((8 * groups, span), F32),
+            pltpu.VMEM((KPAD, 2 * LANES), F32),
+            pltpu.VMEM((2 * FPAD, 8 * KPAD), BF16),
+            dma((3,)),
         ],
         compiler_params=pltpu.CompilerParams(
             dimension_semantics=("arbitrary",), vmem_limit_bytes=ROOM
         ),
         cost_estimate=pl.CostEstimate(flops=10**8, bytes_accessed=8 * 10**6, transcendentals=0),
         name="spectral_output",
-    )(legs, mixed, tau, rate, back)
+    )(legs, tau, rate, back, mixed)
 
     grid_out = pl.pallas_call(
         functools.partial(inverse_kernel, groups),

time: 36 us -> 35.9 us (level)
  starting transfers between devices: 10.6 us -> 9.91 us
  waiting for transfers between devices: 2.58 us -> 3.24 us
    all_to_all x1, waiting for transfers between devices: 2.58 us -> 3.24 us  [per_device(): lax.all_to_all(sending, ('lat', 'fld'), split_axis=0, concat_axis=0, tile...]
    pallas_call x1, Pallas kernels: 5.64 us -> 4.98 us  [per_device(): pl.pallas_call(functools.partial(prepare_kernel, cut_off, pairs, fields,...]
    all_to_all x1, starting transfers between devices: 3.26 us -> 2.61 us  [per_device(): lax.all_to_all(leaving, ('lat', 'fld'), split_axis=0, concat_axis=0, tile...]
    pallas_call x1, Pallas kernels: 8.72 us -> 9.24 us  [per_device(): pl.pallas_call(functools.partial(output_kernel, lats), grid=(groups,), ou...]
where the time goes in v17:
time: 35.9 us; the launch traced here: 35.6 us
  Pallas kernels  21.7 us (60%)
  starting transfers between devices  9.91 us (28%)
  waiting for transfers between devices  3.24 us (9%)
  between operations  0.68 us (2%)
    pallas_call x1, Pallas kernels, per_device(): pl.pallas_call(functools.partial(output_kernel, lats), grid=(groups,), ou...  9.24 us
    all_to_all x1, starting transfers between devices, per_device(): lax.all_to_all(sending, ('lat', 'fld'), split_axis=0, concat_axis=0, tile...  7.31 us
    pallas_call x1, Pallas kernels, per_device(): pl.pallas_call(functools.partial(prepare_kernel, cut_off, pairs, fields,...  4.98 us
    pallas_call x1, Pallas kernels, per_device(): pl.pallas_call(functools.partial(forward_kernel, cut_off, groups), out_sh...  3.62 us
    all_to_all x1, waiting for transfers between devices, per_device(): lax.all_to_all(sending, ('lat', 'fld'), split_axis=0, concat_axis=0, tile...  3.24 us
    all_to_all x1, starting transfers between devices, per_device(): lax.all_to_all(leaving, ('lat', 'fld'), split_axis=0, concat_axis=0, tile...  2.61 us
    pallas_call x1, Pallas kernels, per_device(): pl.pallas_call(functools.partial(inverse_kernel, groups), out_shape=jax.S...  2.49 us
    pallas_call x1, Pallas kernels, per_device(): pl.pallas_call(functools.partial(solve_kernel, fields, rows, lats), out_s...  1.41 us
  transfers between devices with their start and end apart: 2, of which 1 were waited for; matrix products, arithmetic and copies ran while one was open for 0% of the time, Pallas kernels for 40%

profile of v17, /device:TPU:0, one launch (start us, length us, event | category | flops | bytes accessed | tf_op | source)
XLA Modules:
  0.0 35.6 jit_solution(16112766047460740882)
XLA Ops:
  0.6 3.6 %forward_rows.1 = (f32[32,8,128]{2,1,0:T(8,128)}, bf16[256,1280]{1,0:T(8,128)(2,1)S(1)}, bf16[256,1280]{1,0:T(8,128)(2,1)S(1)}, f32[24,1280]{1,0:T(8,128)S(1)}, f32[24,1280]{1,0:T(8,128)S(1)}) custom-call(s32[8]{0:T(128)} %len_hbm.3, s32[8]{0:T(128)} %band_hbm.5, s32[32,40]{1,0:T(8,128)} %fold_hbm.3, bf16[5,1,2,5248]{3,2,1,0:T(2,128)(2,1)} %grid_hbm.1), custom_call_target="tpu_custom_call" | custom-call | tf_op jit(solution)/shard_map/forward_rows/pallas_call | solution.py:673
  4.3 7.3 %all-to-all-start = ((f32[32,8,128]{2,1,0:T(8,128)}), f32[32,8,128]{2,1,0:T(8,128)S(1)}, u32[]{:S(2)}, u32[]{:S(2)}) async-start(f32[32,8,128]{2,1,0:T(8,128)} %get-tuple-element.20), calls=%async_computation | async-start | bytes 262144 | tf_op jit(solution)/shard_map/all_to_all | solution.py:702
  11.6 5.0 %prepare.1 = (bf16[640,1408]{1,0:T(8,128)(2,1)}, f32[1280,128]{1,0:T(8,128)S(1)}, bf16[128,384]{1,0:T(8,128)(2,1)S(1)}, bf16[128,192]{1,0:T(8,128)(2,1)}, bf16[3...) custom-call(s32[32,40]{1,0:T(8,128)} %fold_hbm.3, s32[8]{0:T(128)} %band_hbm.5, f32[20]{0:T(128)} %rates_hbm.1, ...), custom_call_target="tpu_custom_call" | custom-call | flops 100000000 | bytes 8000000 | tf_op jit(solution)/shard_map/prepare/pallas_call | solution.py:704
  16.6 3.2 %all-to-all-done = f32[32,8,128]{2,1,0:T(8,128)S(1)} async-done(((f32[32,8,128]{2,1,0:T(8,128)}), f32[32,8,128]{2,1,0:T(8,128)S(1)}, u32[]{:S(2)}, u32[]{:S(2)}) %all-to-all-start) | async-done | bytes 131104 | tf_op jit(solution)/shard_map/all_to_all | solution.py:702
  19.8 1.4 %solve.1 = (f32[320,128]{1,0:T(8,128)S(1)}, f32[256,128]{1,0:T(8,128)}) custom-call(f32[256,128]{1,0:T(8,128)S(1)} %bitcast.4, f32[1280,128]{1,0:T(8,128)S(1)} %get-tuple-element.21.round_ref, bf16[128,384]{1,0:T(8,128)(2,1)S(1)} %get-tuple-element.22.mix_ref, bf16[384,128]{1,0:T(8,128)(2,1)S(1)} %get-tuple-element.23.turn_ref), custom_call_target="tpu_custom_call" | custom-call | tf_op jit(solution)/shard_map/solve/pallas_call | solution.py:744
  21.2 2.6 %all-to-all-start.1 = ((f32[32,8,128]{2,1,0:T(8,128)}), f32[32,8,128]{2,1,0:T(8,128)S(1)}, u32[]{:S(2)}, u32[]{:S(2)}) async-start(f32[32,8,128]{2,1,0:T(8,128)} %bitcast.7), calls=%async_computation.1 | async-start | bytes 262144 | tf_op jit(solution)/shard_map/all_to_all | solution.py:758
  23.8 9.2 %spectral_output.1 = f32[20,20,2,1281]{3,2,1,0:T(2,128)} custom-call(bf16[640,1408]{1,0:T(8,128)(2,1)} %get-tuple-element.16.eh_hbm, f32[40,1408]{1,0:T(8,128)} %get-tuple-element.17.tau_hbm, f32[24,256]{1,0:T(8,128)} %get-tuple-element.18.rate_hbm, bf16[128,192]{1,0:T(8,128)(2,1)} %get-tuple-element.19.back_hbm, f32[320,128]{1,0:T(8,128)S(1)} %get-tuple-element.24.mixed_ref), custom_call_target="tpu_custom_call" | custom-call | flops 100000000 | bytes 8000000 | tf_op jit(solution)/shard_map/spectral_output/pallas_call | solution.py:761
  33.1 0.0 all-to-all-done.1.msg_ref
  33.1 2.5 %inverse_rows.1 = bf16[5,1,2,5248]{3,2,1,0:T(2,128)(2,1)} custom-call(s32[8]{0:T(128)} %len_hbm.3, s32[8]{0:T(128)} %band_hbm.5, bf16[256,1280]{1,0:T(8,128)(2,1)S(1)} %get-tuple-element.25.tc, bf16[256,1280]{1,0:T(8,128)(2,1)S(1)} %get-tuple-element.26.ts, f32[24,1280]{1,0:T(8,128)S(1)} %get-tuple-element.27.fc, f32[24,1280]{1,0:T(8,128)S(1)} %get-tuple-element.28.fs, ...), custom_call_target="tpu_custom_call" | custom-call | tf_op jit(solution)/shard_map/inverse_rows/pallas_call | solution.py:789
Async XLA Ops:
  4.3 15.5 %all-to-all-start = ((f32[32,8,128]{2,1,0:T(8,128)}), f32[32,8,128]{2,1,0:T(8,128)S(1)}, u32[]{:S(2)}, u32[]{:S(2)}) async-start(f32[32,8,128]{2,1,0:T(8,128)} %get-tuple-element.20), calls=%async_computation | async-start | bytes 262144 | tf_op jit(solution)/shard_map/all_to_all | solution.py:702
  21.2 11.9 %all-to-all-start.1 = ((f32[32,8,128]{2,1,0:T(8,128)}), f32[32,8,128]{2,1,0:T(8,128)S(1)}, u32[]{:S(2)}, u32[]{:S(2)}) async-start(f32[32,8,128]{2,1,0:T(8,128)} %bitcast.7), calls=%async_computation.1 | async-start | bytes 262144 | tf_op jit(solution)/shard_map/all_to_all | solution.py:758

commit v18 on v17

--- a/solution.py
+++ b/solution.py
@@ -580,65 +580,80 @@
             out_ref[at:at + 8, :] = tiles[g]
 
 
-def output_kernel(
-    lats, eh_hbm, tau_hbm, rate_hbm, back_hbm, mixed_ref, spec_ref,
-    bk, eh_s, sems, tau_ref, rate_ref, back_ref, small_sems,
+def modes_kernel(
+    lats, everyone, legs_hbm, tau_hbm, rate_hbm, back_hbm, mixed_ref, damped_ref, bk_ref,
+    legs_ref, tau_ref, rate_ref, back_ref, sems, small_sems,
 ):
+    small = start_all((back_hbm, tau_hbm, rate_hbm), (back_ref, tau_ref, rate_ref), small_sems)
+    span = legs_ref.shape[1]
+    eight = 8 * lats
+    deep = 8 * KPAD
+    groups = legs_ref.shape[0] // (2 * eight)
+    parts = [pl.ds(0, 2 * eight), pl.ds(2 * eight, 2 * eight * (groups - 1))]
+    fetches = start_all(
+        [legs_hbm.at[part] for part in parts], [legs_ref.at[part] for part in parts], sems
+    )
+    slot_pair = (lane_iota((2 * KPAD, 2 * eight)) & (eight - 1)) // (2 * lats)
+    lefts = []
+    for t in range(groups):
+        mine = mixed_ref[eight * t:eight * (t + 1), :]
+        if eight < LANES:
+            mine = jnp.concatenate([mine, jnp.zeros((LANES - eight, LANES), F32)], axis=0)
+        mine = [
+            jnp.transpose(mine[at:at + LANES])[:, 0:min(eight, LANES)]
+            for at in range(0, eight, LANES)
+        ]
+        mine = jnp.concatenate(mine, axis=1) if len(mine) > 1 else mine[0]
+        mine = jnp.concatenate(
+            [
+                jnp.concatenate(
+                    [mine[par * KPAD:(par + 1) * KPAD], mine[(par + 2) * KPAD:(par + 3) * KPAD]],
+                    axis=0,
+                )
+                for par in range(2)
+            ],
+            axis=1,
+        )
+        left = jnp.concatenate([jnp.where(slot_pair == pp, mine, 0.0) for pp in range(4)], axis=0)
+        lefts.append(jnp.concatenate(split(left), axis=1))
+    wait_all(small)
+    tall = 2 * everyone
+    pair_of = lane_iota((tall, deep)) // (2 * KPAD)
+    blocks = []
+    for part in range(2):
+        full = back_ref[part * FPAD:part * FPAD + tall, :].astype(F32)
+        blocks += [jnp.where(pair_of == pp, full, 0.0) for pp in range(4)]
+    bk_ref[...] = jnp.concatenate(blocks, axis=0).astype(BF16)
+    rate = rate_ref[...]
+    for t in range(groups):
+        if t < 2:
+            fetches[t].wait()
+        for start in range(0, span, 2 * LANES):
+            size = min(2 * LANES, span - start)
+            right = legs_ref[2 * eight * t:2 * eight * (t + 1), start:start + size]
+            modes = dot(lefts[t], jnp.concatenate([right, right], axis=0))
+            damped = []
+            for pp in range(4):
+                tau = tau_ref[8 * t + pp:8 * t + pp + 1, start:start + size]
+                factor = pl.reciprocal(1.0 + tau * rate[:, 0:size], approx=True)
+                at = 2 * pp * KPAD
+                damped.append(modes[at:at + KPAD] * factor)
+                damped.append(modes[at + KPAD:at + 2 * KPAD] * factor)
+            damped_ref[deep * t:deep * (t + 1), start:start + size] = jnp.concatenate(
+                damped, axis=0
+            ).astype(BF16)
+
+
+def output_kernel(damped_ref, bk_ref, spec_ref):
     everyone, quad, _, places = spec_ref.shape
-    span = eh_s.shape[1]
-    eight = 8 * lats
+    span = damped_ref.shape[1]
+    deep = 8 * KPAD
     tall = 2 * everyone
-    step = pl.program_id(0)
-
-    def fetch(t):
-        part = pl.ds(pl.multiple_of(2 * eight * t, 16), 2 * eight)
-        return pltpu.make_async_copy(eh_hbm.at[part], eh_s.at[part], sems.at[t])
-
-    @pl.when(step == 0)
-    def _():
-        small = start_all((back_hbm, tau_hbm, rate_hbm), (back_ref, tau_ref, rate_ref), small_sems)
-        for t in range(sems.shape[0]):
-            fetch(t).start()
-        wait_all(small)
-        pair_of = lane_iota((tall, 8 * KPAD)) // (2 * KPAD)
-        full = back_ref[0:tall, :].astype(F32)
-        parts = [jnp.where(pair_of == pp, full, 0.0) for pp in range(4)]
-        bk[...] = jnp.concatenate(parts, axis=0).astype(BF16)
-
-    rate = rate_ref[...]
-    taus = tau_ref[pl.ds(pl.multiple_of(8 * step, 8), 8), :]
-    mine = mixed_ref[pl.ds(pl.multiple_of(eight * step, 8), eight), :]
-    if eight < LANES:
-        mine = jnp.concatenate([mine, jnp.zeros((LANES - eight, LANES), F32)], axis=0)
-    mine = [
-        jnp.transpose(mine[at:at + LANES])[:, 0:min(eight, LANES)] for at in range(0, eight, LANES)
-    ]
-    mine = jnp.concatenate(mine, axis=1) if len(mine) > 1 else mine[0]
-    mine = jnp.concatenate(
-        [
-            jnp.concatenate(
-                [mine[par * KPAD:(par + 1) * KPAD], mine[(par + 2) * KPAD:(par + 3) * KPAD]], axis=0
-            )
-            for par in range(2)
-        ],
-        axis=1,
-    )
-    slot_pair = (lane_iota((2 * KPAD, 2 * eight)) & (eight - 1)) // (2 * lats)
-    left = jnp.concatenate([jnp.where(slot_pair == pp, mine, 0.0) for pp in range(4)], axis=0)
-    left = left.astype(BF16)
-    fetch(step).wait()
-    legs = pl.ds(pl.multiple_of(2 * eight * step, 16), 2 * eight)
+    at = pl.multiple_of(deep * pl.program_id(0), deep)
     for start in range(0, span, 2 * LANES):
         size = min(2 * LANES, span - start)
-        modes = dot(left, eh_s[legs, start:start + size])
-        damped = []
-        for pp in range(4):
-            tau = taus[pp:pp + 1, start:start + size]
-            factor = pl.reciprocal(1.0 + tau * rate[:, 0:size], approx=True)
-            at = 2 * pp * KPAD
-            damped.append(modes[at:at + KPAD] * factor)
-            damped.append(modes[at + KPAD:at + 2 * KPAD] * factor)
-        spec = dot(bk[...], jnp.concatenate(damped, axis=0).astype(BF16))
+        spec = dot(bk_ref[...], damped_ref[pl.ds(at, deep), start:start + size])
+        spec = spec[0:4 * tall] + spec[4 * tall:]
         kept = min(size, places - start)
         for pp in range(4):
             for f in range(everyone):
@@ -758,33 +773,42 @@
     returned = lax.all_to_all(leaving, ("lat", "fld"), split_axis=0, concat_axis=0, tiled=True)
 
     mixed = pltpu.with_memory_space_constraint(mixed, pltpu.VMEM)
-    spectral = pl.pallas_call(
-        functools.partial(output_kernel, lats),
-        grid=(groups,),
-        out_shape=jax.ShapeDtypeStruct((everyone, pairs, 2, places), F32),
-        in_specs=[
-            hbm,
-            hbm,
-            hbm,
-            hbm,
-            vmem,
-        ],
-        out_specs=pl.BlockSpec((everyone, 4, 2, places), lambda t: (0, t, 0, 0)),
+    cost = pl.CostEstimate(flops=10**8, bytes_accessed=8 * 10**6, transcendentals=0)
+    damped, spread_back = pl.pallas_call(
+        functools.partial(modes_kernel, lats, everyone),
+        out_shape=(
+            pltpu.VMEM((groups * 8 * KPAD, span), BF16),
+            pltpu.VMEM((16 * everyone, 8 * KPAD), BF16),
+        ),
+        in_specs=[hbm] * 4 + [vmem],
+        out_specs=(vmem,) * 2,
         scratch_shapes=[
-            pltpu.VMEM((8 * everyone, 8 * KPAD), BF16),
             pltpu.VMEM((groups * 16 * lats, span), BF16),
-            dma((groups,)),
             pltpu.VMEM((8 * groups, span), F32),
             pltpu.VMEM((KPAD, 2 * LANES), F32),
             pltpu.VMEM((2 * FPAD, 8 * KPAD), BF16),
+            dma((2,)),
             dma((3,)),
         ],
+        compiler_params=room,
+        cost_estimate=cost,
+        name="modes",
+    )(legs, tau, rate, back, mixed)
+    damped, spread_back = (
+        pltpu.with_memory_space_constraint(x, pltpu.VMEM) for x in (damped, spread_back)
+    )
+    spectral = pl.pallas_call(
+        output_kernel,
+        grid=(groups,),
+        out_shape=jax.ShapeDtypeStruct((everyone, pairs, 2, places), F32),
+        in_specs=[vmem, vmem],
+        out_specs=pl.BlockSpec((everyone, 4, 2, places), lambda t: (0, t, 0, 0)),
         compiler_params=pltpu.CompilerParams(
             dimension_semantics=("arbitrary",), vmem_limit_bytes=ROOM
         ),
-        cost_estimate=pl.CostEstimate(flops=10**8, bytes_accessed=8 * 10**6, transcendentals=0),
+        cost_estimate=cost,
         name="spectral_output",
-    )(legs, tau, rate, back, mixed)
+    )(damped, spread_back)
 
     grid_out = pl.pallas_call(
         functools.partial(inverse_kernel, groups),

time: 35.9 us -> 34.8 us (0.969)
  Pallas kernels: 21.7 us -> 19.2 us
  waiting for transfers between devices: 3.24 us -> 4.71 us
    pallas_call x1 -> x2, Pallas kernels: 9.24 us -> 6.74 us  [the longest x1 4.04 us: per_device(): pl.pallas_call(output_kernel, grid=(groups,), out_shape=jax.ShapeDtypeStr...]
    all_to_all x1, waiting for transfers between devices: 0.01 us -> 1.48 us  [per_device(): lax.all_to_all(leaving, ('lat', 'fld'), split_axis=0, concat_axis=0, tile...]
  transfers between devices with their start and end apart: 2 -> 2, of which waited for: 1 -> 2; matrix products, arithmetic and copies ran while one was open for 0% -> 0% of each run, Pallas kernels for 40% -> 34%
where the time goes in v18:
time: 34.8 us; the launch traced here: 34.5 us
  Pallas kernels  19.2 us (55%)
  starting transfers between devices  9.92 us (29%)
  waiting for transfers between devices  4.71 us (14%)
  between operations  0.67 us (2%)
    all_to_all x1, starting transfers between devices, per_device(): lax.all_to_all(sending, ('lat', 'fld'), split_axis=0, concat_axis=0, tile...  7.31 us
    pallas_call x1, Pallas kernels, per_device(): pl.pallas_call(functools.partial(prepare_kernel, cut_off, pairs, fields,...  4.99 us
    pallas_call x1, Pallas kernels, per_device(): pl.pallas_call(output_kernel, grid=(groups,), out_shape=jax.ShapeDtypeStr...  4.04 us
    pallas_call x1, Pallas kernels, per_device(): pl.pallas_call(functools.partial(forward_kernel, cut_off, groups), out_sh...  3.61 us
    all_to_all x1, waiting for transfers between devices, per_device(): lax.all_to_all(sending, ('lat', 'fld'), split_axis=0, concat_axis=0, tile...  3.23 us
    pallas_call x1, Pallas kernels, per_device(): pl.pallas_call(functools.partial(modes_kernel, lats, everyone), out_shape...  2.69 us
    all_to_all x1, starting transfers between devices, per_device(): lax.all_to_all(leaving, ('lat', 'fld'), split_axis=0, concat_axis=0, tile...  2.61 us
    pallas_call x1, Pallas kernels, per_device(): pl.pallas_call(functools.partial(inverse_kernel, groups), out_shape=jax.S...  2.48 us
  transfers between devices with their start and end apart: 2, of which 2 were waited for; matrix products, arithmetic and copies ran while one was open for 0% of the time, Pallas kernels for 34%

profile of v18, /device:TPU:0, one launch (start us, length us, event | category | flops | bytes accessed | tf_op | source)
XLA Modules:
  0.0 34.5 jit_solution(1564850424017719951)
XLA Ops:
  0.6 3.6 %forward_rows.1 = (f32[32,8,128]{2,1,0:T(8,128)}, bf16[256,1280]{1,0:T(8,128)(2,1)S(1)}, bf16[256,1280]{1,0:T(8,128)(2,1)S(1)}, f32[24,1280]{1,0:T(8,128)S(1)}, f32[24,1280]{1,0:T(8,128)S(1)}) custom-call(s32[8]{0:T(128)} %len_hbm.3, s32[8]{0:T(128)} %band_hbm.5, s32[32,40]{1,0:T(8,128)} %fold_hbm.3, bf16[5,1,2,5248]{3,2,1,0:T(2,128)(2,1)} %grid_hbm.1), custom_call_target="tpu_custom_call" | custom-call | tf_op jit(solution)/shard_map/forward_rows/pallas_call | solution.py:688
  4.2 7.3 %all-to-all-start = ((f32[32,8,128]{2,1,0:T(8,128)}), f32[32,8,128]{2,1,0:T(8,128)S(1)}, u32[]{:S(2)}, u32[]{:S(2)}) async-start(f32[32,8,128]{2,1,0:T(8,128)} %get-tuple-element.22), calls=%async_computation | async-start | bytes 262144 | tf_op jit(solution)/shard_map/all_to_all | solution.py:717
  11.6 5.0 %prepare.1 = (bf16[640,1408]{1,0:T(8,128)(2,1)}, f32[1280,128]{1,0:T(8,128)S(1)}, bf16[128,384]{1,0:T(8,128)(2,1)S(1)}, bf16[128,192]{1,0:T(8,128)(2,1)}, bf16[3...) custom-call(s32[32,40]{1,0:T(8,128)} %fold_hbm.3, s32[8]{0:T(128)} %band_hbm.5, f32[20]{0:T(128)} %rates_hbm.1, ...), custom_call_target="tpu_custom_call" | custom-call | flops 100000000 | bytes 8000000 | tf_op jit(solution)/shard_map/prepare/pallas_call | solution.py:719
  16.6 3.2 %all-to-all-done = f32[32,8,128]{2,1,0:T(8,128)S(1)} async-done(((f32[32,8,128]{2,1,0:T(8,128)}), f32[32,8,128]{2,1,0:T(8,128)S(1)}, u32[]{:S(2)}, u32[]{:S(2)}) %all-to-all-start) | async-done | bytes 131104 | tf_op jit(solution)/shard_map/all_to_all | solution.py:717
  19.8 1.4 %solve.1 = (f32[320,128]{1,0:T(8,128)S(1)}, f32[256,128]{1,0:T(8,128)}) custom-call(f32[256,128]{1,0:T(8,128)S(1)} %bitcast.4, f32[1280,128]{1,0:T(8,128)S(1)} %get-tuple-element.23.round_ref, bf16[128,384]{1,0:T(8,128)(2,1)S(1)} %get-tuple-element.24.mix_ref, bf16[384,128]{1,0:T(8,128)(2,1)S(1)} %get-tuple-element.25.turn_ref), custom_call_target="tpu_custom_call" | custom-call | tf_op jit(solution)/shard_map/solve/pallas_call | solution.py:759
  21.2 2.6 %all-to-all-start.1 = ((f32[32,8,128]{2,1,0:T(8,128)}), f32[32,8,128]{2,1,0:T(8,128)S(1)}, u32[]{:S(2)}, u32[]{:S(2)}) async-start(f32[32,8,128]{2,1,0:T(8,128)} %bitcast.7), calls=%async_computation.1 | async-start | bytes 262144 | tf_op jit(solution)/shard_map/all_to_all | solution.py:773
  23.8 2.7 %modes.1 = (bf16[960,1408]{1,0:T(8,128)(2,1)S(1)}, bf16[320,192]{1,0:T(8,128)(2,1)S(1)}) custom-call(bf16[640,1408]{1,0:T(8,128)(2,1)} %get-tuple-element.18.legs_hbm, f32[40,1408]{1,0:T(8,128)} %get-tuple-element.19.tau_hbm, f32[24,256]{1,0:T(8,128)} %get-tuple-element.20.rate_hbm, bf16[128,192]{1,0:T(8,128)(2,1)} %get-tuple-element.21.back_hbm, ...), custom_call_target="tpu_custom_call" | custom-call | flops 100000000 | bytes 8000000 | tf_op jit(solution)/shard_map/modes/pallas_call | solution.py:777
  26.5 4.0 %spectral_output.1 = f32[20,20,2,1281]{3,2,1,0:T(2,128)} custom-call(bf16[960,1408]{1,0:T(8,128)(2,1)S(1)} %get-tuple-element.27.damped_ref, bf16[320,192]{1,0:T(8,128)(2,1)S(1)} %get-tuple-element.28.bk_ref), custom_call_target="tpu_custom_call" | custom-call | flops 100000000 | bytes 8000000 | tf_op jit(solution)/shard_map/spectral_output/pallas_call | solution.py:800
  30.5 1.5 %all-to-all-done.1.msg_ref = f32[32,8,128]{2,1,0:T(8,128)S(1)} async-done(((f32[32,8,128]{2,1,0:T(8,128)}), f32[32,8,128]{2,1,0:T(8,128)S(1)}, u32[]{:S(2)}, u32[]{:S(2)}) %all-to-all-start.1) | async-done | bytes 131104 | tf_op jit(solution)/shard_map/all_to_all | solution.py:773
  32.0 2.5 %inverse_rows.1 = bf16[5,1,2,5248]{3,2,1,0:T(2,128)(2,1)} custom-call(s32[8]{0:T(128)} %len_hbm.3, s32[8]{0:T(128)} %band_hbm.5, bf16[256,1280]{1,0:T(8,128)(2,1)S(1)} %get-tuple-element.29.tc, bf16[256,1280]{1,0:T(8,128)(2,1)S(1)} %get-tuple-element.30.ts, f32[24,1280]{1,0:T(8,128)S(1)} %get-tuple-element.31.fc, f32[24,1280]{1,0:T(8,128)S(1)} %get-tuple-element.32.fs, ...), custom_call_target="tpu_custom_call" | custom-call | tf_op jit(solution)/shard_map/inverse_rows/pallas_call | solution.py:813
Async XLA Ops:
  4.2 15.5 %all-to-all-start = ((f32[32,8,128]{2,1,0:T(8,128)}), f32[32,8,128]{2,1,0:T(8,128)S(1)}, u32[]{:S(2)}, u32[]{:S(2)}) async-start(f32[32,8,128]{2,1,0:T(8,128)} %get-tuple-element.22), calls=%async_computation | async-start | bytes 262144 | tf_op jit(solution)/shard_map/all_to_all | solution.py:717
  21.2 10.8 %all-to-all-start.1 = ((f32[32,8,128]{2,1,0:T(8,128)}), f32[32,8,128]{2,1,0:T(8,128)S(1)}, u32[]{:S(2)}, u32[]{:S(2)}) async-start(f32[32,8,128]{2,1,0:T(8,128)} %bitcast.7), calls=%async_computation.1 | async-start | bytes 262144 | tf_op jit(solution)/shard_map/all_to_all | solution.py:773

commit v19 on v18

--- a/solution.py
+++ b/solution.py
@@ -273,11 +273,10 @@
 
 
 def inverse_kernel(
-    groups, len_hbm, band_hbm, tc, ts, fc, fs, msg_ref, grid_ref,
+    groups, len_hbm, band_hbm, tc, ts, fc, fs, place_ref, gather_ref, msg_ref, grid_ref,
     len_ref, band_ref, sems, os,
 ):
     copies = start_all((len_hbm, band_hbm), (len_ref, band_ref), sems)
-    spread_s = spread_matrix()
     fields, _, rows, width = grid_ref.shape
     owners = msg_ref.shape[0]
     slots = tc.shape[1]
@@ -287,16 +286,7 @@
     pieces = jnp.concatenate([high, low], axis=1)
     used = rows * fields
     tall = 2 * TWICE
-    shape = (tall, LANES)
-    base = slot_lane(row_iota(shape), fields, rows)
-    places = []
-    for t in range(groups):
-        source = (base + unit * t + lax.axis_index("fld") * (fields * 2)) & (LANES - 1)
-        source = jnp.where(base < 0, base, source)
-        places.append(jnp.where(lane_iota(shape) == source, 1.0, 0.0))
-    place = jnp.concatenate(places, axis=0).astype(BF16)
-    place = jnp.concatenate([place, place], axis=1)
-    turned = dot_nt(place, pieces)
+    turned = dot_nt(place_ref[...], pieces)
     block = 2 * LANES
     out = jnp.zeros((TWICE * turns // 2, DEEP), F32)
     def twisted(i):
@@ -336,7 +326,7 @@
             if phase % 2:
                 piece = pltpu.roll(piece, TWICE - used, 0)
             os[16 * c:16 * (c + 1), LANES * phase:LANES * (phase + 1)] = piece[0:16].astype(BF16)
-    merged = dot_nt(os[...], spread_s)
+    merged = dot_nt(os[...], gather_ref[...])
     for c in range(chunks):
         begin = 4 * LANES * c
         size = min(4 * LANES, width - begin)
@@ -581,7 +571,8 @@
 
 
 def modes_kernel(
-    lats, everyone, legs_hbm, tau_hbm, rate_hbm, back_hbm, mixed_ref, damped_ref, bk_ref,
+    lats, everyone, fields, rows, legs_hbm, tau_hbm, rate_hbm, back_hbm, mixed_ref,
+    damped_ref, bk_ref, place_ref, gather_ref,
     legs_ref, tau_ref, rate_ref, back_ref, sems, small_sems,
 ):
     small = start_all((back_hbm, tau_hbm, rate_hbm), (back_ref, tau_ref, rate_ref), small_sems)
@@ -616,6 +607,18 @@
         )
         left = jnp.concatenate([jnp.where(slot_pair == pp, mine, 0.0) for pp in range(4)], axis=0)
         lefts.append(jnp.concatenate(split(left), axis=1))
+    gather_ref[...] = spread_matrix()
+    unit = rows * fields * 2
+    tall = 2 * TWICE
+    shape = (tall, LANES)
+    base = slot_lane(row_iota(shape), fields, rows)
+    places = []
+    for t in range(groups):
+        source = (base + unit * t + lax.axis_index("fld") * (fields * 2)) & (LANES - 1)
+        source = jnp.where(base < 0, base, source)
+        places.append(jnp.where(lane_iota(shape) == source, 1.0, 0.0))
+    place = jnp.concatenate(places, axis=0).astype(BF16)
+    place_ref[...] = jnp.concatenate([place, place], axis=1)
     wait_all(small)
     tall = 2 * everyone
     pair_of = lane_iota((tall, deep)) // (2 * KPAD)
@@ -774,14 +777,16 @@
 
     mixed = pltpu.with_memory_space_constraint(mixed, pltpu.VMEM)
     cost = pl.CostEstimate(flops=10**8, bytes_accessed=8 * 10**6, transcendentals=0)
-    damped, spread_back = pl.pallas_call(
-        functools.partial(modes_kernel, lats, everyone),
+    damped, spread_back, place, gather = pl.pallas_call(
+        functools.partial(modes_kernel, lats, everyone, fields, rows),
         out_shape=(
             pltpu.VMEM((groups * 8 * KPAD, span), BF16),
             pltpu.VMEM((16 * everyone, 8 * KPAD), BF16),
+            pltpu.VMEM((2 * TWICE * groups, 2 * LANES), BF16),
+            pltpu.VMEM((4 * LANES, 4 * LANES), BF16),
         ),
         in_specs=[hbm] * 4 + [vmem],
-        out_specs=(vmem,) * 2,
+        out_specs=(vmem,) * 4,
         scratch_shapes=[
             pltpu.VMEM((groups * 16 * lats, span), BF16),
             pltpu.VMEM((8 * groups, span), F32),
@@ -794,8 +799,9 @@
         cost_estimate=cost,
         name="modes",
     )(legs, tau, rate, back, mixed)
-    damped, spread_back = (
-        pltpu.with_memory_space_constraint(x, pltpu.VMEM) for x in (damped, spread_back)
+    damped, spread_back, place, gather = (
+        pltpu.with_memory_space_constraint(x, pltpu.VMEM)
+        for x in (damped, spread_back, place, gather)
     )
     spectral = pl.pallas_call(
         output_kernel,
@@ -813,7 +819,7 @@
     grid_out = pl.pallas_call(
         functools.partial(inverse_kernel, groups),
         out_shape=jax.ShapeDtypeStruct(grid.shape, BF16),
-        in_specs=[hbm] * 2 + [vmem] * 5,
+        in_specs=[hbm] * 2 + [vmem] * 7,
         out_specs=vmem,
         scratch_shapes=[
             pltpu.SMEM(row_lengths.shape, jnp.int32),
@@ -823,7 +829,7 @@
         ],
         compiler_params=room,
         name="inverse_rows",
-    )(row_lengths, band_map, *tables, returned)
+    )(row_lengths, band_map, *tables, place, gather, returned)
     return (jnp.transpose(spectral, (0, 2, 1, 3)), grid_out)
 
 

time: 34.8 us -> 34.7 us (level)
  transfers between devices with their start and end apart: 2 -> 2, of which waited for: 2 -> 2; matrix products, arithmetic and copies ran while one was open for 0% -> 0% of each run, Pallas kernels for 34% -> 35%
where the time goes in v19:
time: 34.7 us; the launch traced here: 34.4 us
  Pallas kernels  19.3 us (56%)
  starting transfers between devices  9.92 us (29%)
  waiting for transfers between devices  4.54 us (13%)
  between operations  0.67 us (2%)
    all_to_all x1, starting transfers between devices, per_device(): lax.all_to_all(sending, ('lat', 'fld'), split_axis=0, concat_axis=0, tile...  7.31 us
    pallas_call x1, Pallas kernels, per_device(): pl.pallas_call(functools.partial(prepare_kernel, cut_off, pairs, fields,...  4.99 us
    pallas_call x1, Pallas kernels, per_device(): pl.pallas_call(output_kernel, grid=(groups,), out_shape=jax.ShapeDtypeStr...  4.04 us
    pallas_call x1, Pallas kernels, per_device(): pl.pallas_call(functools.partial(forward_kernel, cut_off, groups), out_sh...  3.61 us
    all_to_all x1, waiting for transfers between devices, per_device(): lax.all_to_all(sending, ('lat', 'fld'), split_axis=0, concat_axis=0, tile...  3.23 us
    pallas_call x1, Pallas kernels, per_device(): pl.pallas_call(functools.partial(modes_kernel, lats, everyone, fields, ro...  2.87 us
    all_to_all x1, starting transfers between devices, per_device(): lax.all_to_all(leaving, ('lat', 'fld'), split_axis=0, concat_axis=0, tile...  2.61 us
    pallas_call x1, Pallas kernels, per_device(): pl.pallas_call(functools.partial(inverse_kernel, groups), out_shape=jax.S...  2.39 us
  transfers between devices with their start and end apart: 2, of which 2 were waited for; matrix products, arithmetic and copies ran while one was open for 0% of the time, Pallas kernels for 35%

profile of v19, /device:TPU:0, one launch (start us, length us, event | category | flops | bytes accessed | tf_op | source)
XLA Modules:
  0.0 34.4 jit_solution(149827696474560780)
XLA Ops:
  0.6 3.6 %forward_rows.1 = (f32[32,8,128]{2,1,0:T(8,128)}, bf16[256,1280]{1,0:T(8,128)(2,1)S(1)}, bf16[256,1280]{1,0:T(8,128)(2,1)S(1)}, f32[24,1280]{1,0:T(8,128)S(1)}, f32[24,1280]{1,0:T(8,128)S(1)}) custom-call(s32[8]{0:T(128)} %len_hbm.3, s32[8]{0:T(128)} %band_hbm.5, s32[32,40]{1,0:T(8,128)} %fold_hbm.3, bf16[5,1,2,5248]{3,2,1,0:T(2,128)(2,1)} %grid_hbm.1), custom_call_target="tpu_custom_call" | custom-call | tf_op jit(solution)/shard_map/forward_rows/pallas_call | solution.py:691
  4.2 7.3 %all-to-all-start = ((f32[32,8,128]{2,1,0:T(8,128)}), f32[32,8,128]{2,1,0:T(8,128)S(1)}, u32[]{:S(2)}, u32[]{:S(2)}) async-start(f32[32,8,128]{2,1,0:T(8,128)} %get-tuple-element.24), calls=%async_computation | async-start | bytes 262144 | tf_op jit(solution)/shard_map/all_to_all | solution.py:720
  11.6 5.0 %prepare.1 = (bf16[640,1408]{1,0:T(8,128)(2,1)}, f32[1280,128]{1,0:T(8,128)S(1)}, bf16[128,384]{1,0:T(8,128)(2,1)S(1)}, bf16[128,192]{1,0:T(8,128)(2,1)}, bf16[3...) custom-call(s32[32,40]{1,0:T(8,128)} %fold_hbm.3, s32[8]{0:T(128)} %band_hbm.5, f32[20]{0:T(128)} %rates_hbm.1, ...), custom_call_target="tpu_custom_call" | custom-call | flops 100000000 | bytes 8000000 | tf_op jit(solution)/shard_map/prepare/pallas_call | solution.py:722
  16.6 3.2 %all-to-all-done = f32[32,8,128]{2,1,0:T(8,128)S(1)} async-done(((f32[32,8,128]{2,1,0:T(8,128)}), f32[32,8,128]{2,1,0:T(8,128)S(1)}, u32[]{:S(2)}, u32[]{:S(2)}) %all-to-all-start) | async-done | bytes 131104 | tf_op jit(solution)/shard_map/all_to_all | solution.py:720
  19.8 1.4 %solve.1 = (f32[320,128]{1,0:T(8,128)S(1)}, f32[256,128]{1,0:T(8,128)}) custom-call(f32[256,128]{1,0:T(8,128)S(1)} %bitcast.4, f32[1280,128]{1,0:T(8,128)S(1)} %get-tuple-element.25.round_ref, bf16[128,384]{1,0:T(8,128)(2,1)S(1)} %get-tuple-element.26.mix_ref, bf16[384,128]{1,0:T(8,128)(2,1)S(1)} %get-tuple-element.27.turn_ref), custom_call_target="tpu_custom_call" | custom-call | tf_op jit(solution)/shard_map/solve/pallas_call | solution.py:762
  21.2 2.6 %all-to-all-start.1 = ((f32[32,8,128]{2,1,0:T(8,128)}), f32[32,8,128]{2,1,0:T(8,128)S(1)}, u32[]{:S(2)}, u32[]{:S(2)}) async-start(f32[32,8,128]{2,1,0:T(8,128)} %bitcast.7), calls=%async_computation.1 | async-start | bytes 262144 | tf_op jit(solution)/shard_map/all_to_all | solution.py:776
  23.8 2.9 %modes.1 = (bf16[960,1408]{1,0:T(8,128)(2,1)S(1)}, bf16[320,192]{1,0:T(8,128)(2,1)S(1)}, bf16[240,256]{1,0:T(8,128)(2,1)S(1)}, bf16[512,512]{1,0:T(8,128)(2,1)S(1)}) custom-call(bf16[640,1408]{1,0:T(8,128)(2,1)} %get-tuple-element.20.legs_hbm, f32[40,1408]{1,0:T(8,128)} %get-tuple-element.21.tau_hbm, f32[24,256]{1,0:T(8,128)} %get-tuple-element.22.rate_hbm, ...), custom_call_target="tpu_custom_call" | custom-call | flops 100000000 | bytes 8000000 | tf_op jit(solution)/shard_map/modes/pallas_call | solution.py:780
  26.7 4.0 %spectral_output.1 = f32[20,20,2,1281]{3,2,1,0:T(2,128)} custom-call(bf16[960,1408]{1,0:T(8,128)(2,1)S(1)} %get-tuple-element.29.damped_ref, bf16[320,192]{1,0:T(8,128)(2,1)S(1)} %get-tuple-element.30.bk_ref), custom_call_target="tpu_custom_call" | custom-call | flops 100000000 | bytes 8000000 | tf_op jit(solution)/shard_map/spectral_output/pallas_call | solution.py:806
  30.7 1.3 %all-to-all-done.1.msg_ref = f32[32,8,128]{2,1,0:T(8,128)S(1)} async-done(((f32[32,8,128]{2,1,0:T(8,128)}), f32[32,8,128]{2,1,0:T(8,128)S(1)}, u32[]{:S(2)}, u32[]{:S(2)}) %all-to-all-start.1) | async-done | bytes 131104 | tf_op jit(solution)/shard_map/all_to_all | solution.py:776
  32.0 2.4 %inverse_rows.1 = bf16[5,1,2,5248]{3,2,1,0:T(2,128)(2,1)} custom-call(s32[8]{0:T(128)} %len_hbm.3, s32[8]{0:T(128)} %band_hbm.5, bf16[256,1280]{1,0:T(8,128)(2,1)S(1)} %get-tuple-element.31.tc, bf16[256,1280]{1,0:T(8,128)(2,1)S(1)} %get-tuple-element.32.ts, f32[24,1280]{1,0:T(8,128)S(1)} %get-tuple-element.33.fc, f32[24,1280]{1,0:T(8,128)S(1)} %get-tuple-element.34.fs, ...), custom_call_target="tpu_custom_call" | custom-call | tf_op jit(solution)/shard_map/inverse_rows/pallas_call | solution.py:819
Async XLA Ops:
  4.2 15.5 %all-to-all-start = ((f32[32,8,128]{2,1,0:T(8,128)}), f32[32,8,128]{2,1,0:T(8,128)S(1)}, u32[]{:S(2)}, u32[]{:S(2)}) async-start(f32[32,8,128]{2,1,0:T(8,128)} %get-tuple-element.24), calls=%async_computation | async-start | bytes 262144 | tf_op jit(solution)/shard_map/all_to_all | solution.py:720
  21.2 10.8 %all-to-all-start.1 = ((f32[32,8,128]{2,1,0:T(8,128)}), f32[32,8,128]{2,1,0:T(8,128)S(1)}, u32[]{:S(2)}, u32[]{:S(2)}) async-start(f32[32,8,128]{2,1,0:T(8,128)} %bitcast.7), calls=%async_computation.1 | async-start | bytes 262144 | tf_op jit(solution)/shard_map/all_to_all | solution.py:776
